TPU v7x, 32 devices: a whole 2x2x4 slice. The times are simulated.
32 devices in a mesh: rep: 2 (over x), wide: 16 (over z, y, core).
Axes of the slice: x: 2, y: 2, z: 4, core: 2. Of those that a mesh axis runs over, the one named last changes fastest.
Arguments:
- prompt_hidden: bfloat16 [4096, 8192], P(('rep', 'wide')), parts along dimension 0, may hold values from -6 to 6
- resident_latent: bfloat16 [64, 1024, 256], P(('rep', 'wide')), parts along dimension 0, may hold values from -6 to 6
- row_target: int32 [4096], P(('rep', 'wide')), parts along dimension 0, may hold values from 0 to 31, as said below
- row_offset: int32 [4096], P(('rep', 'wide')), parts along dimension 0, may hold values from 0 to 1023, as said below
- context_len: int32 [64], P(('rep', 'wide')), parts along dimension 0, may hold values from 1 to 1024, as said below
- draft_hidden: bfloat16 [64, 4, 8192], P(('rep', 'wide')), parts along dimension 0, may hold values from -6 to 6
- draft_query_heads: bfloat16 [64, 4, 8192], P(('rep', 'wide')), parts along dimension 0, may hold values from -60 to 60
- down_weight: bfloat16 [8192, 256], P('wide'), may hold values from -0.0625 to 0.0625
- key_up_weight: bfloat16 [256, 1024], replicated, may hold values from -0.375 to 0.375
- value_up_weight: bfloat16 [256, 1024], replicated, may hold values from -0.375 to 0.375
Outputs:
- attended: bfloat16 [64, 4, 8192], P(('rep', 'wide')), parts along dimension 0
There are 2 independent parts, one for each index of `rep`. A program takes and returns all parts, laid end to end along the dimension named above; an argument that names none is the same for every part. Nothing has to cross between parts.
Inputs may be any that keep to these rules, and one draw needn't show every extreme that they name: row_target // 2 is the device that decodes the request; the rows held by one device name any one such device at most 16 times and some device exactly 16 times. `row_offset`: the rows of one request take distinct positions that, after its resident rows, fill positions up to context_len of that request exactly: a request with k prompt rows has its resident rows at positions below context_len - k. `context_len`: at least the number of prompt rows of the request.
All inputs are finite; a program needn't handle non-finite values.
Results may differ from a plain program's by a relative error of at most 0.0062.
Values may be sent and summed in bfloat16 or wider, within the bound.
No kernel may reach another device: no remote copies, remote signals or barrier semaphores. Data moves between devices by JAX's collectives and lax.ppermute only.
A program may use at most 128 MiB of HBM per device.

v0:
```python
import math

import jax
import jax.numpy as jnp
from jax import lax
from jax.sharding import PartitionSpec as P

QUERY_HEADS = 64
HEAD_SIZE = 128


def softmax_parts(cache_scores, draft_scores, context_len):
    span_rows = cache_scores.shape[-1]
    draft_count = draft_scores.shape[-1]
    visible = jnp.arange(span_rows, dtype=jnp.int32)[None, :] < context_len[:, None]
    cache_scores = jnp.where(visible[:, None, None, None, :], cache_scores, -jnp.inf)
    causal = jnp.arange(draft_count)[None, :] <= jnp.arange(draft_count)[:, None]
    draft_scores = jnp.where(causal[None, :, None, None, :], draft_scores, -jnp.inf)
    peak_score = jnp.maximum(
        jnp.max(cache_scores, -1, keepdims=True), jnp.max(draft_scores, -1, keepdims=True)
    )
    cache_exp = jnp.exp(cache_scores - peak_score)
    draft_exp = jnp.exp(draft_scores - peak_score)
    denominator = jnp.sum(cache_exp, -1, keepdims=True) + jnp.sum(draft_exp, -1, keepdims=True)
    return (cache_exp / denominator, draft_exp / denominator)


def expanded_attention(
    kv_table, query_float, draft_key_rows, draft_value_rows, context_len, slot_count, span_rows
):
    high = lax.Precision.HIGHEST
    heads_kv = draft_key_rows.shape[2]
    key_value_width = heads_kv * HEAD_SIZE
    score_scale = 1.0 / math.sqrt(HEAD_SIZE)
    key_rows = kv_table[:, :key_value_width].reshape(slot_count, span_rows, heads_kv, HEAD_SIZE)
    value_rows = kv_table[:, key_value_width:].reshape(slot_count, span_rows, heads_kv, HEAD_SIZE)
    cache_scores = (
        jnp.einsum("bikgd,bpkd->bikgp", query_float, key_rows, precision=high) * score_scale
    )
    draft_scores = (
        jnp.einsum("bikgd,bjkd->bikgj", query_float, draft_key_rows, precision=high) * score_scale
    )
    cache_weights, draft_weights = softmax_parts(cache_scores, draft_scores, context_len)
    result = jnp.einsum("bikgp,bpkd->bikgd", cache_weights, value_rows, precision=high)
    return result + jnp.einsum("bikgj,bjkd->bikgd", draft_weights, draft_value_rows, precision=high)


def local(
    prompt_hidden,
    resident_latent,
    row_target,
    row_offset,
    context_len,
    draft_hidden,
    draft_query_heads,
    down_weight,
    key_up_weight,
    value_up_weight,
):
    wide_size = lax.axis_size("wide")
    row_count = prompt_hidden.shape[0]
    slot_count, span_rows, latent_width = resident_latent.shape
    draft_count = draft_hidden.shape[1]
    model_width = draft_hidden.shape[2]
    key_value_width = key_up_weight.shape[1]
    heads_kv = key_value_width // HEAD_SIZE
    group_size = QUERY_HEADS // heads_kv
    most_rows = 2 * ((row_count + wide_size - 1) // wide_size)
    draft_flat = draft_hidden.reshape(slot_count * draft_count, model_width)
    w_piece = lax.all_gather(down_weight, "wide", axis=0, tiled=True)
    prompt_sum = jnp.dot(prompt_hidden, w_piece, preferred_element_type=jnp.float32)
    draft_sum = jnp.dot(draft_flat, w_piece, preferred_element_type=jnp.float32)
    latent = prompt_sum.astype(jnp.bfloat16)
    draft_latent = draft_sum.astype(jnp.bfloat16)
    up_both = jnp.concatenate([key_up_weight, value_up_weight], 1)
    draft_lookup_table = jnp.dot(draft_latent, up_both, preferred_element_type=jnp.float32)
    draft_key_rows = draft_lookup_table[:, :key_value_width].reshape(
        slot_count, draft_count, heads_kv, HEAD_SIZE
    )
    draft_value_rows = draft_lookup_table[:, key_value_width:].reshape(
        slot_count, draft_count, heads_kv, HEAD_SIZE
    )
    query_float = draft_query_heads.astype(jnp.float32).reshape(
        slot_count, draft_count, heads_kv, group_size, HEAD_SIZE
    )
    target_device = row_target // slot_count
    onehot = (target_device[:, None] == jnp.arange(wide_size, dtype=jnp.int32)[None, :]).astype(
        jnp.int32
    )
    earlier = jnp.sum(jnp.cumsum(onehot, 0) * onehot, 1) - 1
    send_place = target_device * most_rows + earlier
    land_code = row_target % slot_count * span_rows + row_offset
    landing = jnp.full((wide_size * most_rows,), -1, jnp.int32).at[send_place].set(land_code)
    landing = landing.reshape(wide_size, most_rows)
    resident_flat = resident_latent.reshape(slot_count * span_rows, latent_width)
    outside = slot_count * span_rows
    expanded = jnp.dot(latent, up_both, preferred_element_type=jnp.float32)
    outgoing = (
        jnp.zeros((wide_size * most_rows, 2 * key_value_width), jnp.float32)
        .at[send_place]
        .set(expanded)
    )
    incoming, arrived_codes = (
        lax.all_to_all(
            outgoing.reshape(wide_size, most_rows, 2 * key_value_width),
            "wide",
            split_axis=0,
            concat_axis=0,
            tiled=True,
        ),
        lax.all_to_all(landing, "wide", split_axis=0, concat_axis=0, tiled=True),
    )
    land_index = jnp.where(arrived_codes >= 0, arrived_codes, outside).reshape(-1)
    kv_table = jnp.dot(resident_flat, up_both, preferred_element_type=jnp.float32)
    kv_table = kv_table.at[land_index].set(incoming.reshape(-1, 2 * key_value_width), mode="drop")
    result = expanded_attention(
        kv_table, query_float, draft_key_rows, draft_value_rows, context_len, slot_count, span_rows
    )
    return result.reshape(slot_count, draft_count, QUERY_HEADS * HEAD_SIZE).astype(jnp.bfloat16)


def solution(mesh):
    placed = (
        P(("rep", "wide"), None),
        P(("rep", "wide"), None, None),
        P(("rep", "wide")),
        P(("rep", "wide")),
        P(("rep", "wide")),
        P(("rep", "wide"), None, None),
        P(("rep", "wide"), None, None),
        P("wide", None),
        P(),
        P(),
    )
    return jax.shard_map(
        local, mesh=mesh, in_specs=placed, out_specs=P(("rep", "wide"), None, None), check_vma=False
    )
```

profile of v0, /device:TPU:13, one launch (start us, length us, event | category | flops | bytes accessed | tf_op | source)
XLA Modules:
  0.0 172.7 jit_solution(11486172711911000561)
XLA Ops:
  6.5 0.7 all-gather.2.cloned.1.call-update
  7.3 0.7 fusion.31
  8.0 0.2 reduce_window_sum.11
  8.2 0.2 select_reduce_fusion
  8.4 1.0 scatter_custom_fusion
  9.4 0.7 all_to_all.11
  10.1 6.6 %all-to-all-start = ((s32[16,1,16]{2,1,0:T(1,128)}), s32[16,1,16]{2,1,0:T(1,128)S(1)}, u32[]{:S(2)}, u32[]{:S(2)}) async-start(s32[16,1,16]{2,1,0:T(1,128)} %all_to_all.11), calls=%async_computation | async-start | bytes 16384 | tf_op jit(solution)/shard_map/all_to_all | solution.py:111
  16.6 1.1 constant_dynamic-update-slice_fusion.1
  17.7 1.1 constant_dynamic-update-slice_fusion
  18.8 41.9 %all-gather.2.cloned.1.call-done = bf16[8192,256]{1,0:T(8,128)(2,1)} async-done(((bf16[512,256]{1,0:T(8,128)(2,1)}), bf16[8192,256]{1,0:T(8,128)(2,1)}) %all-gather.2.cloned.1.call-update) | async-done | bytes 4194320 | tf_op jit(solution)/shard_map/all_gather | solution.py:70
  60.7 4.4 %fusion.12 = f32[128,2048]{1,0:T(8,128)} fusion(bf16[256,2048]{1,0:T(8,128)(2,1)S(1)} %constant_dynamic-update-slice_fusion, bf16[128,8192]{1,0:T(8,128)(2,1)S(1)} %copy-done, bf16[8192,256]{1,0:T(8,128)(2,1)} %all-gather.2.cloned.1.call-done), kind=kOutput, calls=%fused_computation.25 | convolution fusion | flops 671121408 | bytes 8388608 | tf_op jit(solution)/shard_map/dot_general | solution.py:97
  65.1 3.3 %scatter_custom_fusion.1 = f32[256,2048]{1,0:T(8,128)} fusion(s32[128]{0:T(128)S(1)} %compare_select_fusion.2, f32[128,2048]{1,0:T(8,128)} %fusion.12, f32[]{:T(128)} %constant.51.clone.1), kind=kCustom, calls=%fused_computation.32 | custom fusion | bytes 2097664 | tf_op jit(solution)/shard_map/scatter | solution.py:101
  68.4 5.0 %all-to-all-start.1 = ((f32[16,16,2048]{2,1,0:T(8,128)}), f32[16,16,2048]{2,1,0:T(8,128)S(1)}, u32[]{:S(2)}, u32[]{:S(2)}) async-start(f32[16,16,2048]{2,1,0:T(8,128)} %bitcast.66), calls=%async_computation.1 | async-start | bytes 4194304 | tf_op jit(solution)/shard_map/all_to_all | solution.py:104
  73.4 0.2 reshape.110
  73.7 9.3 %convolution_bitcast_fusion = f32[2048,2048]{0,1:T(8,128)} fusion(bf16[256,2048]{1,0:T(8,128)(2,1)S(1)} %constant_dynamic-update-slice_fusion, bf16[2048,256]{1,0:T(8,128)(2,1)} %bitcast.67), kind=kOutput, calls=%fused_computation.3 | convolution fusion | flops 2147483648 | bytes 18874368 | tf_op jit(solution)/shard_map/dot_general | solution.py:114
  83.0 17.6 %copy.16 = f32[2048,2048]{1,0:T(8,128)} copy(f32[2048,2048]{0,1:T(8,128)} %convolution_bitcast_fusion) | data formatting | bytes 33554432 | tf_op jit(solution)/shard_map/dot_general | solution.py:114
  100.7 0.5 broadcast.97
  101.2 0.7 reduce.3
  102.0 3.3 %fusion.13 = f32[8,2048]{1,0:T(8,128)S(1)} fusion(bf16[256,2048]{1,0:T(8,128)(2,1)S(1)} %constant_dynamic-update-slice_fusion, bf16[8,8192]{1,0:T(8,128)(2,1)S(1)} %reshape.111, bf16[8192,256]{1,0:T(8,128)(2,1)} %all-gather.2.cloned.1.call-done), kind=kOutput, calls=%fused_computation.27 | convolution fusion | flops 41945088 | bytes 5439488 | tf_op jit(solution)/shard_map/dot_general | solution.py:76
  105.3 1.9 %fusion.36 = (f32[2,4,8,8]{3,1,2,0:T(4,128)S(1)}, f32[2,4,8,8,4]{3,4,1,2,0:T(4,128)S(1)}) fusion(bf16[2,4,8,8,128]{4,3,2,1,0:T(8,128)(2,1)S(1)} %reshape.110, f32[2,4,8,128,1]{3,2,1,0,4:T(8,128)S(1)} %bitcast.69, pred[4,4]{1,0:T(4,128)(4,1)S(1)} %iota_compare_fusion.2), kind=kOutput, calls=%fused_computation.67 | convolution fusion | flops 3151360 | bytes 174096 | tf_op jit(solution)/shard_map/bikgd,bjkd->bikgj/dot_general | solution.py:41
  107.2 13.7 %all-to-all-done.1 = f32[16,16,2048]{2,1,0:T(8,128)S(1)} async-done(((f32[16,16,2048]{2,1,0:T(8,128)}), f32[16,16,2048]{2,1,0:T(8,128)S(1)}, u32[]{:S(2)}, u32[]{:S(2)}) %all-to-all-start.1) | async-done | bytes 2097184 | tf_op jit(solution)/shard_map/all_to_all | solution.py:104
  120.9 13.3 %scatter_fusion = f32[2048,2048]{1,0:T(8,128)} fusion(f32[2048,2048]{1,0:T(8,128)} %copy.16, s32[256]{0:T(256)S(1)} %bitcast.70, f32[256,2048]{1,0:T(8,128)S(1)} %bitcast.65), kind=kCustom, calls=%fused_computation.2 | custom fusion | bytes 6292480 | tf_op jit(solution)/shard_map/scatter | solution.py:115
  134.1 9.3 %slice_bitcast_fusion = (f32[256,8,8,128]{3,1,2,0:T(8,128)S(1)}, f32[256,8,8,128]{3,1,2,0:T(8,128)}) fusion(f32[2048,2048]{1,0:T(8,128)} %scatter_fusion), kind=kLoop, calls=%fused_computation.6 | loop fusion | bytes 33554432
  143.5 2.1 %copy.37 = f32[256,8,8,128]{3,2,1,0:T(8,128)S(1)} copy(f32[256,8,8,128]{3,1,2,0:T(8,128)S(1)} %get-tuple-element.5) | data formatting | bytes 16777216
  145.6 0.5 bitcast_bitcast_fusion
  146.1 5.4 %bitcast_reduce_fusion = (f32[2,4,8,8]{3,1,2,0:T(4,128)S(1)}, f32[2,8,1024,4,8]{2,4,3,1,0:T(8,128)S(1)}) fusion(pred[2,1024]{1,0:T(4,128)(4,1)S(1)} %iota_compare_fusion.1, bf16[2,4,8,8,128]{4,3,2,1,0:T(8,128)(2,1)S(1)} %reshape.110, f32[2,1024,8,128,1]{3,2,1,0,4:T(8,128)S(1)} %bitcast_bitcast_fusion), kind=kOutput, calls=%fused_computation.13 | convolution fusion | flops 806878720 | bytes 10620928 | tf_op jit(solution)/shard_map/bikgd,bpkd->bikgp/dot_general | solution.py:38
  151.7 0.6 fusion.7
  152.3 5.5 %copy.36 = f32[256,8,8,128]{3,2,1,0:T(8,128)S(1)} copy(f32[256,8,8,128]{3,1,2,0:T(8,128)} %get-tuple-element.6) | data formatting | bytes 16777216
  157.7 0.5 bitcast_bitcast_fusion.1
  158.3 6.2 %fusion.2 = f32[2,8,128,4,8]{2,4,3,1,0:T(8,128)S(1)} fusion(f32[2,1024,8,128,1]{3,2,1,0,4:T(8,128)S(1)} %bitcast_bitcast_fusion.1, f32[2,8,1024,4,8]{2,4,3,1,0:T(8,128)S(1)} %get-tuple-element.12, f32[2,4,8,8]{3,1,2,0:T(4,128)S(1)} %add.46, f32[2,4,8,8]{3,1,2,0:T(4,128)S(1)} %max.8, pred[2,1024]{1,0:T(4,128)(4,1)S(1)} %iota_compare_fusion.1), kind=kOutput, calls=%fused_computation.10 | convolution fusion | flops 807403520 | bytes 10754048 | tf_op jit(solution)/shard_map/bikgp,bpkd->bikgd/dot_general | solution.py:44
  164.6 0.6 fusion.9
  165.2 0.7 convert_element_type.24
  (26 shorter events, 0.5 us)
Async XLA Ops:
  6.5 54.2 %copy-start = (bf16[128,8192]{1,0:T(8,128)(2,1)S(1)}, bf16[128,8192]{1,0:T(8,128)(2,1)}, u32[]{:S(2)}) copy-start(bf16[128,8192]{1,0:T(8,128)(2,1)} %param.10) | copy-start | bytes 6291460
  6.5 54.2 %all-gather.2.cloned.1.call-start = ((), (), s32[]{:S(2)}) async-start(), calls=%async_computation.2 | async-start | bytes 4456448 | tf_op jit(solution)/shard_map/all_gather | solution.py:70
  10.1 58.4 %all-to-all-start = ((s32[16,1,16]{2,1,0:T(1,128)}), s32[16,1,16]{2,1,0:T(1,128)S(1)}, u32[]{:S(2)}, u32[]{:S(2)}) async-start(s32[16,1,16]{2,1,0:T(1,128)} %all_to_all.11), calls=%async_computation | async-start | bytes 16384 | tf_op jit(solution)/shard_map/all_to_all | solution.py:111
  68.4 5.0 %copy-start.2 = (bf16[2,4,8192]{2,1,0:T(4,128)(2,1)S(1)}, bf16[2,4,8192]{2,1,0:T(4,128)(2,1)}, u32[]{:S(2)}) copy-start(bf16[2,4,8192]{2,1,0:T(4,128)(2,1)} %param.16) | copy-start | bytes 393220
  68.4 5.2 %copy-start.3 = (bf16[2,4,8192]{2,1,0:T(4,128)(2,1)S(1)}, bf16[2,4,8192]{2,1,0:T(4,128)(2,1)}, u32[]{:S(2)}) copy-start(bf16[2,4,8192]{2,1,0:T(4,128)(2,1)} %param.15) | copy-start | bytes 393220
  68.4 52.4 %all-to-all-start.1 = ((f32[16,16,2048]{2,1,0:T(8,128)}), f32[16,16,2048]{2,1,0:T(8,128)S(1)}, u32[]{:S(2)}, u32[]{:S(2)}) async-start(f32[16,16,2048]{2,1,0:T(8,128)} %bitcast.66), calls=%async_computation.1 | async-start | bytes 4194304 | tf_op jit(solution)/shard_map/all_to_all | solution.py:104
  83.0 17.6 %copy-start.4 = (s32[2]{0:T(128)S(1)}, s32[2]{0:T(128)}, u32[]{:S(2)}) copy-start(s32[2]{0:T(128)} %param.14) | copy-start | bytes 28
  158.3 7.6 %copy-start.1 = (bf16[128,8192]{1,0:T(8,128)(2,1)S(1)}, bf16[128,8192]{1,0:T(8,128)(2,1)}, u32[]{:S(2)}) copy-start(bf16[128,8192]{1,0:T(8,128)(2,1)} %param.10) | copy-start | bytes 6291460
Sparse Core Ops, SparseCore 0:
  9.5 51.1 all-gather.1
where the time goes:
time: 174 us; the launch traced here: 173 us
  local copies, waits for them, and re-layouts  57.5 us (33%)
  waiting for transfers between devices  56.3 us (32%)
  matrix products  31.2 us (18%)
  between operations  13.6 us (8%)
  starting transfers between devices  11.6 us (7%)
  other arithmetic  2.61 us (2%)
    all_gather x1, waiting for transfers between devices, local(): w_piece = lax.all_gather(down_weight, 'wide', axis=0, tiled=True)  41.9 us
    unnamed x17, local copies, waits for them, and re-layouts  18 us
    dot_general x1, local copies, waits for them, and re-layouts, local(): jnp.dot(resident_flat, up_both, preferred_element_type=jnp.float32)  17.6 us
    all_to_all x1, waiting for transfers between devices, local(): lax.all_to_all(outgoing.reshape(wide_size, most_rows, 2 * key_value_width...  13.7 us
    scatter x1, local copies, waits for them, and re-layouts, local(): kv_table.at[land_index]  13.3 us
    dot_general x1, matrix products, local(): jnp.dot(resident_flat, up_both, preferred_element_type=jnp.float32)  9.35 us
    all_to_all x1, starting transfers between devices, local(): lax.all_to_all(landing, 'wide', split_axis=0, concat_axis=0, tiled=True)  6.55 us
    dot_general x1, matrix products, expanded_attention(): jnp.einsum('bikgp,bpkd->bikgd', cache_weights, value_rows, precision=high)  6.24 us
  transfers between devices with their start and end apart: 3, of which 2 were waited for; matrix products, arithmetic and copies ran while one was open for 26% of the time, Pallas kernels for 0%

commit v1 on v0

v1 whole, which is shorter than its diff:
```python
import math

import jax
import jax.numpy as jnp
from jax import lax
from jax.experimental import pallas as pl
from jax.experimental.pallas import tpu as pltpu
from jax.sharding import PartitionSpec as P

QUERY_HEADS = 64
HEAD_SIZE = 128
FAR = -1e30
NT = (((1,), (1,)), ((), ()))
VMEM_BYTES = 40 * 1024 * 1024


def split_rows(x):
    top = x.astype(jnp.bfloat16)
    rest = (x - top.astype(jnp.float32)).astype(jnp.bfloat16)
    return jnp.concatenate([top, rest], 0)


def join_rows(x):
    half = x.shape[0] // 2
    return x[:half] + x[half:]


def held_kernel(draft_count, limit_ref, query_ref, key_up_ref, cache_ref, turned_ref, peak_ref, total_ref, mixed_ref):
    slot_count, span_rows, _ = cache_ref.shape
    tile = query_ref.shape[0]
    heads_kv = key_up_ref.shape[1] // HEAD_SIZE
    group_size = QUERY_HEADS // heads_kv
    rows = group_size * tile
    scale = math.log2(math.e) / math.sqrt(HEAD_SIZE)

    def head(k, carry):
        pieces = []
        for g in range(group_size):
            lanes = pl.ds(pl.multiple_of((k * group_size + g) * HEAD_SIZE, HEAD_SIZE), HEAD_SIZE)
            pieces.append(query_ref[:, lanes].astype(jnp.float32))
        query = jnp.concatenate(pieces, 0).astype(jnp.bfloat16)
        lanes = pl.ds(pl.multiple_of(k * HEAD_SIZE, HEAD_SIZE), HEAD_SIZE)
        turned = lax.dot_general(query, key_up_ref[:, lanes], NT, preferred_element_type=jnp.float32)
        both = split_rows(turned * scale)
        turned_ref[k] = both
        slot = lax.broadcasted_iota(jnp.int32, (rows, 1), 0) % tile // draft_count
        scores = jnp.full((rows, span_rows), FAR, jnp.float32)
        column = lax.broadcasted_iota(jnp.int32, (rows, span_rows), 1)
        for b in range(slot_count):
            one = join_rows(lax.dot_general(both, cache_ref[b], NT, preferred_element_type=jnp.float32))
            scores = jnp.where((slot == b) & (column < limit_ref[b]), one, scores)
        peak = jnp.max(scores, 1, keepdims=True)
        weights = jnp.exp2(scores - peak)
        peak_ref[k] = peak
        total_ref[k] = jnp.sum(weights, 1, keepdims=True)
        parted = split_rows(weights)
        mixed = jnp.zeros((rows, cache_ref.shape[2]), jnp.float32)
        for b in range(slot_count):
            one = join_rows(jnp.dot(parted, cache_ref[b], preferred_element_type=jnp.float32))
            mixed = jnp.where(slot == b, one, mixed)
        mixed_ref[k] = mixed
        return carry

    lax.fori_loop(0, heads_kv, head, 0)


def down_kernel(place_ref, prompt_ref, draft_ref, weight_ref, outgoing_ref, draft_latent_ref, sum_ref):
    step = pl.program_id(0)

    @pl.when(step == 0)
    def _():
        sum_ref[...] = jnp.zeros_like(sum_ref)

    rows = jnp.concatenate([prompt_ref[...], draft_ref[...]], 0)
    sum_ref[...] += jnp.dot(rows, weight_ref[...], preferred_element_type=jnp.float32)

    @pl.when(step == pl.num_programs(0) - 1)
    def _():
        count = prompt_ref.shape[0]
        latent = sum_ref[:count, :].astype(jnp.bfloat16)
        draft_latent_ref[...] = sum_ref[count:, :].astype(jnp.bfloat16)
        spot = lax.broadcasted_iota(jnp.int32, (outgoing_ref.shape[0], count), 0)
        chosen = jnp.where(spot == place_ref[...], 1.0, 0.0).astype(jnp.bfloat16)
        outgoing_ref[...] = jnp.dot(chosen, latent, preferred_element_type=jnp.float32).astype(jnp.bfloat16)


def late_kernel(
    column_slot_ref, incoming_ref, draft_latent_ref, turned_ref, peak_ref, total_ref, mixed_ref, value_up_ref,
    out_ref, rows_ref,
):
    slot_count, draft_count, _ = out_ref.shape
    tile = slot_count * draft_count
    heads_kv = peak_ref.shape[0]
    rows = peak_ref.shape[1]
    group_size = rows // tile
    arrived = incoming_ref.shape[0]
    drafts = draft_latent_ref.shape[0]
    span = rows_ref.shape[0]
    rows_ref[:arrived, :] = incoming_ref[...]
    rows_ref[arrived : arrived + drafts, :] = draft_latent_ref[...]
    rows_ref[arrived + drafts :, :] = jnp.zeros((span - arrived - drafts, rows_ref.shape[1]), jnp.bfloat16)
    place = lax.broadcasted_iota(jnp.int32, (rows, 1), 0) % tile
    arrived_seen = place // draft_count == column_slot_ref[...]
    column = lax.broadcasted_iota(jnp.int32, (rows, span - arrived), 1)
    draft_seen = (
        (column < tile) & (column // draft_count == place // draft_count) & (column % draft_count <= place % draft_count)
    )
    for k in range(heads_kv):
        scores = join_rows(lax.dot_general(turned_ref[k], rows_ref[...], NT, preferred_element_type=jnp.float32))
        scores = jnp.concatenate(
            [
                jnp.where(arrived_seen, scores[:, :arrived], FAR),
                jnp.where(draft_seen, scores[:, arrived:], FAR),
            ],
            1,
        )
        peak = jnp.maximum(jnp.max(scores, 1, keepdims=True), peak_ref[k])
        weights = jnp.exp2(scores - peak)
        fade = jnp.exp2(peak_ref[k] - peak)
        total = total_ref[k] * fade + jnp.sum(weights, 1, keepdims=True)
        mixed = join_rows(jnp.dot(split_rows(weights), rows_ref[...], preferred_element_type=jnp.float32))
        mixed = (mixed_ref[k] * fade + mixed) / total
        value_up = value_up_ref[:, k * HEAD_SIZE : (k + 1) * HEAD_SIZE]
        result = join_rows(jnp.dot(split_rows(mixed), value_up, preferred_element_type=jnp.float32))
        wide = jnp.concatenate([result[g * tile : (g + 1) * tile] for g in range(group_size)], 1)
        lanes = slice(k * group_size * HEAD_SIZE, (k + 1) * group_size * HEAD_SIZE)
        for b in range(slot_count):
            out_ref[b, :, lanes] = wide[b * draft_count : (b + 1) * draft_count].astype(jnp.bfloat16)


def local(
    prompt_hidden,
    resident_latent,
    row_target,
    row_offset,
    context_len,
    draft_hidden,
    draft_query_heads,
    down_weight,
    key_up_weight,
    value_up_weight,
):
    wide_size = lax.axis_size("wide")
    row_count, model_width = prompt_hidden.shape
    slot_count, span_rows, latent_width = resident_latent.shape
    draft_count = draft_hidden.shape[1]
    heads_kv = key_up_weight.shape[1] // HEAD_SIZE
    group_size = QUERY_HEADS // heads_kv
    tile = slot_count * draft_count
    head_rows = group_size * tile
    most_rows = 2 * ((row_count + wide_size - 1) // wide_size)
    params = pltpu.CompilerParams(vmem_limit_bytes=VMEM_BYTES)
    whole = pl.BlockSpec(memory_space=pltpu.VMEM)

    weight = lax.all_gather(down_weight, "wide", axis=0, tiled=True)

    index = jnp.arange(row_count, dtype=jnp.int32)
    same = (row_target[:, None] == row_target[None, :]) & (index[None, :] < index[:, None])
    rank = jnp.sum(same.astype(jnp.int32), 1)
    front = row_target % slot_count == 0
    place = row_target // slot_count * most_rows + jnp.where(front, rank, most_rows - 1 - rank)
    request = jnp.arange(wide_size * slot_count, dtype=jnp.int32)
    counts = jnp.sum((row_target[None, :] == request[:, None]).astype(jnp.int32), 1)
    counts = lax.all_to_all(counts.reshape(wide_size, slot_count), "wide", split_axis=0, concat_axis=0, tiled=True)
    limit = context_len - jnp.sum(counts, 0)
    spot = jnp.arange(most_rows, dtype=jnp.int32)[None, :]
    column_slot = jnp.where(
        spot < counts[:, 0:1], 0, jnp.where(spot >= most_rows - counts[:, 1:2], 1, -1)
    ).reshape(1, wide_size * most_rows)

    query = draft_query_heads.reshape(tile, QUERY_HEADS * HEAD_SIZE)
    f32 = jnp.float32
    turned, peak, total, mixed = pl.pallas_call(
        lambda *refs: held_kernel(draft_count, *refs),
        out_shape=[
            jax.ShapeDtypeStruct((heads_kv, 2 * head_rows, latent_width), jnp.bfloat16),
            jax.ShapeDtypeStruct((heads_kv, head_rows, 1), f32),
            jax.ShapeDtypeStruct((heads_kv, head_rows, 1), f32),
            jax.ShapeDtypeStruct((heads_kv, head_rows, latent_width), f32),
        ],
        in_specs=[pl.BlockSpec(memory_space=pltpu.SMEM), whole, whole, whole],
        out_specs=[whole] * 4,
        compiler_params=params,
        cost_estimate=pl.CostEstimate(flops=2**32, bytes_accessed=2**22, transcendentals=2**19),
        name="held_rows",
    )(limit, query, key_up_weight, resident_latent)

    draft_flat = jnp.pad(draft_hidden.reshape(tile, model_width), ((0, 16 - tile), (0, 0)))
    steps = 8
    depth = model_width // steps
    outgoing, draft_latent = pl.pallas_call(
        down_kernel,
        grid=(steps,),
        out_shape=[
            jax.ShapeDtypeStruct((wide_size * most_rows, latent_width), jnp.bfloat16),
            jax.ShapeDtypeStruct((16, latent_width), jnp.bfloat16),
        ],
        in_specs=[
            pl.BlockSpec((1, row_count), lambda i: (0, 0)),
            pl.BlockSpec((row_count, depth), lambda i: (0, i)),
            pl.BlockSpec((16, depth), lambda i: (0, i)),
            pl.BlockSpec((depth, latent_width), lambda i: (i, 0)),
        ],
        out_specs=[
            pl.BlockSpec((wide_size * most_rows, latent_width), lambda i: (0, 0)),
            pl.BlockSpec((16, latent_width), lambda i: (0, 0)),
        ],
        scratch_shapes=[pltpu.VMEM((row_count + 16, latent_width), f32)],
        compiler_params=params,
        name="down_rows",
    )(place.reshape(1, row_count), prompt_hidden, draft_flat, weight)

    incoming = lax.all_to_all(
        outgoing.reshape(wide_size, most_rows, latent_width), "wide", split_axis=0, concat_axis=0, tiled=True
    ).reshape(wide_size * most_rows, latent_width)

    span = (wide_size * most_rows + 16 + 127) // 128 * 128
    return pl.pallas_call(
        late_kernel,
        out_shape=jax.ShapeDtypeStruct((slot_count, draft_count, QUERY_HEADS * HEAD_SIZE), jnp.bfloat16),
        in_specs=[whole] * 8,
        out_specs=whole,
        scratch_shapes=[pltpu.VMEM((span, latent_width), jnp.bfloat16)],
        compiler_params=params,
        name="late_rows",
    )(column_slot, incoming, draft_latent, turned, peak, total, mixed, value_up_weight)


def solution(mesh):
    placed = (
        P(("rep", "wide"), None),
        P(("rep", "wide"), None, None),
        P(("rep", "wide")),
        P(("rep", "wide")),
        P(("rep", "wide")),
        P(("rep", "wide"), None, None),
        P(("rep", "wide"), None, None),
        P("wide", None),
        P(),
        P(),
    )
    return jax.shard_map(
        local, mesh=mesh, in_specs=placed, out_specs=P(("rep", "wide"), None, None), check_vma=False
    )
```

time: 174 us -> 95.2 us (0.55)
  the two profiles are of different devices: /device:TPU:13 before, /device:TPU:0 now
where the time goes in v1:
time: 95.2 us; the launch traced here: 94.7 us
  waiting for transfers between devices  43 us (45%)
  Pallas kernels  16.7 us (18%)
  between operations  13.5 us (14%)
  starting transfers between devices  10.9 us (11%)
  local copies, waits for them, and re-layouts  7.59 us (8%)
  other arithmetic  3.12 us (3%)
    all_gather x1, waiting for transfers between devices, local(): weight = lax.all_gather(down_weight, 'wide', axis=0, tiled=True)  39.4 us
    pallas_call x1, Pallas kernels, local(): pl.pallas_call(lambda *refs: held_kernel(draft_count, *refs), out_shape=[...  8.25 us
    all_to_all x1, starting transfers between devices, local(): lax.all_to_all(counts.reshape(wide_size, slot_count), 'wide', split_axis=...  7.39 us
    pallas_call x1, Pallas kernels, local(): pl.pallas_call(late_kernel, out_shape=jax.ShapeDtypeStruct((slot_count, d...  5.31 us
    unnamed x10, local copies, waits for them, and re-layouts  4.82 us
    all_to_all x1, starting transfers between devices, local(): lax.all_to_all(outgoing.reshape(wide_size, most_rows, latent_width), 'wid...  3.51 us
    pallas_call x1, Pallas kernels, local(): pl.pallas_call(down_kernel, grid=(steps,), out_shape=[jax.ShapeDtypeStruc...  3.14 us
    all_to_all x1, waiting for transfers between devices, local(): lax.all_to_all(counts.reshape(wide_size, slot_count), 'wide', split_axis=...  2.83 us
  transfers between devices with their start and end apart: 3, of which 2 were waited for; matrix products, arithmetic and copies ran while one was open for 5% of the time, Pallas kernels for 9%

profile of v1, /device:TPU:0, one launch (start us, length us, event | category | flops | bytes accessed | tf_op | source)
XLA Modules:
  0.0 94.7 jit_solution(14134666117404687250)
XLA Ops:
  6.5 0.0 copy-start.3
  6.5 0.0 all-gather.2.cloned.1.call-start
  6.5 0.7 all-gather.2.cloned.1.call-update
  7.3 0.8 convert_reduce_fusion.1
  8.0 0.7 all_to_all.11
  8.7 7.4 %all-to-all-start = ((s32[16,1,2]{2,1,0:T(1,128)}), s32[16,1,2]{2,1,0:T(1,128)S(1)}, u32[]{:S(2)}, u32[]{:S(2)}) async-start(s32[16,1,2]{2,1,0:T(1,128)} %bitcast), calls=%async_computation | async-start | bytes 16384 | tf_op jit(solution)/shard_map/all_to_all | solution.py:164
  16.1 0.9 reshape.78
  17.1 0.9 convert_reduce_fusion
  18.0 0.7 fusion.2.place_ref
  18.6 0.9 %reshape.81.refs_1_ = bf16[8,8192]{1,0:T(8,128)(2,1)S(1)} reshape(bf16[2,4,8192]{2,1,0:T(4,128)(2,1)} %param.15) | data formatting | bytes 262144 | tf_op jit(solution)/shard_map/reshape | solution.py:171
  19.6 2.8 %all-to-all-done = s32[16,1,2]{2,1,0:T(1,128)S(1)} async-done(((s32[16,1,2]{2,1,0:T(1,128)}), s32[16,1,2]{2,1,0:T(1,128)S(1)}, u32[]{:S(2)}, u32[]{:S(2)}) %all-to-all-start) | async-done | bytes 160 | tf_op jit(solution)/shard_map/all_to_all | solution.py:164
  22.4 0.1 copy.15
  22.5 0.1 select_select_fusion
  22.6 0.1 select_n.43.column_slot_ref
  22.7 0.7 sub.22.refs_0_
  23.4 39.4 %all-gather.2.cloned.1.call-done.weight_ref = bf16[8192,256]{1,0:T(8,128)(2,1)} async-done(((bf16[512,256]{1,0:T(8,128)(2,1)}), bf16[8192,256]{1,0:T(8,128)(2,1)}) %all-gather.2.cloned.1.call-update) | async-done | bytes 4194320 | tf_op jit(solution)/shard_map/all_gather | solution.py:155
  62.8 0.0 copy-start
  62.8 2.2 %copy-done = bf16[8192,256]{1,0:T(8,128)(2,1)S(1)} copy-done((bf16[8192,256]{1,0:T(8,128)(2,1)S(1)}, bf16[8192,256]{1,0:T(8,128)(2,1)}, u32[]{:S(2)}) %copy-start) | copy-done | bytes 4194328
  65.0 0.0 copy-start.1
  65.0 1.6 %copy-done.1 = bf16[128,8192]{1,0:T(8,128)(2,1)S(1)} copy-done((bf16[128,8192]{1,0:T(8,128)(2,1)S(1)}, bf16[128,8192]{1,0:T(8,128)(2,1)}, u32[]{:S(2)}) %copy-start.1) | copy-done | bytes 2097176
  66.6 3.1 %down_rows.1 = (bf16[256,256]{1,0:T(8,128)(2,1)}, bf16[16,256]{1,0:T(8,128)(2,1)S(1)}) custom-call(s32[1,128]{1,0:T(1,128)S(1)} %fusion.2.place_ref, bf16[128,8192]{1,0:T(8,128)(2,1)S(1)} %copy-done.1, bf16[16,8192]{1,0:T(8,128)(2,1)S(1)} %pad.4.draft_ref, bf16[8192,256]{1,0:T(8,128)(2,1)S(1)} %copy-done), custom_call_target="tpu_custom_call" | custom-call | tf_op jit(solution)/shard_map/down_rows/pallas_call | solution.py:191
  69.7 3.5 %all-to-all-start.1 = ((bf16[16,16,256]{2,1,0:T(8,128)(2,1)}), bf16[16,16,256]{2,1,0:T(8,128)(2,1)S(1)}, u32[]{:S(2)}, u32[]{:S(2)}) async-start(bf16[16,16,256]{2,1,0:T(8,128)(2,1)} %bitcast.5), calls=%async_computation.1 | async-start | bytes 262144 | tf_op jit(solution)/shard_map/all_to_all | solution.py:213
  73.3 0.0 copy-done.3
  73.3 0.0 copy-start.4
  73.3 1.0 %copy-done.4 = bf16[256,1024]{1,0:T(8,128)(2,1)S(1)} copy-done((bf16[256,1024]{1,0:T(8,128)(2,1)S(1)}, bf16[256,1024]{1,0:T(8,128)(2,1)}, u32[]{:S(2)}) %copy-start.4) | copy-done | bytes 524312
  74.3 0.0 copy-start.2
  74.3 8.2 %held_rows.1 = (bf16[8,128,256]{2,1,0:T(8,128)(2,1)S(1)}, f32[8,64,1]{2,1,0:T(8,128)S(1)}, f32[8,64,1]{2,1,0:T(8,128)S(1)}, f32[8,64,256]{2,1,0:T(8,128)S(1)}) custom-call(s32[2]{0:T(128)S(1)} %sub.22.refs_0_, bf16[8,8192]{1,0:T(8,128)(2,1)S(1)} %reshape.81.refs_1_, bf16[256,1024]{1,0:T(8,128)(2,1)S(1)} %copy-done.4, bf16[2,1024,256]{2,1,0:T(8,128)(2,1)S(1)} %copy-done.3), custom_call_target="tpu_custom_call" | custom-call | flops 4294967296 | bytes 4194304 | tf_op jit(solution)/shard_map/held_rows/pallas_call | solution.py:173
  82.6 0.0 all-to-all-done.1
  82.6 0.0 copy-done.2
  82.6 5.3 %late_rows.1 = bf16[2,4,8192]{2,1,0:T(4,128)(2,1)} custom-call(s32[1,256]{1,0:T(1,128)S(1)} %select_n.43.column_slot_ref, bf16[256,256]{1,0:T(8,128)(2,1)S(1)} %bitcast.10, bf16[16,256]{1,0:T(8,128)(2,1)S(1)} %get-tuple-element.12.draft_latent_ref, bf16[8,128,256]{2,1,0:T(8,128)(2,1)S(1)} %get-tuple-element.13.turned_ref, ...), custom_call_target="tpu_custom_call" | custom-call | tf_op jit(solution)/shard_map/late_rows/pallas_call | solution.py:218
  (3 shorter events, 0.1 us)
Async XLA Ops:
  6.5 66.7 %copy-start.3 = (bf16[2,1024,256]{2,1,0:T(8,128)(2,1)S(1)}, bf16[2,1024,256]{2,1,0:T(8,128)(2,1)}, u32[]{:S(2)}) copy-start(bf16[2,1024,256]{2,1,0:T(8,128)(2,1)} %refs_3_.1) | copy-start | bytes 3145732
  6.5 56.3 %all-gather.2.cloned.1.call-start = ((), (), s32[]{:S(2)}) async-start(), calls=%async_computation.2 | async-start | bytes 4456448 | tf_op jit(solution)/shard_map/all_gather | solution.py:155
  8.7 13.7 %all-to-all-start = ((s32[16,1,2]{2,1,0:T(1,128)}), s32[16,1,2]{2,1,0:T(1,128)S(1)}, u32[]{:S(2)}, u32[]{:S(2)}) async-start(s32[16,1,2]{2,1,0:T(1,128)} %bitcast), calls=%async_computation | async-start | bytes 16384 | tf_op jit(solution)/shard_map/all_to_all | solution.py:164
  62.8 2.2 %copy-start = (bf16[8192,256]{1,0:T(8,128)(2,1)S(1)}, bf16[8192,256]{1,0:T(8,128)(2,1)}, u32[]{:S(2)}) copy-start(bf16[8192,256]{1,0:T(8,128)(2,1)} %all-gather.2.cloned.1.call-done.weight_ref) | copy-start | bytes 12582916
  65.0 1.6 %copy-start.1 = (bf16[128,8192]{1,0:T(8,128)(2,1)S(1)}, bf16[128,8192]{1,0:T(8,128)(2,1)}, u32[]{:S(2)}) copy-start(bf16[128,8192]{1,0:T(8,128)(2,1)} %prompt_ref.1) | copy-start | bytes 6291460
  69.7 12.8 %all-to-all-start.1 = ((bf16[16,16,256]{2,1,0:T(8,128)(2,1)}), bf16[16,16,256]{2,1,0:T(8,128)(2,1)S(1)}, u32[]{:S(2)}, u32[]{:S(2)}) async-start(bf16[16,16,256]{2,1,0:T(8,128)(2,1)} %bitcast.5), calls=%async_computation.1 | async-start | bytes 262144 | tf_op jit(solution)/shard_map/all_to_all | solution.py:213
  73.3 1.0 %copy-start.4 = (bf16[256,1024]{1,0:T(8,128)(2,1)S(1)}, bf16[256,1024]{1,0:T(8,128)(2,1)}, u32[]{:S(2)}) copy-start(bf16[256,1024]{1,0:T(8,128)(2,1)} %refs_2_.1) | copy-start | bytes 1572868
  74.3 8.3 %copy-start.2 = (bf16[256,1024]{1,0:T(8,128)(2,1)S(1)}, bf16[256,1024]{1,0:T(8,128)(2,1)}, u32[]{:S(2)}) copy-start(bf16[256,1024]{1,0:T(8,128)(2,1)} %value_up_ref.1) | copy-start | bytes 1572868
Sparse Core Ops, SparseCore 0:
  9.5 53.2 all-gather.1

commit v2 on v1

--- a/solution.py
+++ b/solution.py
@@ -1,3 +1,4 @@
+import functools
 import math
 
 import jax
@@ -11,6 +12,7 @@
 HEAD_SIZE = 128
 FAR = -1e30
 NT = (((1,), (1,)), ((), ()))
+HELD_PARTS = 4
 VMEM_BYTES = 40 * 1024 * 1024
 
 
@@ -25,7 +27,7 @@
     return x[:half] + x[half:]
 
 
-def held_kernel(draft_count, limit_ref, query_ref, key_up_ref, cache_ref, turned_ref, peak_ref, total_ref, mixed_ref):
+def held_kernel(first, draft_count, limit_ref, query_ref, key_up_ref, cache_ref, turned_ref, peak_ref, total_ref, mixed_ref):
     slot_count, span_rows, _ = cache_ref.shape
     tile = query_ref.shape[0]
     heads_kv = key_up_ref.shape[1] // HEAD_SIZE
@@ -36,10 +38,10 @@
     def head(k, carry):
         pieces = []
         for g in range(group_size):
-            lanes = pl.ds(pl.multiple_of((k * group_size + g) * HEAD_SIZE, HEAD_SIZE), HEAD_SIZE)
+            lanes = pl.ds(pl.multiple_of(((first + k) * group_size + g) * HEAD_SIZE, HEAD_SIZE), HEAD_SIZE)
             pieces.append(query_ref[:, lanes].astype(jnp.float32))
         query = jnp.concatenate(pieces, 0).astype(jnp.bfloat16)
-        lanes = pl.ds(pl.multiple_of(k * HEAD_SIZE, HEAD_SIZE), HEAD_SIZE)
+        lanes = pl.ds(pl.multiple_of((first + k) * HEAD_SIZE, HEAD_SIZE), HEAD_SIZE)
         turned = lax.dot_general(query, key_up_ref[:, lanes], NT, preferred_element_type=jnp.float32)
         both = split_rows(turned * scale)
         turned_ref[k] = both
@@ -61,37 +63,73 @@
         mixed_ref[k] = mixed
         return carry
 
-    lax.fori_loop(0, heads_kv, head, 0)
-
-
-def down_kernel(place_ref, prompt_ref, draft_ref, weight_ref, outgoing_ref, draft_latent_ref, sum_ref):
-    step = pl.program_id(0)
-
-    @pl.when(step == 0)
-    def _():
-        sum_ref[...] = jnp.zeros_like(sum_ref)
-
-    rows = jnp.concatenate([prompt_ref[...], draft_ref[...]], 0)
-    sum_ref[...] += jnp.dot(rows, weight_ref[...], preferred_element_type=jnp.float32)
-
-    @pl.when(step == pl.num_programs(0) - 1)
-    def _():
-        count = prompt_ref.shape[0]
-        latent = sum_ref[:count, :].astype(jnp.bfloat16)
-        draft_latent_ref[...] = sum_ref[count:, :].astype(jnp.bfloat16)
-        spot = lax.broadcasted_iota(jnp.int32, (outgoing_ref.shape[0], count), 0)
-        chosen = jnp.where(spot == place_ref[...], 1.0, 0.0).astype(jnp.bfloat16)
-        outgoing_ref[...] = jnp.dot(chosen, latent, preferred_element_type=jnp.float32).astype(jnp.bfloat16)
+    lax.fori_loop(0, turned_ref.shape[0], head, 0)
+
+
+def down_kernel(starts_of, me_ref, place_ref, prompt_ref, draft_ref, *refs):
+    starts = starts_of(me_ref[0])
+    weight_refs, (outgoing_ref, draft_latent_ref) = refs[:-2], refs[-2:]
+    count = prompt_ref.shape[0]
+    total = jnp.zeros((count + draft_ref.shape[0], outgoing_ref.shape[1]), jnp.float32)
+    for p, weight_ref in enumerate(weight_refs):
+        depth = weight_ref.shape[0]
+        lanes = pl.ds(pl.multiple_of(starts[p], HEAD_SIZE), depth)
+        rows = jnp.concatenate([prompt_ref[:, lanes], draft_ref[:, lanes]], 0)
+        total += jnp.dot(rows, weight_ref[...], preferred_element_type=jnp.float32)
+    latent = total[:count].astype(jnp.bfloat16)
+    draft_latent_ref[...] = total[count:].astype(jnp.bfloat16)
+    spot = lax.broadcasted_iota(jnp.int32, (outgoing_ref.shape[0], count), 0)
+    chosen = jnp.where(spot == place_ref[...], 1.0, 0.0).astype(jnp.bfloat16)
+    outgoing_ref[...] = jnp.dot(chosen, latent, preferred_element_type=jnp.float32).astype(jnp.bfloat16)
+
+
+def gather_pieces(shard, wide_size):
+    rows = shard.shape[0]
+    if wide_size != 16:
+        return [lax.all_gather(shard, "wide", axis=0, tiled=True)], lambda me: [0]
+    sizes = (wide_size // 4, 2, 2)
+
+    def flat(spot):
+        return (spot[0] * sizes[1] + spot[1]) * sizes[2] + spot[2]
+
+    def spots():
+        return [(z, y, c) for z in range(sizes[0]) for y in range(sizes[1]) for c in range(sizes[2])]
+
+    def move(x, axis, step):
+        pairs = []
+        for spot in spots():
+            to = list(spot)
+            to[axis] = (to[axis] + step) % sizes[axis]
+            pairs.append((flat(spot), flat(to)))
+        return lax.ppermute(x, "wide", pairs)
+
+    held = [((0, 0, 0), shard)]
+    for axis in range(3):
+        came = []
+        for step in range(1, sizes[axis]):
+            for trail, x in held:
+                longer = list(trail)
+                longer[axis] = step
+                came.append((tuple(longer), move(x, axis, step)))
+        held = held + came
+
+    def starts_of(me):
+        here = (me // (sizes[1] * sizes[2]), me // sizes[2] % sizes[1], me % sizes[2])
+        return [
+            flat([(here[a] - trail[a] + sizes[a]) % sizes[a] for a in range(3)]) * rows for trail, _ in held
+        ]
+
+    return [x for _, x in held], starts_of
 
 
 def late_kernel(
-    column_slot_ref, incoming_ref, draft_latent_ref, turned_ref, peak_ref, total_ref, mixed_ref, value_up_ref,
-    out_ref, rows_ref,
+    column_slot_ref, incoming_ref, draft_latent_ref, value_up_ref, *refs
 ):
+    held_refs, (out_ref, rows_ref) = refs[:-2], refs[-2:]
     slot_count, draft_count, _ = out_ref.shape
     tile = slot_count * draft_count
-    heads_kv = peak_ref.shape[0]
-    rows = peak_ref.shape[1]
+    part_heads, rows, _ = held_refs[1].shape
+    heads_kv = part_heads * HELD_PARTS
     group_size = rows // tile
     arrived = incoming_ref.shape[0]
     drafts = draft_latent_ref.shape[0]
@@ -106,7 +144,10 @@
         (column < tile) & (column // draft_count == place // draft_count) & (column % draft_count <= place % draft_count)
     )
     for k in range(heads_kv):
-        scores = join_rows(lax.dot_general(turned_ref[k], rows_ref[...], NT, preferred_element_type=jnp.float32))
+        turned, held_peak, held_total, held_mixed = (
+            ref[k % part_heads] for ref in held_refs[k // part_heads * 4 : k // part_heads * 4 + 4]
+        )
+        scores = join_rows(lax.dot_general(turned, rows_ref[...], NT, preferred_element_type=jnp.float32))
         scores = jnp.concatenate(
             [
                 jnp.where(arrived_seen, scores[:, :arrived], FAR),
@@ -114,12 +155,12 @@
             ],
             1,
         )
-        peak = jnp.maximum(jnp.max(scores, 1, keepdims=True), peak_ref[k])
+        peak = jnp.maximum(jnp.max(scores, 1, keepdims=True), held_peak)
         weights = jnp.exp2(scores - peak)
-        fade = jnp.exp2(peak_ref[k] - peak)
-        total = total_ref[k] * fade + jnp.sum(weights, 1, keepdims=True)
+        fade = jnp.exp2(held_peak - peak)
+        total = held_total * fade + jnp.sum(weights, 1, keepdims=True)
         mixed = join_rows(jnp.dot(split_rows(weights), rows_ref[...], preferred_element_type=jnp.float32))
-        mixed = (mixed_ref[k] * fade + mixed) / total
+        mixed = (held_mixed * fade + mixed) / total
         value_up = value_up_ref[:, k * HEAD_SIZE : (k + 1) * HEAD_SIZE]
         result = join_rows(jnp.dot(split_rows(mixed), value_up, preferred_element_type=jnp.float32))
         wide = jnp.concatenate([result[g * tile : (g + 1) * tile] for g in range(group_size)], 1)
@@ -152,7 +193,7 @@
     params = pltpu.CompilerParams(vmem_limit_bytes=VMEM_BYTES)
     whole = pl.BlockSpec(memory_space=pltpu.VMEM)
 
-    weight = lax.all_gather(down_weight, "wide", axis=0, tiled=True)
+    pieces, starts_of = gather_pieces(down_weight, wide_size)
 
     index = jnp.arange(row_count, dtype=jnp.int32)
     same = (row_target[:, None] == row_target[None, :]) & (index[None, :] < index[:, None])
@@ -170,45 +211,37 @@
 
     query = draft_query_heads.reshape(tile, QUERY_HEADS * HEAD_SIZE)
     f32 = jnp.float32
-    turned, peak, total, mixed = pl.pallas_call(
-        lambda *refs: held_kernel(draft_count, *refs),
-        out_shape=[
-            jax.ShapeDtypeStruct((heads_kv, 2 * head_rows, latent_width), jnp.bfloat16),
-            jax.ShapeDtypeStruct((heads_kv, head_rows, 1), f32),
-            jax.ShapeDtypeStruct((heads_kv, head_rows, 1), f32),
-            jax.ShapeDtypeStruct((heads_kv, head_rows, latent_width), f32),
-        ],
-        in_specs=[pl.BlockSpec(memory_space=pltpu.SMEM), whole, whole, whole],
-        out_specs=[whole] * 4,
-        compiler_params=params,
-        cost_estimate=pl.CostEstimate(flops=2**32, bytes_accessed=2**22, transcendentals=2**19),
-        name="held_rows",
-    )(limit, query, key_up_weight, resident_latent)
+    part_heads = heads_kv // HELD_PARTS
+    held = []
+    for part in range(HELD_PARTS):
+        held += pl.pallas_call(
+            functools.partial(held_kernel, part * part_heads, draft_count),
+            out_shape=[
+                jax.ShapeDtypeStruct((part_heads, 2 * head_rows, latent_width), jnp.bfloat16),
+                jax.ShapeDtypeStruct((part_heads, head_rows, 1), f32),
+                jax.ShapeDtypeStruct((part_heads, head_rows, 1), f32),
+                jax.ShapeDtypeStruct((part_heads, head_rows, latent_width), f32),
+            ],
+            in_specs=[pl.BlockSpec(memory_space=pltpu.SMEM), whole, whole, whole],
+            out_specs=[whole] * 4,
+            compiler_params=params,
+            cost_estimate=pl.CostEstimate(flops=2**30, bytes_accessed=2**21, transcendentals=2**17),
+            name="held_rows",
+        )(limit, query, key_up_weight, resident_latent)
 
     draft_flat = jnp.pad(draft_hidden.reshape(tile, model_width), ((0, 16 - tile), (0, 0)))
-    steps = 8
-    depth = model_width // steps
+    smem = pl.BlockSpec(memory_space=pltpu.SMEM)
     outgoing, draft_latent = pl.pallas_call(
-        down_kernel,
-        grid=(steps,),
+        functools.partial(down_kernel, starts_of),
         out_shape=[
             jax.ShapeDtypeStruct((wide_size * most_rows, latent_width), jnp.bfloat16),
             jax.ShapeDtypeStruct((16, latent_width), jnp.bfloat16),
         ],
-        in_specs=[
-            pl.BlockSpec((1, row_count), lambda i: (0, 0)),
-            pl.BlockSpec((row_count, depth), lambda i: (0, i)),
-            pl.BlockSpec((16, depth), lambda i: (0, i)),
-            pl.BlockSpec((depth, latent_width), lambda i: (i, 0)),
-        ],
-        out_specs=[
-            pl.BlockSpec((wide_size * most_rows, latent_width), lambda i: (0, 0)),
-            pl.BlockSpec((16, latent_width), lambda i: (0, 0)),
-        ],
-        scratch_shapes=[pltpu.VMEM((row_count + 16, latent_width), f32)],
+        in_specs=[smem] + [whole] * (3 + len(pieces)),
+        out_specs=[whole] * 2,
         compiler_params=params,
         name="down_rows",
-    )(place.reshape(1, row_count), prompt_hidden, draft_flat, weight)
+    )(lax.axis_index("wide").reshape(1), place.reshape(1, row_count), prompt_hidden, draft_flat, *pieces)
 
     incoming = lax.all_to_all(
         outgoing.reshape(wide_size, most_rows, latent_width), "wide", split_axis=0, concat_axis=0, tiled=True
@@ -218,12 +251,12 @@
     return pl.pallas_call(
         late_kernel,
         out_shape=jax.ShapeDtypeStruct((slot_count, draft_count, QUERY_HEADS * HEAD_SIZE), jnp.bfloat16),
-        in_specs=[whole] * 8,
+        in_specs=[whole] * (4 + len(held)),
         out_specs=whole,
         scratch_shapes=[pltpu.VMEM((span, latent_width), jnp.bfloat16)],
         compiler_params=params,
         name="late_rows",
-    )(column_slot, incoming, draft_latent, turned, peak, total, mixed, value_up_weight)
+    )(column_slot, incoming, draft_latent, value_up_weight, *held)
 
 
 def solution(mesh):

time: 95.2 us -> 74.4 us (0.78)
  waiting for transfers between devices: 43 us -> 17.4 us
  between operations: 13.5 us -> 0.34 us
  starting transfers between devices: 10.9 us -> 22.4 us
  local copies, waits for them, and re-layouts: 7.59 us -> 12.3 us
    all_gather x1 -> x0, waiting for transfers between devices: 39.4 us -> none  [local(): weight = lax.all_gather(down_weight, 'wide', axis=0, tiled=True)]
    ppermute x0 -> x15, waiting for transfers between devices: none -> 17.4 us  [move(): return lax.ppermute(x, 'wide', pairs)]
    ppermute x0 -> x15, starting transfers between devices: none -> 12.7 us  [move(): return lax.ppermute(x, 'wide', pairs)]
    unnamed x10 -> x46, local copies, waits for them, and re-layouts: 4.82 us -> 8.91 us
    all_to_all x1, waiting for transfers between devices: 2.83 us -> 0.01 us  [local(): lax.all_to_all(counts.reshape(wide_size, slot_count), 'wide', split_axis=...]
    all_to_all x1, starting transfers between devices: 7.39 us -> 4.87 us  [local(): lax.all_to_all(counts.reshape(wide_size, slot_count), 'wide', split_axis=...]
    all_to_all x1, starting transfers between devices: 3.51 us -> 4.8 us  [local(): lax.all_to_all(outgoing.reshape(wide_size, most_rows, latent_width), 'wid...]
    pallas_call x2 -> x5, Pallas kernels: 11.4 us -> 12.2 us  [the longest x4 9.86 us: local(): pl.pallas_call(functools.partial(held_kernel, part * part_heads, draft_co...]
  transfers between devices with their start and end apart: 3 -> 17, of which waited for: 2 -> 4; matrix products, arithmetic and copies ran while one was open for 5% -> 9% of each run, Pallas kernels for 9% -> 13%
where the time goes in v2:
time: 74.4 us; the launch traced here: 73.8 us
  starting transfers between devices  22.4 us (30%)
  Pallas kernels  17.5 us (24%)
  waiting for transfers between devices  17.4 us (23%)
  local copies, waits for them, and re-layouts  12.3 us (17%)
  other arithmetic  3.85 us (5%)
    ppermute x15, waiting for transfers between devices, move(): return lax.ppermute(x, 'wide', pairs)  17.4 us
    ppermute x15, starting transfers between devices, move(): return lax.ppermute(x, 'wide', pairs)  12.7 us
    pallas_call x4, Pallas kernels, local(): pl.pallas_call(functools.partial(held_kernel, part * part_heads, draft_co...  9.86 us
    unnamed x46, local copies, waits for them, and re-layouts  8.91 us
    pallas_call x1, Pallas kernels, local(): pl.pallas_call(late_kernel, out_shape=jax.ShapeDtypeStruct((slot_count, d...  5.32 us
    all_to_all x1, starting transfers between devices, local(): lax.all_to_all(counts.reshape(wide_size, slot_count), 'wide', split_axis=...  4.87 us
    all_to_all x1, starting transfers between devices, local(): lax.all_to_all(outgoing.reshape(wide_size, most_rows, latent_width), 'wid...  4.8 us
    pallas_call x1, Pallas kernels, local(): pl.pallas_call(functools.partial(down_kernel, starts_of), out_shape=[jax....  2.31 us
  transfers between devices with their start and end apart: 17, of which 4 were waited for; matrix products, arithmetic and copies ran while one was open for 9% of the time, Pallas kernels for 13%

profile of v2, /device:TPU:0, one launch (start us, length us, event | category | flops | bytes accessed | tf_op | source)
XLA Modules:
  0.0 73.8 jit_solution(6161513563969431552)
XLA Ops:
  0.0 5.0 %collective-permute-start.2 = (bf16[512,256]{1,0:T(8,128)(2,1)}, bf16[512,256]{1,0:T(8,128)(2,1)S(1)}, u32[]{:S(2)}, u32[]{:S(2)}) collective-permute-start(bf16[512,256]{1,0:T(8,128)(2,1)} %refs_0_.1), channel_id=1, source_target_pairs={{0,12},{1,13},{2,14},{3,15},{4,0},{5,1},{6,2},{7,3},{8,4},{9,5},{1... | collective-permute-start | bytes 786440 | tf_op jit(solution)/shard_map/ppermute | solution.py:104
  5.1 1.0 %collective-permute-start.1 = (bf16[512,256]{1,0:T(8,128)(2,1)}, bf16[512,256]{1,0:T(8,128)(2,1)S(1)}, u32[]{:S(2)}, u32[]{:S(2)}) collective-permute-start(bf16[512,256]{1,0:T(8,128)(2,1)} %refs_0_.1), channel_id=1, source_target_pairs={{0,8},{1,9},{2,10},{3,11},{4,12},{5,13},{6,14},{7,15},{8,0},{9,1},... | collective-permute-start | bytes 786440 | tf_op jit(solution)/shard_map/ppermute | solution.py:104
  6.1 1.5 %collective-permute-start.3 = (bf16[512,256]{1,0:T(8,128)(2,1)}, bf16[512,256]{1,0:T(8,128)(2,1)S(1)}, u32[]{:S(2)}, u32[]{:S(2)}) collective-permute-start(bf16[512,256]{1,0:T(8,128)(2,1)} %refs_0_.1), channel_id=1, source_target_pairs={{0,2},{1,3},{2,0},{3,1},{4,6},{5,7},{6,4},{7,5},{8,10},{9,11},{10,... | collective-permute-start | bytes 786440 | tf_op jit(solution)/shard_map/ppermute | solution.py:104
  7.6 0.8 %convert_reduce_fusion.1 = s32[32]{0:T(128)S(1)} fusion(s32[128]{0:T(128)} %param.12), kind=kLoop, calls=%fused_computation.3 | loop fusion | flops 12256 | bytes 640 | tf_op jit(solution)/shard_map/reduce_sum | solution.py:204
  8.4 0.7 all_to_all.11
  9.1 4.9 %all-to-all-start = ((s32[16,1,2]{2,1,0:T(1,128)}), s32[16,1,2]{2,1,0:T(1,128)S(1)}, u32[]{:S(2)}, u32[]{:S(2)}) async-start(s32[16,1,2]{2,1,0:T(1,128)} %bitcast), calls=%async_computation | async-start | bytes 16384 | tf_op jit(solution)/shard_map/all_to_all | solution.py:205
  13.9 0.9 %convert_reduce_fusion = s32[128]{0:T(128)S(1)} fusion(s32[128]{0:T(128)} %param.12), kind=kLoop, calls=%fused_computation | loop fusion | flops 81792 | bytes 1024 | tf_op jit(solution)/shard_map/reduce_sum | solution.py:200
  14.8 2.0 %collective-permute-start.6 = (bf16[512,256]{1,0:T(8,128)(2,1)S(1)}, bf16[512,256]{1,0:T(8,128)(2,1)}, u32[]{:S(2)}, u32[]{:S(2)}) collective-permute-start(bf16[512,256]{1,0:T(8,128)(2,1)S(1)} %collective-permute-done.2.refs_3_), channel_id=1, source_target_pairs={{0,2},{1,3},{2,0},{3,1},{4,6},{5,7},{6,4},{7,5},{8,10},{9,11},{10,... | collective-permute-start | bytes 786440 | tf_op jit(solution)/shard_map/ppermute | solution.py:104
  16.8 1.8 %collective-permute-done.refs_1_ = bf16[512,256]{1,0:T(8,128)(2,1)S(1)} collective-permute-done((bf16[512,256]{1,0:T(8,128)(2,1)}, bf16[512,256]{1,0:T(8,128)(2,1)S(1)}, u32[]{:S(2)}, u32[]{:S(2)}) %collective-permute-start) | collective-permute-done | bytes 262176 | tf_op jit(solution)/shard_map/ppermute | solution.py:104
  18.6 9.1 %collective-permute-done.1.refs_2_ = bf16[512,256]{1,0:T(8,128)(2,1)S(1)} collective-permute-done((bf16[512,256]{1,0:T(8,128)(2,1)}, bf16[512,256]{1,0:T(8,128)(2,1)S(1)}, u32[]{:S(2)}, u32[]{:S(2)}) %collective-permute-start.1) | collective-permute-done | bytes 262176 | tf_op jit(solution)/shard_map/ppermute | solution.py:104
  27.7 1.5 %collective-permute-start.4 = (bf16[512,256]{1,0:T(8,128)(2,1)S(1)}, bf16[512,256]{1,0:T(8,128)(2,1)}, u32[]{:S(2)}, u32[]{:S(2)}) collective-permute-start(bf16[512,256]{1,0:T(8,128)(2,1)S(1)} %collective-permute-done.refs_1_), channel_id=1, source_target_pairs={{0,2},{1,3},{2,0},{3,1},{4,6},{5,7},{6,4},{7,5},{8,10},{9,11},{10,... | collective-permute-start | bytes 786440 | tf_op jit(solution)/shard_map/ppermute | solution.py:104
  29.8 0.7 fusion.2.place_ref
  30.5 0.9 %reshape.82 = bf16[8,8192]{1,0:T(8,128)(2,1)S(1)} reshape(bf16[2,4,8192]{2,1,0:T(4,128)(2,1)} %param.14) | data formatting | bytes 262144 | tf_op jit(solution)/shard_map/reshape | solution.py:232
  31.5 1.6 %reshape.85.query_ref = bf16[8,8192]{1,0:T(8,128)(2,1)} reshape(bf16[2,4,8192]{2,1,0:T(4,128)(2,1)} %param.15) | data formatting | bytes 262144 | tf_op jit(solution)/shard_map/reshape | solution.py:212
  33.1 0.8 %sub.22.limit_ref = s32[2]{0:T(128)S(1)} subtract(s32[2]{0:T(128)} %param.13, s32[2]{0:T(128)S(1)} %reduce_sum.29) | non-fusion elementwise | flops 2 | bytes 24 | tf_op jit(solution)/shard_map/sub | solution.py:206
  34.0 3.0 %collective-permute-done.4.refs_5_ = bf16[512,256]{1,0:T(8,128)(2,1)} collective-permute-done((bf16[512,256]{1,0:T(8,128)(2,1)S(1)}, bf16[512,256]{1,0:T(8,128)(2,1)}, u32[]{:S(2)}, u32[]{:S(2)}) %collective-permute-start.4) | collective-permute-done | bytes 262176 | tf_op jit(solution)/shard_map/ppermute | solution.py:104
  37.1 3.5 %collective-permute-done.5.refs_6_ = bf16[512,256]{1,0:T(8,128)(2,1)} collective-permute-done((bf16[512,256]{1,0:T(8,128)(2,1)S(1)}, bf16[512,256]{1,0:T(8,128)(2,1)}, u32[]{:S(2)}, u32[]{:S(2)}) %collective-permute-start.5) | collective-permute-done | bytes 262176 | tf_op jit(solution)/shard_map/ppermute | solution.py:104
  41.6 0.9 %copy-done.9 = bf16[8,8192]{1,0:T(8,128)(2,1)S(1)} copy-done((bf16[8,8192]{1,0:T(8,128)(2,1)S(1)}, bf16[8,8192]{1,0:T(8,128)(2,1)}, u32[]{:S(2)}) %copy-start.9) | copy-done | bytes 131096
  42.5 1.2 %copy-done.16 = bf16[2,1024,256]{2,1,0:T(8,128)(2,1)S(1)} copy-done((bf16[2,1024,256]{2,1,0:T(8,128)(2,1)S(1)}, bf16[2,1024,256]{2,1,0:T(8,128)(2,1)}, u32[]{:S(2)}) %copy-start.16) | copy-done | bytes 1048600
  43.7 1.0 %copy-done.19 = bf16[256,1024]{1,0:T(8,128)(2,1)S(1)} copy-done((bf16[256,1024]{1,0:T(8,128)(2,1)S(1)}, bf16[256,1024]{1,0:T(8,128)(2,1)}, u32[]{:S(2)}) %copy-start.19) | copy-done | bytes 524312
  44.8 2.5 %held_rows.4 = (bf16[2,128,256]{2,1,0:T(8,128)(2,1)S(1)}, f32[2,64,1]{2,1,0:T(8,128)S(1)}, f32[2,64,1]{2,1,0:T(8,128)S(1)}, f32[2,64,256]{2,1,0:T(8,128)S(1)}) custom-call(s32[2]{0:T(128)S(1)} %sub.22.limit_ref, bf16[8,8192]{1,0:T(8,128)(2,1)S(1)} %copy-done.9, bf16[256,1024]{1,0:T(8,128)(2,1)S(1)} %copy-done.19, bf16[2,1024,256]{2,1,0:T(8,128)(2,1)S(1)} %copy-done.16), custom_call_target="tpu_custom_call" | custom-call | flops 1073741824 | bytes 2097152 | tf_op jit(solution)/shard_map/held_rows/pallas_call | solution.py:217
  47.9 0.7 select_select_fusion
  48.6 2.3 %down_rows.1 = (bf16[256,256]{1,0:T(8,128)(2,1)S(1)}, bf16[16,256]{1,0:T(8,128)(2,1)S(1)}) custom-call(s32[1]{0:T(128)} %bitcast.4.me_ref, s32[1,128]{1,0:T(1,128)S(1)} %fusion.2.place_ref, bf16[128,8192]{1,0:T(8,128)(2,1)S(1)} %copy-done, bf16[16,8192]{1,0:T(8,128)(2,1)S(1)} %pad.4.draft_ref, bf16[512,256]{1,0:T(8,128)(2,1)S(1)} %copy-done.2, ...), custom_call_target="tpu_custom_call" | custom-call | tf_op jit(solution)/shard_map/down_rows/pallas_call | solution.py:234
  51.6 4.8 %all-to-all-start.1 = ((bf16[16,16,256]{2,1,0:T(8,128)(2,1)}), bf16[16,16,256]{2,1,0:T(8,128)(2,1)S(1)}, u32[]{:S(2)}, u32[]{:S(2)}) async-start(bf16[16,16,256]{2,1,0:T(8,128)(2,1)} %bitcast.12), calls=%async_computation.1 | async-start | bytes 262144 | tf_op jit(solution)/shard_map/all_to_all | solution.py:246
  56.4 0.9 %copy-done.10 = bf16[8,8192]{1,0:T(8,128)(2,1)S(1)} copy-done((bf16[8,8192]{1,0:T(8,128)(2,1)S(1)}, bf16[8,8192]{1,0:T(8,128)(2,1)}, u32[]{:S(2)}) %copy-start.10) | copy-done | bytes 131096
  57.3 1.2 %copy-done.17 = bf16[2,1024,256]{2,1,0:T(8,128)(2,1)S(1)} copy-done((bf16[2,1024,256]{2,1,0:T(8,128)(2,1)S(1)}, bf16[2,1024,256]{2,1,0:T(8,128)(2,1)}, u32[]{:S(2)}) %copy-start.17) | copy-done | bytes 1048600
  58.6 1.0 %copy-done.20 = bf16[256,1024]{1,0:T(8,128)(2,1)S(1)} copy-done((bf16[256,1024]{1,0:T(8,128)(2,1)S(1)}, bf16[256,1024]{1,0:T(8,128)(2,1)}, u32[]{:S(2)}) %copy-start.20) | copy-done | bytes 524312
  59.6 2.5 %held_rows.5 = (bf16[2,128,256]{2,1,0:T(8,128)(2,1)S(1)}, f32[2,64,1]{2,1,0:T(8,128)S(1)}, f32[2,64,1]{2,1,0:T(8,128)S(1)}, f32[2,64,256]{2,1,0:T(8,128)S(1)}) custom-call(s32[2]{0:T(128)S(1)} %sub.22.limit_ref, bf16[8,8192]{1,0:T(8,128)(2,1)S(1)} %copy-done.10, bf16[256,1024]{1,0:T(8,128)(2,1)S(1)} %copy-done.20, bf16[2,1024,256]{2,1,0:T(8,128)(2,1)S(1)} %copy-done.17), custom_call_target="tpu_custom_call" | custom-call | flops 1073741824 | bytes 2097152 | tf_op jit(solution)/shard_map/held_rows/pallas_call | solution.py:217
  62.2 1.2 %copy-done.18 = bf16[2,1024,256]{2,1,0:T(8,128)(2,1)S(1)} copy-done((bf16[2,1024,256]{2,1,0:T(8,128)(2,1)S(1)}, bf16[2,1024,256]{2,1,0:T(8,128)(2,1)}, u32[]{:S(2)}) %copy-start.18) | copy-done | bytes 1048600
  63.4 2.5 %held_rows.6 = (bf16[2,128,256]{2,1,0:T(8,128)(2,1)S(1)}, f32[2,64,1]{2,1,0:T(8,128)S(1)}, f32[2,64,1]{2,1,0:T(8,128)S(1)}, f32[2,64,256]{2,1,0:T(8,128)S(1)}) custom-call(s32[2]{0:T(128)S(1)} %sub.22.limit_ref, bf16[8,8192]{1,0:T(8,128)(2,1)S(1)} %copy-done.10, bf16[256,1024]{1,0:T(8,128)(2,1)S(1)} %copy-done.20, bf16[2,1024,256]{2,1,0:T(8,128)(2,1)S(1)} %copy-done.18), custom_call_target="tpu_custom_call" | custom-call | flops 1073741824 | bytes 2097152 | tf_op jit(solution)/shard_map/held_rows/pallas_call | solution.py:217
  65.9 2.5 %held_rows.7 = (bf16[2,128,256]{2,1,0:T(8,128)(2,1)S(1)}, f32[2,64,1]{2,1,0:T(8,128)S(1)}, f32[2,64,1]{2,1,0:T(8,128)S(1)}, f32[2,64,256]{2,1,0:T(8,128)S(1)}) custom-call(s32[2]{0:T(128)S(1)} %sub.22.limit_ref, bf16[8,8192]{1,0:T(8,128)(2,1)S(1)} %copy-done.10, bf16[256,1024]{1,0:T(8,128)(2,1)S(1)} %copy-done.21, bf16[2,1024,256]{2,1,0:T(8,128)(2,1)S(1)} %copy-done.18), custom_call_target="tpu_custom_call" | custom-call | flops 1073741824 | bytes 2097152 | tf_op jit(solution)/shard_map/held_rows/pallas_call | solution.py:217
  68.5 5.3 %late_rows.1 = bf16[2,4,8192]{2,1,0:T(4,128)(2,1)} custom-call(s32[1,256]{1,0:T(1,128)S(1)} %select_n.43.column_slot_ref, bf16[256,256]{1,0:T(8,128)(2,1)S(1)} %bitcast.11, bf16[16,256]{1,0:T(8,128)(2,1)S(1)} %get-tuple-element.24.draft_latent_ref, bf16[256,1024]{1,0:T(8,128)(2,1)S(1)} %copy-done.1, bf16[2,128,256]{2,1,0:T(8,128)(2,1)S(1)} %get-tuple-element.25.refs_0_, ...), custom_call_target="tpu_custom_call" | custom-call | tf_op jit(solution)/shard_map/late_rows/pallas_call | solution.py:251
  (67 shorter events, 3.2 us)
Async XLA Ops:
  0.0 14.8 %collective-permute-start.2 = (bf16[512,256]{1,0:T(8,128)(2,1)}, bf16[512,256]{1,0:T(8,128)(2,1)S(1)}, u32[]{:S(2)}, u32[]{:S(2)}) collective-permute-start(bf16[512,256]{1,0:T(8,128)(2,1)} %refs_0_.1), channel_id=1, source_target_pairs={{0,12},{1,13},{2,14},{3,15},{4,0},{5,1},{6,2},{7,3},{8,4},{9,5},{1... | collective-permute-start | bytes 786440 | tf_op jit(solution)/shard_map/ppermute | solution.py:104
  5.0 13.5 %collective-permute-start = (bf16[512,256]{1,0:T(8,128)(2,1)}, bf16[512,256]{1,0:T(8,128)(2,1)S(1)}, u32[]{:S(2)}, u32[]{:S(2)}) collective-permute-start(bf16[512,256]{1,0:T(8,128)(2,1)} %refs_0_.1), channel_id=1, source_target_pairs={{0,4},{1,5},{2,6},{3,7},{4,8},{5,9},{6,10},{7,11},{8,12},{9,13},{1... | collective-permute-start | bytes 786440 | tf_op jit(solution)/shard_map/ppermute | solution.py:104
  5.1 22.6 %collective-permute-start.1 = (bf16[512,256]{1,0:T(8,128)(2,1)}, bf16[512,256]{1,0:T(8,128)(2,1)S(1)}, u32[]{:S(2)}, u32[]{:S(2)}) collective-permute-start(bf16[512,256]{1,0:T(8,128)(2,1)} %refs_0_.1), channel_id=1, source_target_pairs={{0,8},{1,9},{2,10},{3,11},{4,12},{5,13},{6,14},{7,15},{8,0},{9,1},... | collective-permute-start | bytes 786440 | tf_op jit(solution)/shard_map/ppermute | solution.py:104
  6.1 23.2 %collective-permute-start.3 = (bf16[512,256]{1,0:T(8,128)(2,1)}, bf16[512,256]{1,0:T(8,128)(2,1)S(1)}, u32[]{:S(2)}, u32[]{:S(2)}) collective-permute-start(bf16[512,256]{1,0:T(8,128)(2,1)} %refs_0_.1), channel_id=1, source_target_pairs={{0,2},{1,3},{2,0},{3,1},{4,6},{5,7},{6,4},{7,5},{8,10},{9,11},{10,... | collective-permute-start | bytes 786440 | tf_op jit(solution)/shard_map/ppermute | solution.py:104
  7.6 21.7 %collective-permute-start.7 = (bf16[512,256]{1,0:T(8,128)(2,1)}, bf16[512,256]{1,0:T(8,128)(2,1)S(1)}, u32[]{:S(2)}, u32[]{:S(2)}) collective-permute-start(bf16[512,256]{1,0:T(8,128)(2,1)} %refs_0_.1), channel_id=1, source_target_pairs={{0,1},{1,0},{2,3},{3,2},{4,5},{5,4},{6,7},{7,6},{8,9},{9,8},{10,11... | collective-permute-start | bytes 786440 | tf_op jit(solution)/shard_map/ppermute | solution.py:104
  9.1 24.0 %all-to-all-start = ((s32[16,1,2]{2,1,0:T(1,128)}), s32[16,1,2]{2,1,0:T(1,128)S(1)}, u32[]{:S(2)}, u32[]{:S(2)}) async-start(s32[16,1,2]{2,1,0:T(1,128)} %bitcast), calls=%async_computation | async-start | bytes 16384 | tf_op jit(solution)/shard_map/all_to_all | solution.py:205
  14.8 25.7 %collective-permute-start.6 = (bf16[512,256]{1,0:T(8,128)(2,1)S(1)}, bf16[512,256]{1,0:T(8,128)(2,1)}, u32[]{:S(2)}, u32[]{:S(2)}) collective-permute-start(bf16[512,256]{1,0:T(8,128)(2,1)S(1)} %collective-permute-done.2.refs_3_), channel_id=1, source_target_pairs={{0,2},{1,3},{2,0},{3,1},{4,6},{5,7},{6,4},{7,5},{8,10},{9,11},{10,... | collective-permute-start | bytes 786440 | tf_op jit(solution)/shard_map/ppermute | solution.py:104
  18.6 22.5 %collective-permute-start.10 = (bf16[512,256]{1,0:T(8,128)(2,1)S(1)}, bf16[512,256]{1,0:T(8,128)(2,1)}, u32[]{:S(2)}, u32[]{:S(2)}) collective-permute-start(bf16[512,256]{1,0:T(8,128)(2,1)S(1)} %collective-permute-done.2.refs_3_), channel_id=1, source_target_pairs={{0,1},{1,0},{2,3},{3,2},{4,5},{5,4},{6,7},{7,6},{8,9},{9,8},{10,11... | collective-permute-start | bytes 786440 | tf_op jit(solution)/shard_map/ppermute | solution.py:104
  27.7 9.3 %collective-permute-start.4 = (bf16[512,256]{1,0:T(8,128)(2,1)S(1)}, bf16[512,256]{1,0:T(8,128)(2,1)}, u32[]{:S(2)}, u32[]{:S(2)}) collective-permute-start(bf16[512,256]{1,0:T(8,128)(2,1)S(1)} %collective-permute-done.refs_1_), channel_id=1, source_target_pairs={{0,2},{1,3},{2,0},{3,1},{4,6},{5,7},{6,4},{7,5},{8,10},{9,11},{10,... | collective-permute-start | bytes 786440 | tf_op jit(solution)/shard_map/ppermute | solution.py:104
  29.2 2.2 %copy-start.3 = (bf16[512,256]{1,0:T(8,128)(2,1)}, bf16[512,256]{1,0:T(8,128)(2,1)S(1)}, u32[]{:S(2)}) copy-start(bf16[512,256]{1,0:T(8,128)(2,1)S(1)} %collective-permute-done.3.refs_4_) | copy-start | bytes 786436
  29.2 11.9 %collective-permute-start.8 = (bf16[512,256]{1,0:T(8,128)(2,1)S(1)}, bf16[512,256]{1,0:T(8,128)(2,1)}, u32[]{:S(2)}, u32[]{:S(2)}) collective-permute-start(bf16[512,256]{1,0:T(8,128)(2,1)S(1)} %collective-permute-done.refs_1_), channel_id=1, source_target_pairs={{0,1},{1,0},{2,3},{3,2},{4,5},{5,4},{6,7},{7,6},{8,9},{9,8},{10,11... | collective-permute-start | bytes 786440 | tf_op jit(solution)/shard_map/ppermute | solution.py:104
  29.2 3.8 %copy-start.5 = (bf16[512,256]{1,0:T(8,128)(2,1)}, bf16[512,256]{1,0:T(8,128)(2,1)S(1)}, u32[]{:S(2)}) copy-start(bf16[512,256]{1,0:T(8,128)(2,1)S(1)} %collective-permute-done.7.refs_8_) | copy-start | bytes 786436
  29.3 11.3 %collective-permute-start.5 = (bf16[512,256]{1,0:T(8,128)(2,1)S(1)}, bf16[512,256]{1,0:T(8,128)(2,1)}, u32[]{:S(2)}, u32[]{:S(2)}) collective-permute-start(bf16[512,256]{1,0:T(8,128)(2,1)S(1)} %collective-permute-done.1.refs_2_), channel_id=1, source_target_pairs={{0,2},{1,3},{2,0},{3,1},{4,6},{5,7},{6,4},{7,5},{8,10},{9,11},{10,... | collective-permute-start | bytes 786440 | tf_op jit(solution)/shard_map/ppermute | solution.py:104
  33.1 15.5 %copy-start = (bf16[128,8192]{1,0:T(8,128)(2,1)S(1)}, bf16[128,8192]{1,0:T(8,128)(2,1)}, u32[]{:S(2)}) copy-start(bf16[128,8192]{1,0:T(8,128)(2,1)} %prompt_ref.1) | copy-start | bytes 6291460
  33.1 15.5 %copy-start.2 = (bf16[512,256]{1,0:T(8,128)(2,1)S(1)}, bf16[512,256]{1,0:T(8,128)(2,1)}, u32[]{:S(2)}) copy-start(bf16[512,256]{1,0:T(8,128)(2,1)} %refs_0_.1) | copy-start | bytes 786436
  34.0 14.6 %copy-start.4 = (bf16[512,256]{1,0:T(8,128)(2,1)S(1)}, bf16[512,256]{1,0:T(8,128)(2,1)}, u32[]{:S(2)}) copy-start(bf16[512,256]{1,0:T(8,128)(2,1)} %copy-done.3) | copy-start | bytes 786436
  34.0 14.6 %copy-start.6 = (bf16[512,256]{1,0:T(8,128)(2,1)S(1)}, bf16[512,256]{1,0:T(8,128)(2,1)}, u32[]{:S(2)}) copy-start(bf16[512,256]{1,0:T(8,128)(2,1)} %copy-done.5) | copy-start | bytes 786436
  37.1 11.5 %collective-permute-start.9 = (bf16[512,256]{1,0:T(8,128)(2,1)S(1)}, bf16[512,256]{1,0:T(8,128)(2,1)S(1)}, u32[]{:S(2)}, u32[]{:S(2)}) collective-permute-start(bf16[512,256]{1,0:T(8,128)(2,1)S(1)} %collective-permute-done.1.refs_2_), channel_id=1, source_target_pairs={{0,1},{1,0},{2,3},{3,2},{4,5},{5,4},{6,7},{7,6},{8,9},{9,8},{10,11... | collective-permute-start | bytes 786440 | tf_op jit(solution)/shard_map/ppermute | solution.py:104
  40.6 8.0 %collective-permute-start.11 = (bf16[512,256]{1,0:T(8,128)(2,1)}, bf16[512,256]{1,0:T(8,128)(2,1)S(1)}, u32[]{:S(2)}, u32[]{:S(2)}) collective-permute-start(bf16[512,256]{1,0:T(8,128)(2,1)} %copy-done.3), channel_id=1, source_target_pairs={{0,1},{1,0},{2,3},{3,2},{4,5},{5,4},{6,7},{7,6},{8,9},{9,8},{10,11... | collective-permute-start | bytes 786440 | tf_op jit(solution)/shard_map/ppermute | solution.py:104
  40.6 8.0 %collective-permute-start.12 = (bf16[512,256]{1,0:T(8,128)(2,1)}, bf16[512,256]{1,0:T(8,128)(2,1)S(1)}, u32[]{:S(2)}, u32[]{:S(2)}) collective-permute-start(bf16[512,256]{1,0:T(8,128)(2,1)} %collective-permute-done.4.refs_5_), channel_id=1, source_target_pairs={{0,1},{1,0},{2,3},{3,2},{4,5},{5,4},{6,7},{7,6},{8,9},{9,8},{10,11... | collective-permute-start | bytes 786440 | tf_op jit(solution)/shard_map/ppermute | solution.py:104
  41.1 7.5 %collective-permute-start.13 = (bf16[512,256]{1,0:T(8,128)(2,1)}, bf16[512,256]{1,0:T(8,128)(2,1)S(1)}, u32[]{:S(2)}, u32[]{:S(2)}) collective-permute-start(bf16[512,256]{1,0:T(8,128)(2,1)} %collective-permute-done.5.refs_6_), channel_id=1, source_target_pairs={{0,1},{1,0},{2,3},{3,2},{4,5},{5,4},{6,7},{7,6},{8,9},{9,8},{10,11... | collective-permute-start | bytes 786440 | tf_op jit(solution)/shard_map/ppermute | solution.py:104
  41.1 7.4 %collective-permute-start.14 = (bf16[512,256]{1,0:T(8,128)(2,1)}, bf16[512,256]{1,0:T(8,128)(2,1)S(1)}, u32[]{:S(2)}, u32[]{:S(2)}) collective-permute-start(bf16[512,256]{1,0:T(8,128)(2,1)} %collective-permute-done.6.refs_7_), channel_id=1, source_target_pairs={{0,1},{1,0},{2,3},{3,2},{4,5},{5,4},{6,7},{7,6},{8,9},{9,8},{10,11... | collective-permute-start | bytes 786440 | tf_op jit(solution)/shard_map/ppermute | solution.py:104
  47.9 3.1 %copy-start.12 = (f32[2,64,1]{2,1,0:T(8,128)}, f32[2,64,1]{2,1,0:T(8,128)S(1)}, u32[]{:S(2)}) copy-start(f32[2,64,1]{2,1,0:T(8,128)S(1)} %get-tuple-element.26.refs_1_) | copy-start | bytes 1540
  47.9 3.1 %copy-start.14 = (f32[2,64,1]{2,1,0:T(8,128)}, f32[2,64,1]{2,1,0:T(8,128)S(1)}, u32[]{:S(2)}) copy-start(f32[2,64,1]{2,1,0:T(8,128)S(1)} %get-tuple-element.27.refs_2_) | copy-start | bytes 1540
  51.6 10.5 %copy-start.22 = (s32[16,16]{1,0:T(8,128)S(1)}, s32[16,16]{1,0:T(8,128)}, u32[]{:S(2)}) copy-start(s32[16,16]{1,0:T(8,128)} %select_select_fusion) | copy-start | bytes 3076
  51.6 16.8 %all-to-all-start.1 = ((bf16[16,16,256]{2,1,0:T(8,128)(2,1)}), bf16[16,16,256]{2,1,0:T(8,128)(2,1)S(1)}, u32[]{:S(2)}, u32[]{:S(2)}) async-start(bf16[16,16,256]{2,1,0:T(8,128)(2,1)} %bitcast.12), calls=%async_computation.1 | async-start | bytes 262144 | tf_op jit(solution)/shard_map/all_to_all | solution.py:246
  62.2 1.2 %copy-start.18 = (bf16[2,1024,256]{2,1,0:T(8,128)(2,1)S(1)}, bf16[2,1024,256]{2,1,0:T(8,128)(2,1)}, u32[]{:S(2)}) copy-start(bf16[2,1024,256]{2,1,0:T(8,128)(2,1)} %cache_ref.7) | copy-start | bytes 3145732
  63.4 2.5 %copy-start.21 = (bf16[256,1024]{1,0:T(8,128)(2,1)S(1)}, bf16[256,1024]{1,0:T(8,128)(2,1)}, u32[]{:S(2)}) copy-start(bf16[256,1024]{1,0:T(8,128)(2,1)} %key_up_ref.7) | copy-start | bytes 1572868
  65.9 2.5 %copy-start.1 = (bf16[256,1024]{1,0:T(8,128)(2,1)S(1)}, bf16[256,1024]{1,0:T(8,128)(2,1)}, u32[]{:S(2)}) copy-start(bf16[256,1024]{1,0:T(8,128)(2,1)} %value_up_ref.1) | copy-start | bytes 1572868
  65.9 2.5 %copy-start.8 = (f32[2,64,256]{2,1,0:T(8,128)S(1)}, f32[2,64,256]{2,1,0:T(8,128)}, u32[]{:S(2)}) copy-start(f32[2,64,256]{2,1,0:T(8,128)} %copy-done.7) | copy-start | bytes 393220
  65.9 2.5 %copy-start.13 = (f32[2,64,1]{2,1,0:T(8,128)S(1)}, f32[2,64,1]{2,1,0:T(8,128)}, u32[]{:S(2)}) copy-start(f32[2,64,1]{2,1,0:T(8,128)} %copy-done.12) | copy-start | bytes 1540
  65.9 2.5 %copy-start.15 = (f32[2,64,1]{2,1,0:T(8,128)S(1)}, f32[2,64,1]{2,1,0:T(8,128)}, u32[]{:S(2)}) copy-start(f32[2,64,1]{2,1,0:T(8,128)} %copy-done.14) | copy-start | bytes 1540
  (8 other events, 7.7 us)

commit v3 on v1

v3 whole, which is shorter than its diff:
```python
import functools
import math

import jax
import jax.numpy as jnp
from jax import lax
from jax.experimental import pallas as pl
from jax.experimental.pallas import tpu as pltpu
from jax.sharding import PartitionSpec as P

QUERY_HEADS = 64
HEAD_SIZE = 128
FAR = -1e30
NT = (((1,), (1,)), ((), ()))
WHOLE = pl.BlockSpec(memory_space=pltpu.VMEM)
SCALARS = pl.BlockSpec(memory_space=pltpu.SMEM)
UNREAD = pl.BlockSpec(memory_space=pl.ANY)


def params(mib):
    return pltpu.CompilerParams(vmem_limit_bytes=mib * 1024 * 1024)


def split_rows(x):
    top = x.astype(jnp.bfloat16)
    rest = (x - top.astype(jnp.float32)).astype(jnp.bfloat16)
    return jnp.concatenate([top, rest], 0)


def join_rows(x):
    half = x.shape[0] // 2
    return x[:half] + x[half:]


def held_kernel(
    limit_ref, query_ref, key_up_ref, cache_ref, turned_ref, peak_ref, total_ref, mixed_ref, float_ref, scores_ref
):
    slot_count, span_rows, _ = cache_ref.shape
    draft_count = query_ref.shape[1]
    heads_kv = key_up_ref.shape[1] // HEAD_SIZE
    group_size = QUERY_HEADS // heads_kv
    rows = group_size * draft_count
    scale = math.log2(math.e) / math.sqrt(HEAD_SIZE)
    step = 256
    for k in range(heads_kv):
        pieces = []
        for b in range(slot_count):
            for g in range(group_size):
                lane = (k * group_size + g) * HEAD_SIZE
                pieces.append(query_ref[b, :, lane : lane + HEAD_SIZE].astype(jnp.float32))
        query = jnp.concatenate(pieces, 0).astype(jnp.bfloat16)
        key_up = key_up_ref[:, k * HEAD_SIZE : (k + 1) * HEAD_SIZE]
        turned = lax.dot_general(query, key_up, NT, preferred_element_type=jnp.float32) * scale
        for b in range(slot_count):
            float_ref[b, k * rows : (k + 1) * rows, :] = turned[b * rows : (b + 1) * rows]
    for b in range(slot_count):
        turned_ref[b] = split_rows(float_ref[b])
        peak = None
        for c in range(0, span_rows, step):
            scores = join_rows(
                lax.dot_general(turned_ref[b], cache_ref[b, c : c + step], NT, preferred_element_type=jnp.float32)
            )
            column = lax.broadcasted_iota(jnp.int32, (1, step), 1) + c
            scores = jnp.where(column < limit_ref[b], scores, FAR)
            scores_ref[:, c : c + step] = scores
            top = jnp.max(scores, 1, keepdims=True)
            peak = top if peak is None else jnp.maximum(peak, top)
        peak_ref[b] = peak
        total = jnp.zeros_like(peak)
        mixed = jnp.zeros(mixed_ref.shape[1:], jnp.float32)
        for c in range(0, span_rows, step):
            weights = jnp.exp2(scores_ref[:, c : c + step] - peak)
            total += jnp.sum(weights, 1, keepdims=True)
            mixed += join_rows(
                jnp.dot(split_rows(weights), cache_ref[b, c : c + step], preferred_element_type=jnp.float32)
            )
        total_ref[b] = total
        mixed_ref[b] = mixed


def down_kernel(trails, starts_of, groups, first, me_ref, *refs):
    row_refs, refs = refs[: 2 * groups], refs[2 * groups :]
    sum_refs = None
    if not first:
        sum_refs, refs = refs[:groups], refs[groups:]
    piece_refs, out_refs = refs[: len(trails)], refs[-groups:]
    starts = starts_of(me_ref, trails)
    count = row_refs[0].shape[0]
    slot_count, draft_count, _ = row_refs[1].shape
    drafts = slot_count * draft_count
    total = None
    for start, piece_ref in zip(starts, piece_refs):
        depth = piece_ref.shape[0]
        lanes = pl.ds(pl.multiple_of(start, HEAD_SIZE), depth)
        stack = [
            row_refs[2 * n + 1][b, :, lanes].astype(jnp.float32) for n in range(groups) for b in range(slot_count)
        ]
        if groups * drafts < 16:
            stack.append(jnp.zeros((16 - groups * drafts, depth), jnp.float32))
        rows = [row_refs[2 * n][:, lanes] for n in range(groups)] + [jnp.concatenate(stack, 0).astype(jnp.bfloat16)]
        product = jnp.dot(jnp.concatenate(rows, 0), piece_ref[...], preferred_element_type=jnp.float32)
        total = product if total is None else total + product
    for n in range(groups):
        prompt_sum = total[n * count : (n + 1) * count]
        draft_sum = total[groups * count + n * drafts : groups * count + (n + 1) * drafts]
        if sum_refs is not None:
            prompt_sum += sum_refs[n][:count, :]
            draft_sum += sum_refs[n][count:, :]
        out_refs[n][:count, :] = prompt_sum
        out_refs[n][count:, :] = draft_sum


def place_kernel(parts, place_ref, *refs):
    sum_refs, (outgoing_ref, draft_latent_ref) = refs[:parts], refs[-2:]
    total = sum_refs[0][...]
    for ref in sum_refs[1:]:
        total += ref[...]
    latent = total.astype(jnp.bfloat16)
    count = place_ref.shape[1]
    draft_latent_ref[...] = total[count:].astype(jnp.bfloat16).astype(jnp.float32)
    spot = lax.broadcasted_iota(jnp.int32, (outgoing_ref.shape[0], count), 0)
    chosen = jnp.where(spot == place_ref[...], 1.0, 0.0).astype(jnp.bfloat16)
    outgoing_ref[...] = jnp.dot(chosen, latent[:count], preferred_element_type=jnp.float32).astype(jnp.bfloat16)


def late_kernel(
    column_slot_ref, incoming_ref, draft_latent_ref, turned_ref, peak_ref, total_ref, mixed_ref, value_up_ref,
    out_ref, rows_ref, parted_ref,
):
    slot_count, draft_count, _ = out_ref.shape
    tile = slot_count * draft_count
    heads_kv = value_up_ref.shape[1] // HEAD_SIZE
    group_size = QUERY_HEADS // heads_kv
    head_rows = group_size * draft_count
    rows = peak_ref.shape[1]
    arrived = incoming_ref.shape[0]
    span = rows_ref.shape[0]
    drafts = jnp.concatenate([draft_latent_ref[...], jnp.zeros((span - arrived - tile, rows_ref.shape[1]), jnp.float32)], 0)
    rows_ref[:arrived, :] = incoming_ref[...]
    rows_ref[arrived:, :] = drafts.astype(jnp.bfloat16)
    token = lax.broadcasted_iota(jnp.int32, (rows, 1), 0) % draft_count
    column = lax.broadcasted_iota(jnp.int32, (rows, span - arrived), 1)
    for b in range(slot_count):
        scores = join_rows(lax.dot_general(turned_ref[b], rows_ref[...], NT, preferred_element_type=jnp.float32))
        draft_seen = (column >= b * draft_count) & (column <= b * draft_count + token)
        scores = jnp.concatenate(
            [
                jnp.where(column_slot_ref[...] == b, scores[:, :arrived], FAR),
                jnp.where(draft_seen, scores[:, arrived:], FAR),
            ],
            1,
        )
        peak = jnp.maximum(jnp.max(scores, 1, keepdims=True), peak_ref[b])
        weights = jnp.exp2(scores - peak)
        fade = jnp.exp2(peak_ref[b] - peak)
        total = total_ref[b] * fade + jnp.sum(weights, 1, keepdims=True)
        mixed = join_rows(jnp.dot(split_rows(weights), rows_ref[...], preferred_element_type=jnp.float32))
        parted_ref[b] = split_rows((mixed_ref[b] * fade + mixed) / total)
    for k in range(heads_kv):
        part = []
        for b in range(slot_count):
            part.append(parted_ref[b, k * head_rows : (k + 1) * head_rows, :])
            part.append(parted_ref[b, rows + k * head_rows : rows + (k + 1) * head_rows, :])
        value_up = value_up_ref[:, k * HEAD_SIZE : (k + 1) * HEAD_SIZE]
        both = jnp.dot(jnp.concatenate(part, 0), value_up, preferred_element_type=jnp.float32)
        for b in range(slot_count):
            result = join_rows(both[b * 2 * head_rows : (b + 1) * 2 * head_rows])
            wide = jnp.concatenate(
                [result[g * draft_count : (g + 1) * draft_count] for g in range(group_size)], 1
            )
            out_ref[b, :, k * group_size * HEAD_SIZE : (k + 1) * group_size * HEAD_SIZE] = wide.astype(jnp.bfloat16)


def down_sums(prompt_hidden, draft_hidden, shard, wide_size):
    shard_rows, latent_width = shard.shape
    count = prompt_hidden.shape[0]
    slot_count, draft_count, _ = draft_hidden.shape
    sum_shape = jax.ShapeDtypeStruct((count + slot_count * draft_count, latent_width), jnp.float32)
    rep, wide = lax.axis_index("rep"), lax.axis_index("wide")
    me = jnp.stack([rep, wide])

    def call(stages, starts_of, groups, rows, tie=()):
        sums = []
        for n, stage in enumerate(stages):
            trails, pieces = [t for t, _ in stage], [x for _, x in stage]
            ties = tie if n == len(stages) - 1 else ()
            sums = pl.pallas_call(
                functools.partial(down_kernel, trails, starts_of, groups, n == 0),
                out_shape=[sum_shape] * groups,
                in_specs=[SCALARS] + [WHOLE] * (len(rows) + len(sums) + len(pieces)) + [UNREAD] * len(ties),
                out_specs=[WHOLE] * groups,
                compiler_params=params(16),
                cost_estimate=pl.CostEstimate(flops=2**28, bytes_accessed=2**20, transcendentals=0),
                name="down_rows",
            )(me, *rows, *sums, *pieces, *ties)
        return sums

    if wide_size != 16 or lax.axis_size("rep") != 2:
        whole = lax.all_gather(shard, "wide", axis=0, tiled=True)
        return lambda tie: call([[(0, whole)]], lambda me_ref, trails: trails, 1, [prompt_hidden, draft_hidden], tie)

    sizes = (2, wide_size // 4, 2, 2)
    spots = [(r, z, y, c) for r in range(2) for z in range(sizes[1]) for y in range(2) for c in range(2)]

    def flat(spot):
        return ((spot[0] * sizes[1] + spot[1]) * 2 + spot[2]) * 2 + spot[3]

    def move(x, axis, step=1):
        pairs = []
        for spot in spots:
            to = list(spot)
            to[axis] = (to[axis] + step) % sizes[axis]
            pairs.append((flat(spot), flat(to)))
        return lax.ppermute(x, ("rep", "wide"), pairs)

    half_rows = shard_rows // 2
    half = lax.dynamic_slice(shard, (rep * half_rows, 0), (half_rows, latent_width))
    z1, z3 = move(half, 1, 1), move(half, 1, -1)
    y0 = move(shard, 2)
    other_prompt, other_draft = move(prompt_hidden, 3), move(draft_hidden, 3)
    yz1, yz3, xz1, xz3 = move(z1, 2), move(z3, 2), move(z1, 0), move(z3, 0)
    z2 = move(z1, 1, 1)
    xz2, yz2 = move(z2, 0), move(z2, 2)
    xyz1, xyz3 = move(yz1, 0), move(yz3, 0)
    yxz2 = move(xz2, 2)

    def starts_of(me_ref, trails):
        rep, wide = me_ref[0], me_ref[1]
        z, y, c = wide // 4, wide // 2 % 2, wide % 2
        starts = []
        for x_step, z_step, y_step, is_half in trails:
            owner = ((z - z_step + sizes[1]) % sizes[1] * 2 + (y + y_step) % 2) * 2 + c
            starts.append(owner * shard_rows + (rep + x_step) % 2 * half_rows * is_half)
        return starts

    stages = [
        [((0, 0, 0, 0), shard), ((0, 0, 1, 0), y0), ((0, 1, 0, 1), z1), ((0, 3, 0, 1), z3)],
        [((0, 1, 1, 1), yz1), ((0, 3, 1, 1), yz3), ((1, 1, 0, 1), xz1), ((1, 3, 0, 1), xz3)],
        [((0, 2, 0, 1), z2), ((0, 2, 1, 1), yz2), ((1, 2, 0, 1), xz2), ((1, 2, 1, 1), yxz2)],
        [((1, 1, 1, 1), xyz1), ((1, 3, 1, 1), xyz3)],
    ]
    rows = [prompt_hidden, draft_hidden, other_prompt, other_draft]

    def finish(tie):
        mine, others = call(stages, starts_of, 2, rows, tie)
        return [mine, move(others, 3)]

    return finish


def local(
    prompt_hidden,
    resident_latent,
    row_target,
    row_offset,
    context_len,
    draft_hidden,
    draft_query_heads,
    down_weight,
    key_up_weight,
    value_up_weight,
):
    f32, bf16 = jnp.float32, jnp.bfloat16
    wide_size = lax.axis_size("wide")
    row_count = prompt_hidden.shape[0]
    slot_count, span_rows, latent_width = resident_latent.shape
    draft_count = draft_hidden.shape[1]
    tile = slot_count * draft_count
    rows = QUERY_HEADS * draft_count
    most_rows = 2 * ((row_count + wide_size - 1) // wide_size)
    arrived = wide_size * most_rows

    finish = down_sums(prompt_hidden, draft_hidden, down_weight, wide_size)

    index = jnp.arange(row_count, dtype=jnp.int32)
    same = (row_target[:, None] == row_target[None, :]) & (index[None, :] < index[:, None])
    rank = jnp.sum(same.astype(jnp.int32), 1)
    front = row_target % slot_count == 0
    place = row_target // slot_count * most_rows + jnp.where(front, rank, most_rows - 1 - rank)
    request = jnp.arange(wide_size * slot_count, dtype=jnp.int32)
    counts = jnp.sum((row_target[None, :] == request[:, None]).astype(jnp.int32), 1)
    counts = lax.all_to_all(counts.reshape(wide_size, slot_count), "wide", split_axis=0, concat_axis=0, tiled=True)
    limit = context_len - jnp.sum(counts, 0)
    spot = jnp.arange(most_rows, dtype=jnp.int32)[None, :]
    column_slot = jnp.where(
        spot < counts[:, 0:1], 0, jnp.where(spot >= most_rows - counts[:, 1:2], 1, -1)
    ).reshape(1, arrived)

    turned, peak, total, mixed = pl.pallas_call(
        held_kernel,
        out_shape=[
            jax.ShapeDtypeStruct((slot_count, 2 * rows, latent_width), bf16),
            jax.ShapeDtypeStruct((slot_count, rows, 1), f32),
            jax.ShapeDtypeStruct((slot_count, rows, 1), f32),
            jax.ShapeDtypeStruct((slot_count, rows, latent_width), f32),
        ],
        in_specs=[SCALARS, WHOLE, WHOLE, WHOLE],
        out_specs=[WHOLE] * 4,
        scratch_shapes=[pltpu.VMEM((slot_count, rows, latent_width), f32), pltpu.VMEM((rows, span_rows), f32)],
        compiler_params=params(24),
        cost_estimate=pl.CostEstimate(flops=2**31, bytes_accessed=2**22, transcendentals=2**19),
        name="held_rows",
    )(limit, draft_query_heads, key_up_weight, resident_latent)

    sums = finish((peak,))
    outgoing, draft_latent = pl.pallas_call(
        functools.partial(place_kernel, len(sums)),
        out_shape=[
            jax.ShapeDtypeStruct((arrived, latent_width), bf16),
            jax.ShapeDtypeStruct((tile, latent_width), f32),
        ],
        in_specs=[WHOLE] * (1 + len(sums)),
        out_specs=[WHOLE] * 2,
        compiler_params=params(16),
        name="place_rows",
    )(place.reshape(1, row_count), *sums)

    incoming = lax.all_to_all(
        outgoing.reshape(wide_size, most_rows, latent_width), "wide", split_axis=0, concat_axis=0, tiled=True
    ).reshape(arrived, latent_width)

    span = (arrived + tile + 127) // 128 * 128
    return pl.pallas_call(
        late_kernel,
        out_shape=jax.ShapeDtypeStruct((slot_count, draft_count, QUERY_HEADS * HEAD_SIZE), bf16),
        in_specs=[WHOLE] * 8,
        out_specs=WHOLE,
        scratch_shapes=[
            pltpu.VMEM((span, latent_width), bf16),
            pltpu.VMEM((slot_count, 2 * rows, latent_width), bf16),
        ],
        compiler_params=params(24),
        name="late_rows",
    )(column_slot, incoming, draft_latent, turned, peak, total, mixed, value_up_weight)


def solution(mesh):
    placed = (
        P(("rep", "wide"), None),
        P(("rep", "wide"), None, None),
        P(("rep", "wide")),
        P(("rep", "wide")),
        P(("rep", "wide")),
        P(("rep", "wide"), None, None),
        P(("rep", "wide"), None, None),
        P("wide", None),
        P(),
        P(),
    )
    return jax.shard_map(
        local, mesh=mesh, in_specs=placed, out_specs=P(("rep", "wide"), None, None), check_vma=False
    )
```

time: 95.2 us -> 66.9 us (0.70)
  waiting for transfers between devices: 43 us -> 15 us
  starting transfers between devices: 10.9 us -> 27.5 us
  between operations: 13.5 us -> 0.26 us
  Pallas kernels: 16.7 us -> 11.2 us
  local copies, waits for them, and re-layouts: 7.59 us -> 9.87 us
    all_gather x1 -> x0, waiting for transfers between devices: 39.4 us -> none  [local(): weight = lax.all_gather(down_weight, 'wide', axis=0, tiled=True)]
    ppermute x0 -> x16, starting transfers between devices: none -> 16.7 us  [move(): return lax.ppermute(x, ('rep', 'wide'), pairs)]
    all_to_all x1, waiting for transfers between devices: 0.01 us -> 7.77 us  [local(): lax.all_to_all(outgoing.reshape(wide_size, most_rows, latent_width), 'wid...]
    ppermute x0 -> x16, waiting for transfers between devices: none -> 6.59 us  [move(): return lax.ppermute(x, ('rep', 'wide'), pairs)]
    unnamed x10 -> x36, local copies, waits for them, and re-layouts: 4.82 us -> 8.06 us
    pallas_call x1, Pallas kernels: 5.31 us -> 2.08 us  [local(): pl.pallas_call(late_kernel, out_shape=jax.ShapeDtypeStruct((slot_count, d...]
    pallas_call x2 -> x6, Pallas kernels: 11.4 us -> 9.17 us  [the longest x4 5.66 us: call(): pl.pallas_call(functools.partial(down_kernel, trails, starts_of, groups,...]
    all_to_all x1, waiting for transfers between devices: 2.83 us -> 0.62 us  [local(): lax.all_to_all(counts.reshape(wide_size, slot_count), 'wide', split_axis=...]
  transfers between devices with their start and end apart: 3 -> 18, of which waited for: 2 -> 5; matrix products, arithmetic and copies ran while one was open for 5% -> 5% of each run, Pallas kernels for 9% -> 10%
where the time goes in v3:
time: 66.9 us; the launch traced here: 66.4 us
  starting transfers between devices  27.5 us (41%)
  waiting for transfers between devices  15 us (22%)
  Pallas kernels  11.2 us (17%)
  local copies, waits for them, and re-layouts  9.87 us (15%)
  other arithmetic  2.52 us (4%)
    ppermute x16, starting transfers between devices, move(): return lax.ppermute(x, ('rep', 'wide'), pairs)  16.7 us
    unnamed x36, local copies, waits for them, and re-layouts  8.06 us
    all_to_all x1, waiting for transfers between devices, local(): lax.all_to_all(outgoing.reshape(wide_size, most_rows, latent_width), 'wid...  7.77 us
    ppermute x16, waiting for transfers between devices, move(): return lax.ppermute(x, ('rep', 'wide'), pairs)  6.59 us
    all_to_all x1, starting transfers between devices, local(): lax.all_to_all(counts.reshape(wide_size, slot_count), 'wide', split_axis=...  5.77 us
    pallas_call x4, Pallas kernels, call(): pl.pallas_call(functools.partial(down_kernel, trails, starts_of, groups,...  5.66 us
    all_to_all x1, starting transfers between devices, local(): lax.all_to_all(outgoing.reshape(wide_size, most_rows, latent_width), 'wid...  5.08 us
    pallas_call x1, Pallas kernels, local(): pl.pallas_call(held_kernel, out_shape=[jax.ShapeDtypeStruct((slot_count,...  2.67 us
  transfers between devices with their start and end apart: 18, of which 5 were waited for; matrix products, arithmetic and copies ran while one was open for 5% of the time, Pallas kernels for 10%

profile of v3, /device:TPU:0, one launch (start us, length us, event | category | flops | bytes accessed | tf_op | source)
XLA Modules:
  0.0 66.4 jit_solution(6733260032261079575)
XLA Ops:
  0.5 2.5 %collective-permute-start.2 = (bf16[512,256]{1,0:T(8,128)(2,1)}, bf16[512,256]{1,0:T(8,128)(2,1)S(1)}, u32[]{:S(2)}, u32[]{:S(2)}) collective-permute-start(bf16[512,256]{1,0:T(8,128)(2,1)} %refs_4_.1), channel_id=1, source_target_pairs={{0,2},{1,3},{2,0},{3,1},{4,6},{5,7},{6,4},{7,5},{8,10},{9,11},{10,... | collective-permute-start | bytes 786440 | tf_op jit(solution)/shard_map/ppermute | solution.py:214
  3.0 0.9 %constant_dynamic-slice_fusion = bf16[256,256]{1,0:T(8,128)(2,1)S(1)} fusion(bf16[512,256]{1,0:T(8,128)(2,1)} %refs_4_.1, s32[]{:T(128)S(6)} %select_n.50), kind=kLoop, calls=%fused_computation.19 | loop fusion | bytes 262148 | tf_op jit(solution)/shard_map/dynamic_slice | solution.py:217
  3.9 1.6 %collective-permute-start.3 = (bf16[256,256]{1,0:T(8,128)(2,1)S(1)}, bf16[256,256]{1,0:T(8,128)(2,1)S(1)}, u32[]{:S(2)}, u32[]{:S(2)}) collective-permute-start(bf16[256,256]{1,0:T(8,128)(2,1)S(1)} %constant_dynamic-slice_fusion), channel_id=1, source_target_pairs={{0,4},{1,5},{2,6},{3,7},{4,8},{5,9},{6,10},{7,11},{8,12},{9,13},{1... | collective-permute-start | bytes 393224 | tf_op jit(solution)/shard_map/ppermute | solution.py:214
  5.6 2.3 %collective-permute-start.4 = (bf16[256,256]{1,0:T(8,128)(2,1)S(1)}, bf16[256,256]{1,0:T(8,128)(2,1)}, u32[]{:S(2)}, u32[]{:S(2)}) collective-permute-start(bf16[256,256]{1,0:T(8,128)(2,1)S(1)} %constant_dynamic-slice_fusion), channel_id=1, source_target_pairs={{0,12},{1,13},{2,14},{3,15},{4,0},{5,1},{6,2},{7,3},{8,4},{9,5},{1... | collective-permute-start | bytes 393224 | tf_op jit(solution)/shard_map/ppermute | solution.py:214
  7.9 4.3 %collective-permute-done.3.refs_6_ = bf16[256,256]{1,0:T(8,128)(2,1)S(1)} collective-permute-done((bf16[256,256]{1,0:T(8,128)(2,1)S(1)}, bf16[256,256]{1,0:T(8,128)(2,1)S(1)}, u32[]{:S(2)}, u32[]{:S(2)}) %collective-permute-start.3) | collective-permute-done | bytes 131104 | tf_op jit(solution)/shard_map/ppermute | solution.py:214
  12.2 0.8 %convert_reduce_fusion.1 = s32[32]{0:T(128)S(1)} fusion(s32[128]{0:T(128)} %param.12), kind=kLoop, calls=%fused_computation.3 | loop fusion | flops 12256 | bytes 640 | tf_op jit(solution)/shard_map/reduce_sum | solution.py:281
  13.0 0.7 %all_to_all.11 = s32[16,1,2]{2,0,1:T(8,128)} reshape(s32[32]{0:T(128)S(1)} %convert_reduce_fusion.1) | data formatting | bytes 256 | tf_op jit(solution)/shard_map/all_to_all | solution.py:282
  13.7 5.8 %all-to-all-start = ((s32[16,1,2]{2,1,0:T(1,128)}), s32[16,1,2]{2,1,0:T(1,128)S(1)}, u32[]{:S(2)}, u32[]{:S(2)}) async-start(s32[16,1,2]{2,1,0:T(1,128)} %bitcast), calls=%async_computation | async-start | bytes 16384 | tf_op jit(solution)/shard_map/all_to_all | solution.py:282
  19.4 2.0 %collective-permute-start.5 = (bf16[256,256]{1,0:T(8,128)(2,1)S(1)}, bf16[256,256]{1,0:T(8,128)(2,1)}, u32[]{:S(2)}, u32[]{:S(2)}) collective-permute-start(bf16[256,256]{1,0:T(8,128)(2,1)S(1)} %collective-permute-done.3.refs_6_), channel_id=1, source_target_pairs={{0,2},{1,3},{2,0},{3,1},{4,6},{5,7},{6,4},{7,5},{8,10},{9,11},{10,... | collective-permute-start | bytes 393224 | tf_op jit(solution)/shard_map/ppermute | solution.py:214
  21.4 1.5 %collective-permute-start.7 = (bf16[256,256]{1,0:T(8,128)(2,1)S(1)}, bf16[256,256]{1,0:T(8,128)(2,1)S(1)}, u32[]{:S(2)}, u32[]{:S(2)}) collective-permute-start(bf16[256,256]{1,0:T(8,128)(2,1)S(1)} %collective-permute-done.3.refs_6_), channel_id=1, source_target_pairs={{0,16},{1,17},{2,18},{3,19},{4,20},{5,21},{6,22},{7,23},{8,24},{9,... | collective-permute-start | bytes 393224 | tf_op jit(solution)/shard_map/ppermute | solution.py:214
  24.2 0.9 %convert_reduce_fusion = s32[128]{0:T(128)S(1)} fusion(s32[128]{0:T(128)} %param.12), kind=kLoop, calls=%fused_computation | loop fusion | flops 81792 | bytes 1024 | tf_op jit(solution)/shard_map/reduce_sum | solution.py:277
  26.6 1.6 %collective-permute-start.8 = (bf16[256,256]{1,0:T(8,128)(2,1)}, bf16[256,256]{1,0:T(8,128)(2,1)S(1)}, u32[]{:S(2)}, u32[]{:S(2)}) collective-permute-start(bf16[256,256]{1,0:T(8,128)(2,1)} %collective-permute-done.4.refs_7_), channel_id=1, source_target_pairs={{0,16},{1,17},{2,18},{3,19},{4,20},{5,21},{6,22},{7,23},{8,24},{9,... | collective-permute-start | bytes 393224 | tf_op jit(solution)/shard_map/ppermute | solution.py:214
  28.1 0.8 %collective-permute-done.6.refs_7_ = bf16[256,256]{1,0:T(8,128)(2,1)} collective-permute-done((bf16[256,256]{1,0:T(8,128)(2,1)}, bf16[256,256]{1,0:T(8,128)(2,1)}, u32[]{:S(2)}, u32[]{:S(2)}) %collective-permute-start.6) | collective-permute-done | bytes 131104 | tf_op jit(solution)/shard_map/ppermute | solution.py:214
  28.9 1.1 %collective-permute-start.10 = (bf16[256,256]{1,0:T(8,128)(2,1)}, bf16[256,256]{1,0:T(8,128)(2,1)S(1)}, u32[]{:S(2)}, u32[]{:S(2)}) collective-permute-start(bf16[256,256]{1,0:T(8,128)(2,1)} %collective-permute-done.9.refs_6_), channel_id=1, source_target_pairs={{0,2},{1,3},{2,0},{3,1},{4,6},{5,7},{6,4},{7,5},{8,10},{9,11},{10,... | collective-permute-start | bytes 393224 | tf_op jit(solution)/shard_map/ppermute | solution.py:214
  30.6 1.5 %collective-permute-start.13 = (bf16[256,256]{1,0:T(8,128)(2,1)}, bf16[256,256]{1,0:T(8,128)(2,1)S(1)}, u32[]{:S(2)}, u32[]{:S(2)}) collective-permute-start(bf16[256,256]{1,0:T(8,128)(2,1)} %collective-permute-done.5.refs_6_), channel_id=1, source_target_pairs={{0,16},{1,17},{2,18},{3,19},{4,20},{5,21},{6,22},{7,23},{8,24},{9,... | collective-permute-start | bytes 393224 | tf_op jit(solution)/shard_map/ppermute | solution.py:214
  32.6 1.0 %collective-permute-start.12 = (bf16[256,256]{1,0:T(8,128)(2,1)}, bf16[256,256]{1,0:T(8,128)(2,1)S(1)}, u32[]{:S(2)}, u32[]{:S(2)}) collective-permute-start(bf16[256,256]{1,0:T(8,128)(2,1)} %collective-permute-done.11.refs_8_), channel_id=1, source_target_pairs={{0,2},{1,3},{2,0},{3,1},{4,6},{5,7},{6,4},{7,5},{8,10},{9,11},{10,... | collective-permute-start | bytes 393224 | tf_op jit(solution)/shard_map/ppermute | solution.py:214
  33.6 1.2 %copy-done.14 = bf16[2,1024,256]{2,1,0:T(8,128)(2,1)S(1)} copy-done((bf16[2,1024,256]{2,1,0:T(8,128)(2,1)S(1)}, bf16[2,1024,256]{2,1,0:T(8,128)(2,1)}, u32[]{:S(2)}) %copy-start.14) | copy-done | bytes 1048600
  34.8 1.0 %copy-done.15 = bf16[256,1024]{1,0:T(8,128)(2,1)S(1)} copy-done((bf16[256,1024]{1,0:T(8,128)(2,1)S(1)}, bf16[256,1024]{1,0:T(8,128)(2,1)}, u32[]{:S(2)}) %copy-start.15) | copy-done | bytes 524312
  35.9 0.9 %copy-done.16 = bf16[2,4,8192]{2,1,0:T(4,128)(2,1)S(1)} copy-done((bf16[2,4,8192]{2,1,0:T(4,128)(2,1)S(1)}, bf16[2,4,8192]{2,1,0:T(4,128)(2,1)}, u32[]{:S(2)}) %copy-start.16) | copy-done | bytes 131096
  36.8 2.7 %held_rows.1 = (bf16[2,512,256]{2,1,0:T(8,128)(2,1)S(1)}, f32[2,256,1]{2,1,0:T(8,128)S(1)}, f32[2,256,1]{2,1,0:T(8,128)S(1)}, f32[2,256,256]{2,1,0:T(8,128)S(1)}) custom-call(s32[2]{0:T(128)S(1)} %sub.22.limit_ref, bf16[2,4,8192]{2,1,0:T(4,128)(2,1)S(1)} %copy-done.16, bf16[256,1024]{1,0:T(8,128)(2,1)S(1)} %copy-done.15, bf16[2,1024,256]{2,1,0:T(8,128)(2,1)S(1)} %copy-done.14), custom_call_target="tpu_custom_call" | custom-call | flops 2147483648 | bytes 4194304 | tf_op jit(solution)/shard_map/held_rows/pallas_call | solution.py:289
  39.5 1.6 %down_rows.4 = (f32[136,256]{1,0:T(8,128)S(1)}, f32[136,256]{1,0:T(8,128)S(1)}) custom-call(s32[2]{0:T(128)S(1)} %pad_add_fusion.me_ref, bf16[128,8192]{1,0:T(8,128)(2,1)S(1)} %copy-done, bf16[2,4,8192]{2,1,0:T(4,128)(2,1)S(1)} %copy-done.1, bf16[128,8192]{1,0:T(8,128)(2,1)S(1)} %collective-permute-done.refs_2_, ...), custom_call_target="tpu_custom_call" | custom-call | flops 268435456 | bytes 1048576 | tf_op jit(solution)/shard_map/down_rows/pallas_call | solution.py:187
  41.2 1.3 %down_rows.5 = (f32[136,256]{1,0:T(8,128)S(1)}, f32[136,256]{1,0:T(8,128)S(1)}) custom-call(s32[2]{0:T(128)S(1)} %pad_add_fusion.me_ref, bf16[128,8192]{1,0:T(8,128)(2,1)S(1)} %copy-done, bf16[2,4,8192]{2,1,0:T(4,128)(2,1)S(1)} %copy-done.1, bf16[128,8192]{1,0:T(8,128)(2,1)S(1)} %collective-permute-done.refs_2_, ...), custom_call_target="tpu_custom_call" | custom-call | flops 268435456 | bytes 1048576 | tf_op jit(solution)/shard_map/down_rows/pallas_call | solution.py:187
  42.5 1.3 %down_rows.6 = (f32[136,256]{1,0:T(8,128)S(1)}, f32[136,256]{1,0:T(8,128)S(1)}) custom-call(s32[2]{0:T(128)S(1)} %pad_add_fusion.me_ref, bf16[128,8192]{1,0:T(8,128)(2,1)S(1)} %copy-done, bf16[2,4,8192]{2,1,0:T(4,128)(2,1)S(1)} %copy-done.1, bf16[128,8192]{1,0:T(8,128)(2,1)S(1)} %collective-permute-done.refs_2_, ...), custom_call_target="tpu_custom_call" | custom-call | flops 268435456 | bytes 1048576 | tf_op jit(solution)/shard_map/down_rows/pallas_call | solution.py:187
  43.9 1.4 %down_rows.7 = (f32[136,256]{1,0:T(8,128)S(1)}, f32[136,256]{1,0:T(8,128)}) custom-call(s32[2]{0:T(128)S(1)} %pad_add_fusion.me_ref, bf16[128,8192]{1,0:T(8,128)(2,1)S(1)} %copy-done, bf16[2,4,8192]{2,1,0:T(4,128)(2,1)S(1)} %copy-done.1, bf16[128,8192]{1,0:T(8,128)(2,1)S(1)} %collective-permute-done.refs_2_, ...), custom_call_target="tpu_custom_call" | custom-call | flops 268435456 | bytes 1048576 | tf_op jit(solution)/shard_map/down_rows/pallas_call | solution.py:187
  46.1 1.5 %collective-permute-done.15.refs_1_ = f32[136,256]{1,0:T(8,128)S(1)} collective-permute-done((f32[136,256]{1,0:T(8,128)}, f32[136,256]{1,0:T(8,128)S(1)}, u32[]{:S(2)}, u32[]{:S(2)}) %collective-permute-start.15) | collective-permute-done | bytes 139296 | tf_op jit(solution)/shard_map/ppermute | solution.py:214
  47.5 0.9 %copy-done.9 = f32[136,256]{1,0:T(8,128)S(1)} copy-done((f32[136,256]{1,0:T(8,128)S(1)}, f32[136,256]{1,0:T(8,128)}, u32[]{:S(2)}) %copy-start.9) | copy-done | bytes 139288
  48.5 0.8 %place_rows.1 = (bf16[256,256]{1,0:T(8,128)(2,1)}, f32[8,256]{1,0:T(8,128)S(1)}) custom-call(s32[1,128]{1,0:T(1,128)S(1)} %fusion.2.place_ref, f32[136,256]{1,0:T(8,128)S(1)} %copy-done.9, f32[136,256]{1,0:T(8,128)S(1)} %collective-permute-done.15.refs_1_), custom_call_target="tpu_custom_call" | custom-call | tf_op jit(solution)/shard_map/place_rows/pallas_call | solution.py:306
  49.3 5.1 %all-to-all-start.1 = ((bf16[16,16,256]{2,1,0:T(8,128)(2,1)}), bf16[16,16,256]{2,1,0:T(8,128)(2,1)S(1)}, u32[]{:S(2)}, u32[]{:S(2)}) async-start(bf16[16,16,256]{2,1,0:T(8,128)(2,1)} %bitcast.7), calls=%async_computation.1 | async-start | bytes 262144 | tf_op jit(solution)/shard_map/all_to_all | solution.py:318
  54.5 7.8 %all-to-all-done.1 = bf16[16,16,256]{2,1,0:T(8,128)(2,1)S(1)} async-done(((bf16[16,16,256]{2,1,0:T(8,128)(2,1)}), bf16[16,16,256]{2,1,0:T(8,128)(2,1)S(1)}, u32[]{:S(2)}, u32[]{:S(2)}) %all-to-all-start.1) | async-done | bytes 131104 | tf_op jit(solution)/shard_map/all_to_all | solution.py:318
  62.3 1.0 %copy-done.5 = f32[2,256,256]{2,1,0:T(8,128)S(1)} copy-done((f32[2,256,256]{2,1,0:T(8,128)S(1)}, f32[2,256,256]{2,1,0:T(8,128)}, u32[]{:S(2)}) %copy-start.5) | copy-done | bytes 524312
  63.4 0.9 %copy-done.7 = f32[2,256,1]{2,1,0:T(8,128)S(1)} copy-done((f32[2,256,1]{2,1,0:T(8,128)S(1)}, f32[2,256,1]{2,1,0:T(8,128)}, u32[]{:S(2)}) %copy-start.7) | copy-done | bytes 2072
  64.3 2.1 %late_rows.1 = bf16[2,4,8192]{2,1,0:T(4,128)(2,1)} custom-call(s32[1,256]{1,0:T(1,128)S(1)} %select_n.46.column_slot_ref, bf16[256,256]{1,0:T(8,128)(2,1)S(1)} %bitcast.12, f32[8,256]{1,0:T(8,128)S(1)} %get-tuple-element.29.draft_latent_ref, bf16[2,512,256]{2,1,0:T(8,128)(2,1)S(1)} %get-tuple-element.30.turned_ref, ...), custom_call_target="tpu_custom_call" | custom-call | tf_op jit(solution)/shard_map/late_rows/pallas_call | solution.py:323
  (59 shorter events, 5.3 us)
Async XLA Ops:
  0.0 32.6 %collective-permute-start = (bf16[128,8192]{1,0:T(8,128)(2,1)}, bf16[128,8192]{1,0:T(8,128)(2,1)S(1)}, u32[]{:S(2)}, u32[]{:S(2)}) collective-permute-start(bf16[128,8192]{1,0:T(8,128)(2,1)} %refs_0_.7), channel_id=1, source_target_pairs={{0,1},{1,0},{2,3},{3,2},{4,5},{5,4},{6,7},{7,6},{8,9},{9,8},{10,11... | collective-permute-start | bytes 6291464 | tf_op jit(solution)/shard_map/ppermute | solution.py:214
  0.5 23.1 %collective-permute-start.2 = (bf16[512,256]{1,0:T(8,128)(2,1)}, bf16[512,256]{1,0:T(8,128)(2,1)S(1)}, u32[]{:S(2)}, u32[]{:S(2)}) collective-permute-start(bf16[512,256]{1,0:T(8,128)(2,1)} %refs_4_.1), channel_id=1, source_target_pairs={{0,2},{1,3},{2,0},{3,1},{4,6},{5,7},{6,4},{7,5},{8,10},{9,11},{10,... | collective-permute-start | bytes 786440 | tf_op jit(solution)/shard_map/ppermute | solution.py:214
  3.9 8.3 %collective-permute-start.3 = (bf16[256,256]{1,0:T(8,128)(2,1)S(1)}, bf16[256,256]{1,0:T(8,128)(2,1)S(1)}, u32[]{:S(2)}, u32[]{:S(2)}) collective-permute-start(bf16[256,256]{1,0:T(8,128)(2,1)S(1)} %constant_dynamic-slice_fusion), channel_id=1, source_target_pairs={{0,4},{1,5},{2,6},{3,7},{4,8},{5,9},{6,10},{7,11},{8,12},{9,13},{1... | collective-permute-start | bytes 393224 | tf_op jit(solution)/shard_map/ppermute | solution.py:214
  5.5 13.9 %collective-permute-start.1 = (bf16[2,4,8192]{2,1,0:T(4,128)(2,1)}, bf16[2,4,8192]{2,1,0:T(4,128)(2,1)S(1)}, u32[]{:S(2)}, u32[]{:S(2)}) collective-permute-start(bf16[2,4,8192]{2,1,0:T(4,128)(2,1)} %refs_1_.7), channel_id=1, source_target_pairs={{0,1},{1,0},{2,3},{3,2},{4,5},{5,4},{6,7},{7,6},{8,9},{9,8},{10,11... | collective-permute-start | bytes 393224 | tf_op jit(solution)/shard_map/ppermute | solution.py:214
  5.6 15.9 %collective-permute-start.4 = (bf16[256,256]{1,0:T(8,128)(2,1)S(1)}, bf16[256,256]{1,0:T(8,128)(2,1)}, u32[]{:S(2)}, u32[]{:S(2)}) collective-permute-start(bf16[256,256]{1,0:T(8,128)(2,1)S(1)} %constant_dynamic-slice_fusion), channel_id=1, source_target_pairs={{0,12},{1,13},{2,14},{3,15},{4,0},{5,1},{6,2},{7,3},{8,4},{9,5},{1... | collective-permute-start | bytes 393224 | tf_op jit(solution)/shard_map/ppermute | solution.py:214
  12.2 11.5 %collective-permute-start.9 = (bf16[256,256]{1,0:T(8,128)(2,1)S(1)}, bf16[256,256]{1,0:T(8,128)(2,1)}, u32[]{:S(2)}, u32[]{:S(2)}) collective-permute-start(bf16[256,256]{1,0:T(8,128)(2,1)S(1)} %collective-permute-done.3.refs_6_), channel_id=1, source_target_pairs={{0,4},{1,5},{2,6},{3,7},{4,8},{5,9},{6,10},{7,11},{8,12},{9,13},{1... | collective-permute-start | bytes 393224 | tf_op jit(solution)/shard_map/ppermute | solution.py:214
  13.7 12.2 %all-to-all-start = ((s32[16,1,2]{2,1,0:T(1,128)}), s32[16,1,2]{2,1,0:T(1,128)S(1)}, u32[]{:S(2)}, u32[]{:S(2)}) async-start(s32[16,1,2]{2,1,0:T(1,128)} %bitcast), calls=%async_computation | async-start | bytes 16384 | tf_op jit(solution)/shard_map/all_to_all | solution.py:282
  19.4 7.1 %collective-permute-start.5 = (bf16[256,256]{1,0:T(8,128)(2,1)S(1)}, bf16[256,256]{1,0:T(8,128)(2,1)}, u32[]{:S(2)}, u32[]{:S(2)}) collective-permute-start(bf16[256,256]{1,0:T(8,128)(2,1)S(1)} %collective-permute-done.3.refs_6_), channel_id=1, source_target_pairs={{0,2},{1,3},{2,0},{3,1},{4,6},{5,7},{6,4},{7,5},{8,10},{9,11},{10,... | collective-permute-start | bytes 393224 | tf_op jit(solution)/shard_map/ppermute | solution.py:214
  21.4 8.5 %collective-permute-start.7 = (bf16[256,256]{1,0:T(8,128)(2,1)S(1)}, bf16[256,256]{1,0:T(8,128)(2,1)S(1)}, u32[]{:S(2)}, u32[]{:S(2)}) collective-permute-start(bf16[256,256]{1,0:T(8,128)(2,1)S(1)} %collective-permute-done.3.refs_6_), channel_id=1, source_target_pairs={{0,16},{1,17},{2,18},{3,19},{4,20},{5,21},{6,22},{7,23},{8,24},{9,... | collective-permute-start | bytes 393224 | tf_op jit(solution)/shard_map/ppermute | solution.py:214
  23.6 5.3 %collective-permute-start.6 = (bf16[256,256]{1,0:T(8,128)(2,1)}, bf16[256,256]{1,0:T(8,128)(2,1)}, u32[]{:S(2)}, u32[]{:S(2)}) collective-permute-start(bf16[256,256]{1,0:T(8,128)(2,1)} %collective-permute-done.4.refs_7_), channel_id=1, source_target_pairs={{0,2},{1,3},{2,0},{3,1},{4,6},{5,7},{6,4},{7,5},{8,10},{9,11},{10,... | collective-permute-start | bytes 393224 | tf_op jit(solution)/shard_map/ppermute | solution.py:214
  23.7 8.4 %collective-permute-start.11 = (bf16[256,256]{1,0:T(8,128)(2,1)}, bf16[256,256]{1,0:T(8,128)(2,1)}, u32[]{:S(2)}, u32[]{:S(2)}) collective-permute-start(bf16[256,256]{1,0:T(8,128)(2,1)} %collective-permute-done.9.refs_6_), channel_id=1, source_target_pairs={{0,16},{1,17},{2,18},{3,19},{4,20},{5,21},{6,22},{7,23},{8,24},{9,... | collective-permute-start | bytes 393224 | tf_op jit(solution)/shard_map/ppermute | solution.py:214
  26.5 12.9 %copy-start = (bf16[128,8192]{1,0:T(8,128)(2,1)S(1)}, bf16[128,8192]{1,0:T(8,128)(2,1)}, u32[]{:S(2)}) copy-start(bf16[128,8192]{1,0:T(8,128)(2,1)} %refs_0_.7) | copy-start | bytes 6291460
  26.5 13.0 %copy-start.1 = (bf16[2,4,8192]{2,1,0:T(4,128)(2,1)S(1)}, bf16[2,4,8192]{2,1,0:T(4,128)(2,1)}, u32[]{:S(2)}) copy-start(bf16[2,4,8192]{2,1,0:T(4,128)(2,1)} %refs_1_.7) | copy-start | bytes 393220
  26.5 13.0 %copy-start.2 = (bf16[512,256]{1,0:T(8,128)(2,1)S(1)}, bf16[512,256]{1,0:T(8,128)(2,1)}, u32[]{:S(2)}) copy-start(bf16[512,256]{1,0:T(8,128)(2,1)} %refs_4_.1) | copy-start | bytes 786436
  26.5 13.0 %copy-start.11 = (bf16[256,256]{1,0:T(8,128)(2,1)S(1)}, bf16[256,256]{1,0:T(8,128)(2,1)}, u32[]{:S(2)}) copy-start(bf16[256,256]{1,0:T(8,128)(2,1)} %copy-done.10) | copy-start | bytes 393220
  26.6 14.6 %collective-permute-start.8 = (bf16[256,256]{1,0:T(8,128)(2,1)}, bf16[256,256]{1,0:T(8,128)(2,1)S(1)}, u32[]{:S(2)}, u32[]{:S(2)}) collective-permute-start(bf16[256,256]{1,0:T(8,128)(2,1)} %collective-permute-done.4.refs_7_), channel_id=1, source_target_pairs={{0,16},{1,17},{2,18},{3,19},{4,20},{5,21},{6,22},{7,23},{8,24},{9,... | collective-permute-start | bytes 393224 | tf_op jit(solution)/shard_map/ppermute | solution.py:214
  28.9 13.6 %collective-permute-start.10 = (bf16[256,256]{1,0:T(8,128)(2,1)}, bf16[256,256]{1,0:T(8,128)(2,1)S(1)}, u32[]{:S(2)}, u32[]{:S(2)}) collective-permute-start(bf16[256,256]{1,0:T(8,128)(2,1)} %collective-permute-done.9.refs_6_), channel_id=1, source_target_pairs={{0,2},{1,3},{2,0},{3,1},{4,6},{5,7},{6,4},{7,5},{8,10},{9,11},{10,... | collective-permute-start | bytes 393224 | tf_op jit(solution)/shard_map/ppermute | solution.py:214
  30.6 13.2 %collective-permute-start.13 = (bf16[256,256]{1,0:T(8,128)(2,1)}, bf16[256,256]{1,0:T(8,128)(2,1)S(1)}, u32[]{:S(2)}, u32[]{:S(2)}) collective-permute-start(bf16[256,256]{1,0:T(8,128)(2,1)} %collective-permute-done.5.refs_6_), channel_id=1, source_target_pairs={{0,16},{1,17},{2,18},{3,19},{4,20},{5,21},{6,22},{7,23},{8,24},{9,... | collective-permute-start | bytes 393224 | tf_op jit(solution)/shard_map/ppermute | solution.py:214
  32.1 11.7 %collective-permute-start.14 = (bf16[256,256]{1,0:T(8,128)(2,1)}, bf16[256,256]{1,0:T(8,128)(2,1)S(1)}, u32[]{:S(2)}, u32[]{:S(2)}) collective-permute-start(bf16[256,256]{1,0:T(8,128)(2,1)} %collective-permute-done.6.refs_7_), channel_id=1, source_target_pairs={{0,16},{1,17},{2,18},{3,19},{4,20},{5,21},{6,22},{7,23},{8,24},{9,... | collective-permute-start | bytes 393224 | tf_op jit(solution)/shard_map/ppermute | solution.py:214
  32.6 9.9 %collective-permute-start.12 = (bf16[256,256]{1,0:T(8,128)(2,1)}, bf16[256,256]{1,0:T(8,128)(2,1)S(1)}, u32[]{:S(2)}, u32[]{:S(2)}) collective-permute-start(bf16[256,256]{1,0:T(8,128)(2,1)} %collective-permute-done.11.refs_8_), channel_id=1, source_target_pairs={{0,2},{1,3},{2,0},{3,1},{4,6},{5,7},{6,4},{7,5},{8,10},{9,11},{10,... | collective-permute-start | bytes 393224 | tf_op jit(solution)/shard_map/ppermute | solution.py:214
  33.6 1.2 %copy-start.14 = (bf16[2,1024,256]{2,1,0:T(8,128)(2,1)S(1)}, bf16[2,1024,256]{2,1,0:T(8,128)(2,1)}, u32[]{:S(2)}) copy-start(bf16[2,1024,256]{2,1,0:T(8,128)(2,1)} %cache_ref.1) | copy-start | bytes 3145732
  34.8 1.0 %copy-start.15 = (bf16[256,1024]{1,0:T(8,128)(2,1)S(1)}, bf16[256,1024]{1,0:T(8,128)(2,1)}, u32[]{:S(2)}) copy-start(bf16[256,1024]{1,0:T(8,128)(2,1)} %key_up_ref.1) | copy-start | bytes 1572868
  39.5 1.6 %copy-start.4 = (f32[2,256,256]{2,1,0:T(8,128)}, f32[2,256,256]{2,1,0:T(8,128)S(1)}, u32[]{:S(2)}) copy-start(f32[2,256,256]{2,1,0:T(8,128)S(1)} %get-tuple-element.32.mixed_ref) | copy-start | bytes 1572868
  39.5 1.6 %copy-start.6 = (f32[2,256,1]{2,1,0:T(8,128)}, f32[2,256,1]{2,1,0:T(8,128)S(1)}, u32[]{:S(2)}) copy-start(f32[2,256,1]{2,1,0:T(8,128)S(1)} %get-tuple-element.31.total_ref) | copy-start | bytes 6148
  39.5 1.6 %copy-start.13 = (bf16[256,256]{1,0:T(8,128)(2,1)S(1)}, bf16[256,256]{1,0:T(8,128)(2,1)}, u32[]{:S(2)}) copy-start(bf16[256,256]{1,0:T(8,128)(2,1)} %copy-done.12) | copy-start | bytes 393220
  43.9 2.1 %copy-start.17 = (s32[128]{0:T(128)S(1)}, s32[128]{0:T(128)}, u32[]{:S(2)}) copy-start(s32[128]{0:T(128)} %param.12) | copy-start | bytes 1540
  43.9 18.4 %copy-start.3 = (bf16[256,1024]{1,0:T(8,128)(2,1)S(1)}, bf16[256,1024]{1,0:T(8,128)(2,1)}, u32[]{:S(2)}) copy-start(bf16[256,1024]{1,0:T(8,128)(2,1)} %value_up_ref.1) | copy-start | bytes 1572868
  46.0 1.6 %collective-permute-start.15 = (f32[136,256]{1,0:T(8,128)}, f32[136,256]{1,0:T(8,128)S(1)}, u32[]{:S(2)}, u32[]{:S(2)}) collective-permute-start(f32[136,256]{1,0:T(8,128)} %get-tuple-element.27), channel_id=1, source_target_pairs={{0,1},{1,0},{2,3},{3,2},{4,5},{5,4},{6,7},{7,6},{8,9},{9,8},{10,11... | collective-permute-start | bytes 417800 | tf_op jit(solution)/shard_map/ppermute | solution.py:214
  47.5 0.9 %copy-start.9 = (f32[136,256]{1,0:T(8,128)S(1)}, f32[136,256]{1,0:T(8,128)}, u32[]{:S(2)}) copy-start(f32[136,256]{1,0:T(8,128)} %copy-done.8) | copy-start | bytes 417796
  49.3 13.0 %all-to-all-start.1 = ((bf16[16,16,256]{2,1,0:T(8,128)(2,1)}), bf16[16,16,256]{2,1,0:T(8,128)(2,1)S(1)}, u32[]{:S(2)}, u32[]{:S(2)}) async-start(bf16[16,16,256]{2,1,0:T(8,128)(2,1)} %bitcast.7), calls=%async_computation.1 | async-start | bytes 262144 | tf_op jit(solution)/shard_map/all_to_all | solution.py:318
  62.3 1.0 %copy-start.5 = (f32[2,256,256]{2,1,0:T(8,128)S(1)}, f32[2,256,256]{2,1,0:T(8,128)}, u32[]{:S(2)}) copy-start(f32[2,256,256]{2,1,0:T(8,128)} %copy-done.4) | copy-start | bytes 1572868
  63.4 0.9 %copy-start.7 = (f32[2,256,1]{2,1,0:T(8,128)S(1)}, f32[2,256,1]{2,1,0:T(8,128)}, u32[]{:S(2)}) copy-start(f32[2,256,1]{2,1,0:T(8,128)} %copy-done.6) | copy-start | bytes 6148
  (4 other events, 2.9 us)

commit v4 on v3

v4 whole, which is shorter than its diff:
```python
import functools
import math

import jax
import jax.numpy as jnp
from jax import lax
from jax.experimental import pallas as pl
from jax.experimental.pallas import tpu as pltpu
from jax.sharding import PartitionSpec as P

QUERY_HEADS = 64
HEAD_SIZE = 128
FAR = -1e30
NT = (((1,), (1,)), ((), ()))
WHOLE = pl.BlockSpec(memory_space=pltpu.VMEM)
SCALARS = pl.BlockSpec(memory_space=pltpu.SMEM)
UNREAD = pl.BlockSpec(memory_space=pl.ANY)


def params(mib):
    return pltpu.CompilerParams(vmem_limit_bytes=mib * 1024 * 1024)


def split_rows(x):
    top = x.astype(jnp.bfloat16)
    rest = (x - top.astype(jnp.float32)).astype(jnp.bfloat16)
    return jnp.concatenate([top, rest], 0)


def join_rows(x):
    half = x.shape[0] // 2
    return x[:half] + x[half:]


def held_kernel(
    limit_ref, query_hbm, key_up_hbm, cache_hbm, turned_ref, peak_ref, total_ref, mixed_ref,
    query_ref, key_up_ref, cache_ref, float_ref, scores_ref, sems,
):
    copies = [
        pltpu.make_async_copy(source, target, sems.at[n])
        for n, (source, target) in enumerate(
            [(query_hbm, query_ref), (key_up_hbm, key_up_ref), (cache_hbm, cache_ref)]
        )
    ]
    for copy in copies:
        copy.start()
    slot_count, span_rows, _ = cache_ref.shape
    draft_count = query_ref.shape[1]
    heads_kv = key_up_ref.shape[1] // HEAD_SIZE
    group_size = QUERY_HEADS // heads_kv
    rows = group_size * draft_count
    scale = math.log2(math.e) / math.sqrt(HEAD_SIZE)
    step = 256
    copies[0].wait()
    copies[1].wait()
    for k in range(heads_kv):
        pieces = []
        for b in range(slot_count):
            for g in range(group_size):
                lane = (k * group_size + g) * HEAD_SIZE
                pieces.append(query_ref[b, :, lane : lane + HEAD_SIZE].astype(jnp.float32))
        query = jnp.concatenate(pieces, 0).astype(jnp.bfloat16)
        key_up = key_up_ref[:, k * HEAD_SIZE : (k + 1) * HEAD_SIZE]
        turned = lax.dot_general(query, key_up, NT, preferred_element_type=jnp.float32) * scale
        for b in range(slot_count):
            float_ref[b, k * rows : (k + 1) * rows, :] = turned[b * rows : (b + 1) * rows]
    copies[2].wait()
    for b in range(slot_count):
        turned_ref[b] = split_rows(float_ref[b])
        peak = None
        for c in range(0, span_rows, step):
            scores = join_rows(
                lax.dot_general(turned_ref[b], cache_ref[b, c : c + step], NT, preferred_element_type=jnp.float32)
            )
            column = lax.broadcasted_iota(jnp.int32, (1, step), 1) + c
            scores = jnp.where(column < limit_ref[b : b + 1, 0:1], scores, FAR)
            scores_ref[:, c : c + step] = scores
            top = jnp.max(scores, 1, keepdims=True)
            peak = top if peak is None else jnp.maximum(peak, top)
        peak_ref[b] = peak
        total = jnp.zeros_like(peak)
        mixed = jnp.zeros(mixed_ref.shape[1:], jnp.float32)
        for c in range(0, span_rows, step):
            weights = jnp.exp2(scores_ref[:, c : c + step] - peak)
            total += jnp.sum(weights, 1, keepdims=True)
            mixed += join_rows(
                jnp.dot(split_rows(weights), cache_ref[b, c : c + step], preferred_element_type=jnp.float32)
            )
        total_ref[b] = total
        mixed_ref[b] = mixed


def piece_sums(starts, spans, row_refs, refs):
    groups = len(row_refs) // 2
    slot_count, draft_count, _ = row_refs[1].shape
    drafts = groups * slot_count * draft_count
    total = None
    for start, (n, first, depth) in zip(starts, spans):
        lanes = pl.ds(pl.multiple_of(start, HEAD_SIZE), depth)
        stack = [ref[b, :, lanes].astype(jnp.float32) for ref in row_refs[1::2] for b in range(slot_count)]
        if drafts < 16:
            stack.append(jnp.zeros((16 - drafts, depth), jnp.float32))
        rows = [ref[:, lanes] for ref in row_refs[0::2]] + [jnp.concatenate(stack, 0).astype(jnp.bfloat16)]
        piece = refs[n][first : first + depth, :]
        product = jnp.dot(jnp.concatenate(rows, 0), piece, preferred_element_type=jnp.float32)
        total = product if total is None else total + product
    return total


def down_kernel(starts_of, spans, first, *refs):
    row_refs, refs, out_ref = refs[:4], refs[4:-1], refs[-1]
    total = piece_sums(starts_of(), spans, row_refs, refs)
    out_ref[...] = total if first else total + refs[-1][...]


def down_place_kernel(starts_of, spans, *refs):
    row_refs, refs, (keep_ref, send_ref) = refs[:4], refs[4:-2], refs[-2:]
    place_ref, sum_ref, refs = refs[0], refs[1], refs[2:]
    total = piece_sums(starts_of(), spans, row_refs, refs) + sum_ref[...]
    slots, width = keep_ref.shape[0] - 8, keep_ref.shape[1]
    count = place_ref.shape[1]
    parts = []
    left = total[:count]
    for _ in range(3):
        part = left.astype(jnp.bfloat16)
        parts.append(part)
        left = left - part.astype(jnp.float32)
    parts = jnp.concatenate(parts, 1)
    core = lax.axis_index("wide") % 2
    spot = lax.broadcasted_iota(jnp.int32, (slots, count), 0)
    for ref, target, draft in ((keep_ref, core, count), (send_ref, 1 - core, count + 8)):
        chosen = jnp.where(spot + target * slots == place_ref[...], 1.0, 0.0).astype(jnp.bfloat16)
        moved = jnp.dot(chosen, parts, preferred_element_type=jnp.float32)
        ref[:slots, :] = moved[:, :width] + moved[:, width : 2 * width] + moved[:, 2 * width :]
        ref[slots:, :] = total[draft : draft + 8]


def route_kernel(blocks, keep_ref, came_ref, draft_latent_ref, *refs):
    out_refs, float_ref = refs[:-1], refs[-1]
    float_ref[...] = keep_ref[...] + came_ref[...]
    slots = float_ref.shape[0] - 8
    draft_latent_ref[...] = float_ref[slots:, :].astype(jnp.bfloat16).astype(jnp.float32)
    size = slots // len(out_refs)
    for block, ref in zip(blocks(), out_refs):
        rows = pl.ds(pl.multiple_of(block * size, size), size)
        ref[...] = float_ref[rows, :].astype(jnp.bfloat16)


def start_kernel(most_rows, target_ref, other_ref, shard_hbm, place_ref, half_ref, full_ref, sems):
    half_rows, shard_rows = half_ref.shape[0] - 16, full_ref.shape[0] - 16
    mine = pl.ds(pl.multiple_of(lax.axis_index("rep") * half_rows, half_rows), half_rows)
    copies = [
        pltpu.make_async_copy(shard_hbm.at[mine], half_ref.at[:half_rows], sems.at[0]),
        pltpu.make_async_copy(shard_hbm, full_ref.at[:shard_rows], sems.at[1]),
    ]
    for copy in copies:
        copy.start()
    core = lax.axis_index("wide") % 2
    width, count = half_ref.shape[1], target_ref.shape[1]
    f32, bf16 = jnp.float32, jnp.bfloat16
    earlier = lax.broadcasted_iota(jnp.int32, (count, count), 0) < lax.broadcasted_iota(jnp.int32, (count, count), 1)
    earlier = jnp.where(earlier, 1.0, 0.0).astype(bf16)
    counts = []
    for n, (ref, owner) in enumerate(((target_ref, core), (other_ref, 1 - core))):
        target = ref[...]
        hit = jnp.where(lax.broadcasted_iota(jnp.int32, (width, count), 0) == target, 1.0, 0.0)
        counts.append(lax.dot_general(jnp.ones((16, count), bf16), hit.astype(bf16), NT, preferred_element_type=f32))
        before = jnp.dot(hit[:64].astype(bf16), earlier, preferred_element_type=f32)
        rank = jnp.sum(hit[:64] * before, 0, keepdims=True).astype(jnp.int32)
        spot = jnp.where(target % 2 == 0, rank, most_rows - 1 - rank)
        chip, side = target // 4, target // 2 % 2
        slots = place_ref.shape[1]
        place_ref[:, n * count : (n + 1) * count] = side * slots + (chip * 2 + owner) * most_rows + spot
    low = jnp.where(core == 0, counts[0], counts[1])
    high = jnp.where(core == 0, counts[1], counts[0])
    block = jnp.where(lax.broadcasted_iota(jnp.int32, (16, width), 0) == 0, low, high).astype(bf16)
    half_ref[half_rows:, :] = block
    full_ref[shard_rows:, :] = block
    for copy in copies:
        copy.wait()


def join_kernel(one_ref, two_ref, out_ref):
    rows = one_ref.shape[0]
    out_ref[:rows, :] = one_ref[...]
    out_ref[rows:, :] = two_ref[...]


def count_kernel(most_rows, spans, context_ref, *refs):
    refs, (limit_ref, column_slot_ref) = refs[:-2], refs[-2:]
    counts = jnp.concatenate([refs[n][first : first + 16, :].astype(jnp.float32)[:2] for n, first in spans], 0)
    lane = lax.broadcasted_iota(jnp.int32, counts.shape, 1)
    row = lax.broadcasted_iota(jnp.int32, counts.shape, 0)
    spread = []
    for b in range(2):
        number = jnp.sum(jnp.where(lane == lax.axis_index("wide") * 2 + b, counts, 0.0), 1, keepdims=True)
        limit = context_ref[b] - jnp.sum(number, 0, keepdims=True).astype(jnp.int32)
        limit_ref[b : b + 1, :] = jnp.broadcast_to(limit, (1, limit_ref.shape[1]))
        spread.append(jnp.sum(jnp.where(lane // most_rows == row, number, 0.0), 0, keepdims=True).astype(jnp.int32))
    spot = lax.broadcasted_iota(jnp.int32, column_slot_ref.shape, 1) % most_rows
    column_slot_ref[...] = jnp.where(spot < spread[0], 0, jnp.where(spot >= most_rows - spread[1], 1, -1))


def plain_down_kernel(place_ref, prompt_ref, draft_ref, weight_ref, outgoing_ref, draft_latent_ref):
    count, depth = prompt_ref.shape
    total = piece_sums([0], [(0, 0, depth)], [prompt_ref, draft_ref], [weight_ref])
    draft_latent_ref[...] = total[count : count + 8].astype(jnp.bfloat16).astype(jnp.float32)
    spot = lax.broadcasted_iota(jnp.int32, (outgoing_ref.shape[0], count), 0)
    chosen = jnp.where(spot == place_ref[...], 1.0, 0.0).astype(jnp.bfloat16)
    latent = total[:count].astype(jnp.bfloat16)
    outgoing_ref[...] = jnp.dot(chosen, latent, preferred_element_type=jnp.float32).astype(jnp.bfloat16)


def late_kernel(
    column_slot_ref, draft_latent_ref, turned_ref, peak_ref, total_ref, mixed_ref, value_up_ref, *refs
):
    incoming_refs, (out_ref, rows_ref, parted_ref) = refs[:-3], refs[-3:]
    slot_count, draft_count, _ = out_ref.shape
    tile = slot_count * draft_count
    heads_kv = value_up_ref.shape[1] // HEAD_SIZE
    group_size = QUERY_HEADS // heads_kv
    head_rows = group_size * draft_count
    rows = peak_ref.shape[1]
    block = incoming_refs[0].shape[0]
    arrived = block * len(incoming_refs)
    span = rows_ref.shape[0]
    drafts = jnp.concatenate([draft_latent_ref[...], jnp.zeros((span - arrived - tile, rows_ref.shape[1]), jnp.float32)], 0)
    for n, ref in enumerate(incoming_refs):
        rows_ref[n * block : (n + 1) * block, :] = ref[...]
    rows_ref[arrived:, :] = drafts.astype(jnp.bfloat16)
    token = lax.broadcasted_iota(jnp.int32, (rows, 1), 0) % draft_count
    column = lax.broadcasted_iota(jnp.int32, (rows, span - arrived), 1)
    for b in range(slot_count):
        scores = join_rows(lax.dot_general(turned_ref[b], rows_ref[...], NT, preferred_element_type=jnp.float32))
        draft_seen = (column >= b * draft_count) & (column <= b * draft_count + token)
        scores = jnp.concatenate(
            [
                jnp.where(column_slot_ref[...] == b, scores[:, :arrived], FAR),
                jnp.where(draft_seen, scores[:, arrived:], FAR),
            ],
            1,
        )
        peak = jnp.maximum(jnp.max(scores, 1, keepdims=True), peak_ref[b])
        weights = jnp.exp2(scores - peak)
        fade = jnp.exp2(peak_ref[b] - peak)
        total = total_ref[b] * fade + jnp.sum(weights, 1, keepdims=True)
        mixed = join_rows(jnp.dot(split_rows(weights), rows_ref[...], preferred_element_type=jnp.float32))
        parted_ref[b] = split_rows((mixed_ref[b] * fade + mixed) / total)
    for k in range(heads_kv):
        part = []
        for b in range(slot_count):
            part.append(parted_ref[b, k * head_rows : (k + 1) * head_rows, :])
            part.append(parted_ref[b, rows + k * head_rows : rows + (k + 1) * head_rows, :])
        value_up = value_up_ref[:, k * HEAD_SIZE : (k + 1) * HEAD_SIZE]
        both = jnp.dot(jnp.concatenate(part, 0), value_up, preferred_element_type=jnp.float32)
        for b in range(slot_count):
            result = join_rows(both[b * 2 * head_rows : (b + 1) * 2 * head_rows])
            wide = jnp.concatenate(
                [result[g * draft_count : (g + 1) * draft_count] for g in range(group_size)], 1
            )
            out_ref[b, :, k * group_size * HEAD_SIZE : (k + 1) * group_size * HEAD_SIZE] = wide.astype(jnp.bfloat16)


def deliver(prompt_hidden, draft_hidden, shard, row_target, context_len):
    shard_rows, width = shard.shape
    count = prompt_hidden.shape[0]
    sizes = (2, 4, 2, 2)
    spots = [(r, z, y, c) for r in range(2) for z in range(4) for y in range(2) for c in range(2)]
    most_rows = count // 8
    f32, bf16 = jnp.float32, jnp.bfloat16

    def flat(spot):
        return ((spot[0] * 4 + spot[1]) * 2 + spot[2]) * 2 + spot[3]

    def move(x, *steps):
        pairs = []
        for spot in spots:
            to = [(spot[a] + steps[a]) % sizes[a] for a in range(4)]
            pairs.append((flat(spot), flat(to)))
        return lax.ppermute(x, ("rep", "wide"), pairs)

    def array(rows, dtype=bf16):
        return jax.ShapeDtypeStruct((rows, width), dtype)

    def call(kernel, out_shape, name, *operands, specs=None, flops=2**24, **more):
        return pl.pallas_call(
            kernel,
            out_shape=out_shape,
            in_specs=specs or [WHOLE] * len(operands),
            out_specs=[WHOLE] * len(out_shape) if isinstance(out_shape, list) else WHOLE,
            compiler_params=params(16),
            cost_estimate=pl.CostEstimate(flops=flops, bytes_accessed=2**20, transcendentals=0),
            name=name,
            **more,
        )(*operands)

    target = row_target.reshape(1, count)
    other_target = move(target, 0, 0, 0, 1)
    half_rows = shard_rows // 2
    ext = half_rows + 16
    place, half, full = call(
        functools.partial(start_kernel, most_rows),
        [jax.ShapeDtypeStruct((1, 2 * count), jnp.int32), array(ext), array(shard_rows + 16)],
        "start_rows",
        target,
        other_target,
        pltpu.with_memory_space_constraint(shard, pltpu.HBM),
        specs=[WHOLE, WHOLE, pl.BlockSpec(memory_space=pltpu.HBM)],
        scratch_shapes=[pltpu.SemaphoreType.DMA((2,))],
    )
    z1, z3 = move(half, 0, 1, 0, 0), move(half, 0, 3, 0, 0)
    y0 = move(full, 0, 0, 1, 0)
    other_prompt, other_draft = move(prompt_hidden, 0, 0, 0, 1), move(draft_hidden, 0, 0, 0, 1)
    z2 = move(z1, 0, 1, 0, 0)
    z13 = call(join_kernel, array(2 * ext), "join_pieces", z1, z3)
    yz13, xz13 = move(z13, 0, 0, 1, 0), move(z13, 1, 0, 0, 0)
    yz2, xz2 = move(z2, 0, 0, 1, 0), move(z2, 1, 0, 0, 0)
    xyz13 = move(yz13, 1, 0, 0, 0)
    yxz2 = move(xz2, 0, 0, 1, 0)

    def starts_of(trails):
        def starts():
            rep, wide = lax.axis_index("rep"), lax.axis_index("wide")
            z, y, c = wide // 4, wide // 2 % 2, wide % 2
            return [
                (((z + 4 - z_step) % 4 * 2 + (y + y_step) % 2) * 2 + c) * shard_rows
                + (0 if x_step is None else (rep + x_step) % 2 * half_rows)
                for x_step, z_step, y_step in trails
            ]

        return starts

    rows = [prompt_hidden, draft_hidden, other_prompt, other_draft]
    stages = [
        ([full, y0], [(0, 0, shard_rows, (None, 0, 0)), (1, 0, shard_rows, (None, 0, 1))]),
        (
            [z13, yz13],
            [(0, 0, half_rows, (0, 1, 0)), (0, ext, half_rows, (0, 3, 0)),
             (1, 0, half_rows, (0, 1, 1)), (1, ext, half_rows, (0, 3, 1))],
        ),
        (
            [xz13, z2, yz2],
            [(0, 0, half_rows, (1, 1, 0)), (0, ext, half_rows, (1, 3, 0)),
             (1, 0, half_rows, (0, 2, 0)), (2, 0, half_rows, (0, 2, 1))],
        ),
        (
            [xz2, yxz2, xyz13],
            [(0, 0, half_rows, (1, 2, 0)), (1, 0, half_rows, (1, 2, 1)),
             (2, 0, half_rows, (1, 1, 1)), (2, ext, half_rows, (1, 3, 1))],
        ),
    ]
    sums = []
    total_rows = 2 * count + 16
    for n, (pieces, uses) in enumerate(stages[:-1]):
        spans, trails = [use[:3] for use in uses], [use[3] for use in uses]
        sums = [
            call(
                functools.partial(down_kernel, starts_of(trails), spans, n == 0),
                array(total_rows, f32), "down_rows", *rows, *pieces, *sums, flops=2**28,
            )
        ]

    trails = [(0, 0), (1, 0), (3, 0), (2, 0), (0, 1), (1, 1), (3, 1), (2, 1)]
    limit, column_slot = call(
        functools.partial(
            count_kernel, most_rows,
            [(0, half_rows), (1, half_rows), (1, ext + half_rows), (2, half_rows),
             (3, shard_rows), (4, half_rows), (4, ext + half_rows), (5, half_rows)],
        ),
        [jax.ShapeDtypeStruct((2, 128), jnp.int32), jax.ShapeDtypeStruct((1, 2 * count), jnp.int32)],
        "count_rows",
        context_len, half, z13, z2, y0, yz13, yz2,
        specs=[SCALARS] + [WHOLE] * 6,
    )

    def finish(tie):
        pieces, uses = stages[-1]
        spans, ways = [use[:3] for use in uses], [use[3] for use in uses]
        keep, send = call(
            functools.partial(down_place_kernel, starts_of(ways), spans),
            [array(2 * count + 8, f32)] * 2, "down_place_rows", *rows, place, *sums, *pieces, tie,
            specs=[WHOLE] * (6 + len(pieces)) + [UNREAD], flops=2**28,
        )
        came = move(send, 0, 0, 0, 1)

        def blocks():
            wide = lax.axis_index("wide")
            z, y = wide // 4, wide // 2 % 2
            return [(z + z_step) % 4 * 2 + (y + y_step) % 2 for z_step, y_step in trails]

        draft_latent, *outgoing = call(
            functools.partial(route_kernel, blocks),
            [array(8, f32)] + [array(2 * most_rows)] * len(trails), "route_rows", keep, came,
            scratch_shapes=[pltpu.VMEM((2 * count + 8, width), f32)],
        )
        incoming = [x if n == 0 else move(x, 0, *trails[n], 0) for n, x in enumerate(outgoing)]
        return draft_latent, incoming

    return limit, column_slot, finish


def deliver_plain(prompt_hidden, draft_hidden, shard, row_target, context_len):
    wide_size = lax.axis_size("wide")
    row_count = prompt_hidden.shape[0]
    slot_count, draft_count, _ = draft_hidden.shape
    latent_width = shard.shape[1]
    most_rows = 2 * ((row_count + wide_size - 1) // wide_size)
    arrived = wide_size * most_rows
    weight = lax.all_gather(shard, "wide", axis=0, tiled=True)
    index = jnp.arange(row_count, dtype=jnp.int32)
    same = (row_target[:, None] == row_target[None, :]) & (index[None, :] < index[:, None])
    rank = jnp.sum(same.astype(jnp.int32), 1)
    front = row_target % slot_count == 0
    place = row_target // slot_count * most_rows + jnp.where(front, rank, most_rows - 1 - rank)
    request = jnp.arange(wide_size * slot_count, dtype=jnp.int32)
    counts = jnp.sum((row_target[None, :] == request[:, None]).astype(jnp.int32), 1)
    counts = lax.all_to_all(counts.reshape(wide_size, slot_count), "wide", split_axis=0, concat_axis=0, tiled=True)
    limit = jnp.broadcast_to((context_len - jnp.sum(counts, 0))[:, None], (slot_count, 128))
    spot = jnp.arange(most_rows, dtype=jnp.int32)[None, :]
    column_slot = jnp.where(
        spot < counts[:, 0:1], 0, jnp.where(spot >= most_rows - counts[:, 1:2], 1, -1)
    ).reshape(1, arrived)

    def finish(tie):
        outgoing, draft_latent = pl.pallas_call(
            plain_down_kernel,
            out_shape=[
                jax.ShapeDtypeStruct((arrived, latent_width), jnp.bfloat16),
                jax.ShapeDtypeStruct((slot_count * draft_count, latent_width), jnp.float32),
            ],
            in_specs=[WHOLE] * 4,
            out_specs=[WHOLE] * 2,
            compiler_params=params(24),
            name="down_rows",
        )(place.reshape(1, row_count), prompt_hidden, draft_hidden, weight)
        incoming = lax.all_to_all(
            outgoing.reshape(wide_size, most_rows, latent_width), "wide", split_axis=0, concat_axis=0, tiled=True
        )
        return draft_latent, [incoming.reshape(arrived, latent_width)]

    return limit, column_slot, finish


def local(
    prompt_hidden,
    resident_latent,
    row_target,
    row_offset,
    context_len,
    draft_hidden,
    draft_query_heads,
    down_weight,
    key_up_weight,
    value_up_weight,
):
    f32, bf16 = jnp.float32, jnp.bfloat16
    slot_count, span_rows, latent_width = resident_latent.shape
    draft_count = draft_hidden.shape[1]
    rows = QUERY_HEADS * draft_count
    known = lax.axis_size("wide") == 16 and lax.axis_size("rep") == 2
    limit, column_slot, finish = (deliver if known else deliver_plain)(
        prompt_hidden, draft_hidden, down_weight, row_target, context_len
    )
    hbm = pl.BlockSpec(memory_space=pltpu.HBM)
    turned, peak, total, mixed = pl.pallas_call(
        held_kernel,
        out_shape=[
            jax.ShapeDtypeStruct((slot_count, 2 * rows, latent_width), bf16),
            jax.ShapeDtypeStruct((slot_count, rows, 1), f32),
            jax.ShapeDtypeStruct((slot_count, rows, 1), f32),
            jax.ShapeDtypeStruct((slot_count, rows, latent_width), f32),
        ],
        in_specs=[WHOLE, hbm, hbm, hbm],
        out_specs=[WHOLE] * 4,
        scratch_shapes=[
            pltpu.VMEM(draft_query_heads.shape, bf16),
            pltpu.VMEM(key_up_weight.shape, bf16),
            pltpu.VMEM(resident_latent.shape, bf16),
            pltpu.VMEM((slot_count, rows, latent_width), f32),
            pltpu.VMEM((rows, span_rows), f32),
            pltpu.SemaphoreType.DMA((3,)),
        ],
        compiler_params=params(16),
        cost_estimate=pl.CostEstimate(flops=2**31, bytes_accessed=2**22, transcendentals=2**19),
        name="held_rows",
    )(limit, *(pltpu.with_memory_space_constraint(x, pltpu.HBM) for x in (draft_query_heads, key_up_weight, resident_latent)))

    draft_latent, incoming = finish(peak)
    arrived = column_slot.shape[1]
    span = (arrived + slot_count * draft_count + 127) // 128 * 128
    return pl.pallas_call(
        late_kernel,
        out_shape=jax.ShapeDtypeStruct((slot_count, draft_count, QUERY_HEADS * HEAD_SIZE), bf16),
        in_specs=[WHOLE] * (7 + len(incoming)),
        out_specs=WHOLE,
        scratch_shapes=[
            pltpu.VMEM((span, latent_width), bf16),
            pltpu.VMEM((slot_count, 2 * rows, latent_width), bf16),
        ],
        compiler_params=params(16),
        name="late_rows",
    )(column_slot, draft_latent, turned, peak, total, mixed, value_up_weight, *incoming)


def solution(mesh):
    placed = (
        P(("rep", "wide"), None),
        P(("rep", "wide"), None, None),
        P(("rep", "wide")),
        P(("rep", "wide")),
        P(("rep", "wide")),
        P(("rep", "wide"), None, None),
        P(("rep", "wide"), None, None),
        P("wide", None),
        P(),
        P(),
    )
    return jax.shard_map(
        local, mesh=mesh, in_specs=placed, out_specs=P(("rep", "wide"), None, None), check_vma=False
    )
```

time: 66.9 us -> 62.1 us (0.928)
  waiting for transfers between devices: 15 us -> 25.8 us
  local copies, waits for them, and re-layouts: 9.87 us -> 1.33 us
  other arithmetic: 2.52 us -> 0 us
  starting transfers between devices: 27.5 us -> 25.3 us
  Pallas kernels: 11.2 us -> 9.4 us
    ppermute x16 -> x21, waiting for transfers between devices: 6.59 us -> 25.8 us  [move(): return lax.ppermute(x, ('rep', 'wide'), pairs)]
    all_to_all x2 -> x0, starting transfers between devices: 10.9 us -> none  [the longest x1 5.77 us: local(): lax.all_to_all(counts.reshape(wide_size, slot_count), 'wide', split_axis=...]
    ppermute x16 -> x21, starting transfers between devices: 16.7 us -> 25.3 us  [move(): return lax.ppermute(x, ('rep', 'wide'), pairs)]
    all_to_all x2 -> x0, waiting for transfers between devices: 8.39 us -> none  [the longest x1 7.77 us: local(): lax.all_to_all(outgoing.reshape(wide_size, most_rows, latent_width), 'wid...]
    unnamed x36 -> x10, local copies, waits for them, and re-layouts: 8.06 us -> 1.33 us
    pallas_call x5 -> x8, Pallas kernels: 6.5 us -> 3.7 us  [call(): pl.pallas_call(kernel, out_shape=out_shape, in_specs=specs or [WHOLE] * l...]
    reduce_sum x3 -> x0, other arithmetic: 1.7 us -> none  [the longest x1 0.9 us: local(): rank = jnp.sum(same.astype(jnp.int32), 1)]
    dynamic_slice x1 -> x0, local copies, waits for them, and re-layouts: 0.95 us -> none  [down_sums(): lax.dynamic_slice(shard, (rep * half_rows, 0), (half_rows, latent_width))]
  transfers between devices with their start and end apart: 18 -> 21, of which waited for: 5 -> 10; matrix products, arithmetic and copies ran while one was open for 5% -> 0% of each run, Pallas kernels for 10% -> 10%
where the time goes in v4:
time: 62.1 us; the launch traced here: 61.9 us
  waiting for transfers between devices  25.8 us (42%)
  starting transfers between devices  25.3 us (41%)
  Pallas kernels  9.4 us (15%)
  local copies, waits for them, and re-layouts  1.33 us (2%)
    ppermute x21, waiting for transfers between devices, move(): return lax.ppermute(x, ('rep', 'wide'), pairs)  25.8 us
    ppermute x21, starting transfers between devices, move(): return lax.ppermute(x, ('rep', 'wide'), pairs)  25.3 us
    pallas_call x8, Pallas kernels, call(): pl.pallas_call(kernel, out_shape=out_shape, in_specs=specs or [WHOLE] * l...  3.7 us
    pallas_call x1, Pallas kernels, local(): pl.pallas_call(held_kernel, out_shape=[jax.ShapeDtypeStruct((slot_count,...  3.6 us
    pallas_call x1, Pallas kernels, local(): pl.pallas_call(late_kernel, out_shape=jax.ShapeDtypeStruct((slot_count, d...  2.1 us
    unnamed x10, local copies, waits for them, and re-layouts  1.33 us
  transfers between devices with their start and end apart: 21, of which 10 were waited for; matrix products, arithmetic and copies ran while one was open for 0% of the time, Pallas kernels for 10%

profile of v4, /device:TPU:0, one launch (start us, length us, event | category | flops | bytes accessed | tf_op | source)
XLA Modules:
  0.0 61.9 jit_solution(16849259982333946162)
XLA Ops:
  0.5 3.9 %collective-permute-done.other_ref = s32[1,128]{1,0:T(1,128)S(1)} collective-permute-done((s32[1,128]{1,0:T(1,128)}, s32[1,128]{1,0:T(1,128)S(1)}, u32[]{:S(2)}, u32[]{:S(2)}) %collective-permute-start) | collective-permute-done | bytes 544 | tf_op jit(solution)/shard_map/ppermute | solution.py:280
  4.5 0.7 %copy-done.3 = s32[128]{0:T(128)S(1)} copy-done((s32[128]{0:T(128)S(1)}, s32[128]{0:T(128)}, u32[]{:S(2)}) %copy-start.3) | copy-done | bytes 536
  5.1 1.1 %start_rows.1 = (s32[1,256]{1,0:T(1,128)S(1)}, bf16[272,256]{1,0:T(8,128)(2,1)S(1)}, bf16[528,256]{1,0:T(8,128)(2,1)S(1)}) custom-call(s32[1,128]{1,0:T(1,128)S(1)} %bitcast.2, s32[1,128]{1,0:T(1,128)S(1)} %collective-permute-done.other_ref, bf16[512,256]{1,0:T(8,128)(2,1)} %shard_hbm.1), custom_call_target="tpu_custom_call" | custom-call | flops 16777216 | bytes 1048576 | tf_op jit(solution)/shard_map/start_rows/pallas_call | solution.py:286
  6.2 3.0 %collective-permute-start.1 = (bf16[272,256]{1,0:T(8,128)(2,1)S(1)}, bf16[272,256]{1,0:T(8,128)(2,1)S(1)}, u32[]{:S(2)}, u32[]{:S(2)}) collective-permute-start(bf16[272,256]{1,0:T(8,128)(2,1)S(1)} %get-tuple-element.25.refs_0_), channel_id=1, source_target_pairs={{0,4},{1,5},{2,6},{3,7},{4,8},{5,9},{6,10},{7,11},{8,12},{9,13},{1... | collective-permute-start | bytes 417800 | tf_op jit(solution)/shard_map/ppermute | solution.py:280
  9.2 2.1 %collective-permute-start.2 = (bf16[272,256]{1,0:T(8,128)(2,1)S(1)}, bf16[272,256]{1,0:T(8,128)(2,1)S(1)}, u32[]{:S(2)}, u32[]{:S(2)}) collective-permute-start(bf16[272,256]{1,0:T(8,128)(2,1)S(1)} %get-tuple-element.25.refs_0_), channel_id=1, source_target_pairs={{0,12},{1,13},{2,14},{3,15},{4,0},{5,1},{6,2},{7,3},{8,4},{9,5},{1... | collective-permute-start | bytes 417800 | tf_op jit(solution)/shard_map/ppermute | solution.py:280
  11.3 1.7 %collective-permute-start.4 = (bf16[528,256]{1,0:T(8,128)(2,1)S(1)}, bf16[528,256]{1,0:T(8,128)(2,1)S(1)}, u32[]{:S(2)}, u32[]{:S(2)}) collective-permute-start(bf16[528,256]{1,0:T(8,128)(2,1)S(1)} %get-tuple-element.26.refs_4_), channel_id=1, source_target_pairs={{0,2},{1,3},{2,0},{3,1},{4,6},{5,7},{6,4},{7,5},{8,10},{9,11},{10,... | collective-permute-start | bytes 811016 | tf_op jit(solution)/shard_map/ppermute | solution.py:280
  13.0 2.8 %collective-permute-done.1.one_ref = bf16[272,256]{1,0:T(8,128)(2,1)S(1)} collective-permute-done((bf16[272,256]{1,0:T(8,128)(2,1)S(1)}, bf16[272,256]{1,0:T(8,128)(2,1)S(1)}, u32[]{:S(2)}, u32[]{:S(2)}) %collective-permute-start.1) | collective-permute-done | bytes 139296 | tf_op jit(solution)/shard_map/ppermute | solution.py:280
  15.7 1.9 %collective-permute-done.2.two_ref = bf16[272,256]{1,0:T(8,128)(2,1)S(1)} collective-permute-done((bf16[272,256]{1,0:T(8,128)(2,1)S(1)}, bf16[272,256]{1,0:T(8,128)(2,1)S(1)}, u32[]{:S(2)}, u32[]{:S(2)}) %collective-permute-start.2) | collective-permute-done | bytes 139296 | tf_op jit(solution)/shard_map/ppermute | solution.py:280
  17.6 1.6 %collective-permute-start.5 = (bf16[544,256]{1,0:T(8,128)(2,1)S(1)}, bf16[544,256]{1,0:T(8,128)(2,1)S(1)}, u32[]{:S(2)}, u32[]{:S(2)}) collective-permute-start(bf16[544,256]{1,0:T(8,128)(2,1)S(1)} %join_pieces.1.refs_1_.refs_4_), channel_id=1, source_target_pairs={{0,2},{1,3},{2,0},{3,1},{4,6},{5,7},{6,4},{7,5},{8,10},{9,11},{10,... | collective-permute-start | bytes 835592 | tf_op jit(solution)/shard_map/ppermute | solution.py:280
  19.2 1.1 %collective-permute-start.3 = (bf16[272,256]{1,0:T(8,128)(2,1)S(1)}, bf16[272,256]{1,0:T(8,128)(2,1)S(1)}, u32[]{:S(2)}, u32[]{:S(2)}) collective-permute-start(bf16[272,256]{1,0:T(8,128)(2,1)S(1)} %collective-permute-done.1.one_ref), channel_id=1, source_target_pairs={{0,4},{1,5},{2,6},{3,7},{4,8},{5,9},{6,10},{7,11},{8,12},{9,13},{1... | collective-permute-start | bytes 417800 | tf_op jit(solution)/shard_map/ppermute | solution.py:280
  20.4 5.7 %collective-permute-done.3.refs_2_.refs_5_ = bf16[272,256]{1,0:T(8,128)(2,1)S(1)} collective-permute-done((bf16[272,256]{1,0:T(8,128)(2,1)S(1)}, bf16[272,256]{1,0:T(8,128)(2,1)S(1)}, u32[]{:S(2)}, u32[]{:S(2)}) %collective-permute-start.3) | collective-permute-done | bytes 139296 | tf_op jit(solution)/shard_map/ppermute | solution.py:280
  26.1 1.5 %collective-permute-start.10 = (bf16[272,256]{1,0:T(8,128)(2,1)S(1)}, bf16[272,256]{1,0:T(8,128)(2,1)S(1)}, u32[]{:S(2)}, u32[]{:S(2)}) collective-permute-start(bf16[272,256]{1,0:T(8,128)(2,1)S(1)} %collective-permute-done.3.refs_2_.refs_5_), channel_id=1, source_target_pairs={{0,16},{1,17},{2,18},{3,19},{4,20},{5,21},{6,22},{7,23},{8,24},{9,... | collective-permute-start | bytes 417800 | tf_op jit(solution)/shard_map/ppermute | solution.py:280
  27.6 0.5 collective-permute-start.6
  28.1 0.5 collective-permute-start.9
  28.6 4.0 %collective-permute-done.10.refs_6_ = bf16[272,256]{1,0:T(8,128)(2,1)S(1)} collective-permute-done((bf16[272,256]{1,0:T(8,128)(2,1)S(1)}, bf16[272,256]{1,0:T(8,128)(2,1)S(1)}, u32[]{:S(2)}, u32[]{:S(2)}) %collective-permute-start.10) | collective-permute-done | bytes 139296 | tf_op jit(solution)/shard_map/ppermute | solution.py:280
  33.1 0.5 collective-permute-done.6.refs_5_.refs_6_
  33.6 1.1 %collective-permute-start.12 = (bf16[544,256]{1,0:T(8,128)(2,1)S(1)}, bf16[544,256]{1,0:T(8,128)(2,1)S(1)}, u32[]{:S(2)}, u32[]{:S(2)}) collective-permute-start(bf16[544,256]{1,0:T(8,128)(2,1)S(1)} %collective-permute-done.5.refs_4_.refs_5_), channel_id=1, source_target_pairs={{0,16},{1,17},{2,18},{3,19},{4,20},{5,21},{6,22},{7,23},{8,24},{9,... | collective-permute-start | bytes 835592 | tf_op jit(solution)/shard_map/ppermute | solution.py:280
  34.7 0.7 %copy-done.4 = s32[2]{0:T(128)S(1)} copy-done((s32[2]{0:T(128)S(1)}, s32[2]{0:T(128)}, u32[]{:S(2)}) %copy-start.4) | copy-done | bytes 32
  35.3 0.6 %count_rows.1 = (s32[2,128]{1,0:T(2,128)S(1)}, s32[1,256]{1,0:T(1,128)S(1)}) custom-call(s32[2]{0:T(128)S(1)} %copy-done.4, bf16[272,256]{1,0:T(8,128)(2,1)S(1)} %get-tuple-element.25.refs_0_, bf16[544,256]{1,0:T(8,128)(2,1)S(1)} %join_pieces.1.refs_1_.refs_4_, bf16[272,256]{1,0:T(8,128)(2,1)S(1)} %collective-permute-done.3.refs_2_.refs_5_, ...), custom_call_target="tpu_custom_call" | custom-call | flops 16777216 | bytes 1048576 | tf_op jit(solution)/shard_map/count_rows/pallas_call | solution.py:286
  36.0 3.6 %held_rows.1 = (bf16[2,512,256]{2,1,0:T(8,128)(2,1)S(1)}, f32[2,256,1]{2,1,0:T(8,128)S(1)}, f32[2,256,1]{2,1,0:T(8,128)S(1)}, f32[2,256,256]{2,1,0:T(8,128)S(1)}) custom-call(s32[2,128]{1,0:T(2,128)S(1)} %get-tuple-element.29.limit_ref, bf16[2,4,8192]{2,1,0:T(4,128)(2,1)} %query_hbm.1, bf16[256,1024]{1,0:T(8,128)(2,1)} %key_up_hbm.1, ...), custom_call_target="tpu_custom_call" | custom-call | flops 2147483648 | bytes 4194304 | tf_op jit(solution)/shard_map/held_rows/pallas_call | solution.py:465
  40.7 0.9 %collective-permute-done.12.refs_8_ = bf16[544,256]{1,0:T(8,128)(2,1)S(1)} collective-permute-done((bf16[544,256]{1,0:T(8,128)(2,1)S(1)}, bf16[544,256]{1,0:T(8,128)(2,1)S(1)}, u32[]{:S(2)}, u32[]{:S(2)}) %collective-permute-start.12) | collective-permute-done | bytes 278560 | tf_op jit(solution)/shard_map/ppermute | solution.py:280
  41.6 0.9 %down_place_rows.1 = (f32[264,256]{1,0:T(8,128)S(1)}, f32[264,256]{1,0:T(8,128)S(1)}) custom-call(bf16[128,8192]{1,0:T(8,128)(2,1)S(1)} %copy-done, bf16[2,4,8192]{2,1,0:T(4,128)(2,1)S(1)} %copy-done.1, bf16[128,8192]{1,0:T(8,128)(2,1)S(1)} %collective-permute-done.7.refs_2_, bf16[2,4,8192]{2,1,0:T(4,128)(2,1)S(1)} %collective-permute-done.8.refs_3_, ...), custom_call_target="tpu_custom_call" | custom-call | flops 268435456 | bytes 1048576 | tf_op jit(solution)/shard_map/down_place_rows/pallas_call | solution.py:286
  42.6 1.5 %collective-permute-done.13.came_ref = f32[264,256]{1,0:T(8,128)S(1)} collective-permute-done((f32[264,256]{1,0:T(8,128)S(1)}, f32[264,256]{1,0:T(8,128)S(1)}, u32[]{:S(2)}, u32[]{:S(2)}) %collective-permute-start.13) | collective-permute-done | bytes 270368 | tf_op jit(solution)/shard_map/ppermute | solution.py:280
  44.2 0.5 collective-permute-start.14
  44.7 3.4 %collective-permute-start.15 = (bf16[32,256]{1,0:T(8,128)(2,1)S(1)}, bf16[32,256]{1,0:T(8,128)(2,1)S(1)}, u32[]{:S(2)}, u32[]{:S(2)}) collective-permute-start(bf16[32,256]{1,0:T(8,128)(2,1)S(1)} %get-tuple-element.39), channel_id=1, source_target_pairs={{0,12},{1,13},{2,14},{3,15},{4,0},{5,1},{6,2},{7,3},{8,4},{9,5},{1... | collective-permute-start | bytes 49160 | tf_op jit(solution)/shard_map/ppermute | solution.py:280
  48.1 1.5 %collective-permute-start.17 = (bf16[32,256]{1,0:T(8,128)(2,1)S(1)}, bf16[32,256]{1,0:T(8,128)(2,1)S(1)}, u32[]{:S(2)}, u32[]{:S(2)}) collective-permute-start(bf16[32,256]{1,0:T(8,128)(2,1)S(1)} %get-tuple-element.41), channel_id=1, source_target_pairs={{0,2},{1,3},{2,0},{3,1},{4,6},{5,7},{6,4},{7,5},{8,10},{9,11},{10,... | collective-permute-start | bytes 49160 | tf_op jit(solution)/shard_map/ppermute | solution.py:280
  49.5 0.6 collective-permute-start.18
  50.1 4.2 %collective-permute-start.19 = (bf16[32,256]{1,0:T(8,128)(2,1)S(1)}, bf16[32,256]{1,0:T(8,128)(2,1)S(1)}, u32[]{:S(2)}, u32[]{:S(2)}) collective-permute-start(bf16[32,256]{1,0:T(8,128)(2,1)S(1)} %get-tuple-element.43), channel_id=1, source_target_pairs={{0,14},{1,15},{2,12},{3,13},{4,2},{5,3},{6,0},{7,1},{8,6},{9,7},{1... | collective-permute-start | bytes 49160 | tf_op jit(solution)/shard_map/ppermute | solution.py:280
  54.3 1.1 %collective-permute-start.20 = (bf16[32,256]{1,0:T(8,128)(2,1)S(1)}, bf16[32,256]{1,0:T(8,128)(2,1)S(1)}, u32[]{:S(2)}, u32[]{:S(2)}) collective-permute-start(bf16[32,256]{1,0:T(8,128)(2,1)S(1)} %get-tuple-element.44), channel_id=1, source_target_pairs={{0,10},{1,11},{2,8},{3,9},{4,14},{5,15},{6,12},{7,13},{8,2},{9,3},... | collective-permute-start | bytes 49160 | tf_op jit(solution)/shard_map/ppermute | solution.py:280
  55.4 0.6 collective-permute-done.18.refs_5_
  56.0 3.8 %collective-permute-done.20.refs_7_ = bf16[32,256]{1,0:T(8,128)(2,1)S(1)} collective-permute-done((bf16[32,256]{1,0:T(8,128)(2,1)S(1)}, bf16[32,256]{1,0:T(8,128)(2,1)S(1)}, u32[]{:S(2)}, u32[]{:S(2)}) %collective-permute-start.20) | collective-permute-done | bytes 16416 | tf_op jit(solution)/shard_map/ppermute | solution.py:280
  59.8 2.1 %late_rows.1 = bf16[2,4,8192]{2,1,0:T(4,128)(2,1)} custom-call(s32[1,256]{1,0:T(1,128)S(1)} %get-tuple-element.27.column_slot_ref, f32[8,256]{1,0:T(8,128)S(1)} %get-tuple-element.33.draft_latent_ref, bf16[2,512,256]{2,1,0:T(8,128)(2,1)S(1)} %get-tuple-element.34.turned_ref, f32[2,256,1]{2,1,0:T(8,128)S(1)} %get-tuple-element.30.refs_9_.peak_ref, ...), custom_call_target="tpu_custom_call" | custom-call | tf_op jit(solution)/shard_map/late_rows/pallas_call | solution.py:491
  (30 shorter events, 2.1 us)
Async XLA Ops:
  0.0 39.6 %collective-permute-start.7 = (bf16[128,8192]{1,0:T(8,128)(2,1)}, bf16[128,8192]{1,0:T(8,128)(2,1)S(1)}, u32[]{:S(2)}, u32[]{:S(2)}) collective-permute-start(bf16[128,8192]{1,0:T(8,128)(2,1)} %refs_0_.7), channel_id=1, source_target_pairs={{0,1},{1,0},{2,3},{3,2},{4,5},{5,4},{6,7},{7,6},{8,9},{9,8},{10,11... | collective-permute-start | bytes 6291464 | tf_op jit(solution)/shard_map/ppermute | solution.py:280
  0.5 4.0 %collective-permute-start = (s32[1,128]{1,0:T(1,128)}, s32[1,128]{1,0:T(1,128)S(1)}, u32[]{:S(2)}, u32[]{:S(2)}) collective-permute-start(s32[1,128]{1,0:T(1,128)} %bitcast.1), channel_id=1, source_target_pairs={{0,1},{1,0},{2,3},{3,2},{4,5},{5,4},{6,7},{7,6},{8,9},{9,8},{10,11... | collective-permute-start | bytes 1544 | tf_op jit(solution)/shard_map/ppermute | solution.py:280
  4.5 0.7 %copy-start.3 = (s32[128]{0:T(128)S(1)}, s32[128]{0:T(128)}, u32[]{:S(2)}) copy-start(s32[128]{0:T(128)} %param.12) | copy-start | bytes 1540
  6.2 9.5 %collective-permute-start.1 = (bf16[272,256]{1,0:T(8,128)(2,1)S(1)}, bf16[272,256]{1,0:T(8,128)(2,1)S(1)}, u32[]{:S(2)}, u32[]{:S(2)}) collective-permute-start(bf16[272,256]{1,0:T(8,128)(2,1)S(1)} %get-tuple-element.25.refs_0_), channel_id=1, source_target_pairs={{0,4},{1,5},{2,6},{3,7},{4,8},{5,9},{6,10},{7,11},{8,12},{9,13},{1... | collective-permute-start | bytes 417800 | tf_op jit(solution)/shard_map/ppermute | solution.py:280
  9.2 8.4 %collective-permute-start.2 = (bf16[272,256]{1,0:T(8,128)(2,1)S(1)}, bf16[272,256]{1,0:T(8,128)(2,1)S(1)}, u32[]{:S(2)}, u32[]{:S(2)}) collective-permute-start(bf16[272,256]{1,0:T(8,128)(2,1)S(1)} %get-tuple-element.25.refs_0_), channel_id=1, source_target_pairs={{0,12},{1,13},{2,14},{3,15},{4,0},{5,1},{6,2},{7,3},{8,4},{9,5},{1... | collective-permute-start | bytes 417800 | tf_op jit(solution)/shard_map/ppermute | solution.py:280
  11.3 16.8 %collective-permute-start.4 = (bf16[528,256]{1,0:T(8,128)(2,1)S(1)}, bf16[528,256]{1,0:T(8,128)(2,1)S(1)}, u32[]{:S(2)}, u32[]{:S(2)}) collective-permute-start(bf16[528,256]{1,0:T(8,128)(2,1)S(1)} %get-tuple-element.26.refs_4_), channel_id=1, source_target_pairs={{0,2},{1,3},{2,0},{3,1},{4,6},{5,7},{6,4},{7,5},{8,10},{9,11},{10,... | collective-permute-start | bytes 811016 | tf_op jit(solution)/shard_map/ppermute | solution.py:280
  17.6 11.0 %collective-permute-start.5 = (bf16[544,256]{1,0:T(8,128)(2,1)S(1)}, bf16[544,256]{1,0:T(8,128)(2,1)S(1)}, u32[]{:S(2)}, u32[]{:S(2)}) collective-permute-start(bf16[544,256]{1,0:T(8,128)(2,1)S(1)} %join_pieces.1.refs_1_.refs_4_), channel_id=1, source_target_pairs={{0,2},{1,3},{2,0},{3,1},{4,6},{5,7},{6,4},{7,5},{8,10},{9,11},{10,... | collective-permute-start | bytes 835592 | tf_op jit(solution)/shard_map/ppermute | solution.py:280
  19.2 6.9 %collective-permute-start.3 = (bf16[272,256]{1,0:T(8,128)(2,1)S(1)}, bf16[272,256]{1,0:T(8,128)(2,1)S(1)}, u32[]{:S(2)}, u32[]{:S(2)}) collective-permute-start(bf16[272,256]{1,0:T(8,128)(2,1)S(1)} %collective-permute-done.1.one_ref), channel_id=1, source_target_pairs={{0,4},{1,5},{2,6},{3,7},{4,8},{5,9},{6,10},{7,11},{8,12},{9,13},{1... | collective-permute-start | bytes 417800 | tf_op jit(solution)/shard_map/ppermute | solution.py:280
  26.1 6.6 %collective-permute-start.10 = (bf16[272,256]{1,0:T(8,128)(2,1)S(1)}, bf16[272,256]{1,0:T(8,128)(2,1)S(1)}, u32[]{:S(2)}, u32[]{:S(2)}) collective-permute-start(bf16[272,256]{1,0:T(8,128)(2,1)S(1)} %collective-permute-done.3.refs_2_.refs_5_), channel_id=1, source_target_pairs={{0,16},{1,17},{2,18},{3,19},{4,20},{5,21},{6,22},{7,23},{8,24},{9,... | collective-permute-start | bytes 417800 | tf_op jit(solution)/shard_map/ppermute | solution.py:280
  27.6 6.0 %collective-permute-start.6 = (bf16[272,256]{1,0:T(8,128)(2,1)S(1)}, bf16[272,256]{1,0:T(8,128)(2,1)S(1)}, u32[]{:S(2)}, u32[]{:S(2)}) collective-permute-start(bf16[272,256]{1,0:T(8,128)(2,1)S(1)} %collective-permute-done.3.refs_2_.refs_5_), channel_id=1, source_target_pairs={{0,2},{1,3},{2,0},{3,1},{4,6},{5,7},{6,4},{7,5},{8,10},{9,11},{10,... | collective-permute-start | bytes 417800 | tf_op jit(solution)/shard_map/ppermute | solution.py:280
  28.1 12.2 %collective-permute-start.9 = (bf16[544,256]{1,0:T(8,128)(2,1)S(1)}, bf16[544,256]{1,0:T(8,128)(2,1)S(1)}, u32[]{:S(2)}, u32[]{:S(2)}) collective-permute-start(bf16[544,256]{1,0:T(8,128)(2,1)S(1)} %join_pieces.1.refs_1_.refs_4_), channel_id=1, source_target_pairs={{0,16},{1,17},{2,18},{3,19},{4,20},{5,21},{6,22},{7,23},{8,24},{9,... | collective-permute-start | bytes 835592 | tf_op jit(solution)/shard_map/ppermute | solution.py:280
  28.6 11.0 %collective-permute-start.8 = (bf16[2,4,8192]{2,1,0:T(4,128)(2,1)}, bf16[2,4,8192]{2,1,0:T(4,128)(2,1)S(1)}, u32[]{:S(2)}, u32[]{:S(2)}) collective-permute-start(bf16[2,4,8192]{2,1,0:T(4,128)(2,1)} %refs_1_.7), channel_id=1, source_target_pairs={{0,1},{1,0},{2,3},{3,2},{4,5},{5,4},{6,7},{7,6},{8,9},{9,8},{10,11... | collective-permute-start | bytes 393224 | tf_op jit(solution)/shard_map/ppermute | solution.py:280
  32.7 8.0 %collective-permute-start.11 = (bf16[272,256]{1,0:T(8,128)(2,1)S(1)}, bf16[272,256]{1,0:T(8,128)(2,1)S(1)}, u32[]{:S(2)}, u32[]{:S(2)}) collective-permute-start(bf16[272,256]{1,0:T(8,128)(2,1)S(1)} %collective-permute-done.10.refs_6_), channel_id=1, source_target_pairs={{0,2},{1,3},{2,0},{3,1},{4,6},{5,7},{6,4},{7,5},{8,10},{9,11},{10,... | collective-permute-start | bytes 417800 | tf_op jit(solution)/shard_map/ppermute | solution.py:280
  33.6 8.0 %collective-permute-start.12 = (bf16[544,256]{1,0:T(8,128)(2,1)S(1)}, bf16[544,256]{1,0:T(8,128)(2,1)S(1)}, u32[]{:S(2)}, u32[]{:S(2)}) collective-permute-start(bf16[544,256]{1,0:T(8,128)(2,1)S(1)} %collective-permute-done.5.refs_4_.refs_5_), channel_id=1, source_target_pairs={{0,16},{1,17},{2,18},{3,19},{4,20},{5,21},{6,22},{7,23},{8,24},{9,... | collective-permute-start | bytes 835592 | tf_op jit(solution)/shard_map/ppermute | solution.py:280
  34.7 0.7 %copy-start.4 = (s32[2]{0:T(128)S(1)}, s32[2]{0:T(128)}, u32[]{:S(2)}) copy-start(s32[2]{0:T(128)} %context_ref.1) | copy-start | bytes 28
  36.0 3.7 %copy-start = (bf16[128,8192]{1,0:T(8,128)(2,1)S(1)}, bf16[128,8192]{1,0:T(8,128)(2,1)}, u32[]{:S(2)}) copy-start(bf16[128,8192]{1,0:T(8,128)(2,1)} %refs_0_.7) | copy-start | bytes 6291460
  36.0 3.7 %copy-start.1 = (bf16[2,4,8192]{2,1,0:T(4,128)(2,1)S(1)}, bf16[2,4,8192]{2,1,0:T(4,128)(2,1)}, u32[]{:S(2)}) copy-start(bf16[2,4,8192]{2,1,0:T(4,128)(2,1)} %refs_1_.7) | copy-start | bytes 393220
  41.6 18.2 %copy-start.2 = (bf16[256,1024]{1,0:T(8,128)(2,1)S(1)}, bf16[256,1024]{1,0:T(8,128)(2,1)}, u32[]{:S(2)}) copy-start(bf16[256,1024]{1,0:T(8,128)(2,1)} %value_up_ref.1) | copy-start | bytes 1572868
  42.5 1.6 %collective-permute-start.13 = (f32[264,256]{1,0:T(8,128)S(1)}, f32[264,256]{1,0:T(8,128)S(1)}, u32[]{:S(2)}, u32[]{:S(2)}) collective-permute-start(f32[264,256]{1,0:T(8,128)S(1)} %get-tuple-element.32), channel_id=1, source_target_pairs={{0,1},{1,0},{2,3},{3,2},{4,5},{5,4},{6,7},{7,6},{8,9},{9,8},{10,11... | collective-permute-start | bytes 811016 | tf_op jit(solution)/shard_map/ppermute | solution.py:280
  44.2 5.9 %collective-permute-start.14 = (bf16[32,256]{1,0:T(8,128)(2,1)S(1)}, bf16[32,256]{1,0:T(8,128)(2,1)S(1)}, u32[]{:S(2)}, u32[]{:S(2)}) collective-permute-start(bf16[32,256]{1,0:T(8,128)(2,1)S(1)} %get-tuple-element.38), channel_id=1, source_target_pairs={{0,4},{1,5},{2,6},{3,7},{4,8},{5,9},{6,10},{7,11},{8,12},{9,13},{1... | collective-permute-start | bytes 49160 | tf_op jit(solution)/shard_map/ppermute | solution.py:280
  44.7 9.6 %collective-permute-start.15 = (bf16[32,256]{1,0:T(8,128)(2,1)S(1)}, bf16[32,256]{1,0:T(8,128)(2,1)S(1)}, u32[]{:S(2)}, u32[]{:S(2)}) collective-permute-start(bf16[32,256]{1,0:T(8,128)(2,1)S(1)} %get-tuple-element.39), channel_id=1, source_target_pairs={{0,12},{1,13},{2,14},{3,15},{4,0},{5,1},{6,2},{7,3},{8,4},{9,5},{1... | collective-permute-start | bytes 49160 | tf_op jit(solution)/shard_map/ppermute | solution.py:280
  48.1 7.3 %collective-permute-start.16 = (bf16[32,256]{1,0:T(8,128)(2,1)S(1)}, bf16[32,256]{1,0:T(8,128)(2,1)S(1)}, u32[]{:S(2)}, u32[]{:S(2)}) collective-permute-start(bf16[32,256]{1,0:T(8,128)(2,1)S(1)} %get-tuple-element.40), channel_id=1, source_target_pairs={{0,8},{1,9},{2,10},{3,11},{4,12},{5,13},{6,14},{7,15},{8,0},{9,1},... | collective-permute-start | bytes 49160 | tf_op jit(solution)/shard_map/ppermute | solution.py:280
  48.1 7.3 %collective-permute-start.17 = (bf16[32,256]{1,0:T(8,128)(2,1)S(1)}, bf16[32,256]{1,0:T(8,128)(2,1)S(1)}, u32[]{:S(2)}, u32[]{:S(2)}) collective-permute-start(bf16[32,256]{1,0:T(8,128)(2,1)S(1)} %get-tuple-element.41), channel_id=1, source_target_pairs={{0,2},{1,3},{2,0},{3,1},{4,6},{5,7},{6,4},{7,5},{8,10},{9,11},{10,... | collective-permute-start | bytes 49160 | tf_op jit(solution)/shard_map/ppermute | solution.py:280
  49.5 6.5 %collective-permute-start.18 = (bf16[32,256]{1,0:T(8,128)(2,1)S(1)}, bf16[32,256]{1,0:T(8,128)(2,1)S(1)}, u32[]{:S(2)}, u32[]{:S(2)}) collective-permute-start(bf16[32,256]{1,0:T(8,128)(2,1)S(1)} %get-tuple-element.42), channel_id=1, source_target_pairs={{0,6},{1,7},{2,4},{3,5},{4,10},{5,11},{6,8},{7,9},{8,14},{9,15},{1... | collective-permute-start | bytes 49160 | tf_op jit(solution)/shard_map/ppermute | solution.py:280
  50.1 5.9 %collective-permute-start.19 = (bf16[32,256]{1,0:T(8,128)(2,1)S(1)}, bf16[32,256]{1,0:T(8,128)(2,1)S(1)}, u32[]{:S(2)}, u32[]{:S(2)}) collective-permute-start(bf16[32,256]{1,0:T(8,128)(2,1)S(1)} %get-tuple-element.43), channel_id=1, source_target_pairs={{0,14},{1,15},{2,12},{3,13},{4,2},{5,3},{6,0},{7,1},{8,6},{9,7},{1... | collective-permute-start | bytes 49160 | tf_op jit(solution)/shard_map/ppermute | solution.py:280
  54.3 5.5 %collective-permute-start.20 = (bf16[32,256]{1,0:T(8,128)(2,1)S(1)}, bf16[32,256]{1,0:T(8,128)(2,1)S(1)}, u32[]{:S(2)}, u32[]{:S(2)}) collective-permute-start(bf16[32,256]{1,0:T(8,128)(2,1)S(1)} %get-tuple-element.44), channel_id=1, source_target_pairs={{0,10},{1,11},{2,8},{3,9},{4,14},{5,15},{6,12},{7,13},{8,2},{9,3},... | collective-permute-start | bytes 49160 | tf_op jit(solution)/shard_map/ppermute | solution.py:280

commit v5 on v4

--- a/solution.py
+++ b/solution.py
@@ -91,16 +91,10 @@
 
 
 def piece_sums(starts, spans, row_refs, refs):
-    groups = len(row_refs) // 2
-    slot_count, draft_count, _ = row_refs[1].shape
-    drafts = groups * slot_count * draft_count
     total = None
     for start, (n, first, depth) in zip(starts, spans):
         lanes = pl.ds(pl.multiple_of(start, HEAD_SIZE), depth)
-        stack = [ref[b, :, lanes].astype(jnp.float32) for ref in row_refs[1::2] for b in range(slot_count)]
-        if drafts < 16:
-            stack.append(jnp.zeros((16 - drafts, depth), jnp.float32))
-        rows = [ref[:, lanes] for ref in row_refs[0::2]] + [jnp.concatenate(stack, 0).astype(jnp.bfloat16)]
+        rows = [ref[:, lanes] for ref in row_refs]
         piece = refs[n][first : first + depth, :]
         product = jnp.dot(jnp.concatenate(rows, 0), piece, preferred_element_type=jnp.float32)
         total = product if total is None else total + product
@@ -108,13 +102,13 @@
 
 
 def down_kernel(starts_of, spans, first, *refs):
-    row_refs, refs, out_ref = refs[:4], refs[4:-1], refs[-1]
+    row_refs, refs, out_ref = refs[:3], refs[3:-1], refs[-1]
     total = piece_sums(starts_of(), spans, row_refs, refs)
     out_ref[...] = total if first else total + refs[-1][...]
 
 
 def down_place_kernel(starts_of, spans, *refs):
-    row_refs, refs, (keep_ref, send_ref) = refs[:4], refs[4:-2], refs[-2:]
+    row_refs, refs, (keep_ref, send_ref) = refs[:3], refs[3:-2], refs[-2:]
     place_ref, sum_ref, refs = refs[0], refs[1], refs[2:]
     total = piece_sums(starts_of(), spans, row_refs, refs) + sum_ref[...]
     slots, width = keep_ref.shape[0] - 8, keep_ref.shape[1]
@@ -135,75 +129,110 @@
         ref[slots:, :] = total[draft : draft + 8]
 
 
-def route_kernel(blocks, keep_ref, came_ref, draft_latent_ref, *refs):
-    out_refs, float_ref = refs[:-1], refs[-1]
+def route_kernel(keep_ref, came_ref, draft_latent_ref, stay_ref, send_ref, float_ref):
     float_ref[...] = keep_ref[...] + came_ref[...]
     slots = float_ref.shape[0] - 8
     draft_latent_ref[...] = float_ref[slots:, :].astype(jnp.bfloat16).astype(jnp.float32)
-    size = slots // len(out_refs)
-    for block, ref in zip(blocks(), out_refs):
-        rows = pl.ds(pl.multiple_of(block * size, size), size)
-        ref[...] = float_ref[rows, :].astype(jnp.bfloat16)
-
-
-def start_kernel(most_rows, target_ref, other_ref, shard_hbm, place_ref, half_ref, full_ref, sems):
+    size = slots // 8
+    wide = lax.axis_index("wide")
+    z, y = wide // 4, wide // 2 % 2
+    for other, ref in ((0, stay_ref), (1, send_ref)):
+        for n, (high, low) in enumerate(((0, 0), (0, 1), (1, 0), (1, 1))):
+            there = (z // 2 + high) % 2 * 2 + (z + low) % 2
+            block = there * 2 + (y + other) % 2
+            rows = pl.ds(pl.multiple_of(block * size, size), size)
+            ref[n * size : (n + 1) * size, :] = float_ref[rows, :].astype(jnp.bfloat16)
+
+
+def mix_kernel(outer, keep_ref, came_ref, stay_ref, send_ref):
+    half = keep_ref.shape[0] // 2
+    size = half // outer
+    for ref, first in ((stay_ref, 0), (send_ref, half)):
+        for n in range(outer):
+            for m, source in enumerate((keep_ref, came_ref)):
+                spot = (n * 2 + m) * size
+                ref[spot : spot + size, :] = source[first + n * size : first + (n + 1) * size, :]
+
+
+def start_kernel(target_hbm, shard_hbm, half_ref, full_ref, target_ref, sems):
     half_rows, shard_rows = half_ref.shape[0] - 16, full_ref.shape[0] - 16
     mine = pl.ds(pl.multiple_of(lax.axis_index("rep") * half_rows, half_rows), half_rows)
     copies = [
-        pltpu.make_async_copy(shard_hbm.at[mine], half_ref.at[:half_rows], sems.at[0]),
-        pltpu.make_async_copy(shard_hbm, full_ref.at[:shard_rows], sems.at[1]),
+        pltpu.make_async_copy(target_hbm, target_ref, sems.at[0]),
+        pltpu.make_async_copy(shard_hbm.at[mine], half_ref.at[:half_rows], sems.at[1]),
+        pltpu.make_async_copy(shard_hbm, full_ref.at[:shard_rows], sems.at[2]),
     ]
     for copy in copies:
         copy.start()
-    core = lax.axis_index("wide") % 2
     width, count = half_ref.shape[1], target_ref.shape[1]
-    f32, bf16 = jnp.float32, jnp.bfloat16
-    earlier = lax.broadcasted_iota(jnp.int32, (count, count), 0) < lax.broadcasted_iota(jnp.int32, (count, count), 1)
-    earlier = jnp.where(earlier, 1.0, 0.0).astype(bf16)
-    counts = []
-    for n, (ref, owner) in enumerate(((target_ref, core), (other_ref, 1 - core))):
-        target = ref[...]
-        hit = jnp.where(lax.broadcasted_iota(jnp.int32, (width, count), 0) == target, 1.0, 0.0)
-        counts.append(lax.dot_general(jnp.ones((16, count), bf16), hit.astype(bf16), NT, preferred_element_type=f32))
-        before = jnp.dot(hit[:64].astype(bf16), earlier, preferred_element_type=f32)
-        rank = jnp.sum(hit[:64] * before, 0, keepdims=True).astype(jnp.int32)
-        spot = jnp.where(target % 2 == 0, rank, most_rows - 1 - rank)
-        chip, side = target // 4, target // 2 % 2
-        slots = place_ref.shape[1]
-        place_ref[:, n * count : (n + 1) * count] = side * slots + (chip * 2 + owner) * most_rows + spot
-    low = jnp.where(core == 0, counts[0], counts[1])
-    high = jnp.where(core == 0, counts[1], counts[0])
-    block = jnp.where(lax.broadcasted_iota(jnp.int32, (16, width), 0) == 0, low, high).astype(bf16)
-    half_ref[half_rows:, :] = block
-    full_ref[shard_rows:, :] = block
-    for copy in copies:
-        copy.wait()
-
-
-def join_kernel(one_ref, two_ref, out_ref):
+    copies[0].wait()
+    hit = lax.broadcasted_iota(jnp.int32, (width, count), 0) == target_ref[...]
+    hit = jnp.where(hit, 1.0, 0.0).astype(jnp.bfloat16)
+    block = lax.dot_general(jnp.ones((16, count), jnp.bfloat16), hit, NT, preferred_element_type=jnp.float32)
+    half_ref[half_rows:, :] = block.astype(jnp.bfloat16)
+    full_ref[shard_rows:, :] = block.astype(jnp.bfloat16)
+    copies[1].wait()
+    copies[2].wait()
+
+
+def join_kernel(one_ref, two_ref, _, out_ref):
     rows = one_ref.shape[0]
     out_ref[:rows, :] = one_ref[...]
     out_ref[rows:, :] = two_ref[...]
 
 
-def count_kernel(most_rows, spans, context_ref, *refs):
-    refs, (limit_ref, column_slot_ref) = refs[:-2], refs[-2:]
-    counts = jnp.concatenate([refs[n][first : first + 16, :].astype(jnp.float32)[:2] for n, first in spans], 0)
+def pack_kernel(spans, target_ref, draft_ref, *refs):
+    refs, out_ref = refs[:-1], refs[-1]
+    slot_count, draft_count, model_width = draft_ref.shape
+    drafts = slot_count * draft_count
+    rows = [draft_ref[b].astype(jnp.float32) for b in range(slot_count)]
+    counts = [refs[n][first : first + 16, :].astype(jnp.float32)[:1] for n, first in spans]
+    counts.append(target_ref[...].astype(jnp.float32))
+    used = sum(x.shape[1] for x in counts)
+    counts.append(jnp.zeros((1, model_width - used), jnp.float32))
+    rows.append(jnp.broadcast_to(jnp.concatenate(counts, 1), (16 - drafts, model_width)))
+    out_ref[...] = jnp.concatenate(rows, 0).astype(jnp.bfloat16)
+
+
+def count_kernel(most_rows, context_ref, mine_ref, other_ref, _, limit_ref, column_slot_ref, place_ref, draft_ref):
+    f32, bf16 = jnp.float32, jnp.bfloat16
+    count, width = place_ref.shape[1] // 2, 256
+    wide = lax.axis_index("wide")
+    core = wide % 2
+    mine, other = mine_ref[...].astype(f32), other_ref[...].astype(f32)
+    draft_ref[...] = jnp.concatenate([mine[:8], other[:8]], 0).astype(bf16)
+    low = jnp.where(core == 0, mine[8:9], other[8:9])
+    high = jnp.where(core == 0, other[8:9], mine[8:9])
+    counts = []
+    for n in range(8):
+        counts += [low[:, n * width : (n + 1) * width], high[:, n * width : (n + 1) * width]]
+    counts = jnp.concatenate(counts, 0)
     lane = lax.broadcasted_iota(jnp.int32, counts.shape, 1)
     row = lax.broadcasted_iota(jnp.int32, counts.shape, 0)
     spread = []
     for b in range(2):
-        number = jnp.sum(jnp.where(lane == lax.axis_index("wide") * 2 + b, counts, 0.0), 1, keepdims=True)
+        number = jnp.sum(jnp.where(lane == wide * 2 + b, counts, 0.0), 1, keepdims=True)
         limit = context_ref[b] - jnp.sum(number, 0, keepdims=True).astype(jnp.int32)
         limit_ref[b : b + 1, :] = jnp.broadcast_to(limit, (1, limit_ref.shape[1]))
         spread.append(jnp.sum(jnp.where(lane // most_rows == row, number, 0.0), 0, keepdims=True).astype(jnp.int32))
     spot = lax.broadcasted_iota(jnp.int32, column_slot_ref.shape, 1) % most_rows
     column_slot_ref[...] = jnp.where(spot < spread[0], 0, jnp.where(spot >= most_rows - spread[1], 1, -1))
+    earlier = lax.broadcasted_iota(jnp.int32, (count, count), 0) < lax.broadcasted_iota(jnp.int32, (count, count), 1)
+    earlier = jnp.where(earlier, 1.0, 0.0).astype(bf16)
+    for n, (rows, owner) in enumerate(((mine, core), (other, 1 - core))):
+        target = rows[8:9, 8 * width : 8 * width + count].astype(jnp.int32)
+        hit = jnp.where(lax.broadcasted_iota(jnp.int32, (64, count), 0) == target, 1.0, 0.0)
+        before = jnp.dot(hit.astype(bf16), earlier, preferred_element_type=f32)
+        rank = jnp.sum(hit * before, 0, keepdims=True).astype(jnp.int32)
+        spot = jnp.where(target % 2 == 0, rank, most_rows - 1 - rank)
+        chip, side = target // 4, target // 2 % 2
+        place_ref[:, n * count : (n + 1) * count] = side * 2 * count + (chip * 2 + owner) * most_rows + spot
 
 
 def plain_down_kernel(place_ref, prompt_ref, draft_ref, weight_ref, outgoing_ref, draft_latent_ref):
-    count, depth = prompt_ref.shape
-    total = piece_sums([0], [(0, 0, depth)], [prompt_ref, draft_ref], [weight_ref])
+    count = prompt_ref.shape[0]
+    rows = jnp.concatenate([prompt_ref[...], draft_ref[...]], 0)
+    total = jnp.dot(rows, weight_ref[...], preferred_element_type=jnp.float32)
     draft_latent_ref[...] = total[count : count + 8].astype(jnp.bfloat16).astype(jnp.float32)
     spot = lax.broadcasted_iota(jnp.int32, (outgoing_ref.shape[0], count), 0)
     chosen = jnp.where(spot == place_ref[...], 1.0, 0.0).astype(jnp.bfloat16)
@@ -264,7 +293,6 @@
 def deliver(prompt_hidden, draft_hidden, shard, row_target, context_len):
     shard_rows, width = shard.shape
     count = prompt_hidden.shape[0]
-    sizes = (2, 4, 2, 2)
     spots = [(r, z, y, c) for r in range(2) for z in range(4) for y in range(2) for c in range(2)]
     most_rows = count // 8
     f32, bf16 = jnp.float32, jnp.bfloat16
@@ -272,129 +300,129 @@
     def flat(spot):
         return ((spot[0] * 4 + spot[1]) * 2 + spot[2]) * 2 + spot[3]
 
-    def move(x, *steps):
-        pairs = []
-        for spot in spots:
-            to = [(spot[a] + steps[a]) % sizes[a] for a in range(4)]
-            pairs.append((flat(spot), flat(to)))
+    def swap(x, r=0, z=0, y=0, c=0):
+        pairs = [(flat(spot), flat([a ^ b for a, b in zip(spot, (r, z, y, c))])) for spot in spots]
         return lax.ppermute(x, ("rep", "wide"), pairs)
 
     def array(rows, dtype=bf16):
         return jax.ShapeDtypeStruct((rows, width), dtype)
 
-    def call(kernel, out_shape, name, *operands, specs=None, flops=2**24, **more):
+    def call(kernel, out_shape, name, *operands, specs=None, flops=2**20, **more):
         return pl.pallas_call(
             kernel,
             out_shape=out_shape,
             in_specs=specs or [WHOLE] * len(operands),
             out_specs=[WHOLE] * len(out_shape) if isinstance(out_shape, list) else WHOLE,
             compiler_params=params(16),
-            cost_estimate=pl.CostEstimate(flops=flops, bytes_accessed=2**20, transcendentals=0),
+            cost_estimate=pl.CostEstimate(flops=flops, bytes_accessed=2**16, transcendentals=0),
             name=name,
             **more,
         )(*operands)
 
-    target = row_target.reshape(1, count)
-    other_target = move(target, 0, 0, 0, 1)
+    hbm = pl.BlockSpec(memory_space=pltpu.HBM)
     half_rows = shard_rows // 2
     ext = half_rows + 16
-    place, half, full = call(
-        functools.partial(start_kernel, most_rows),
-        [jax.ShapeDtypeStruct((1, 2 * count), jnp.int32), array(ext), array(shard_rows + 16)],
+    half, full, target = call(
+        start_kernel,
+        [array(ext), array(shard_rows + 16), jax.ShapeDtypeStruct((1, count), jnp.int32)],
         "start_rows",
-        target,
-        other_target,
-        pltpu.with_memory_space_constraint(shard, pltpu.HBM),
-        specs=[WHOLE, WHOLE, pl.BlockSpec(memory_space=pltpu.HBM)],
-        scratch_shapes=[pltpu.SemaphoreType.DMA((2,))],
+        *(pltpu.with_memory_space_constraint(x, pltpu.HBM) for x in (row_target.reshape(1, count), shard)),
+        specs=[hbm, hbm],
+        scratch_shapes=[pltpu.SemaphoreType.DMA((3,))],
     )
-    z1, z3 = move(half, 0, 1, 0, 0), move(half, 0, 3, 0, 0)
-    y0 = move(full, 0, 0, 1, 0)
-    other_prompt, other_draft = move(prompt_hidden, 0, 0, 0, 1), move(draft_hidden, 0, 0, 0, 1)
-    z2 = move(z1, 0, 1, 0, 0)
-    z13 = call(join_kernel, array(2 * ext), "join_pieces", z1, z3)
-    yz13, xz13 = move(z13, 0, 0, 1, 0), move(z13, 1, 0, 0, 0)
-    yz2, xz2 = move(z2, 0, 0, 1, 0), move(z2, 1, 0, 0, 0)
-    xyz13 = move(yz13, 1, 0, 0, 0)
-    yxz2 = move(xz2, 0, 0, 1, 0)
-
-    def starts_of(trails):
+    za, zb = swap(half, z=1), swap(half, z=2)
+    y0 = swap(full, y=1)
+    other_prompt = swap(prompt_hidden, c=1)
+    zab = call(join_kernel, array(2 * ext), "join_pieces", za, zb, y0, specs=[WHOLE, WHOLE, UNREAD])
+    yab, xab = swap(zab, y=1), swap(zab, r=1)
+    zc = swap(zb, z=1)
+    yc, xc = swap(zc, y=1), swap(zc, r=1)
+    xyab = swap(yab, r=1)
+    yxc = swap(xc, y=1)
+
+    order = [
+        (half, half_rows), (y0, shard_rows), (zab, ext + half_rows), (yab, ext + half_rows),
+        (zab, half_rows), (yab, half_rows), (zc, half_rows), (yc, half_rows),
+    ]
+    pack = call(
+        functools.partial(pack_kernel, [(n, first) for n, (_, first) in enumerate(order)]),
+        jax.ShapeDtypeStruct((16, draft_hidden.shape[2]), bf16), "pack_rows",
+        target, draft_hidden, *(x for x, _ in order), xab,
+        specs=[WHOLE] * (2 + len(order)) + [UNREAD],
+    )
+    other_pack = swap(pack, c=1)
+    limit, column_slot, place, drafts = call(
+        functools.partial(count_kernel, most_rows),
+        [
+            jax.ShapeDtypeStruct((2, 128), jnp.int32),
+            jax.ShapeDtypeStruct((1, 2 * count), jnp.int32),
+            jax.ShapeDtypeStruct((1, 2 * count), jnp.int32),
+            jax.ShapeDtypeStruct(pack.shape, bf16),
+        ],
+        "count_rows", context_len, pack, other_pack, xc,
+        specs=[SCALARS, WHOLE, WHOLE, UNREAD],
+    )
+
+    def starts_of(uses):
         def starts():
             rep, wide = lax.axis_index("rep"), lax.axis_index("wide")
             z, y, c = wide // 4, wide // 2 % 2, wide % 2
-            return [
-                (((z + 4 - z_step) % 4 * 2 + (y + y_step) % 2) * 2 + c) * shard_rows
-                + (0 if x_step is None else (rep + x_step) % 2 * half_rows)
-                for x_step, z_step, y_step in trails
-            ]
+            found = []
+            for _, _, _, (x_step, z_step, y_step) in uses:
+                owner_z = (z // 2 + z_step // 2) % 2 * 2 + (z + z_step) % 2
+                owner = (owner_z * 2 + (y + y_step) % 2) * 2 + c
+                found.append(owner * shard_rows + (0 if x_step is None else (rep + x_step) % 2 * half_rows))
+            return found
 
         return starts
 
-    rows = [prompt_hidden, draft_hidden, other_prompt, other_draft]
+    rows = [prompt_hidden, other_prompt, drafts]
     stages = [
         ([full, y0], [(0, 0, shard_rows, (None, 0, 0)), (1, 0, shard_rows, (None, 0, 1))]),
         (
-            [z13, yz13],
-            [(0, 0, half_rows, (0, 1, 0)), (0, ext, half_rows, (0, 3, 0)),
-             (1, 0, half_rows, (0, 1, 1)), (1, ext, half_rows, (0, 3, 1))],
+            [zab, yab],
+            [(0, 0, half_rows, (0, 1, 0)), (0, ext, half_rows, (0, 2, 0)),
+             (1, 0, half_rows, (0, 1, 1)), (1, ext, half_rows, (0, 2, 1))],
         ),
         (
-            [xz13, z2, yz2],
-            [(0, 0, half_rows, (1, 1, 0)), (0, ext, half_rows, (1, 3, 0)),
-             (1, 0, half_rows, (0, 2, 0)), (2, 0, half_rows, (0, 2, 1))],
+            [xab, zc, yc],
+            [(0, 0, half_rows, (1, 1, 0)), (0, ext, half_rows, (1, 2, 0)),
+             (1, 0, half_rows, (0, 3, 0)), (2, 0, half_rows, (0, 3, 1))],
         ),
         (
-            [xz2, yxz2, xyz13],
-            [(0, 0, half_rows, (1, 2, 0)), (1, 0, half_rows, (1, 2, 1)),
-             (2, 0, half_rows, (1, 1, 1)), (2, ext, half_rows, (1, 3, 1))],
+            [xc, yxc, xyab],
+            [(0, 0, half_rows, (1, 3, 0)), (1, 0, half_rows, (1, 3, 1)),
+             (2, 0, half_rows, (1, 1, 1)), (2, ext, half_rows, (1, 2, 1))],
         ),
     ]
     sums = []
     total_rows = 2 * count + 16
     for n, (pieces, uses) in enumerate(stages[:-1]):
-        spans, trails = [use[:3] for use in uses], [use[3] for use in uses]
         sums = [
             call(
-                functools.partial(down_kernel, starts_of(trails), spans, n == 0),
-                array(total_rows, f32), "down_rows", *rows, *pieces, *sums, flops=2**28,
+                functools.partial(down_kernel, starts_of(uses), [use[:3] for use in uses], n == 0),
+                array(total_rows, f32), "down_rows", *rows, *pieces, *sums, flops=2**26,
             )
         ]
 
-    trails = [(0, 0), (1, 0), (3, 0), (2, 0), (0, 1), (1, 1), (3, 1), (2, 1)]
-    limit, column_slot = call(
-        functools.partial(
-            count_kernel, most_rows,
-            [(0, half_rows), (1, half_rows), (1, ext + half_rows), (2, half_rows),
-             (3, shard_rows), (4, half_rows), (4, ext + half_rows), (5, half_rows)],
-        ),
-        [jax.ShapeDtypeStruct((2, 128), jnp.int32), jax.ShapeDtypeStruct((1, 2 * count), jnp.int32)],
-        "count_rows",
-        context_len, half, z13, z2, y0, yz13, yz2,
-        specs=[SCALARS] + [WHOLE] * 6,
-    )
-
     def finish(tie):
         pieces, uses = stages[-1]
-        spans, ways = [use[:3] for use in uses], [use[3] for use in uses]
         keep, send = call(
-            functools.partial(down_place_kernel, starts_of(ways), spans),
+            functools.partial(down_place_kernel, starts_of(uses), [use[:3] for use in uses]),
             [array(2 * count + 8, f32)] * 2, "down_place_rows", *rows, place, *sums, *pieces, tie,
-            specs=[WHOLE] * (6 + len(pieces)) + [UNREAD], flops=2**28,
+            specs=[WHOLE] * (5 + len(pieces)) + [UNREAD], flops=2**26,
         )
-        came = move(send, 0, 0, 0, 1)
-
-        def blocks():
-            wide = lax.axis_index("wide")
-            z, y = wide // 4, wide // 2 % 2
-            return [(z + z_step) % 4 * 2 + (y + y_step) % 2 for z_step, y_step in trails]
-
-        draft_latent, *outgoing = call(
-            functools.partial(route_kernel, blocks),
-            [array(8, f32)] + [array(2 * most_rows)] * len(trails), "route_rows", keep, came,
+        came = swap(send, c=1)
+        block = array(count)
+        draft_latent, stay, send = call(
+            route_kernel, [array(8, f32), block, block], "route_rows", keep, came,
             scratch_shapes=[pltpu.VMEM((2 * count + 8, width), f32)],
         )
-        incoming = [x if n == 0 else move(x, 0, *trails[n], 0) for n, x in enumerate(outgoing)]
-        return draft_latent, incoming
+        came = swap(send, y=1)
+        stay, send = call(functools.partial(mix_kernel, 2), [block, block], "mix_rows", stay, came)
+        came = swap(send, z=2)
+        stay, send = call(functools.partial(mix_kernel, 1), [block, block], "mix_rows", stay, came)
+        return draft_latent, [stay, swap(send, z=1)]
 
     return limit, column_slot, finish
 
@@ -421,6 +449,9 @@
         spot < counts[:, 0:1], 0, jnp.where(spot >= most_rows - counts[:, 1:2], 1, -1)
     ).reshape(1, arrived)
 
+    tile = slot_count * draft_count
+    draft_flat = jnp.pad(draft_hidden.reshape(tile, draft_hidden.shape[2]), ((0, 16 - tile), (0, 0)))
+
     def finish(tie):
         outgoing, draft_latent = pl.pallas_call(
             plain_down_kernel,
@@ -432,7 +463,7 @@
             out_specs=[WHOLE] * 2,
             compiler_params=params(24),
             name="down_rows",
-        )(place.reshape(1, row_count), prompt_hidden, draft_hidden, weight)
+        )(place.reshape(1, row_count), prompt_hidden, draft_flat, weight)
         incoming = lax.all_to_all(
             outgoing.reshape(wide_size, most_rows, latent_width), "wide", split_axis=0, concat_axis=0, tiled=True
         )

time: 62.1 us -> 59.2 us (0.953)
  starting transfers between devices: 25.3 us -> 18.3 us
  waiting for transfers between devices: 25.8 us -> 30.2 us
    ppermute x21 -> x16, starting transfers between devices: 25.3 us -> 18.3 us  [swap(): return lax.ppermute(x, ('rep', 'wide'), pairs)]
    ppermute x21 -> x16, waiting for transfers between devices: 25.8 us -> 30.2 us  [swap(): return lax.ppermute(x, ('rep', 'wide'), pairs)]
    unnamed x10 -> x8, local copies, waits for them, and re-layouts: 1.33 us -> 0.92 us
    pallas_call x8 -> x11, Pallas kernels: 3.7 us -> 3.82 us  [call(): pl.pallas_call(kernel, out_shape=out_shape, in_specs=specs or [WHOLE] * l...]
  transfers between devices with their start and end apart: 21 -> 16, of which waited for: 10 -> 8; matrix products, arithmetic and copies ran while one was open for 0% -> 0% of each run, Pallas kernels for 10% -> 11%
where the time goes in v5:
time: 59.2 us; the launch traced here: 59.1 us
  waiting for transfers between devices  30.2 us (51%)
  starting transfers between devices  18.3 us (31%)
  Pallas kernels  9.53 us (16%)
  local copies, waits for them, and re-layouts  0.92 us (2%)
    ppermute x16, waiting for transfers between devices, swap(): return lax.ppermute(x, ('rep', 'wide'), pairs)  30.2 us
    ppermute x16, starting transfers between devices, swap(): return lax.ppermute(x, ('rep', 'wide'), pairs)  18.3 us
    pallas_call x11, Pallas kernels, call(): pl.pallas_call(kernel, out_shape=out_shape, in_specs=specs or [WHOLE] * l...  3.82 us
    pallas_call x1, Pallas kernels, local(): pl.pallas_call(held_kernel, out_shape=[jax.ShapeDtypeStruct((slot_count,...  3.6 us
    pallas_call x1, Pallas kernels, local(): pl.pallas_call(late_kernel, out_shape=jax.ShapeDtypeStruct((slot_count, d...  2.11 us
  transfers between devices with their start and end apart: 16, of which 8 were waited for; matrix products, arithmetic and copies ran while one was open for 0% of the time, Pallas kernels for 11%

profile of v5, /device:TPU:0, one launch (start us, length us, event | category | flops | bytes accessed | tf_op | source)
XLA Modules:
  0.0 59.1 jit_solution(1669525043089740477)
XLA Ops:
  0.0 0.5 collective-permute-start.9
  0.5 1.1 %start_rows.1 = (bf16[272,256]{1,0:T(8,128)(2,1)S(1)}, bf16[528,256]{1,0:T(8,128)(2,1)S(1)}, s32[1,128]{1,0:T(1,128)S(1)}) custom-call(s32[1,128]{1,0:T(1,128)} %bitcast.1, bf16[512,256]{1,0:T(8,128)(2,1)} %shard_hbm.1), custom_call_target="tpu_custom_call" | custom-call | flops 1048576 | bytes 65536 | tf_op jit(solution)/shard_map/start_rows/pallas_call | solution.py:311
  1.5 2.6 %collective-permute-start = (bf16[528,256]{1,0:T(8,128)(2,1)S(1)}, bf16[528,256]{1,0:T(8,128)(2,1)S(1)}, u32[]{:S(2)}, u32[]{:S(2)}) collective-permute-start(bf16[528,256]{1,0:T(8,128)(2,1)S(1)} %get-tuple-element.27.refs_3_), channel_id=1, source_target_pairs={{0,2},{1,3},{2,0},{3,1},{4,6},{5,7},{6,4},{7,5},{8,10},{9,11},{10,... | collective-permute-start | bytes 811016 | tf_op jit(solution)/shard_map/ppermute | solution.py:305
  4.1 2.6 %collective-permute-start.2 = (bf16[272,256]{1,0:T(8,128)(2,1)S(1)}, bf16[272,256]{1,0:T(8,128)(2,1)S(1)}, u32[]{:S(2)}, u32[]{:S(2)}) collective-permute-start(bf16[272,256]{1,0:T(8,128)(2,1)S(1)} %get-tuple-element.26.refs_0_), channel_id=1, source_target_pairs={{0,8},{1,9},{2,10},{3,11},{4,12},{5,13},{6,14},{7,15},{8,0},{9,1},... | collective-permute-start | bytes 417800 | tf_op jit(solution)/shard_map/ppermute | solution.py:305
  6.7 1.6 %collective-permute-start.1 = (bf16[272,256]{1,0:T(8,128)(2,1)S(1)}, bf16[272,256]{1,0:T(8,128)(2,1)S(1)}, u32[]{:S(2)}, u32[]{:S(2)}) collective-permute-start(bf16[272,256]{1,0:T(8,128)(2,1)S(1)} %get-tuple-element.26.refs_0_), channel_id=1, source_target_pairs={{0,4},{1,5},{2,6},{3,7},{4,0},{5,1},{6,2},{7,3},{8,12},{9,13},{10,... | collective-permute-start | bytes 417800 | tf_op jit(solution)/shard_map/ppermute | solution.py:305
  8.3 5.6 %collective-permute-done.2.two_ref = bf16[272,256]{1,0:T(8,128)(2,1)S(1)} collective-permute-done((bf16[272,256]{1,0:T(8,128)(2,1)S(1)}, bf16[272,256]{1,0:T(8,128)(2,1)S(1)}, u32[]{:S(2)}, u32[]{:S(2)}) %collective-permute-start.2) | collective-permute-done | bytes 139296 | tf_op jit(solution)/shard_map/ppermute | solution.py:305
  13.9 0.6 collective-permute-start.4
  14.5 0.6 collective-permute-start.3
  15.1 1.5 %collective-permute-start.6 = (bf16[544,256]{1,0:T(8,128)(2,1)S(1)}, bf16[544,256]{1,0:T(8,128)(2,1)S(1)}, u32[]{:S(2)}, u32[]{:S(2)}) collective-permute-start(bf16[544,256]{1,0:T(8,128)(2,1)S(1)} %join_pieces.1.refs_2_.refs_4_.refs_3_), channel_id=1, source_target_pairs={{0,16},{1,17},{2,18},{3,19},{4,20},{5,21},{6,22},{7,23},{8,24},{9,... | collective-permute-start | bytes 835592 | tf_op jit(solution)/shard_map/ppermute | solution.py:305
  16.6 2.4 %collective-permute-done.4.refs_6_.refs_4_ = bf16[272,256]{1,0:T(8,128)(2,1)S(1)} collective-permute-done((bf16[272,256]{1,0:T(8,128)(2,1)S(1)}, bf16[272,256]{1,0:T(8,128)(2,1)S(1)}, u32[]{:S(2)}, u32[]{:S(2)}) %collective-permute-start.4) | collective-permute-done | bytes 139296 | tf_op jit(solution)/shard_map/ppermute | solution.py:305
  19.0 0.6 collective-permute-start.5
  19.5 6.3 %collective-permute-done.5.refs_7_.refs_5_ = bf16[272,256]{1,0:T(8,128)(2,1)S(1)} collective-permute-done((bf16[272,256]{1,0:T(8,128)(2,1)S(1)}, bf16[272,256]{1,0:T(8,128)(2,1)S(1)}, u32[]{:S(2)}, u32[]{:S(2)}) %collective-permute-start.5) | collective-permute-done | bytes 139296 | tf_op jit(solution)/shard_map/ppermute | solution.py:305
  25.9 0.9 %copy-done.2 = bf16[2,4,8192]{2,1,0:T(4,128)(2,1)S(1)} copy-done((bf16[2,4,8192]{2,1,0:T(4,128)(2,1)S(1)}, bf16[2,4,8192]{2,1,0:T(4,128)(2,1)}, u32[]{:S(2)}) %copy-start.2) | copy-done | bytes 131096
  26.8 0.1 collective-permute-start.7
  26.9 1.6 %collective-permute-start.8 = (bf16[272,256]{1,0:T(8,128)(2,1)S(1)}, bf16[272,256]{1,0:T(8,128)(2,1)S(1)}, u32[]{:S(2)}, u32[]{:S(2)}) collective-permute-start(bf16[272,256]{1,0:T(8,128)(2,1)S(1)} %collective-permute-done.4.refs_6_.refs_4_), channel_id=1, source_target_pairs={{0,16},{1,17},{2,18},{3,19},{4,20},{5,21},{6,22},{7,23},{8,24},{9,... | collective-permute-start | bytes 417800 | tf_op jit(solution)/shard_map/ppermute | solution.py:305
  28.5 0.5 collective-permute-start.11
  29.0 4.4 %collective-permute-done.8._.refs_5_ = bf16[272,256]{1,0:T(8,128)(2,1)S(1)} collective-permute-done((bf16[272,256]{1,0:T(8,128)(2,1)S(1)}, bf16[272,256]{1,0:T(8,128)(2,1)S(1)}, u32[]{:S(2)}, u32[]{:S(2)}) %collective-permute-start.8) | collective-permute-done | bytes 139296 | tf_op jit(solution)/shard_map/ppermute | solution.py:305
  33.5 0.5 collective-permute-start.10
  34.0 0.7 %count_rows.1 = (s32[2,128]{1,0:T(2,128)S(1)}, s32[1,256]{1,0:T(1,128)S(1)}, s32[1,256]{1,0:T(1,128)S(1)}, bf16[16,8192]{1,0:T(8,128)(2,1)S(1)}) custom-call(s32[2]{0:T(128)S(1)} %copy-done.3, bf16[16,8192]{1,0:T(8,128)(2,1)S(1)} %pack_rows.1.mine_ref, bf16[16,8192]{1,0:T(8,128)(2,1)S(1)} %collective-permute-done.7.other_ref, ...), custom_call_target="tpu_custom_call" | custom-call | flops 1048576 | bytes 65536 | tf_op jit(solution)/shard_map/count_rows/pallas_call | solution.py:311
  34.7 3.6 %held_rows.1 = (bf16[2,512,256]{2,1,0:T(8,128)(2,1)S(1)}, f32[2,256,1]{2,1,0:T(8,128)S(1)}, f32[2,256,1]{2,1,0:T(8,128)S(1)}, f32[2,256,256]{2,1,0:T(8,128)S(1)}) custom-call(s32[2,128]{1,0:T(2,128)S(1)} %get-tuple-element.31.limit_ref, bf16[2,4,8192]{2,1,0:T(4,128)(2,1)} %query_hbm.1, bf16[256,1024]{1,0:T(8,128)(2,1)} %key_up_hbm.1, ...), custom_call_target="tpu_custom_call" | custom-call | flops 2147483648 | bytes 4194304 | tf_op jit(solution)/shard_map/held_rows/pallas_call | solution.py:496
  38.3 0.3 down_rows.3.refs_5_
  38.6 0.3 down_rows.4.refs_6_
  39.0 0.3 down_rows.5.refs_4_
  39.4 0.9 %down_place_rows.1 = (f32[264,256]{1,0:T(8,128)S(1)}, f32[264,256]{1,0:T(8,128)S(1)}) custom-call(bf16[128,8192]{1,0:T(8,128)(2,1)S(1)} %copy-done, bf16[128,8192]{1,0:T(8,128)(2,1)S(1)} %collective-permute-done.9.refs_1_, bf16[16,8192]{1,0:T(8,128)(2,1)S(1)} %get-tuple-element.29.refs_2_, s32[1,256]{1,0:T(1,128)S(1)} %get-tuple-element.30.refs_3_, ...), custom_call_target="tpu_custom_call" | custom-call | flops 67108864 | bytes 65536 | tf_op jit(solution)/shard_map/down_place_rows/pallas_call | solution.py:311
  40.4 1.5 %collective-permute-done.12.came_ref = f32[264,256]{1,0:T(8,128)S(1)} collective-permute-done((f32[264,256]{1,0:T(8,128)S(1)}, f32[264,256]{1,0:T(8,128)S(1)}, u32[]{:S(2)}, u32[]{:S(2)}) %collective-permute-start.12) | collective-permute-done | bytes 270368 | tf_op jit(solution)/shard_map/ppermute | solution.py:305
  42.0 1.6 %collective-permute-start.13 = (bf16[128,256]{1,0:T(8,128)(2,1)S(1)}, bf16[128,256]{1,0:T(8,128)(2,1)S(1)}, u32[]{:S(2)}, u32[]{:S(2)}) collective-permute-start(bf16[128,256]{1,0:T(8,128)(2,1)S(1)} %get-tuple-element.40), channel_id=1, source_target_pairs={{0,2},{1,3},{2,0},{3,1},{4,6},{5,7},{6,4},{7,5},{8,10},{9,11},{10,... | collective-permute-start | bytes 196616 | tf_op jit(solution)/shard_map/ppermute | solution.py:305
  43.5 2.7 %collective-permute-done.13.came_ref = bf16[128,256]{1,0:T(8,128)(2,1)S(1)} collective-permute-done((bf16[128,256]{1,0:T(8,128)(2,1)S(1)}, bf16[128,256]{1,0:T(8,128)(2,1)S(1)}, u32[]{:S(2)}, u32[]{:S(2)}) %collective-permute-start.13) | collective-permute-done | bytes 65568 | tf_op jit(solution)/shard_map/ppermute | solution.py:305
  46.3 3.4 %collective-permute-start.14 = (bf16[128,256]{1,0:T(8,128)(2,1)S(1)}, bf16[128,256]{1,0:T(8,128)(2,1)S(1)}, u32[]{:S(2)}, u32[]{:S(2)}) collective-permute-start(bf16[128,256]{1,0:T(8,128)(2,1)S(1)} %get-tuple-element.42), channel_id=1, source_target_pairs={{0,8},{1,9},{2,10},{3,11},{4,12},{5,13},{6,14},{7,15},{8,0},{9,1},... | collective-permute-start | bytes 196616 | tf_op jit(solution)/shard_map/ppermute | solution.py:305
  49.7 2.9 %collective-permute-done.14.came_ref = bf16[128,256]{1,0:T(8,128)(2,1)S(1)} collective-permute-done((bf16[128,256]{1,0:T(8,128)(2,1)S(1)}, bf16[128,256]{1,0:T(8,128)(2,1)S(1)}, u32[]{:S(2)}, u32[]{:S(2)}) %collective-permute-start.14) | collective-permute-done | bytes 65568 | tf_op jit(solution)/shard_map/ppermute | solution.py:305
  52.7 0.1 collective-permute-start.15
  52.7 4.3 %collective-permute-done.15.refs_1_ = bf16[128,256]{1,0:T(8,128)(2,1)S(1)} collective-permute-done((bf16[128,256]{1,0:T(8,128)(2,1)S(1)}, bf16[128,256]{1,0:T(8,128)(2,1)S(1)}, u32[]{:S(2)}, u32[]{:S(2)}) %collective-permute-start.15) | collective-permute-done | bytes 65568 | tf_op jit(solution)/shard_map/ppermute | solution.py:305
  57.0 2.1 %late_rows.1 = bf16[2,4,8192]{2,1,0:T(4,128)(2,1)} custom-call(s32[1,256]{1,0:T(1,128)S(1)} %get-tuple-element.28.column_slot_ref, f32[8,256]{1,0:T(8,128)S(1)} %get-tuple-element.35.draft_latent_ref, bf16[2,512,256]{2,1,0:T(8,128)(2,1)S(1)} %get-tuple-element.36.turned_ref, f32[2,256,1]{2,1,0:T(8,128)S(1)} %get-tuple-element.32.refs_8_.peak_ref, ...), custom_call_target="tpu_custom_call" | custom-call | tf_op jit(solution)/shard_map/late_rows/pallas_call | solution.py:522
  (21 shorter events, 0.2 us)
Async XLA Ops:
  0.0 34.0 %copy-start.3 = (s32[2]{0:T(128)S(1)}, s32[2]{0:T(128)}, u32[]{:S(2)}) copy-start(s32[2]{0:T(128)} %context_ref.1) | copy-start | bytes 28
  0.0 38.3 %collective-permute-start.9 = (bf16[128,8192]{1,0:T(8,128)(2,1)}, bf16[128,8192]{1,0:T(8,128)(2,1)S(1)}, u32[]{:S(2)}, u32[]{:S(2)}) collective-permute-start(bf16[128,8192]{1,0:T(8,128)(2,1)} %refs_0_.7), channel_id=1, source_target_pairs={{0,1},{1,0},{2,3},{3,2},{4,5},{5,4},{6,7},{7,6},{8,9},{9,8},{10,11... | collective-permute-start | bytes 6291464 | tf_op jit(solution)/shard_map/ppermute | solution.py:305
  1.5 12.9 %collective-permute-start = (bf16[528,256]{1,0:T(8,128)(2,1)S(1)}, bf16[528,256]{1,0:T(8,128)(2,1)S(1)}, u32[]{:S(2)}, u32[]{:S(2)}) collective-permute-start(bf16[528,256]{1,0:T(8,128)(2,1)S(1)} %get-tuple-element.27.refs_3_), channel_id=1, source_target_pairs={{0,2},{1,3},{2,0},{3,1},{4,6},{5,7},{6,4},{7,5},{8,10},{9,11},{10,... | collective-permute-start | bytes 811016 | tf_op jit(solution)/shard_map/ppermute | solution.py:305
  4.1 9.8 %collective-permute-start.2 = (bf16[272,256]{1,0:T(8,128)(2,1)S(1)}, bf16[272,256]{1,0:T(8,128)(2,1)S(1)}, u32[]{:S(2)}, u32[]{:S(2)}) collective-permute-start(bf16[272,256]{1,0:T(8,128)(2,1)S(1)} %get-tuple-element.26.refs_0_), channel_id=1, source_target_pairs={{0,8},{1,9},{2,10},{3,11},{4,12},{5,13},{6,14},{7,15},{8,0},{9,1},... | collective-permute-start | bytes 417800 | tf_op jit(solution)/shard_map/ppermute | solution.py:305
  6.7 7.8 %collective-permute-start.1 = (bf16[272,256]{1,0:T(8,128)(2,1)S(1)}, bf16[272,256]{1,0:T(8,128)(2,1)S(1)}, u32[]{:S(2)}, u32[]{:S(2)}) collective-permute-start(bf16[272,256]{1,0:T(8,128)(2,1)S(1)} %get-tuple-element.26.refs_0_), channel_id=1, source_target_pairs={{0,4},{1,5},{2,6},{3,7},{4,0},{5,1},{6,2},{7,3},{8,12},{9,13},{10,... | collective-permute-start | bytes 417800 | tf_op jit(solution)/shard_map/ppermute | solution.py:305
  13.9 5.1 %collective-permute-start.4 = (bf16[272,256]{1,0:T(8,128)(2,1)S(1)}, bf16[272,256]{1,0:T(8,128)(2,1)S(1)}, u32[]{:S(2)}, u32[]{:S(2)}) collective-permute-start(bf16[272,256]{1,0:T(8,128)(2,1)S(1)} %collective-permute-done.2.two_ref), channel_id=1, source_target_pairs={{0,4},{1,5},{2,6},{3,7},{4,0},{5,1},{6,2},{7,3},{8,12},{9,13},{10,... | collective-permute-start | bytes 417800 | tf_op jit(solution)/shard_map/ppermute | solution.py:305
  14.5 11.4 %collective-permute-start.3 = (bf16[544,256]{1,0:T(8,128)(2,1)S(1)}, bf16[544,256]{1,0:T(8,128)(2,1)S(1)}, u32[]{:S(2)}, u32[]{:S(2)}) collective-permute-start(bf16[544,256]{1,0:T(8,128)(2,1)S(1)} %join_pieces.1.refs_2_.refs_4_.refs_3_), channel_id=1, source_target_pairs={{0,2},{1,3},{2,0},{3,1},{4,6},{5,7},{6,4},{7,5},{8,10},{9,11},{10,... | collective-permute-start | bytes 835592 | tf_op jit(solution)/shard_map/ppermute | solution.py:305
  15.1 10.8 %collective-permute-start.6 = (bf16[544,256]{1,0:T(8,128)(2,1)S(1)}, bf16[544,256]{1,0:T(8,128)(2,1)S(1)}, u32[]{:S(2)}, u32[]{:S(2)}) collective-permute-start(bf16[544,256]{1,0:T(8,128)(2,1)S(1)} %join_pieces.1.refs_2_.refs_4_.refs_3_), channel_id=1, source_target_pairs={{0,16},{1,17},{2,18},{3,19},{4,20},{5,21},{6,22},{7,23},{8,24},{9,... | collective-permute-start | bytes 835592 | tf_op jit(solution)/shard_map/ppermute | solution.py:305
  19.0 6.9 %collective-permute-start.5 = (bf16[272,256]{1,0:T(8,128)(2,1)S(1)}, bf16[272,256]{1,0:T(8,128)(2,1)S(1)}, u32[]{:S(2)}, u32[]{:S(2)}) collective-permute-start(bf16[272,256]{1,0:T(8,128)(2,1)S(1)} %collective-permute-done.4.refs_6_.refs_4_), channel_id=1, source_target_pairs={{0,2},{1,3},{2,0},{3,1},{4,6},{5,7},{6,4},{7,5},{8,10},{9,11},{10,... | collective-permute-start | bytes 417800 | tf_op jit(solution)/shard_map/ppermute | solution.py:305
  25.9 0.9 %copy-start.2 = (bf16[2,4,8192]{2,1,0:T(4,128)(2,1)S(1)}, bf16[2,4,8192]{2,1,0:T(4,128)(2,1)}, u32[]{:S(2)}) copy-start(bf16[2,4,8192]{2,1,0:T(4,128)(2,1)} %draft_ref.1) | copy-start | bytes 393220
  26.8 7.1 %collective-permute-start.7 = (bf16[16,8192]{1,0:T(8,128)(2,1)S(1)}, bf16[16,8192]{1,0:T(8,128)(2,1)S(1)}, u32[]{:S(2)}, u32[]{:S(2)}) collective-permute-start(bf16[16,8192]{1,0:T(8,128)(2,1)S(1)} %pack_rows.1.mine_ref), channel_id=1, source_target_pairs={{0,1},{1,0},{2,3},{3,2},{4,5},{5,4},{6,7},{7,6},{8,9},{9,8},{10,11... | collective-permute-start | bytes 786440 | tf_op jit(solution)/shard_map/ppermute | solution.py:305
  26.9 6.5 %collective-permute-start.8 = (bf16[272,256]{1,0:T(8,128)(2,1)S(1)}, bf16[272,256]{1,0:T(8,128)(2,1)S(1)}, u32[]{:S(2)}, u32[]{:S(2)}) collective-permute-start(bf16[272,256]{1,0:T(8,128)(2,1)S(1)} %collective-permute-done.4.refs_6_.refs_4_), channel_id=1, source_target_pairs={{0,16},{1,17},{2,18},{3,19},{4,20},{5,21},{6,22},{7,23},{8,24},{9,... | collective-permute-start | bytes 417800 | tf_op jit(solution)/shard_map/ppermute | solution.py:305
  28.5 10.9 %collective-permute-start.11 = (bf16[544,256]{1,0:T(8,128)(2,1)S(1)}, bf16[544,256]{1,0:T(8,128)(2,1)S(1)}, u32[]{:S(2)}, u32[]{:S(2)}) collective-permute-start(bf16[544,256]{1,0:T(8,128)(2,1)S(1)} %collective-permute-done.3.refs_3_.refs_5_.refs_4_), channel_id=1, source_target_pairs={{0,16},{1,17},{2,18},{3,19},{4,20},{5,21},{6,22},{7,23},{8,24},{9,... | collective-permute-start | bytes 835592 | tf_op jit(solution)/shard_map/ppermute | solution.py:305
  33.5 5.9 %collective-permute-start.10 = (bf16[272,256]{1,0:T(8,128)(2,1)S(1)}, bf16[272,256]{1,0:T(8,128)(2,1)S(1)}, u32[]{:S(2)}, u32[]{:S(2)}) collective-permute-start(bf16[272,256]{1,0:T(8,128)(2,1)S(1)} %collective-permute-done.8._.refs_5_), channel_id=1, source_target_pairs={{0,2},{1,3},{2,0},{3,1},{4,6},{5,7},{6,4},{7,5},{8,10},{9,11},{10,... | collective-permute-start | bytes 417800 | tf_op jit(solution)/shard_map/ppermute | solution.py:305
  34.7 3.6 %copy-start = (bf16[128,8192]{1,0:T(8,128)(2,1)S(1)}, bf16[128,8192]{1,0:T(8,128)(2,1)}, u32[]{:S(2)}) copy-start(bf16[128,8192]{1,0:T(8,128)(2,1)} %refs_0_.7) | copy-start | bytes 6291460
  39.4 17.6 %copy-start.1 = (bf16[256,1024]{1,0:T(8,128)(2,1)S(1)}, bf16[256,1024]{1,0:T(8,128)(2,1)}, u32[]{:S(2)}) copy-start(bf16[256,1024]{1,0:T(8,128)(2,1)} %value_up_ref.1) | copy-start | bytes 1572868
  40.3 1.6 %collective-permute-start.12 = (f32[264,256]{1,0:T(8,128)S(1)}, f32[264,256]{1,0:T(8,128)S(1)}, u32[]{:S(2)}, u32[]{:S(2)}) collective-permute-start(f32[264,256]{1,0:T(8,128)S(1)} %get-tuple-element.34), channel_id=1, source_target_pairs={{0,1},{1,0},{2,3},{3,2},{4,5},{5,4},{6,7},{7,6},{8,9},{9,8},{10,11... | collective-permute-start | bytes 811016 | tf_op jit(solution)/shard_map/ppermute | solution.py:305
  42.0 4.3 %collective-permute-start.13 = (bf16[128,256]{1,0:T(8,128)(2,1)S(1)}, bf16[128,256]{1,0:T(8,128)(2,1)S(1)}, u32[]{:S(2)}, u32[]{:S(2)}) collective-permute-start(bf16[128,256]{1,0:T(8,128)(2,1)S(1)} %get-tuple-element.40), channel_id=1, source_target_pairs={{0,2},{1,3},{2,0},{3,1},{4,6},{5,7},{6,4},{7,5},{8,10},{9,11},{10,... | collective-permute-start | bytes 196616 | tf_op jit(solution)/shard_map/ppermute | solution.py:305
  46.3 6.3 %collective-permute-start.14 = (bf16[128,256]{1,0:T(8,128)(2,1)S(1)}, bf16[128,256]{1,0:T(8,128)(2,1)S(1)}, u32[]{:S(2)}, u32[]{:S(2)}) collective-permute-start(bf16[128,256]{1,0:T(8,128)(2,1)S(1)} %get-tuple-element.42), channel_id=1, source_target_pairs={{0,8},{1,9},{2,10},{3,11},{4,12},{5,13},{6,14},{7,15},{8,0},{9,1},... | collective-permute-start | bytes 196616 | tf_op jit(solution)/shard_map/ppermute | solution.py:305
  52.7 4.3 %collective-permute-start.15 = (bf16[128,256]{1,0:T(8,128)(2,1)S(1)}, bf16[128,256]{1,0:T(8,128)(2,1)S(1)}, u32[]{:S(2)}, u32[]{:S(2)}) collective-permute-start(bf16[128,256]{1,0:T(8,128)(2,1)S(1)} %get-tuple-element.44), channel_id=1, source_target_pairs={{0,4},{1,5},{2,6},{3,7},{4,0},{5,1},{6,2},{7,3},{8,12},{9,13},{10,... | collective-permute-start | bytes 196616 | tf_op jit(solution)/shard_map/ppermute | solution.py:305

commit v6 on v5

--- a/solution.py
+++ b/solution.py
@@ -154,13 +154,14 @@
                 ref[spot : spot + size, :] = source[first + n * size : first + (n + 1) * size, :]
 
 
-def start_kernel(target_hbm, shard_hbm, half_ref, full_ref, target_ref, sems):
+def start_kernel(target_hbm, shard_hbm, draft_hbm, half_ref, full_ref, target_ref, draft_ref, sems):
     half_rows, shard_rows = half_ref.shape[0] - 16, full_ref.shape[0] - 16
     mine = pl.ds(pl.multiple_of(lax.axis_index("rep") * half_rows, half_rows), half_rows)
     copies = [
         pltpu.make_async_copy(target_hbm, target_ref, sems.at[0]),
         pltpu.make_async_copy(shard_hbm.at[mine], half_ref.at[:half_rows], sems.at[1]),
         pltpu.make_async_copy(shard_hbm, full_ref.at[:shard_rows], sems.at[2]),
+        pltpu.make_async_copy(draft_hbm, draft_ref, sems.at[3]),
     ]
     for copy in copies:
         copy.start()
@@ -171,11 +172,11 @@
     block = lax.dot_general(jnp.ones((16, count), jnp.bfloat16), hit, NT, preferred_element_type=jnp.float32)
     half_ref[half_rows:, :] = block.astype(jnp.bfloat16)
     full_ref[shard_rows:, :] = block.astype(jnp.bfloat16)
-    copies[1].wait()
-    copies[2].wait()
-
-
-def join_kernel(one_ref, two_ref, _, out_ref):
+    for copy in copies[1:]:
+        copy.wait()
+
+
+def join_kernel(one_ref, two_ref, y0_ref, prompt_ref, out_ref):
     rows = one_ref.shape[0]
     out_ref[:rows, :] = one_ref[...]
     out_ref[rows:, :] = two_ref[...]
@@ -194,7 +195,7 @@
     out_ref[...] = jnp.concatenate(rows, 0).astype(jnp.bfloat16)
 
 
-def count_kernel(most_rows, context_ref, mine_ref, other_ref, _, limit_ref, column_slot_ref, place_ref, draft_ref):
+def count_kernel(most_rows, context_ref, mine_ref, other_ref, limit_ref, column_slot_ref, place_ref, draft_ref):
     f32, bf16 = jnp.float32, jnp.bfloat16
     count, width = place_ref.shape[1] // 2, 256
     wide = lax.axis_index("wide")
@@ -322,18 +323,23 @@
     hbm = pl.BlockSpec(memory_space=pltpu.HBM)
     half_rows = shard_rows // 2
     ext = half_rows + 16
-    half, full, target = call(
+    half, full, target, draft_rows = call(
         start_kernel,
-        [array(ext), array(shard_rows + 16), jax.ShapeDtypeStruct((1, count), jnp.int32)],
+        [
+            array(ext),
+            array(shard_rows + 16),
+            jax.ShapeDtypeStruct((1, count), jnp.int32),
+            jax.ShapeDtypeStruct(draft_hidden.shape, bf16),
+        ],
         "start_rows",
-        *(pltpu.with_memory_space_constraint(x, pltpu.HBM) for x in (row_target.reshape(1, count), shard)),
-        specs=[hbm, hbm],
-        scratch_shapes=[pltpu.SemaphoreType.DMA((3,))],
+        *(pltpu.with_memory_space_constraint(x, pltpu.HBM) for x in (row_target.reshape(1, count), shard, draft_hidden)),
+        specs=[hbm] * 3,
+        scratch_shapes=[pltpu.SemaphoreType.DMA((4,))],
     )
     za, zb = swap(half, z=1), swap(half, z=2)
     y0 = swap(full, y=1)
     other_prompt = swap(prompt_hidden, c=1)
-    zab = call(join_kernel, array(2 * ext), "join_pieces", za, zb, y0, specs=[WHOLE, WHOLE, UNREAD])
+    zab = call(join_kernel, array(2 * ext), "join_pieces", za, zb, y0, other_prompt, specs=[WHOLE, WHOLE, UNREAD, UNREAD])
     yab, xab = swap(zab, y=1), swap(zab, r=1)
     zc = swap(zb, z=1)
     yc, xc = swap(zc, y=1), swap(zc, r=1)
@@ -347,8 +353,8 @@
     pack = call(
         functools.partial(pack_kernel, [(n, first) for n, (_, first) in enumerate(order)]),
         jax.ShapeDtypeStruct((16, draft_hidden.shape[2]), bf16), "pack_rows",
-        target, draft_hidden, *(x for x, _ in order), xab,
-        specs=[WHOLE] * (2 + len(order)) + [UNREAD],
+        target, draft_rows, *(x for x, _ in order), xab, xc,
+        specs=[WHOLE] * (2 + len(order)) + [UNREAD] * 2,
     )
     other_pack = swap(pack, c=1)
     limit, column_slot, place, drafts = call(
@@ -359,8 +365,8 @@
             jax.ShapeDtypeStruct((1, 2 * count), jnp.int32),
             jax.ShapeDtypeStruct(pack.shape, bf16),
         ],
-        "count_rows", context_len, pack, other_pack, xc,
-        specs=[SCALARS, WHOLE, WHOLE, UNREAD],
+        "count_rows", context_len, pack, other_pack,
+        specs=[SCALARS, WHOLE, WHOLE],
     )
 
     def starts_of(uses):
@@ -512,7 +518,7 @@
             pltpu.SemaphoreType.DMA((3,)),
         ],
         compiler_params=params(16),
-        cost_estimate=pl.CostEstimate(flops=2**31, bytes_accessed=2**22, transcendentals=2**19),
+        cost_estimate=pl.CostEstimate(flops=2**20, bytes_accessed=2**16, transcendentals=0),
         name="held_rows",
     )(limit, *(pltpu.with_memory_space_constraint(x, pltpu.HBM) for x in (draft_query_heads, key_up_weight, resident_latent)))
 

time: 59.2 us -> 56 us (0.946)
  starting transfers between devices: 18.3 us -> 17.2 us
  waiting for transfers between devices: 30.2 us -> 29.1 us
  local copies, waits for them, and re-layouts: 0.92 us -> 0.01 us
    ppermute x16, waiting for transfers between devices: 30.2 us -> 29.1 us  [swap(): return lax.ppermute(x, ('rep', 'wide'), pairs)]
    ppermute x16, starting transfers between devices: 18.3 us -> 17.2 us  [swap(): return lax.ppermute(x, ('rep', 'wide'), pairs)]
    unnamed x8 -> x6, local copies, waits for them, and re-layouts: 0.92 us -> 0.01 us
  transfers between devices with their start and end apart: 16 -> 16, of which waited for: 8 -> 10; matrix products, arithmetic and copies ran while one was open for 0% -> 0% of each run, Pallas kernels for 11% -> 11%
where the time goes in v6:
time: 56 us; the launch traced here: 55.8 us
  waiting for transfers between devices  29.1 us (52%)
  starting transfers between devices  17.2 us (31%)
  Pallas kernels  9.41 us (17%)
    ppermute x16, waiting for transfers between devices, swap(): return lax.ppermute(x, ('rep', 'wide'), pairs)  29.1 us
    ppermute x16, starting transfers between devices, swap(): return lax.ppermute(x, ('rep', 'wide'), pairs)  17.2 us
    pallas_call x11, Pallas kernels, call(): pl.pallas_call(kernel, out_shape=out_shape, in_specs=specs or [WHOLE] * l...  3.85 us
    pallas_call x1, Pallas kernels, local(): pl.pallas_call(held_kernel, out_shape=[jax.ShapeDtypeStruct((slot_count,...  3.45 us
    pallas_call x1, Pallas kernels, local(): pl.pallas_call(late_kernel, out_shape=jax.ShapeDtypeStruct((slot_count, d...  2.11 us
  transfers between devices with their start and end apart: 16, of which 10 were waited for; matrix products, arithmetic and copies ran while one was open for 0% of the time, Pallas kernels for 11%

profile of v6, /device:TPU:0, one launch (start us, length us, event | category | flops | bytes accessed | tf_op | source)
XLA Modules:
  0.0 55.8 jit_solution(11584221516659709105)
XLA Ops:
  0.0 0.5 collective-permute-start.3
  0.5 1.1 %start_rows.1 = (bf16[272,256]{1,0:T(8,128)(2,1)S(1)}, bf16[528,256]{1,0:T(8,128)(2,1)S(1)}, s32[1,128]{1,0:T(1,128)S(1)}, bf16[2,4,8192]{2,1,0:T(4,128)(2,1)S(1)}) custom-call(s32[1,128]{1,0:T(1,128)} %bitcast.1, bf16[512,256]{1,0:T(8,128)(2,1)} %shard_hbm.1, bf16[2,4,8192]{2,1,0:T(4,128)(2,1)} %draft_hbm.1), custom_call_target="tpu_custom_call" | custom-call | flops 1048576 | bytes 65536 | tf_op jit(solution)/shard_map/start_rows/pallas_call | solution.py:312
  1.6 2.6 %collective-permute-start = (bf16[528,256]{1,0:T(8,128)(2,1)S(1)}, bf16[528,256]{1,0:T(8,128)(2,1)S(1)}, u32[]{:S(2)}, u32[]{:S(2)}) collective-permute-start(bf16[528,256]{1,0:T(8,128)(2,1)S(1)} %get-tuple-element.29.refs_3_), channel_id=1, source_target_pairs={{0,2},{1,3},{2,0},{3,1},{4,6},{5,7},{6,4},{7,5},{8,10},{9,11},{10,... | collective-permute-start | bytes 811016 | tf_op jit(solution)/shard_map/ppermute | solution.py:306
  4.1 2.6 %collective-permute-start.2 = (bf16[272,256]{1,0:T(8,128)(2,1)S(1)}, bf16[272,256]{1,0:T(8,128)(2,1)S(1)}, u32[]{:S(2)}, u32[]{:S(2)}) collective-permute-start(bf16[272,256]{1,0:T(8,128)(2,1)S(1)} %get-tuple-element.28.refs_0_), channel_id=1, source_target_pairs={{0,8},{1,9},{2,10},{3,11},{4,12},{5,13},{6,14},{7,15},{8,0},{9,1},... | collective-permute-start | bytes 417800 | tf_op jit(solution)/shard_map/ppermute | solution.py:306
  6.7 1.6 %collective-permute-start.1 = (bf16[272,256]{1,0:T(8,128)(2,1)S(1)}, bf16[272,256]{1,0:T(8,128)(2,1)S(1)}, u32[]{:S(2)}, u32[]{:S(2)}) collective-permute-start(bf16[272,256]{1,0:T(8,128)(2,1)S(1)} %get-tuple-element.28.refs_0_), channel_id=1, source_target_pairs={{0,4},{1,5},{2,6},{3,7},{4,0},{5,1},{6,2},{7,3},{8,12},{9,13},{10,... | collective-permute-start | bytes 417800 | tf_op jit(solution)/shard_map/ppermute | solution.py:306
  8.3 5.6 %collective-permute-done.2.two_ref = bf16[272,256]{1,0:T(8,128)(2,1)S(1)} collective-permute-done((bf16[272,256]{1,0:T(8,128)(2,1)S(1)}, bf16[272,256]{1,0:T(8,128)(2,1)S(1)}, u32[]{:S(2)}, u32[]{:S(2)}) %collective-permute-start.2) | collective-permute-done | bytes 139296 | tf_op jit(solution)/shard_map/ppermute | solution.py:306
  13.9 0.6 %collective-permute-start.5 = (bf16[272,256]{1,0:T(8,128)(2,1)S(1)}, bf16[272,256]{1,0:T(8,128)(2,1)S(1)}, u32[]{:S(2)}, u32[]{:S(2)}) collective-permute-start(bf16[272,256]{1,0:T(8,128)(2,1)S(1)} %collective-permute-done.2.two_ref), channel_id=1, source_target_pairs={{0,4},{1,5},{2,6},{3,7},{4,0},{5,1},{6,2},{7,3},{8,12},{9,13},{10,... | collective-permute-start | bytes 417800 | tf_op jit(solution)/shard_map/ppermute | solution.py:306
  14.5 1.6 %collective-permute-start.7 = (bf16[544,256]{1,0:T(8,128)(2,1)S(1)}, bf16[544,256]{1,0:T(8,128)(2,1)S(1)}, u32[]{:S(2)}, u32[]{:S(2)}) collective-permute-start(bf16[544,256]{1,0:T(8,128)(2,1)S(1)} %join_pieces.1.refs_2_.refs_4_.refs_3_), channel_id=1, source_target_pairs={{0,16},{1,17},{2,18},{3,19},{4,20},{5,21},{6,22},{7,23},{8,24},{9,... | collective-permute-start | bytes 835592 | tf_op jit(solution)/shard_map/ppermute | solution.py:306
  16.1 0.5 collective-permute-start.4
  16.6 2.4 %collective-permute-done.5.refs_6_.refs_4_ = bf16[272,256]{1,0:T(8,128)(2,1)S(1)} collective-permute-done((bf16[272,256]{1,0:T(8,128)(2,1)S(1)}, bf16[272,256]{1,0:T(8,128)(2,1)S(1)}, u32[]{:S(2)}, u32[]{:S(2)}) %collective-permute-start.5) | collective-permute-done | bytes 139296 | tf_op jit(solution)/shard_map/ppermute | solution.py:306
  19.0 1.5 %collective-permute-start.8 = (bf16[272,256]{1,0:T(8,128)(2,1)S(1)}, bf16[272,256]{1,0:T(8,128)(2,1)S(1)}, u32[]{:S(2)}, u32[]{:S(2)}) collective-permute-start(bf16[272,256]{1,0:T(8,128)(2,1)S(1)} %collective-permute-done.5.refs_6_.refs_4_), channel_id=1, source_target_pairs={{0,16},{1,17},{2,18},{3,19},{4,20},{5,21},{6,22},{7,23},{8,24},{9,... | collective-permute-start | bytes 417800 | tf_op jit(solution)/shard_map/ppermute | solution.py:306
  20.5 0.5 collective-permute-start.6
  21.0 4.9 %collective-permute-done.8.refs_9_.refs_5_ = bf16[272,256]{1,0:T(8,128)(2,1)S(1)} collective-permute-done((bf16[272,256]{1,0:T(8,128)(2,1)S(1)}, bf16[272,256]{1,0:T(8,128)(2,1)S(1)}, u32[]{:S(2)}, u32[]{:S(2)}) %collective-permute-start.8) | collective-permute-done | bytes 139296 | tf_op jit(solution)/shard_map/ppermute | solution.py:306
  25.9 1.2 %collective-permute-done.6.refs_7_.refs_5_ = bf16[272,256]{1,0:T(8,128)(2,1)S(1)} collective-permute-done((bf16[272,256]{1,0:T(8,128)(2,1)S(1)}, bf16[272,256]{1,0:T(8,128)(2,1)S(1)}, u32[]{:S(2)}, u32[]{:S(2)}) %collective-permute-start.6) | collective-permute-done | bytes 139296 | tf_op jit(solution)/shard_map/ppermute | solution.py:306
  27.2 0.1 collective-permute-start.9
  27.3 0.6 %collective-permute-start.11 = (bf16[544,256]{1,0:T(8,128)(2,1)S(1)}, bf16[544,256]{1,0:T(8,128)(2,1)S(1)}, u32[]{:S(2)}, u32[]{:S(2)}) collective-permute-start(bf16[544,256]{1,0:T(8,128)(2,1)S(1)} %collective-permute-done.4.refs_3_.refs_5_.refs_4_), channel_id=1, source_target_pairs={{0,16},{1,17},{2,18},{3,19},{4,20},{5,21},{6,22},{7,23},{8,24},{9,... | collective-permute-start | bytes 835592 | tf_op jit(solution)/shard_map/ppermute | solution.py:306
  27.9 0.5 collective-permute-start.10
  28.4 0.4 collective-permute-done.9.other_ref
  28.8 0.7 %count_rows.1 = (s32[2,128]{1,0:T(2,128)S(1)}, s32[1,256]{1,0:T(1,128)S(1)}, s32[1,256]{1,0:T(1,128)S(1)}, bf16[16,8192]{1,0:T(8,128)(2,1)S(1)}) custom-call(s32[2]{0:T(128)S(1)} %copy-done.2, bf16[16,8192]{1,0:T(8,128)(2,1)S(1)} %pack_rows.1.mine_ref, bf16[16,8192]{1,0:T(8,128)(2,1)S(1)} %collective-permute-done.9.other_ref), custom_call_target="tpu_custom_call" | custom-call | flops 1048576 | bytes 65536 | tf_op jit(solution)/shard_map/count_rows/pallas_call | solution.py:312
  29.5 3.4 %held_rows.1 = (bf16[2,512,256]{2,1,0:T(8,128)(2,1)S(1)}, f32[2,256,1]{2,1,0:T(8,128)S(1)}, f32[2,256,1]{2,1,0:T(8,128)S(1)}, f32[2,256,256]{2,1,0:T(8,128)S(1)}) custom-call(s32[2,128]{1,0:T(2,128)S(1)} %get-tuple-element.33.limit_ref, bf16[2,4,8192]{2,1,0:T(4,128)(2,1)} %query_hbm.1, bf16[256,1024]{1,0:T(8,128)(2,1)} %key_up_hbm.1, ...), custom_call_target="tpu_custom_call" | custom-call | flops 1048576 | bytes 65536 | tf_op jit(solution)/shard_map/held_rows/pallas_call | solution.py:502
  33.0 0.3 down_rows.3.refs_5_
  33.3 0.3 down_rows.4.refs_6_
  33.7 0.3 down_rows.5.refs_4_
  34.0 2.3 %collective-permute-done.11.refs_7_ = bf16[544,256]{1,0:T(8,128)(2,1)S(1)} collective-permute-done((bf16[544,256]{1,0:T(8,128)(2,1)S(1)}, bf16[544,256]{1,0:T(8,128)(2,1)S(1)}, u32[]{:S(2)}, u32[]{:S(2)}) %collective-permute-start.11) | collective-permute-done | bytes 278560 | tf_op jit(solution)/shard_map/ppermute | solution.py:306
  36.4 0.9 %down_place_rows.1 = (f32[264,256]{1,0:T(8,128)S(1)}, f32[264,256]{1,0:T(8,128)S(1)}) custom-call(bf16[128,8192]{1,0:T(8,128)(2,1)S(1)} %copy-done, bf16[128,8192]{1,0:T(8,128)(2,1)S(1)} %collective-permute-done.3.prompt_ref.refs_1_, bf16[16,8192]{1,0:T(8,128)(2,1)S(1)} %get-tuple-element.31.refs_2_, s32[1,256]{1,0:T(1,128)S(1)} %get-tuple-element.32.refs_3_, ...), custom_call_target="tpu_custom_call" | custom-call | flops 67108864 | bytes 65536 | tf_op jit(solution)/shard_map/down_place_rows/pallas_call | solution.py:312
  37.3 1.5 %collective-permute-done.12.came_ref = f32[264,256]{1,0:T(8,128)S(1)} collective-permute-done((f32[264,256]{1,0:T(8,128)S(1)}, f32[264,256]{1,0:T(8,128)S(1)}, u32[]{:S(2)}, u32[]{:S(2)}) %collective-permute-start.12) | collective-permute-done | bytes 270368 | tf_op jit(solution)/shard_map/ppermute | solution.py:306
  38.9 0.6 %collective-permute-start.13 = (bf16[128,256]{1,0:T(8,128)(2,1)S(1)}, bf16[128,256]{1,0:T(8,128)(2,1)S(1)}, u32[]{:S(2)}, u32[]{:S(2)}) collective-permute-start(bf16[128,256]{1,0:T(8,128)(2,1)S(1)} %get-tuple-element.42), channel_id=1, source_target_pairs={{0,2},{1,3},{2,0},{3,1},{4,6},{5,7},{6,4},{7,5},{8,10},{9,11},{10,... | collective-permute-start | bytes 196616 | tf_op jit(solution)/shard_map/ppermute | solution.py:306
  39.5 3.8 %collective-permute-done.13.came_ref = bf16[128,256]{1,0:T(8,128)(2,1)S(1)} collective-permute-done((bf16[128,256]{1,0:T(8,128)(2,1)S(1)}, bf16[128,256]{1,0:T(8,128)(2,1)S(1)}, u32[]{:S(2)}, u32[]{:S(2)}) %collective-permute-start.13) | collective-permute-done | bytes 65568 | tf_op jit(solution)/shard_map/ppermute | solution.py:306
  43.3 3.4 %collective-permute-start.14 = (bf16[128,256]{1,0:T(8,128)(2,1)S(1)}, bf16[128,256]{1,0:T(8,128)(2,1)S(1)}, u32[]{:S(2)}, u32[]{:S(2)}) collective-permute-start(bf16[128,256]{1,0:T(8,128)(2,1)S(1)} %get-tuple-element.44), channel_id=1, source_target_pairs={{0,8},{1,9},{2,10},{3,11},{4,12},{5,13},{6,14},{7,15},{8,0},{9,1},... | collective-permute-start | bytes 196616 | tf_op jit(solution)/shard_map/ppermute | solution.py:306
  46.7 2.7 %collective-permute-done.14.came_ref = bf16[128,256]{1,0:T(8,128)(2,1)S(1)} collective-permute-done((bf16[128,256]{1,0:T(8,128)(2,1)S(1)}, bf16[128,256]{1,0:T(8,128)(2,1)S(1)}, u32[]{:S(2)}, u32[]{:S(2)}) %collective-permute-start.14) | collective-permute-done | bytes 65568 | tf_op jit(solution)/shard_map/ppermute | solution.py:306
  49.5 4.3 %collective-permute-done.15.refs_1_ = bf16[128,256]{1,0:T(8,128)(2,1)S(1)} collective-permute-done((bf16[128,256]{1,0:T(8,128)(2,1)S(1)}, bf16[128,256]{1,0:T(8,128)(2,1)S(1)}, u32[]{:S(2)}, u32[]{:S(2)}) %collective-permute-start.15) | collective-permute-done | bytes 65568 | tf_op jit(solution)/shard_map/ppermute | solution.py:306
  53.7 2.1 %late_rows.1 = bf16[2,4,8192]{2,1,0:T(4,128)(2,1)} custom-call(s32[1,256]{1,0:T(1,128)S(1)} %get-tuple-element.30.column_slot_ref, f32[8,256]{1,0:T(8,128)S(1)} %get-tuple-element.37.draft_latent_ref, bf16[2,512,256]{2,1,0:T(8,128)(2,1)S(1)} %get-tuple-element.38.turned_ref, f32[2,256,1]{2,1,0:T(8,128)S(1)} %get-tuple-element.34.refs_8_.peak_ref, ...), custom_call_target="tpu_custom_call" | custom-call | tf_op jit(solution)/shard_map/late_rows/pallas_call | solution.py:528
  (19 shorter events, 0.3 us)
Async XLA Ops:
  0.0 14.5 %collective-permute-start.3 = (bf16[128,8192]{1,0:T(8,128)(2,1)}, bf16[128,8192]{1,0:T(8,128)(2,1)S(1)}, u32[]{:S(2)}, u32[]{:S(2)}) collective-permute-start(bf16[128,8192]{1,0:T(8,128)(2,1)} %refs_0_.7), channel_id=1, source_target_pairs={{0,1},{1,0},{2,3},{3,2},{4,5},{5,4},{6,7},{7,6},{8,9},{9,8},{10,11... | collective-permute-start | bytes 6291464 | tf_op jit(solution)/shard_map/ppermute | solution.py:306
  1.6 13.0 %collective-permute-start = (bf16[528,256]{1,0:T(8,128)(2,1)S(1)}, bf16[528,256]{1,0:T(8,128)(2,1)S(1)}, u32[]{:S(2)}, u32[]{:S(2)}) collective-permute-start(bf16[528,256]{1,0:T(8,128)(2,1)S(1)} %get-tuple-element.29.refs_3_), channel_id=1, source_target_pairs={{0,2},{1,3},{2,0},{3,1},{4,6},{5,7},{6,4},{7,5},{8,10},{9,11},{10,... | collective-permute-start | bytes 811016 | tf_op jit(solution)/shard_map/ppermute | solution.py:306
  4.1 24.7 %copy-start.2 = (s32[2]{0:T(128)S(1)}, s32[2]{0:T(128)}, u32[]{:S(2)}) copy-start(s32[2]{0:T(128)} %context_ref.1) | copy-start | bytes 28
  4.1 9.8 %collective-permute-start.2 = (bf16[272,256]{1,0:T(8,128)(2,1)S(1)}, bf16[272,256]{1,0:T(8,128)(2,1)S(1)}, u32[]{:S(2)}, u32[]{:S(2)}) collective-permute-start(bf16[272,256]{1,0:T(8,128)(2,1)S(1)} %get-tuple-element.28.refs_0_), channel_id=1, source_target_pairs={{0,8},{1,9},{2,10},{3,11},{4,12},{5,13},{6,14},{7,15},{8,0},{9,1},... | collective-permute-start | bytes 417800 | tf_op jit(solution)/shard_map/ppermute | solution.py:306
  6.7 7.8 %collective-permute-start.1 = (bf16[272,256]{1,0:T(8,128)(2,1)S(1)}, bf16[272,256]{1,0:T(8,128)(2,1)S(1)}, u32[]{:S(2)}, u32[]{:S(2)}) collective-permute-start(bf16[272,256]{1,0:T(8,128)(2,1)S(1)} %get-tuple-element.28.refs_0_), channel_id=1, source_target_pairs={{0,4},{1,5},{2,6},{3,7},{4,0},{5,1},{6,2},{7,3},{8,12},{9,13},{10,... | collective-permute-start | bytes 417800 | tf_op jit(solution)/shard_map/ppermute | solution.py:306
  13.9 5.1 %collective-permute-start.5 = (bf16[272,256]{1,0:T(8,128)(2,1)S(1)}, bf16[272,256]{1,0:T(8,128)(2,1)S(1)}, u32[]{:S(2)}, u32[]{:S(2)}) collective-permute-start(bf16[272,256]{1,0:T(8,128)(2,1)S(1)} %collective-permute-done.2.two_ref), channel_id=1, source_target_pairs={{0,4},{1,5},{2,6},{3,7},{4,0},{5,1},{6,2},{7,3},{8,12},{9,13},{10,... | collective-permute-start | bytes 417800 | tf_op jit(solution)/shard_map/ppermute | solution.py:306
  14.5 12.6 %collective-permute-start.7 = (bf16[544,256]{1,0:T(8,128)(2,1)S(1)}, bf16[544,256]{1,0:T(8,128)(2,1)S(1)}, u32[]{:S(2)}, u32[]{:S(2)}) collective-permute-start(bf16[544,256]{1,0:T(8,128)(2,1)S(1)} %join_pieces.1.refs_2_.refs_4_.refs_3_), channel_id=1, source_target_pairs={{0,16},{1,17},{2,18},{3,19},{4,20},{5,21},{6,22},{7,23},{8,24},{9,... | collective-permute-start | bytes 835592 | tf_op jit(solution)/shard_map/ppermute | solution.py:306
  16.1 11.0 %collective-permute-start.4 = (bf16[544,256]{1,0:T(8,128)(2,1)S(1)}, bf16[544,256]{1,0:T(8,128)(2,1)S(1)}, u32[]{:S(2)}, u32[]{:S(2)}) collective-permute-start(bf16[544,256]{1,0:T(8,128)(2,1)S(1)} %join_pieces.1.refs_2_.refs_4_.refs_3_), channel_id=1, source_target_pairs={{0,2},{1,3},{2,0},{3,1},{4,6},{5,7},{6,4},{7,5},{8,10},{9,11},{10,... | collective-permute-start | bytes 835592 | tf_op jit(solution)/shard_map/ppermute | solution.py:306
  19.0 6.9 %collective-permute-start.8 = (bf16[272,256]{1,0:T(8,128)(2,1)S(1)}, bf16[272,256]{1,0:T(8,128)(2,1)S(1)}, u32[]{:S(2)}, u32[]{:S(2)}) collective-permute-start(bf16[272,256]{1,0:T(8,128)(2,1)S(1)} %collective-permute-done.5.refs_6_.refs_4_), channel_id=1, source_target_pairs={{0,16},{1,17},{2,18},{3,19},{4,20},{5,21},{6,22},{7,23},{8,24},{9,... | collective-permute-start | bytes 417800 | tf_op jit(solution)/shard_map/ppermute | solution.py:306
  20.5 6.6 %collective-permute-start.6 = (bf16[272,256]{1,0:T(8,128)(2,1)S(1)}, bf16[272,256]{1,0:T(8,128)(2,1)S(1)}, u32[]{:S(2)}, u32[]{:S(2)}) collective-permute-start(bf16[272,256]{1,0:T(8,128)(2,1)S(1)} %collective-permute-done.5.refs_6_.refs_4_), channel_id=1, source_target_pairs={{0,2},{1,3},{2,0},{3,1},{4,6},{5,7},{6,4},{7,5},{8,10},{9,11},{10,... | collective-permute-start | bytes 417800 | tf_op jit(solution)/shard_map/ppermute | solution.py:306
  27.1 5.8 %copy-start = (bf16[128,8192]{1,0:T(8,128)(2,1)S(1)}, bf16[128,8192]{1,0:T(8,128)(2,1)}, u32[]{:S(2)}) copy-start(bf16[128,8192]{1,0:T(8,128)(2,1)} %refs_0_.7) | copy-start | bytes 6291460
  27.2 1.6 %collective-permute-start.9 = (bf16[16,8192]{1,0:T(8,128)(2,1)S(1)}, bf16[16,8192]{1,0:T(8,128)(2,1)S(1)}, u32[]{:S(2)}, u32[]{:S(2)}) collective-permute-start(bf16[16,8192]{1,0:T(8,128)(2,1)S(1)} %pack_rows.1.mine_ref), channel_id=1, source_target_pairs={{0,1},{1,0},{2,3},{3,2},{4,5},{5,4},{6,7},{7,6},{8,9},{9,8},{10,11... | collective-permute-start | bytes 786440 | tf_op jit(solution)/shard_map/ppermute | solution.py:306
  27.3 9.1 %collective-permute-start.11 = (bf16[544,256]{1,0:T(8,128)(2,1)S(1)}, bf16[544,256]{1,0:T(8,128)(2,1)S(1)}, u32[]{:S(2)}, u32[]{:S(2)}) collective-permute-start(bf16[544,256]{1,0:T(8,128)(2,1)S(1)} %collective-permute-done.4.refs_3_.refs_5_.refs_4_), channel_id=1, source_target_pairs={{0,16},{1,17},{2,18},{3,19},{4,20},{5,21},{6,22},{7,23},{8,24},{9,... | collective-permute-start | bytes 835592 | tf_op jit(solution)/shard_map/ppermute | solution.py:306
  27.9 6.1 %collective-permute-start.10 = (bf16[272,256]{1,0:T(8,128)(2,1)S(1)}, bf16[272,256]{1,0:T(8,128)(2,1)S(1)}, u32[]{:S(2)}, u32[]{:S(2)}) collective-permute-start(bf16[272,256]{1,0:T(8,128)(2,1)S(1)} %collective-permute-done.8.refs_9_.refs_5_), channel_id=1, source_target_pairs={{0,2},{1,3},{2,0},{3,1},{4,6},{5,7},{6,4},{7,5},{8,10},{9,11},{10,... | collective-permute-start | bytes 417800 | tf_op jit(solution)/shard_map/ppermute | solution.py:306
  36.4 17.4 %copy-start.1 = (bf16[256,1024]{1,0:T(8,128)(2,1)S(1)}, bf16[256,1024]{1,0:T(8,128)(2,1)}, u32[]{:S(2)}) copy-start(bf16[256,1024]{1,0:T(8,128)(2,1)} %value_up_ref.1) | copy-start | bytes 1572868
  37.3 1.6 %collective-permute-start.12 = (f32[264,256]{1,0:T(8,128)S(1)}, f32[264,256]{1,0:T(8,128)S(1)}, u32[]{:S(2)}, u32[]{:S(2)}) collective-permute-start(f32[264,256]{1,0:T(8,128)S(1)} %get-tuple-element.36), channel_id=1, source_target_pairs={{0,1},{1,0},{2,3},{3,2},{4,5},{5,4},{6,7},{7,6},{8,9},{9,8},{10,11... | collective-permute-start | bytes 811016 | tf_op jit(solution)/shard_map/ppermute | solution.py:306
  38.9 4.3 %collective-permute-start.13 = (bf16[128,256]{1,0:T(8,128)(2,1)S(1)}, bf16[128,256]{1,0:T(8,128)(2,1)S(1)}, u32[]{:S(2)}, u32[]{:S(2)}) collective-permute-start(bf16[128,256]{1,0:T(8,128)(2,1)S(1)} %get-tuple-element.42), channel_id=1, source_target_pairs={{0,2},{1,3},{2,0},{3,1},{4,6},{5,7},{6,4},{7,5},{8,10},{9,11},{10,... | collective-permute-start | bytes 196616 | tf_op jit(solution)/shard_map/ppermute | solution.py:306
  43.3 6.1 %collective-permute-start.14 = (bf16[128,256]{1,0:T(8,128)(2,1)S(1)}, bf16[128,256]{1,0:T(8,128)(2,1)S(1)}, u32[]{:S(2)}, u32[]{:S(2)}) collective-permute-start(bf16[128,256]{1,0:T(8,128)(2,1)S(1)} %get-tuple-element.44), channel_id=1, source_target_pairs={{0,8},{1,9},{2,10},{3,11},{4,12},{5,13},{6,14},{7,15},{8,0},{9,1},... | collective-permute-start | bytes 196616 | tf_op jit(solution)/shard_map/ppermute | solution.py:306
  49.4 4.3 %collective-permute-start.15 = (bf16[128,256]{1,0:T(8,128)(2,1)S(1)}, bf16[128,256]{1,0:T(8,128)(2,1)S(1)}, u32[]{:S(2)}, u32[]{:S(2)}) collective-permute-start(bf16[128,256]{1,0:T(8,128)(2,1)S(1)} %get-tuple-element.46), channel_id=1, source_target_pairs={{0,4},{1,5},{2,6},{3,7},{4,0},{5,1},{6,2},{7,3},{8,12},{9,13},{10,... | collective-permute-start | bytes 196616 | tf_op jit(solution)/shard_map/ppermute | solution.py:306

commit v7 on v6

--- a/solution.py
+++ b/solution.py
@@ -33,7 +33,7 @@
 
 
 def held_kernel(
-    limit_ref, query_hbm, key_up_hbm, cache_hbm, turned_ref, peak_ref, total_ref, mixed_ref,
+    arrived, context_ref, query_hbm, key_up_hbm, cache_hbm, turned_ref, peak_ref, total_ref, mixed_ref, window_ref,
     query_ref, key_up_ref, cache_ref, float_ref, scores_ref, sems,
 ):
     copies = [
@@ -66,6 +66,8 @@
             float_ref[b, k * rows : (k + 1) * rows, :] = turned[b * rows : (b + 1) * rows]
     copies[2].wait()
     for b in range(slot_count):
+        first = pl.multiple_of(window_start(context_ref[b], arrived, window_ref.shape[1], span_rows), 128)
+        window_ref[b] = cache_ref[b, pl.ds(first, window_ref.shape[1]), :]
         turned_ref[b] = split_rows(float_ref[b])
         peak = None
         for c in range(0, span_rows, step):
@@ -73,7 +75,7 @@
                 lax.dot_general(turned_ref[b], cache_ref[b, c : c + step], NT, preferred_element_type=jnp.float32)
             )
             column = lax.broadcasted_iota(jnp.int32, (1, step), 1) + c
-            scores = jnp.where(column < limit_ref[b : b + 1, 0:1], scores, FAR)
+            scores = jnp.where(column < context_ref[b] - arrived, scores, FAR)
             scores_ref[:, c : c + step] = scores
             top = jnp.max(scores, 1, keepdims=True)
             peak = top if peak is None else jnp.maximum(peak, top)
@@ -90,6 +92,32 @@
         mixed_ref[b] = mixed
 
 
+def window_start(context, arrived, size, span_rows):
+    return jnp.clip((context - arrived) // 128 * 128, 0, span_rows - size)
+
+
+def window_kernel(
+    arrived, span_rows, context_ref, limit_ref, turned_ref, peak_ref, total_ref, mixed_ref, window_ref,
+    new_peak_ref, new_total_ref, new_mixed_ref,
+):
+    slot_count, size, _ = window_ref.shape
+    for b in range(slot_count):
+        first = window_start(context_ref[b], arrived, size, span_rows)
+        scores = join_rows(
+            lax.dot_general(turned_ref[b], window_ref[b], NT, preferred_element_type=jnp.float32)
+        )
+        column = lax.broadcasted_iota(jnp.int32, (1, size), 1) + first
+        seen = (column >= context_ref[b] - arrived) & (column < limit_ref[b : b + 1, 0:1])
+        scores = jnp.where(seen, scores, FAR)
+        peak = jnp.maximum(jnp.max(scores, 1, keepdims=True), peak_ref[b])
+        weights = jnp.exp2(scores - peak)
+        fade = jnp.exp2(peak_ref[b] - peak)
+        new_peak_ref[b] = peak
+        new_total_ref[b] = total_ref[b] * fade + jnp.sum(weights, 1, keepdims=True)
+        mixed = join_rows(jnp.dot(split_rows(weights), window_ref[b], preferred_element_type=jnp.float32))
+        new_mixed_ref[b] = mixed_ref[b] * fade + mixed
+
+
 def piece_sums(starts, spans, row_refs, refs):
     total = None
     for start, (n, first, depth) in zip(starts, spans):
@@ -102,19 +130,20 @@
 
 
 def down_kernel(starts_of, spans, first, *refs):
-    row_refs, refs, out_ref = refs[:3], refs[3:-1], refs[-1]
+    row_refs, refs, out_ref = refs[:2], refs[2:-1], refs[-1]
     total = piece_sums(starts_of(), spans, row_refs, refs)
     out_ref[...] = total if first else total + refs[-1][...]
 
 
 def down_place_kernel(starts_of, spans, *refs):
-    row_refs, refs, (keep_ref, send_ref) = refs[:3], refs[3:-2], refs[-2:]
+    row_refs, refs, (keep_ref, send_ref) = refs[:2], refs[2:-2], refs[-2:]
     place_ref, sum_ref, refs = refs[0], refs[1], refs[2:]
     total = piece_sums(starts_of(), spans, row_refs, refs) + sum_ref[...]
     slots, width = keep_ref.shape[0] - 8, keep_ref.shape[1]
     count = place_ref.shape[1]
+    mine, both = count // 2, row_refs[0].shape[0]
     parts = []
-    left = total[:count]
+    left = jnp.concatenate([total[:mine], total[both : both + mine]], 0)
     for _ in range(3):
         part = left.astype(jnp.bfloat16)
         parts.append(part)
@@ -122,7 +151,7 @@
     parts = jnp.concatenate(parts, 1)
     core = lax.axis_index("wide") % 2
     spot = lax.broadcasted_iota(jnp.int32, (slots, count), 0)
-    for ref, target, draft in ((keep_ref, core, count), (send_ref, 1 - core, count + 8)):
+    for ref, target, draft in ((keep_ref, core, mine), (send_ref, 1 - core, both + mine)):
         chosen = jnp.where(spot + target * slots == place_ref[...], 1.0, 0.0).astype(jnp.bfloat16)
         moved = jnp.dot(chosen, parts, preferred_element_type=jnp.float32)
         ref[:slots, :] = moved[:, :width] + moved[:, width : 2 * width] + moved[:, 2 * width :]
@@ -154,7 +183,9 @@
                 ref[spot : spot + size, :] = source[first + n * size : first + (n + 1) * size, :]
 
 
-def start_kernel(target_hbm, shard_hbm, draft_hbm, half_ref, full_ref, target_ref, draft_ref, sems):
+def start_kernel(
+    target_hbm, shard_hbm, prompt_hbm, draft_hbm, half_ref, full_ref, target_ref, rows_ref, draft_ref, sems
+):
     half_rows, shard_rows = half_ref.shape[0] - 16, full_ref.shape[0] - 16
     mine = pl.ds(pl.multiple_of(lax.axis_index("rep") * half_rows, half_rows), half_rows)
     copies = [
@@ -162,6 +193,7 @@
         pltpu.make_async_copy(shard_hbm.at[mine], half_ref.at[:half_rows], sems.at[1]),
         pltpu.make_async_copy(shard_hbm, full_ref.at[:shard_rows], sems.at[2]),
         pltpu.make_async_copy(draft_hbm, draft_ref, sems.at[3]),
+        pltpu.make_async_copy(prompt_hbm, rows_ref.at[: prompt_hbm.shape[0]], sems.at[4]),
     ]
     for copy in copies:
         copy.start()
@@ -172,38 +204,40 @@
     block = lax.dot_general(jnp.ones((16, count), jnp.bfloat16), hit, NT, preferred_element_type=jnp.float32)
     half_ref[half_rows:, :] = block.astype(jnp.bfloat16)
     full_ref[shard_rows:, :] = block.astype(jnp.bfloat16)
-    for copy in copies[1:]:
-        copy.wait()
-
-
-def join_kernel(one_ref, two_ref, y0_ref, prompt_ref, out_ref):
-    rows = one_ref.shape[0]
+    copies[3].wait()
+    rows = [draft_ref[b].astype(jnp.float32) for b in range(draft_ref.shape[0])]
+    rows.append(jnp.zeros((8, rows_ref.shape[1]), jnp.float32))
+    rows_ref[count:, :] = jnp.concatenate(rows, 0).astype(jnp.bfloat16)
+    for n in (1, 2, 4):
+        copies[n].wait()
+
+
+def join_kernel(one_ref, two_ref, *refs):
+    rows, out_ref = one_ref.shape[0], refs[-1]
     out_ref[:rows, :] = one_ref[...]
     out_ref[rows:, :] = two_ref[...]
 
 
-def pack_kernel(spans, target_ref, draft_ref, *refs):
-    refs, out_ref = refs[:-1], refs[-1]
-    slot_count, draft_count, model_width = draft_ref.shape
-    drafts = slot_count * draft_count
-    rows = [draft_ref[b].astype(jnp.float32) for b in range(slot_count)]
-    counts = [refs[n][first : first + 16, :].astype(jnp.float32)[:1] for n, first in spans]
-    counts.append(target_ref[...].astype(jnp.float32))
-    used = sum(x.shape[1] for x in counts)
-    counts.append(jnp.zeros((1, model_width - used), jnp.float32))
-    rows.append(jnp.broadcast_to(jnp.concatenate(counts, 1), (16 - drafts, model_width)))
-    out_ref[...] = jnp.concatenate(rows, 0).astype(jnp.bfloat16)
-
-
-def count_kernel(most_rows, context_ref, mine_ref, other_ref, limit_ref, column_slot_ref, place_ref, draft_ref):
+def copy_kernel(one_ref, tie_ref, out_ref):
+    out_ref[...] = one_ref[...]
+
+
+def pack_kernel(spans, target_ref, *refs):
+    out_ref, width = refs[-1], refs[0].shape[1]
+    for m, (n, first) in enumerate(spans):
+        out_ref[:, m * width : (m + 1) * width] = refs[n][first : first + 16, :]
+    target = jnp.broadcast_to(target_ref[...].astype(jnp.float32), (16, target_ref.shape[1]))
+    out_ref[:, len(spans) * width :] = target.astype(jnp.bfloat16)
+
+
+def count_kernel(most_rows, context_ref, mine_ref, other_ref, limit_ref, column_slot_ref, place_ref):
     f32, bf16 = jnp.float32, jnp.bfloat16
     count, width = place_ref.shape[1] // 2, 256
     wide = lax.axis_index("wide")
     core = wide % 2
     mine, other = mine_ref[...].astype(f32), other_ref[...].astype(f32)
-    draft_ref[...] = jnp.concatenate([mine[:8], other[:8]], 0).astype(bf16)
-    low = jnp.where(core == 0, mine[8:9], other[8:9])
-    high = jnp.where(core == 0, other[8:9], mine[8:9])
+    low = jnp.where(core == 0, mine[:1], other[:1])
+    high = jnp.where(core == 0, other[:1], mine[:1])
     counts = []
     for n in range(8):
         counts += [low[:, n * width : (n + 1) * width], high[:, n * width : (n + 1) * width]]
@@ -221,7 +255,7 @@
     earlier = lax.broadcasted_iota(jnp.int32, (count, count), 0) < lax.broadcasted_iota(jnp.int32, (count, count), 1)
     earlier = jnp.where(earlier, 1.0, 0.0).astype(bf16)
     for n, (rows, owner) in enumerate(((mine, core), (other, 1 - core))):
-        target = rows[8:9, 8 * width : 8 * width + count].astype(jnp.int32)
+        target = rows[:1, 8 * width : 8 * width + count].astype(jnp.int32)
         hit = jnp.where(lax.broadcasted_iota(jnp.int32, (64, count), 0) == target, 1.0, 0.0)
         before = jnp.dot(hit.astype(bf16), earlier, preferred_element_type=f32)
         rank = jnp.sum(hit * before, 0, keepdims=True).astype(jnp.int32)
@@ -291,7 +325,7 @@
             out_ref[b, :, k * group_size * HEAD_SIZE : (k + 1) * group_size * HEAD_SIZE] = wide.astype(jnp.bfloat16)
 
 
-def deliver(prompt_hidden, draft_hidden, shard, row_target, context_len):
+def deliver(prompt_hidden, draft_hidden, shard, row_target, context_len, held):
     shard_rows, width = shard.shape
     count = prompt_hidden.shape[0]
     spots = [(r, z, y, c) for r in range(2) for z in range(4) for y in range(2) for c in range(2)]
@@ -323,27 +357,34 @@
     hbm = pl.BlockSpec(memory_space=pltpu.HBM)
     half_rows = shard_rows // 2
     ext = half_rows + 16
-    half, full, target, draft_rows = call(
+    padded = (count + 16, prompt_hidden.shape[1])
+    half, full, target, rows = call(
         start_kernel,
         [
             array(ext),
             array(shard_rows + 16),
             jax.ShapeDtypeStruct((1, count), jnp.int32),
-            jax.ShapeDtypeStruct(draft_hidden.shape, bf16),
+            jax.ShapeDtypeStruct(padded, bf16),
         ],
         "start_rows",
-        *(pltpu.with_memory_space_constraint(x, pltpu.HBM) for x in (row_target.reshape(1, count), shard, draft_hidden)),
-        specs=[hbm] * 3,
-        scratch_shapes=[pltpu.SemaphoreType.DMA((4,))],
+        *(
+            pltpu.with_memory_space_constraint(x, pltpu.HBM)
+            for x in (row_target.reshape(1, count), shard, prompt_hidden, draft_hidden)
+        ),
+        specs=[hbm] * 4,
+        scratch_shapes=[pltpu.VMEM(draft_hidden.shape, bf16), pltpu.SemaphoreType.DMA((5,))],
     )
     za, zb = swap(half, z=1), swap(half, z=2)
     y0 = swap(full, y=1)
-    other_prompt = swap(prompt_hidden, c=1)
-    zab = call(join_kernel, array(2 * ext), "join_pieces", za, zb, y0, other_prompt, specs=[WHOLE, WHOLE, UNREAD, UNREAD])
+    rows = [rows, swap(rows, c=1)]
+    zab = call(
+        join_kernel, array(2 * ext), "join_pieces", za, zb, y0, rows[1], held, specs=[WHOLE] * 2 + [UNREAD] * 3
+    )
     yab, xab = swap(zab, y=1), swap(zab, r=1)
     zc = swap(zb, z=1)
-    yc, xc = swap(zc, y=1), swap(zc, r=1)
+    xc = swap(zc, r=1)
     xyab = swap(yab, r=1)
+    yc = swap(call(copy_kernel, array(ext), "copy_piece", zc, yab, specs=[WHOLE, UNREAD]), y=1)
     yxc = swap(xc, y=1)
 
     order = [
@@ -352,18 +393,17 @@
     ]
     pack = call(
         functools.partial(pack_kernel, [(n, first) for n, (_, first) in enumerate(order)]),
-        jax.ShapeDtypeStruct((16, draft_hidden.shape[2]), bf16), "pack_rows",
-        target, draft_rows, *(x for x, _ in order), xab, xc,
-        specs=[WHOLE] * (2 + len(order)) + [UNREAD] * 2,
+        jax.ShapeDtypeStruct((16, len(order) * width + count), bf16), "pack_rows",
+        target, *(x for x, _ in order), xab, xc,
+        specs=[WHOLE] * (1 + len(order)) + [UNREAD] * 2,
     )
     other_pack = swap(pack, c=1)
-    limit, column_slot, place, drafts = call(
+    limit, column_slot, place = call(
         functools.partial(count_kernel, most_rows),
         [
             jax.ShapeDtypeStruct((2, 128), jnp.int32),
             jax.ShapeDtypeStruct((1, 2 * count), jnp.int32),
             jax.ShapeDtypeStruct((1, 2 * count), jnp.int32),
-            jax.ShapeDtypeStruct(pack.shape, bf16),
         ],
         "count_rows", context_len, pack, other_pack,
         specs=[SCALARS, WHOLE, WHOLE],
@@ -382,7 +422,6 @@
 
         return starts
 
-    rows = [prompt_hidden, other_prompt, drafts]
     stages = [
         ([full, y0], [(0, 0, shard_rows, (None, 0, 0)), (1, 0, shard_rows, (None, 0, 1))]),
         (
@@ -402,7 +441,7 @@
         ),
     ]
     sums = []
-    total_rows = 2 * count + 16
+    total_rows = 2 * padded[0]
     for n, (pieces, uses) in enumerate(stages[:-1]):
         sums = [
             call(
@@ -416,7 +455,7 @@
         keep, send = call(
             functools.partial(down_place_kernel, starts_of(uses), [use[:3] for use in uses]),
             [array(2 * count + 8, f32)] * 2, "down_place_rows", *rows, place, *sums, *pieces, tie,
-            specs=[WHOLE] * (5 + len(pieces)) + [UNREAD], flops=2**26,
+            specs=[WHOLE] * (4 + len(pieces)) + [UNREAD], flops=2**26,
         )
         came = swap(send, c=1)
         block = array(count)
@@ -433,7 +472,7 @@
     return limit, column_slot, finish
 
 
-def deliver_plain(prompt_hidden, draft_hidden, shard, row_target, context_len):
+def deliver_plain(prompt_hidden, draft_hidden, shard, row_target, context_len, held):
     wide_size = lax.axis_size("wide")
     row_count = prompt_hidden.shape[0]
     slot_count, draft_count, _ = draft_hidden.shape
@@ -494,21 +533,24 @@
     slot_count, span_rows, latent_width = resident_latent.shape
     draft_count = draft_hidden.shape[1]
     rows = QUERY_HEADS * draft_count
-    known = lax.axis_size("wide") == 16 and lax.axis_size("rep") == 2
-    limit, column_slot, finish = (deliver if known else deliver_plain)(
-        prompt_hidden, draft_hidden, down_weight, row_target, context_len
-    )
+    wide_size, row_count = lax.axis_size("wide"), prompt_hidden.shape[0]
+    arrived = 2 * ((row_count + wide_size - 1) // wide_size) * wide_size
+    window = min(arrived + 128, span_rows)
     hbm = pl.BlockSpec(memory_space=pltpu.HBM)
-    turned, peak, total, mixed = pl.pallas_call(
-        held_kernel,
+    stats = [
+        jax.ShapeDtypeStruct((slot_count, rows, 1), f32),
+        jax.ShapeDtypeStruct((slot_count, rows, 1), f32),
+        jax.ShapeDtypeStruct((slot_count, rows, latent_width), f32),
+    ]
+    turned, peak, total, mixed, edge = pl.pallas_call(
+        functools.partial(held_kernel, arrived),
         out_shape=[
             jax.ShapeDtypeStruct((slot_count, 2 * rows, latent_width), bf16),
-            jax.ShapeDtypeStruct((slot_count, rows, 1), f32),
-            jax.ShapeDtypeStruct((slot_count, rows, 1), f32),
-            jax.ShapeDtypeStruct((slot_count, rows, latent_width), f32),
+            *stats,
+            jax.ShapeDtypeStruct((slot_count, window, latent_width), bf16),
         ],
-        in_specs=[WHOLE, hbm, hbm, hbm],
-        out_specs=[WHOLE] * 4,
+        in_specs=[SCALARS, hbm, hbm, hbm],
+        out_specs=[WHOLE] * 5,
         scratch_shapes=[
             pltpu.VMEM(draft_query_heads.shape, bf16),
             pltpu.VMEM(key_up_weight.shape, bf16),
@@ -518,12 +560,24 @@
             pltpu.SemaphoreType.DMA((3,)),
         ],
         compiler_params=params(16),
+        cost_estimate=pl.CostEstimate(flops=2**31, bytes_accessed=2**21, transcendentals=0),
+        name="held_rows",
+    )(context_len, *(pltpu.with_memory_space_constraint(x, pltpu.HBM) for x in (draft_query_heads, key_up_weight, resident_latent)))
+    known = wide_size == 16 and lax.axis_size("rep") == 2
+    limit, column_slot, finish = (deliver if known else deliver_plain)(
+        prompt_hidden, draft_hidden, down_weight, row_target, context_len, peak
+    )
+    peak, total, mixed = pl.pallas_call(
+        functools.partial(window_kernel, arrived, span_rows),
+        out_shape=stats,
+        in_specs=[SCALARS] + [WHOLE] * 6,
+        out_specs=[WHOLE] * 3,
+        compiler_params=params(16),
         cost_estimate=pl.CostEstimate(flops=2**20, bytes_accessed=2**16, transcendentals=0),
-        name="held_rows",
-    )(limit, *(pltpu.with_memory_space_constraint(x, pltpu.HBM) for x in (draft_query_heads, key_up_weight, resident_latent)))
+        name="window_rows",
+    )(context_len, limit, turned, peak, total, mixed, edge)
 
     draft_latent, incoming = finish(peak)
-    arrived = column_slot.shape[1]
     span = (arrived + slot_count * draft_count + 127) // 128 * 128
     return pl.pallas_call(
         late_kernel,

time: 56 us -> 54.9 us (0.980)
  waiting for transfers between devices: 29.1 us -> 22.4 us
  Pallas kernels: 9.41 us -> 12.9 us
  starting transfers between devices: 17.2 us -> 19.3 us
    ppermute x16, waiting for transfers between devices: 29.1 us -> 22.4 us  [swap(): return lax.ppermute(x, ('rep', 'wide'), pairs)]
    pallas_call x1 -> x2, Pallas kernels: 3.45 us -> 6.09 us  [the longest x1 4.01 us: local(): pl.pallas_call(functools.partial(held_kernel, arrived), out_shape=[jax.Sh...]
    ppermute x16, starting transfers between devices: 17.2 us -> 19.3 us  [swap(): return lax.ppermute(x, ('rep', 'wide'), pairs)]
    pallas_call x11 -> x12, Pallas kernels: 3.85 us -> 4.66 us  [call(): pl.pallas_call(kernel, out_shape=out_shape, in_specs=specs or [WHOLE] * l...]
  transfers between devices with their start and end apart: 16 -> 16, of which waited for: 10 -> 9; matrix products, arithmetic and copies ran while one was open for 0% -> 0% of each run, Pallas kernels for 11% -> 14%
where the time goes in v7:
time: 54.9 us; the launch traced here: 54.7 us
  waiting for transfers between devices  22.4 us (41%)
  starting transfers between devices  19.3 us (35%)
  Pallas kernels  12.9 us (23%)
    ppermute x16, waiting for transfers between devices, swap(): return lax.ppermute(x, ('rep', 'wide'), pairs)  22.4 us
    ppermute x16, starting transfers between devices, swap(): return lax.ppermute(x, ('rep', 'wide'), pairs)  19.3 us
    pallas_call x12, Pallas kernels, call(): pl.pallas_call(kernel, out_shape=out_shape, in_specs=specs or [WHOLE] * l...  4.66 us
    pallas_call x1, Pallas kernels, local(): pl.pallas_call(functools.partial(held_kernel, arrived), out_shape=[jax.Sh...  4.01 us
    pallas_call x1, Pallas kernels, local(): pl.pallas_call(late_kernel, out_shape=jax.ShapeDtypeStruct((slot_count, d...  2.11 us
    pallas_call x1, Pallas kernels, local(): pl.pallas_call(functools.partial(window_kernel, arrived, span_rows), out_...  2.08 us
  transfers between devices with their start and end apart: 16, of which 9 were waited for; matrix products, arithmetic and copies ran while one was open for 0% of the time, Pallas kernels for 14%

profile of v7, /device:TPU:0, one launch (start us, length us, event | category | flops | bytes accessed | tf_op | source)
XLA Modules:
  0.0 54.7 jit_solution(5234455371923748552)
XLA Ops:
  0.0 1.9 %start_rows.1 = (bf16[272,256]{1,0:T(8,128)(2,1)S(1)}, bf16[528,256]{1,0:T(8,128)(2,1)S(1)}, s32[1,128]{1,0:T(1,128)S(1)}, bf16[144,8192]{1,0:T(8,128)(2,1)S(1)}) custom-call(s32[1,128]{1,0:T(1,128)} %bitcast.1, bf16[512,256]{1,0:T(8,128)(2,1)} %shard_hbm.1, bf16[128,8192]{1,0:T(8,128)(2,1)} %prompt_hbm.1, bf16[2,4,8192]{2,1,0:T(4,128)(2,1)} %draft_hbm.1), custom_call_target="tpu_custom_call" | custom-call | flops 1048576 | bytes 65536 | tf_op jit(solution)/shard_map/start_rows/pallas_call | solution.py:346
  1.9 0.5 collective-permute-start.3
  2.4 2.6 %collective-permute-start = (bf16[528,256]{1,0:T(8,128)(2,1)S(1)}, bf16[528,256]{1,0:T(8,128)(2,1)S(1)}, u32[]{:S(2)}, u32[]{:S(2)}) collective-permute-start(bf16[528,256]{1,0:T(8,128)(2,1)S(1)} %get-tuple-element.31.refs_2_), channel_id=1, source_target_pairs={{0,2},{1,3},{2,0},{3,1},{4,6},{5,7},{6,4},{7,5},{8,10},{9,11},{10,... | collective-permute-start | bytes 811016 | tf_op jit(solution)/shard_map/ppermute | solution.py:340
  5.0 1.6 %collective-permute-start.1 = (bf16[272,256]{1,0:T(8,128)(2,1)S(1)}, bf16[272,256]{1,0:T(8,128)(2,1)S(1)}, u32[]{:S(2)}, u32[]{:S(2)}) collective-permute-start(bf16[272,256]{1,0:T(8,128)(2,1)S(1)} %get-tuple-element.30.refs_0_), channel_id=1, source_target_pairs={{0,4},{1,5},{2,6},{3,7},{4,0},{5,1},{6,2},{7,3},{8,12},{9,13},{10,... | collective-permute-start | bytes 417800 | tf_op jit(solution)/shard_map/ppermute | solution.py:340
  6.6 2.6 %collective-permute-start.2 = (bf16[272,256]{1,0:T(8,128)(2,1)S(1)}, bf16[272,256]{1,0:T(8,128)(2,1)S(1)}, u32[]{:S(2)}, u32[]{:S(2)}) collective-permute-start(bf16[272,256]{1,0:T(8,128)(2,1)S(1)} %get-tuple-element.30.refs_0_), channel_id=1, source_target_pairs={{0,8},{1,9},{2,10},{3,11},{4,12},{5,13},{6,14},{7,15},{8,0},{9,1},... | collective-permute-start | bytes 417800 | tf_op jit(solution)/shard_map/ppermute | solution.py:340
  9.2 4.0 %held_rows.1 = (bf16[2,512,256]{2,1,0:T(8,128)(2,1)S(1)}, f32[2,256,1]{2,1,0:T(8,128)S(1)}, f32[2,256,1]{2,1,0:T(8,128)S(1)}, f32[2,256,256]{2,1,0:T(8,128)S(1)}, bf16[2,384,256]{2,1,0:T(8,128)(2,1)S(1)}) custom-call(s32[2]{0:T(128)S(1)} %copy-done.1, bf16[2,4,8192]{2,1,0:T(4,128)(2,1)} %query_hbm.1, bf16[256,1024]{1,0:T(8,128)(2,1)} %key_up_hbm.1, ...), custom_call_target="tpu_custom_call" | custom-call | flops 2147483648 | bytes 2097152 | tf_op jit(solution)/shard_map/held_rows/pallas_call | solution.py:545
  13.2 0.3 collective-permute-done.1.one_ref
  13.5 2.5 %collective-permute-done.2.two_ref = bf16[272,256]{1,0:T(8,128)(2,1)S(1)} collective-permute-done((bf16[272,256]{1,0:T(8,128)(2,1)S(1)}, bf16[272,256]{1,0:T(8,128)(2,1)S(1)}, u32[]{:S(2)}, u32[]{:S(2)}) %collective-permute-start.2) | collective-permute-done | bytes 139296 | tf_op jit(solution)/shard_map/ppermute | solution.py:340
  16.0 0.6 %collective-permute-start.4 = (bf16[544,256]{1,0:T(8,128)(2,1)S(1)}, bf16[544,256]{1,0:T(8,128)(2,1)S(1)}, u32[]{:S(2)}, u32[]{:S(2)}) collective-permute-start(bf16[544,256]{1,0:T(8,128)(2,1)S(1)} %join_pieces.1.refs_2_.refs_4_), channel_id=1, source_target_pairs={{0,2},{1,3},{2,0},{3,1},{4,6},{5,7},{6,4},{7,5},{8,10},{9,11},{10,... | collective-permute-start | bytes 835592 | tf_op jit(solution)/shard_map/ppermute | solution.py:340
  16.6 0.4 collective-permute-start.5
  17.0 1.5 %collective-permute-start.7 = (bf16[544,256]{1,0:T(8,128)(2,1)S(1)}, bf16[544,256]{1,0:T(8,128)(2,1)S(1)}, u32[]{:S(2)}, u32[]{:S(2)}) collective-permute-start(bf16[544,256]{1,0:T(8,128)(2,1)S(1)} %join_pieces.1.refs_2_.refs_4_), channel_id=1, source_target_pairs={{0,16},{1,17},{2,18},{3,19},{4,20},{5,21},{6,22},{7,23},{8,24},{9,... | collective-permute-start | bytes 835592 | tf_op jit(solution)/shard_map/ppermute | solution.py:340
  18.5 3.1 %collective-permute-done.5.one_ref.refs_6_.refs_3_ = bf16[272,256]{1,0:T(8,128)(2,1)S(1)} collective-permute-done((bf16[272,256]{1,0:T(8,128)(2,1)S(1)}, bf16[272,256]{1,0:T(8,128)(2,1)S(1)}, u32[]{:S(2)}, u32[]{:S(2)}) %collective-permute-start.5) | collective-permute-done | bytes 139296 | tf_op jit(solution)/shard_map/ppermute | solution.py:340
  21.6 1.5 %collective-permute-start.8 = (bf16[272,256]{1,0:T(8,128)(2,1)S(1)}, bf16[272,256]{1,0:T(8,128)(2,1)S(1)}, u32[]{:S(2)}, u32[]{:S(2)}) collective-permute-start(bf16[272,256]{1,0:T(8,128)(2,1)S(1)} %collective-permute-done.5.one_ref.refs_6_.refs_3_), channel_id=1, source_target_pairs={{0,16},{1,17},{2,18},{3,19},{4,20},{5,21},{6,22},{7,23},{8,24},{9,... | collective-permute-start | bytes 417800 | tf_op jit(solution)/shard_map/ppermute | solution.py:340
  23.1 1.2 %collective-permute-start.11 = (bf16[544,256]{1,0:T(8,128)(2,1)S(1)}, bf16[544,256]{1,0:T(8,128)(2,1)S(1)}, u32[]{:S(2)}, u32[]{:S(2)}) collective-permute-start(bf16[544,256]{1,0:T(8,128)(2,1)S(1)} %collective-permute-done.4.tie_ref.refs_3_.refs_5_), channel_id=1, source_target_pairs={{0,16},{1,17},{2,18},{3,19},{4,20},{5,21},{6,22},{7,23},{8,24},{9,... | collective-permute-start | bytes 835592 | tf_op jit(solution)/shard_map/ppermute | solution.py:340
  24.3 0.9 %collective-permute-start.6 = (bf16[272,256]{1,0:T(8,128)(2,1)S(1)}, bf16[272,256]{1,0:T(8,128)(2,1)S(1)}, u32[]{:S(2)}, u32[]{:S(2)}) collective-permute-start(bf16[272,256]{1,0:T(8,128)(2,1)S(1)} %copy_piece.1), channel_id=1, source_target_pairs={{0,2},{1,3},{2,0},{3,1},{4,6},{5,7},{6,4},{7,5},{8,10},{9,11},{10,... | collective-permute-start | bytes 417800 | tf_op jit(solution)/shard_map/ppermute | solution.py:340
  25.3 4.3 %collective-permute-done.8.refs_9_.refs_4_ = bf16[272,256]{1,0:T(8,128)(2,1)S(1)} collective-permute-done((bf16[272,256]{1,0:T(8,128)(2,1)S(1)}, bf16[272,256]{1,0:T(8,128)(2,1)S(1)}, u32[]{:S(2)}, u32[]{:S(2)}) %collective-permute-start.8) | collective-permute-done | bytes 139296 | tf_op jit(solution)/shard_map/ppermute | solution.py:340
  29.6 1.5 %collective-permute-start.10 = (bf16[272,256]{1,0:T(8,128)(2,1)S(1)}, bf16[272,256]{1,0:T(8,128)(2,1)S(1)}, u32[]{:S(2)}, u32[]{:S(2)}) collective-permute-start(bf16[272,256]{1,0:T(8,128)(2,1)S(1)} %collective-permute-done.8.refs_9_.refs_4_), channel_id=1, source_target_pairs={{0,2},{1,3},{2,0},{3,1},{4,6},{5,7},{6,4},{7,5},{8,10},{9,11},{10,... | collective-permute-start | bytes 417800 | tf_op jit(solution)/shard_map/ppermute | solution.py:340
  31.2 0.3 down_rows.3.refs_4_
  31.6 0.4 down_rows.4.refs_5_
  31.9 0.3 down_rows.5.refs_3_
  32.5 0.7 %count_rows.1 = (s32[2,128]{1,0:T(2,128)S(1)}, s32[1,256]{1,0:T(1,128)S(1)}, s32[1,256]{1,0:T(1,128)S(1)}) custom-call(s32[2]{0:T(128)S(1)} %copy-done.1, bf16[16,2176]{1,0:T(8,128)(2,1)S(1)} %pack_rows.1.mine_ref, bf16[16,2176]{1,0:T(8,128)(2,1)S(1)} %collective-permute-done.9.other_ref), custom_call_target="tpu_custom_call" | custom-call | flops 1048576 | bytes 65536 | tf_op jit(solution)/shard_map/count_rows/pallas_call | solution.py:346
  33.2 2.1 %window_rows.1 = (f32[2,256,1]{2,1,0:T(8,128)S(1)}, f32[2,256,1]{2,1,0:T(8,128)S(1)}, f32[2,256,256]{2,1,0:T(8,128)S(1)}) custom-call(s32[2]{0:T(128)S(1)} %copy-done.1, s32[2,128]{1,0:T(2,128)S(1)} %get-tuple-element.36.limit_ref, bf16[2,512,256]{2,1,0:T(8,128)(2,1)S(1)} %get-tuple-element.37.turned_ref, ...), custom_call_target="tpu_custom_call" | custom-call | flops 1048576 | bytes 65536 | tf_op jit(solution)/shard_map/window_rows/pallas_call | solution.py:570
  35.3 0.9 %down_place_rows.1 = (f32[264,256]{1,0:T(8,128)S(1)}, f32[264,256]{1,0:T(8,128)S(1)}) custom-call(bf16[144,8192]{1,0:T(8,128)(2,1)S(1)} %get-tuple-element.32.refs_0_, bf16[144,8192]{1,0:T(8,128)(2,1)S(1)} %collective-permute-done.3.refs_1_, s32[1,256]{1,0:T(1,128)S(1)} %get-tuple-element.35.refs_2_, f32[288,256]{1,0:T(8,128)S(1)} %down_rows.5.refs_3_, ...), custom_call_target="tpu_custom_call" | custom-call | flops 67108864 | bytes 65536 | tf_op jit(solution)/shard_map/down_place_rows/pallas_call | solution.py:346
  36.2 0.4 collective-permute-start.12
  36.6 1.2 %collective-permute-done.12.came_ref = f32[264,256]{1,0:T(8,128)S(1)} collective-permute-done((f32[264,256]{1,0:T(8,128)S(1)}, f32[264,256]{1,0:T(8,128)S(1)}, u32[]{:S(2)}, u32[]{:S(2)}) %collective-permute-start.12) | collective-permute-done | bytes 270368 | tf_op jit(solution)/shard_map/ppermute | solution.py:340
  37.9 0.9 %collective-permute-start.13 = (bf16[128,256]{1,0:T(8,128)(2,1)S(1)}, bf16[128,256]{1,0:T(8,128)(2,1)S(1)}, u32[]{:S(2)}, u32[]{:S(2)}) collective-permute-start(bf16[128,256]{1,0:T(8,128)(2,1)S(1)} %get-tuple-element.48), channel_id=1, source_target_pairs={{0,2},{1,3},{2,0},{3,1},{4,6},{5,7},{6,4},{7,5},{8,10},{9,11},{10,... | collective-permute-start | bytes 196616 | tf_op jit(solution)/shard_map/ppermute | solution.py:340
  38.9 3.4 %collective-permute-done.13.came_ref = bf16[128,256]{1,0:T(8,128)(2,1)S(1)} collective-permute-done((bf16[128,256]{1,0:T(8,128)(2,1)S(1)}, bf16[128,256]{1,0:T(8,128)(2,1)S(1)}, u32[]{:S(2)}, u32[]{:S(2)}) %collective-permute-start.13) | collective-permute-done | bytes 65568 | tf_op jit(solution)/shard_map/ppermute | solution.py:340
  42.3 2.6 %collective-permute-start.14 = (bf16[128,256]{1,0:T(8,128)(2,1)S(1)}, bf16[128,256]{1,0:T(8,128)(2,1)S(1)}, u32[]{:S(2)}, u32[]{:S(2)}) collective-permute-start(bf16[128,256]{1,0:T(8,128)(2,1)S(1)} %get-tuple-element.50), channel_id=1, source_target_pairs={{0,8},{1,9},{2,10},{3,11},{4,12},{5,13},{6,14},{7,15},{8,0},{9,1},... | collective-permute-start | bytes 196616 | tf_op jit(solution)/shard_map/ppermute | solution.py:340
  45.0 3.3 %collective-permute-done.14.came_ref = bf16[128,256]{1,0:T(8,128)(2,1)S(1)} collective-permute-done((bf16[128,256]{1,0:T(8,128)(2,1)S(1)}, bf16[128,256]{1,0:T(8,128)(2,1)S(1)}, u32[]{:S(2)}, u32[]{:S(2)}) %collective-permute-start.14) | collective-permute-done | bytes 65568 | tf_op jit(solution)/shard_map/ppermute | solution.py:340
  48.2 0.4 collective-permute-start.15
  48.6 4.0 %collective-permute-done.15.refs_1_ = bf16[128,256]{1,0:T(8,128)(2,1)S(1)} collective-permute-done((bf16[128,256]{1,0:T(8,128)(2,1)S(1)}, bf16[128,256]{1,0:T(8,128)(2,1)S(1)}, u32[]{:S(2)}, u32[]{:S(2)}) %collective-permute-start.15) | collective-permute-done | bytes 65568 | tf_op jit(solution)/shard_map/ppermute | solution.py:340
  52.6 2.1 %late_rows.1 = bf16[2,4,8192]{2,1,0:T(4,128)(2,1)} custom-call(s32[1,256]{1,0:T(1,128)S(1)} %get-tuple-element.34.column_slot_ref, f32[8,256]{1,0:T(8,128)S(1)} %get-tuple-element.44.draft_latent_ref, bf16[2,512,256]{2,1,0:T(8,128)(2,1)S(1)} %get-tuple-element.37.turned_ref, f32[2,256,1]{2,1,0:T(8,128)S(1)} %get-tuple-element.41.refs_7_.peak_ref, ...), custom_call_target="tpu_custom_call" | custom-call | tf_op jit(solution)/shard_map/late_rows/pallas_call | solution.py:582
  (19 shorter events, 0.4 us)
Async XLA Ops:
  0.0 9.2 %copy-start.1 = (s32[2]{0:T(128)S(1)}, s32[2]{0:T(128)}, u32[]{:S(2)}) copy-start(s32[2]{0:T(128)} %context_ref.5) | copy-start | bytes 28
  1.9 14.1 %collective-permute-start.3 = (bf16[144,8192]{1,0:T(8,128)(2,1)S(1)}, bf16[144,8192]{1,0:T(8,128)(2,1)S(1)}, u32[]{:S(2)}, u32[]{:S(2)}) collective-permute-start(bf16[144,8192]{1,0:T(8,128)(2,1)S(1)} %get-tuple-element.32.refs_0_), channel_id=1, source_target_pairs={{0,1},{1,0},{2,3},{3,2},{4,5},{5,4},{6,7},{7,6},{8,9},{9,8},{10,11... | collective-permute-start | bytes 7077896 | tf_op jit(solution)/shard_map/ppermute | solution.py:340
  2.4 13.6 %collective-permute-start = (bf16[528,256]{1,0:T(8,128)(2,1)S(1)}, bf16[528,256]{1,0:T(8,128)(2,1)S(1)}, u32[]{:S(2)}, u32[]{:S(2)}) collective-permute-start(bf16[528,256]{1,0:T(8,128)(2,1)S(1)} %get-tuple-element.31.refs_2_), channel_id=1, source_target_pairs={{0,2},{1,3},{2,0},{3,1},{4,6},{5,7},{6,4},{7,5},{8,10},{9,11},{10,... | collective-permute-start | bytes 811016 | tf_op jit(solution)/shard_map/ppermute | solution.py:340
  5.0 8.5 %collective-permute-start.1 = (bf16[272,256]{1,0:T(8,128)(2,1)S(1)}, bf16[272,256]{1,0:T(8,128)(2,1)S(1)}, u32[]{:S(2)}, u32[]{:S(2)}) collective-permute-start(bf16[272,256]{1,0:T(8,128)(2,1)S(1)} %get-tuple-element.30.refs_0_), channel_id=1, source_target_pairs={{0,4},{1,5},{2,6},{3,7},{4,0},{5,1},{6,2},{7,3},{8,12},{9,13},{10,... | collective-permute-start | bytes 417800 | tf_op jit(solution)/shard_map/ppermute | solution.py:340
  6.6 9.4 %collective-permute-start.2 = (bf16[272,256]{1,0:T(8,128)(2,1)S(1)}, bf16[272,256]{1,0:T(8,128)(2,1)S(1)}, u32[]{:S(2)}, u32[]{:S(2)}) collective-permute-start(bf16[272,256]{1,0:T(8,128)(2,1)S(1)} %get-tuple-element.30.refs_0_), channel_id=1, source_target_pairs={{0,8},{1,9},{2,10},{3,11},{4,12},{5,13},{6,14},{7,15},{8,0},{9,1},... | collective-permute-start | bytes 417800 | tf_op jit(solution)/shard_map/ppermute | solution.py:340
  16.0 7.1 %collective-permute-start.4 = (bf16[544,256]{1,0:T(8,128)(2,1)S(1)}, bf16[544,256]{1,0:T(8,128)(2,1)S(1)}, u32[]{:S(2)}, u32[]{:S(2)}) collective-permute-start(bf16[544,256]{1,0:T(8,128)(2,1)S(1)} %join_pieces.1.refs_2_.refs_4_), channel_id=1, source_target_pairs={{0,2},{1,3},{2,0},{3,1},{4,6},{5,7},{6,4},{7,5},{8,10},{9,11},{10,... | collective-permute-start | bytes 835592 | tf_op jit(solution)/shard_map/ppermute | solution.py:340
  16.6 5.1 %collective-permute-start.5 = (bf16[272,256]{1,0:T(8,128)(2,1)S(1)}, bf16[272,256]{1,0:T(8,128)(2,1)S(1)}, u32[]{:S(2)}, u32[]{:S(2)}) collective-permute-start(bf16[272,256]{1,0:T(8,128)(2,1)S(1)} %collective-permute-done.2.two_ref), channel_id=1, source_target_pairs={{0,4},{1,5},{2,6},{3,7},{4,0},{5,1},{6,2},{7,3},{8,12},{9,13},{10,... | collective-permute-start | bytes 417800 | tf_op jit(solution)/shard_map/ppermute | solution.py:340
  17.0 14.1 %collective-permute-start.7 = (bf16[544,256]{1,0:T(8,128)(2,1)S(1)}, bf16[544,256]{1,0:T(8,128)(2,1)S(1)}, u32[]{:S(2)}, u32[]{:S(2)}) collective-permute-start(bf16[544,256]{1,0:T(8,128)(2,1)S(1)} %join_pieces.1.refs_2_.refs_4_), channel_id=1, source_target_pairs={{0,16},{1,17},{2,18},{3,19},{4,20},{5,21},{6,22},{7,23},{8,24},{9,... | collective-permute-start | bytes 835592 | tf_op jit(solution)/shard_map/ppermute | solution.py:340
  21.6 8.0 %collective-permute-start.8 = (bf16[272,256]{1,0:T(8,128)(2,1)S(1)}, bf16[272,256]{1,0:T(8,128)(2,1)S(1)}, u32[]{:S(2)}, u32[]{:S(2)}) collective-permute-start(bf16[272,256]{1,0:T(8,128)(2,1)S(1)} %collective-permute-done.5.one_ref.refs_6_.refs_3_), channel_id=1, source_target_pairs={{0,16},{1,17},{2,18},{3,19},{4,20},{5,21},{6,22},{7,23},{8,24},{9,... | collective-permute-start | bytes 417800 | tf_op jit(solution)/shard_map/ppermute | solution.py:340
  23.1 12.2 %collective-permute-start.11 = (bf16[544,256]{1,0:T(8,128)(2,1)S(1)}, bf16[544,256]{1,0:T(8,128)(2,1)S(1)}, u32[]{:S(2)}, u32[]{:S(2)}) collective-permute-start(bf16[544,256]{1,0:T(8,128)(2,1)S(1)} %collective-permute-done.4.tie_ref.refs_3_.refs_5_), channel_id=1, source_target_pairs={{0,16},{1,17},{2,18},{3,19},{4,20},{5,21},{6,22},{7,23},{8,24},{9,... | collective-permute-start | bytes 835592 | tf_op jit(solution)/shard_map/ppermute | solution.py:340
  24.3 6.8 %collective-permute-start.6 = (bf16[272,256]{1,0:T(8,128)(2,1)S(1)}, bf16[272,256]{1,0:T(8,128)(2,1)S(1)}, u32[]{:S(2)}, u32[]{:S(2)}) collective-permute-start(bf16[272,256]{1,0:T(8,128)(2,1)S(1)} %copy_piece.1), channel_id=1, source_target_pairs={{0,2},{1,3},{2,0},{3,1},{4,6},{5,7},{6,4},{7,5},{8,10},{9,11},{10,... | collective-permute-start | bytes 417800 | tf_op jit(solution)/shard_map/ppermute | solution.py:340
  29.6 5.7 %collective-permute-start.10 = (bf16[272,256]{1,0:T(8,128)(2,1)S(1)}, bf16[272,256]{1,0:T(8,128)(2,1)S(1)}, u32[]{:S(2)}, u32[]{:S(2)}) collective-permute-start(bf16[272,256]{1,0:T(8,128)(2,1)S(1)} %collective-permute-done.8.refs_9_.refs_4_), channel_id=1, source_target_pairs={{0,2},{1,3},{2,0},{3,1},{4,6},{5,7},{6,4},{7,5},{8,10},{9,11},{10,... | collective-permute-start | bytes 417800 | tf_op jit(solution)/shard_map/ppermute | solution.py:340
  31.1 1.3 %collective-permute-start.9 = (bf16[16,2176]{1,0:T(8,128)(2,1)S(1)}, bf16[16,2176]{1,0:T(8,128)(2,1)S(1)}, u32[]{:S(2)}, u32[]{:S(2)}) collective-permute-start(bf16[16,2176]{1,0:T(8,128)(2,1)S(1)} %pack_rows.1.mine_ref), channel_id=1, source_target_pairs={{0,1},{1,0},{2,3},{3,2},{4,5},{5,4},{6,7},{7,6},{8,9},{9,8},{10,11... | collective-permute-start | bytes 208904 | tf_op jit(solution)/shard_map/ppermute | solution.py:340
  35.3 17.3 %copy-start = (bf16[256,1024]{1,0:T(8,128)(2,1)S(1)}, bf16[256,1024]{1,0:T(8,128)(2,1)}, u32[]{:S(2)}) copy-start(bf16[256,1024]{1,0:T(8,128)(2,1)} %value_up_ref.1) | copy-start | bytes 1572868
  36.2 1.6 %collective-permute-start.12 = (f32[264,256]{1,0:T(8,128)S(1)}, f32[264,256]{1,0:T(8,128)S(1)}, u32[]{:S(2)}, u32[]{:S(2)}) collective-permute-start(f32[264,256]{1,0:T(8,128)S(1)} %get-tuple-element.43), channel_id=1, source_target_pairs={{0,1},{1,0},{2,3},{3,2},{4,5},{5,4},{6,7},{7,6},{8,9},{9,8},{10,11... | collective-permute-start | bytes 811016 | tf_op jit(solution)/shard_map/ppermute | solution.py:340
  37.9 4.4 %collective-permute-start.13 = (bf16[128,256]{1,0:T(8,128)(2,1)S(1)}, bf16[128,256]{1,0:T(8,128)(2,1)S(1)}, u32[]{:S(2)}, u32[]{:S(2)}) collective-permute-start(bf16[128,256]{1,0:T(8,128)(2,1)S(1)} %get-tuple-element.48), channel_id=1, source_target_pairs={{0,2},{1,3},{2,0},{3,1},{4,6},{5,7},{6,4},{7,5},{8,10},{9,11},{10,... | collective-permute-start | bytes 196616 | tf_op jit(solution)/shard_map/ppermute | solution.py:340
  42.3 5.9 %collective-permute-start.14 = (bf16[128,256]{1,0:T(8,128)(2,1)S(1)}, bf16[128,256]{1,0:T(8,128)(2,1)S(1)}, u32[]{:S(2)}, u32[]{:S(2)}) collective-permute-start(bf16[128,256]{1,0:T(8,128)(2,1)S(1)} %get-tuple-element.50), channel_id=1, source_target_pairs={{0,8},{1,9},{2,10},{3,11},{4,12},{5,13},{6,14},{7,15},{8,0},{9,1},... | collective-permute-start | bytes 196616 | tf_op jit(solution)/shard_map/ppermute | solution.py:340
  48.2 4.3 %collective-permute-start.15 = (bf16[128,256]{1,0:T(8,128)(2,1)S(1)}, bf16[128,256]{1,0:T(8,128)(2,1)S(1)}, u32[]{:S(2)}, u32[]{:S(2)}) collective-permute-start(bf16[128,256]{1,0:T(8,128)(2,1)S(1)} %get-tuple-element.52), channel_id=1, source_target_pairs={{0,4},{1,5},{2,6},{3,7},{4,0},{5,1},{6,2},{7,3},{8,12},{9,13},{10,... | collective-permute-start | bytes 196616 | tf_op jit(solution)/shard_map/ppermute | solution.py:340

commit v8 on v7

--- a/solution.py
+++ b/solution.py
@@ -97,25 +97,34 @@
 
 
 def window_kernel(
-    arrived, span_rows, context_ref, limit_ref, turned_ref, peak_ref, total_ref, mixed_ref, window_ref,
-    new_peak_ref, new_total_ref, new_mixed_ref,
+    arrived, span_rows, draft_count, context_ref, limit_ref, turned_ref, peak_ref, total_ref, mixed_ref, window_ref,
+    draft_latent_ref, new_peak_ref, new_total_ref, new_mixed_ref,
 ):
-    slot_count, size, _ = window_ref.shape
+    slot_count, size, width = window_ref.shape
+    rows = peak_ref.shape[1]
+    drafts = draft_latent_ref[...]
+    drafts = jnp.concatenate([drafts, jnp.zeros((128 - drafts.shape[0], width), jnp.float32)], 0).astype(jnp.bfloat16)
+    token = lax.broadcasted_iota(jnp.int32, (rows, 1), 0) % draft_count
+    spot = lax.broadcasted_iota(jnp.int32, (rows, 128), 1)
     for b in range(slot_count):
         first = window_start(context_ref[b], arrived, size, span_rows)
-        scores = join_rows(
-            lax.dot_general(turned_ref[b], window_ref[b], NT, preferred_element_type=jnp.float32)
-        )
+        scores = join_rows(lax.dot_general(turned_ref[b], window_ref[b], NT, preferred_element_type=jnp.float32))
         column = lax.broadcasted_iota(jnp.int32, (1, size), 1) + first
         seen = (column >= context_ref[b] - arrived) & (column < limit_ref[b : b + 1, 0:1])
         scores = jnp.where(seen, scores, FAR)
-        peak = jnp.maximum(jnp.max(scores, 1, keepdims=True), peak_ref[b])
-        weights = jnp.exp2(scores - peak)
+        draft_scores = join_rows(lax.dot_general(turned_ref[b], drafts, NT, preferred_element_type=jnp.float32))
+        draft_seen = (spot >= b * draft_count) & (spot <= b * draft_count + token)
+        draft_scores = jnp.where(draft_seen, draft_scores, FAR)
+        peak = jnp.maximum(jnp.max(scores, 1, keepdims=True), jnp.max(draft_scores, 1, keepdims=True))
+        peak = jnp.maximum(peak, peak_ref[b])
+        weights, draft_weights = jnp.exp2(scores - peak), jnp.exp2(draft_scores - peak)
         fade = jnp.exp2(peak_ref[b] - peak)
         new_peak_ref[b] = peak
-        new_total_ref[b] = total_ref[b] * fade + jnp.sum(weights, 1, keepdims=True)
-        mixed = join_rows(jnp.dot(split_rows(weights), window_ref[b], preferred_element_type=jnp.float32))
-        new_mixed_ref[b] = mixed_ref[b] * fade + mixed
+        total = jnp.sum(weights, 1, keepdims=True) + jnp.sum(draft_weights, 1, keepdims=True)
+        new_total_ref[b] = total_ref[b] * fade + total
+        mixed = jnp.dot(split_rows(weights), window_ref[b], preferred_element_type=jnp.float32)
+        mixed += jnp.dot(split_rows(draft_weights), drafts, preferred_element_type=jnp.float32)
+        new_mixed_ref[b] = mixed_ref[b] * fade + join_rows(mixed)
 
 
 def piece_sums(starts, spans, row_refs, refs):
@@ -213,13 +222,18 @@
 
 
 def join_kernel(one_ref, two_ref, *refs):
-    rows, out_ref = one_ref.shape[0], refs[-1]
+    rows, (out_ref, bare_ref) = one_ref.shape[0], refs[-2:]
     out_ref[:rows, :] = one_ref[...]
     out_ref[rows:, :] = two_ref[...]
-
-
-def copy_kernel(one_ref, tie_ref, out_ref):
-    out_ref[...] = one_ref[...]
+    bare_ref[: rows - 16, :] = one_ref[: rows - 16, :]
+    bare_ref[rows - 16 :, :] = two_ref[: rows - 16, :]
+
+
+def copy_kernel(spans, one_ref, *refs):
+    done = 0
+    for first, count in spans:
+        refs[-1][done : done + count, :] = one_ref[first : first + count, :]
+        done += count
 
 
 def pack_kernel(spans, target_ref, *refs):
@@ -275,35 +289,19 @@
     outgoing_ref[...] = jnp.dot(chosen, latent, preferred_element_type=jnp.float32).astype(jnp.bfloat16)
 
 
-def late_kernel(
-    column_slot_ref, draft_latent_ref, turned_ref, peak_ref, total_ref, mixed_ref, value_up_ref, *refs
-):
+def late_kernel(column_slot_ref, turned_ref, peak_ref, total_ref, mixed_ref, value_up_ref, *refs):
     incoming_refs, (out_ref, rows_ref, parted_ref) = refs[:-3], refs[-3:]
     slot_count, draft_count, _ = out_ref.shape
-    tile = slot_count * draft_count
     heads_kv = value_up_ref.shape[1] // HEAD_SIZE
     group_size = QUERY_HEADS // heads_kv
     head_rows = group_size * draft_count
     rows = peak_ref.shape[1]
     block = incoming_refs[0].shape[0]
-    arrived = block * len(incoming_refs)
-    span = rows_ref.shape[0]
-    drafts = jnp.concatenate([draft_latent_ref[...], jnp.zeros((span - arrived - tile, rows_ref.shape[1]), jnp.float32)], 0)
     for n, ref in enumerate(incoming_refs):
         rows_ref[n * block : (n + 1) * block, :] = ref[...]
-    rows_ref[arrived:, :] = drafts.astype(jnp.bfloat16)
-    token = lax.broadcasted_iota(jnp.int32, (rows, 1), 0) % draft_count
-    column = lax.broadcasted_iota(jnp.int32, (rows, span - arrived), 1)
     for b in range(slot_count):
         scores = join_rows(lax.dot_general(turned_ref[b], rows_ref[...], NT, preferred_element_type=jnp.float32))
-        draft_seen = (column >= b * draft_count) & (column <= b * draft_count + token)
-        scores = jnp.concatenate(
-            [
-                jnp.where(column_slot_ref[...] == b, scores[:, :arrived], FAR),
-                jnp.where(draft_seen, scores[:, arrived:], FAR),
-            ],
-            1,
-        )
+        scores = jnp.where(column_slot_ref[...] == b, scores, FAR)
         peak = jnp.maximum(jnp.max(scores, 1, keepdims=True), peak_ref[b])
         weights = jnp.exp2(scores - peak)
         fade = jnp.exp2(peak_ref[b] - peak)
@@ -377,14 +375,22 @@
     za, zb = swap(half, z=1), swap(half, z=2)
     y0 = swap(full, y=1)
     rows = [rows, swap(rows, c=1)]
-    zab = call(
-        join_kernel, array(2 * ext), "join_pieces", za, zb, y0, rows[1], held, specs=[WHOLE] * 2 + [UNREAD] * 3
+    zab, bare = call(
+        join_kernel, [array(2 * ext), array(2 * half_rows)], "join_pieces", za, zb, y0, rows[1], held,
+        specs=[WHOLE] * 2 + [UNREAD] * 3,
     )
-    yab, xab = swap(zab, y=1), swap(zab, r=1)
+    yab, xab = swap(zab, y=1), swap(bare, r=1)
     zc = swap(zb, z=1)
-    xc = swap(zc, r=1)
-    xyab = swap(yab, r=1)
-    yc = swap(call(copy_kernel, array(ext), "copy_piece", zc, yab, specs=[WHOLE, UNREAD]), y=1)
+
+    def copy(x, spans, *ties):
+        return call(
+            functools.partial(copy_kernel, spans), array(sum(rows for _, rows in spans)), "copy_piece", x, *ties,
+            specs=[WHOLE] + [UNREAD] * len(ties),
+        )
+
+    xc = swap(copy(zc, [(0, half_rows)]), r=1)
+    xyab = swap(copy(yab, [(0, half_rows), (ext, half_rows)]), r=1)
+    yc = swap(copy(zc, [(0, ext)], yab), y=1)
     yxc = swap(xc, y=1)
 
     order = [
@@ -431,13 +437,13 @@
         ),
         (
             [xab, zc, yc],
-            [(0, 0, half_rows, (1, 1, 0)), (0, ext, half_rows, (1, 2, 0)),
+            [(0, 0, half_rows, (1, 1, 0)), (0, half_rows, half_rows, (1, 2, 0)),
              (1, 0, half_rows, (0, 3, 0)), (2, 0, half_rows, (0, 3, 1))],
         ),
         (
             [xc, yxc, xyab],
             [(0, 0, half_rows, (1, 3, 0)), (1, 0, half_rows, (1, 3, 1)),
-             (2, 0, half_rows, (1, 1, 1)), (2, ext, half_rows, (1, 2, 1))],
+             (2, 0, half_rows, (1, 1, 1)), (2, half_rows, half_rows, (1, 2, 1))],
         ),
     ]
     sums = []
@@ -450,12 +456,11 @@
             )
         ]
 
-    def finish(tie):
+    def finish():
         pieces, uses = stages[-1]
         keep, send = call(
             functools.partial(down_place_kernel, starts_of(uses), [use[:3] for use in uses]),
-            [array(2 * count + 8, f32)] * 2, "down_place_rows", *rows, place, *sums, *pieces, tie,
-            specs=[WHOLE] * (4 + len(pieces)) + [UNREAD], flops=2**26,
+            [array(2 * count + 8, f32)] * 2, "down_place_rows", *rows, place, *sums, *pieces, flops=2**26,
         )
         came = swap(send, c=1)
         block = array(count)
@@ -497,7 +502,7 @@
     tile = slot_count * draft_count
     draft_flat = jnp.pad(draft_hidden.reshape(tile, draft_hidden.shape[2]), ((0, 16 - tile), (0, 0)))
 
-    def finish(tie):
+    def finish():
         outgoing, draft_latent = pl.pallas_call(
             plain_down_kernel,
             out_shape=[
@@ -567,30 +572,28 @@
     limit, column_slot, finish = (deliver if known else deliver_plain)(
         prompt_hidden, draft_hidden, down_weight, row_target, context_len, peak
     )
+    draft_latent, incoming = finish()
     peak, total, mixed = pl.pallas_call(
-        functools.partial(window_kernel, arrived, span_rows),
+        functools.partial(window_kernel, arrived, span_rows, draft_count),
         out_shape=stats,
-        in_specs=[SCALARS] + [WHOLE] * 6,
+        in_specs=[SCALARS] + [WHOLE] * 7,
         out_specs=[WHOLE] * 3,
         compiler_params=params(16),
-        cost_estimate=pl.CostEstimate(flops=2**20, bytes_accessed=2**16, transcendentals=0),
+        cost_estimate=pl.CostEstimate(flops=2**30, bytes_accessed=2**16, transcendentals=0),
         name="window_rows",
-    )(context_len, limit, turned, peak, total, mixed, edge)
-
-    draft_latent, incoming = finish(peak)
-    span = (arrived + slot_count * draft_count + 127) // 128 * 128
+    )(context_len, limit, turned, peak, total, mixed, edge, draft_latent)
     return pl.pallas_call(
         late_kernel,
         out_shape=jax.ShapeDtypeStruct((slot_count, draft_count, QUERY_HEADS * HEAD_SIZE), bf16),
-        in_specs=[WHOLE] * (7 + len(incoming)),
+        in_specs=[WHOLE] * (6 + len(incoming)),
         out_specs=WHOLE,
         scratch_shapes=[
-            pltpu.VMEM((span, latent_width), bf16),
+            pltpu.VMEM((arrived, latent_width), bf16),
             pltpu.VMEM((slot_count, 2 * rows, latent_width), bf16),
         ],
         compiler_params=params(16),
         name="late_rows",
-    )(column_slot, draft_latent, turned, peak, total, mixed, value_up_weight, *incoming)
+    )(column_slot, turned, peak, total, mixed, value_up_weight, *incoming)
 
 
 def solution(mesh):

time: 54.9 us -> 53.7 us (0.978)
  waiting for transfers between devices: 22.4 us -> 20.3 us
  starting transfers between devices: 19.3 us -> 19.9 us
    ppermute x16, waiting for transfers between devices: 22.4 us -> 20.3 us  [swap(): return lax.ppermute(x, ('rep', 'wide'), pairs)]
    ppermute x16, starting transfers between devices: 19.3 us -> 19.9 us  [swap(): return lax.ppermute(x, ('rep', 'wide'), pairs)]
    pallas_call x12 -> x14, Pallas kernels: 4.66 us -> 4.7 us  [call(): pl.pallas_call(kernel, out_shape=out_shape, in_specs=specs or [WHOLE] * l...]
  transfers between devices with their start and end apart: 16 -> 16, of which waited for: 9 -> 10; matrix products, arithmetic and copies ran while one was open for 0% -> 0% of each run, Pallas kernels for 14% -> 15%
where the time goes in v8:
time: 53.7 us; the launch traced here: 53.5 us
  waiting for transfers between devices  20.3 us (38%)
  starting transfers between devices  19.9 us (37%)
  Pallas kernels  13.2 us (25%)
    ppermute x16, waiting for transfers between devices, swap(): return lax.ppermute(x, ('rep', 'wide'), pairs)  20.3 us
    ppermute x16, starting transfers between devices, swap(): return lax.ppermute(x, ('rep', 'wide'), pairs)  19.9 us
    pallas_call x14, Pallas kernels, call(): pl.pallas_call(kernel, out_shape=out_shape, in_specs=specs or [WHOLE] * l...  4.7 us
    pallas_call x1, Pallas kernels, local(): pl.pallas_call(functools.partial(held_kernel, arrived), out_shape=[jax.Sh...  4.01 us
    pallas_call x1, Pallas kernels, local(): pl.pallas_call(functools.partial(window_kernel, arrived, span_rows, draft...  2.24 us
    pallas_call x1, Pallas kernels, local(): pl.pallas_call(late_kernel, out_shape=jax.ShapeDtypeStruct((slot_count, d...  2.23 us
  transfers between devices with their start and end apart: 16, of which 10 were waited for; matrix products, arithmetic and copies ran while one was open for 0% of the time, Pallas kernels for 15%

profile of v8, /device:TPU:0, one launch (start us, length us, event | category | flops | bytes accessed | tf_op | source)
XLA Modules:
  0.0 53.5 jit_solution(17713719678189002859)
XLA Ops:
  0.0 1.9 %start_rows.1 = (bf16[272,256]{1,0:T(8,128)(2,1)S(1)}, bf16[528,256]{1,0:T(8,128)(2,1)S(1)}, s32[1,128]{1,0:T(1,128)S(1)}, bf16[144,8192]{1,0:T(8,128)(2,1)S(1)}) custom-call(s32[1,128]{1,0:T(1,128)} %bitcast.1, bf16[512,256]{1,0:T(8,128)(2,1)} %shard_hbm.1, bf16[128,8192]{1,0:T(8,128)(2,1)} %prompt_hbm.1, bf16[2,4,8192]{2,1,0:T(4,128)(2,1)} %draft_hbm.1), custom_call_target="tpu_custom_call" | custom-call | flops 1048576 | bytes 65536 | tf_op jit(solution)/shard_map/start_rows/pallas_call | solution.py:344
  1.9 0.5 collective-permute-start.3
  2.4 2.6 %collective-permute-start = (bf16[528,256]{1,0:T(8,128)(2,1)S(1)}, bf16[528,256]{1,0:T(8,128)(2,1)S(1)}, u32[]{:S(2)}, u32[]{:S(2)}) collective-permute-start(bf16[528,256]{1,0:T(8,128)(2,1)S(1)} %get-tuple-element.33.refs_2_), channel_id=1, source_target_pairs={{0,2},{1,3},{2,0},{3,1},{4,6},{5,7},{6,4},{7,5},{8,10},{9,11},{10,... | collective-permute-start | bytes 811016 | tf_op jit(solution)/shard_map/ppermute | solution.py:338
  5.0 1.6 %collective-permute-start.1 = (bf16[272,256]{1,0:T(8,128)(2,1)S(1)}, bf16[272,256]{1,0:T(8,128)(2,1)S(1)}, u32[]{:S(2)}, u32[]{:S(2)}) collective-permute-start(bf16[272,256]{1,0:T(8,128)(2,1)S(1)} %get-tuple-element.32.refs_0_), channel_id=1, source_target_pairs={{0,4},{1,5},{2,6},{3,7},{4,0},{5,1},{6,2},{7,3},{8,12},{9,13},{10,... | collective-permute-start | bytes 417800 | tf_op jit(solution)/shard_map/ppermute | solution.py:338
  6.6 2.6 %collective-permute-start.2 = (bf16[272,256]{1,0:T(8,128)(2,1)S(1)}, bf16[272,256]{1,0:T(8,128)(2,1)S(1)}, u32[]{:S(2)}, u32[]{:S(2)}) collective-permute-start(bf16[272,256]{1,0:T(8,128)(2,1)S(1)} %get-tuple-element.32.refs_0_), channel_id=1, source_target_pairs={{0,8},{1,9},{2,10},{3,11},{4,12},{5,13},{6,14},{7,15},{8,0},{9,1},... | collective-permute-start | bytes 417800 | tf_op jit(solution)/shard_map/ppermute | solution.py:338
  9.2 4.0 %held_rows.1 = (bf16[2,512,256]{2,1,0:T(8,128)(2,1)S(1)}, f32[2,256,1]{2,1,0:T(8,128)S(1)}, f32[2,256,1]{2,1,0:T(8,128)S(1)}, f32[2,256,256]{2,1,0:T(8,128)S(1)}, bf16[2,384,256]{2,1,0:T(8,128)(2,1)S(1)}) custom-call(s32[2]{0:T(128)S(1)} %copy-done.1, bf16[2,4,8192]{2,1,0:T(4,128)(2,1)} %query_hbm.1, bf16[256,1024]{1,0:T(8,128)(2,1)} %key_up_hbm.1, ...), custom_call_target="tpu_custom_call" | custom-call | flops 2147483648 | bytes 2097152 | tf_op jit(solution)/shard_map/held_rows/pallas_call | solution.py:550
  13.2 0.3 collective-permute-done.1.one_ref
  13.5 2.5 %collective-permute-done.2.two_ref = bf16[272,256]{1,0:T(8,128)(2,1)S(1)} collective-permute-done((bf16[272,256]{1,0:T(8,128)(2,1)S(1)}, bf16[272,256]{1,0:T(8,128)(2,1)S(1)}, u32[]{:S(2)}, u32[]{:S(2)}) %collective-permute-start.2) | collective-permute-done | bytes 139296 | tf_op jit(solution)/shard_map/ppermute | solution.py:338
  16.0 0.6 %collective-permute-start.4 = (bf16[544,256]{1,0:T(8,128)(2,1)S(1)}, bf16[544,256]{1,0:T(8,128)(2,1)S(1)}, u32[]{:S(2)}, u32[]{:S(2)}) collective-permute-start(bf16[544,256]{1,0:T(8,128)(2,1)S(1)} %get-tuple-element.36.refs_2_.refs_4_), channel_id=1, source_target_pairs={{0,2},{1,3},{2,0},{3,1},{4,6},{5,7},{6,4},{7,5},{8,10},{9,11},{10,... | collective-permute-start | bytes 835592 | tf_op jit(solution)/shard_map/ppermute | solution.py:338
  16.6 0.4 collective-permute-start.5
  17.0 1.5 %collective-permute-start.7 = (bf16[512,256]{1,0:T(8,128)(2,1)S(1)}, bf16[512,256]{1,0:T(8,128)(2,1)S(1)}, u32[]{:S(2)}, u32[]{:S(2)}) collective-permute-start(bf16[512,256]{1,0:T(8,128)(2,1)S(1)} %get-tuple-element.37), channel_id=1, source_target_pairs={{0,16},{1,17},{2,18},{3,19},{4,20},{5,21},{6,22},{7,23},{8,24},{9,... | collective-permute-start | bytes 786440 | tf_op jit(solution)/shard_map/ppermute | solution.py:338
  18.5 3.1 %collective-permute-done.5.one_ref.refs_6_.refs_3_ = bf16[272,256]{1,0:T(8,128)(2,1)S(1)} collective-permute-done((bf16[272,256]{1,0:T(8,128)(2,1)S(1)}, bf16[272,256]{1,0:T(8,128)(2,1)S(1)}, u32[]{:S(2)}, u32[]{:S(2)}) %collective-permute-start.5) | collective-permute-done | bytes 139296 | tf_op jit(solution)/shard_map/ppermute | solution.py:338
  21.7 1.6 %collective-permute-start.8 = (bf16[256,256]{1,0:T(8,128)(2,1)S(1)}, bf16[256,256]{1,0:T(8,128)(2,1)S(1)}, u32[]{:S(2)}, u32[]{:S(2)}) collective-permute-start(bf16[256,256]{1,0:T(8,128)(2,1)S(1)} %copy_piece.4), channel_id=1, source_target_pairs={{0,16},{1,17},{2,18},{3,19},{4,20},{5,21},{6,22},{7,23},{8,24},{9,... | collective-permute-start | bytes 393224 | tf_op jit(solution)/shard_map/ppermute | solution.py:338
  23.2 1.0 %collective-permute-start.11 = (bf16[512,256]{1,0:T(8,128)(2,1)S(1)}, bf16[512,256]{1,0:T(8,128)(2,1)S(1)}, u32[]{:S(2)}, u32[]{:S(2)}) collective-permute-start(bf16[512,256]{1,0:T(8,128)(2,1)S(1)} %copy_piece.5), channel_id=1, source_target_pairs={{0,16},{1,17},{2,18},{3,19},{4,20},{5,21},{6,22},{7,23},{8,24},{9,... | collective-permute-start | bytes 786440 | tf_op jit(solution)/shard_map/ppermute | solution.py:338
  24.3 1.2 %collective-permute-start.6 = (bf16[272,256]{1,0:T(8,128)(2,1)S(1)}, bf16[272,256]{1,0:T(8,128)(2,1)S(1)}, u32[]{:S(2)}, u32[]{:S(2)}) collective-permute-start(bf16[272,256]{1,0:T(8,128)(2,1)S(1)} %copy_piece.3), channel_id=1, source_target_pairs={{0,2},{1,3},{2,0},{3,1},{4,6},{5,7},{6,4},{7,5},{8,10},{9,11},{10,... | collective-permute-start | bytes 417800 | tf_op jit(solution)/shard_map/ppermute | solution.py:338
  25.4 3.7 %collective-permute-done.8.refs_9_.refs_4_ = bf16[256,256]{1,0:T(8,128)(2,1)S(1)} collective-permute-done((bf16[256,256]{1,0:T(8,128)(2,1)S(1)}, bf16[256,256]{1,0:T(8,128)(2,1)S(1)}, u32[]{:S(2)}, u32[]{:S(2)}) %collective-permute-start.8) | collective-permute-done | bytes 131104 | tf_op jit(solution)/shard_map/ppermute | solution.py:338
  29.1 1.5 %collective-permute-start.10 = (bf16[256,256]{1,0:T(8,128)(2,1)S(1)}, bf16[256,256]{1,0:T(8,128)(2,1)S(1)}, u32[]{:S(2)}, u32[]{:S(2)}) collective-permute-start(bf16[256,256]{1,0:T(8,128)(2,1)S(1)} %collective-permute-done.8.refs_9_.refs_4_), channel_id=1, source_target_pairs={{0,2},{1,3},{2,0},{3,1},{4,6},{5,7},{6,4},{7,5},{8,10},{9,11},{10,... | collective-permute-start | bytes 393224 | tf_op jit(solution)/shard_map/ppermute | solution.py:338
  30.7 0.3 down_rows.3.refs_4_
  31.1 0.4 down_rows.4.refs_5_
  31.4 0.3 down_rows.5.refs_3_
  32.0 0.7 %count_rows.1 = (s32[2,128]{1,0:T(2,128)S(1)}, s32[1,256]{1,0:T(1,128)S(1)}, s32[1,256]{1,0:T(1,128)S(1)}) custom-call(s32[2]{0:T(128)S(1)} %copy-done.1, bf16[16,2176]{1,0:T(8,128)(2,1)S(1)} %pack_rows.1.mine_ref, bf16[16,2176]{1,0:T(8,128)(2,1)S(1)} %collective-permute-done.9.other_ref), custom_call_target="tpu_custom_call" | custom-call | flops 1048576 | bytes 65536 | tf_op jit(solution)/shard_map/count_rows/pallas_call | solution.py:344
  32.7 1.4 %collective-permute-done.10.refs_5_ = bf16[256,256]{1,0:T(8,128)(2,1)S(1)} collective-permute-done((bf16[256,256]{1,0:T(8,128)(2,1)S(1)}, bf16[256,256]{1,0:T(8,128)(2,1)S(1)}, u32[]{:S(2)}, u32[]{:S(2)}) %collective-permute-start.10) | collective-permute-done | bytes 131104 | tf_op jit(solution)/shard_map/ppermute | solution.py:338
  34.1 0.9 %down_place_rows.1 = (f32[264,256]{1,0:T(8,128)S(1)}, f32[264,256]{1,0:T(8,128)S(1)}) custom-call(bf16[144,8192]{1,0:T(8,128)(2,1)S(1)} %get-tuple-element.34.refs_0_, bf16[144,8192]{1,0:T(8,128)(2,1)S(1)} %collective-permute-done.3.refs_1_, s32[1,256]{1,0:T(1,128)S(1)} %get-tuple-element.44.refs_2_, f32[288,256]{1,0:T(8,128)S(1)} %down_rows.5.refs_3_, ...), custom_call_target="tpu_custom_call" | custom-call | flops 67108864 | bytes 65536 | tf_op jit(solution)/shard_map/down_place_rows/pallas_call | solution.py:344
  35.1 1.5 %collective-permute-done.12.came_ref = f32[264,256]{1,0:T(8,128)S(1)} collective-permute-done((f32[264,256]{1,0:T(8,128)S(1)}, f32[264,256]{1,0:T(8,128)S(1)}, u32[]{:S(2)}, u32[]{:S(2)}) %collective-permute-start.12) | collective-permute-done | bytes 270368 | tf_op jit(solution)/shard_map/ppermute | solution.py:338
  36.7 1.6 %collective-permute-start.13 = (bf16[128,256]{1,0:T(8,128)(2,1)S(1)}, bf16[128,256]{1,0:T(8,128)(2,1)S(1)}, u32[]{:S(2)}, u32[]{:S(2)}) collective-permute-start(bf16[128,256]{1,0:T(8,128)(2,1)S(1)} %get-tuple-element.52), channel_id=1, source_target_pairs={{0,2},{1,3},{2,0},{3,1},{4,6},{5,7},{6,4},{7,5},{8,10},{9,11},{10,... | collective-permute-start | bytes 196616 | tf_op jit(solution)/shard_map/ppermute | solution.py:338
  38.3 2.7 %collective-permute-done.13.came_ref = bf16[128,256]{1,0:T(8,128)(2,1)S(1)} collective-permute-done((bf16[128,256]{1,0:T(8,128)(2,1)S(1)}, bf16[128,256]{1,0:T(8,128)(2,1)S(1)}, u32[]{:S(2)}, u32[]{:S(2)}) %collective-permute-start.13) | collective-permute-done | bytes 65568 | tf_op jit(solution)/shard_map/ppermute | solution.py:338
  41.0 2.6 %collective-permute-start.14 = (bf16[128,256]{1,0:T(8,128)(2,1)S(1)}, bf16[128,256]{1,0:T(8,128)(2,1)S(1)}, u32[]{:S(2)}, u32[]{:S(2)}) collective-permute-start(bf16[128,256]{1,0:T(8,128)(2,1)S(1)} %get-tuple-element.54), channel_id=1, source_target_pairs={{0,8},{1,9},{2,10},{3,11},{4,12},{5,13},{6,14},{7,15},{8,0},{9,1},... | collective-permute-start | bytes 196616 | tf_op jit(solution)/shard_map/ppermute | solution.py:338
  43.7 3.3 %collective-permute-done.14.came_ref = bf16[128,256]{1,0:T(8,128)(2,1)S(1)} collective-permute-done((bf16[128,256]{1,0:T(8,128)(2,1)S(1)}, bf16[128,256]{1,0:T(8,128)(2,1)S(1)}, u32[]{:S(2)}, u32[]{:S(2)}) %collective-permute-start.14) | collective-permute-done | bytes 65568 | tf_op jit(solution)/shard_map/ppermute | solution.py:338
  47.0 0.5 collective-permute-start.15
  47.4 2.2 %window_rows.1 = (f32[2,256,1]{2,1,0:T(8,128)S(1)}, f32[2,256,1]{2,1,0:T(8,128)S(1)}, f32[2,256,256]{2,1,0:T(8,128)S(1)}) custom-call(s32[2]{0:T(128)S(1)} %copy-done.1, s32[2,128]{1,0:T(2,128)S(1)} %get-tuple-element.40.limit_ref, bf16[2,512,256]{2,1,0:T(8,128)(2,1)S(1)} %get-tuple-element.39.turned_ref, ...), custom_call_target="tpu_custom_call" | custom-call | flops 1073741824 | bytes 65536 | tf_op jit(solution)/shard_map/window_rows/pallas_call | solution.py:576
  49.7 1.6 %collective-permute-done.15.refs_1_ = bf16[128,256]{1,0:T(8,128)(2,1)S(1)} collective-permute-done((bf16[128,256]{1,0:T(8,128)(2,1)S(1)}, bf16[128,256]{1,0:T(8,128)(2,1)S(1)}, u32[]{:S(2)}, u32[]{:S(2)}) %collective-permute-start.15) | collective-permute-done | bytes 65568 | tf_op jit(solution)/shard_map/ppermute | solution.py:338
  51.3 2.2 %late_rows.1 = bf16[2,4,8192]{2,1,0:T(4,128)(2,1)} custom-call(s32[1,256]{1,0:T(1,128)S(1)} %get-tuple-element.38.column_slot_ref, bf16[2,512,256]{2,1,0:T(8,128)(2,1)S(1)} %get-tuple-element.39.turned_ref, f32[2,256,1]{2,1,0:T(8,128)S(1)} %get-tuple-element.48.peak_ref, f32[2,256,1]{2,1,0:T(8,128)S(1)} %get-tuple-element.49.total_ref, ...), custom_call_target="tpu_custom_call" | custom-call | tf_op jit(solution)/shard_map/late_rows/pallas_call | solution.py:585
  (21 shorter events, 0.5 us)
Async XLA Ops:
  0.0 9.2 %copy-start.1 = (s32[2]{0:T(128)S(1)}, s32[2]{0:T(128)}, u32[]{:S(2)}) copy-start(s32[2]{0:T(128)} %context_ref.5) | copy-start | bytes 28
  1.9 14.1 %collective-permute-start.3 = (bf16[144,8192]{1,0:T(8,128)(2,1)S(1)}, bf16[144,8192]{1,0:T(8,128)(2,1)S(1)}, u32[]{:S(2)}, u32[]{:S(2)}) collective-permute-start(bf16[144,8192]{1,0:T(8,128)(2,1)S(1)} %get-tuple-element.34.refs_0_), channel_id=1, source_target_pairs={{0,1},{1,0},{2,3},{3,2},{4,5},{5,4},{6,7},{7,6},{8,9},{9,8},{10,11... | collective-permute-start | bytes 7077896 | tf_op jit(solution)/shard_map/ppermute | solution.py:338
  2.4 13.6 %collective-permute-start = (bf16[528,256]{1,0:T(8,128)(2,1)S(1)}, bf16[528,256]{1,0:T(8,128)(2,1)S(1)}, u32[]{:S(2)}, u32[]{:S(2)}) collective-permute-start(bf16[528,256]{1,0:T(8,128)(2,1)S(1)} %get-tuple-element.33.refs_2_), channel_id=1, source_target_pairs={{0,2},{1,3},{2,0},{3,1},{4,6},{5,7},{6,4},{7,5},{8,10},{9,11},{10,... | collective-permute-start | bytes 811016 | tf_op jit(solution)/shard_map/ppermute | solution.py:338
  5.0 8.5 %collective-permute-start.1 = (bf16[272,256]{1,0:T(8,128)(2,1)S(1)}, bf16[272,256]{1,0:T(8,128)(2,1)S(1)}, u32[]{:S(2)}, u32[]{:S(2)}) collective-permute-start(bf16[272,256]{1,0:T(8,128)(2,1)S(1)} %get-tuple-element.32.refs_0_), channel_id=1, source_target_pairs={{0,4},{1,5},{2,6},{3,7},{4,0},{5,1},{6,2},{7,3},{8,12},{9,13},{10,... | collective-permute-start | bytes 417800 | tf_op jit(solution)/shard_map/ppermute | solution.py:338
  6.6 9.4 %collective-permute-start.2 = (bf16[272,256]{1,0:T(8,128)(2,1)S(1)}, bf16[272,256]{1,0:T(8,128)(2,1)S(1)}, u32[]{:S(2)}, u32[]{:S(2)}) collective-permute-start(bf16[272,256]{1,0:T(8,128)(2,1)S(1)} %get-tuple-element.32.refs_0_), channel_id=1, source_target_pairs={{0,8},{1,9},{2,10},{3,11},{4,12},{5,13},{6,14},{7,15},{8,0},{9,1},... | collective-permute-start | bytes 417800 | tf_op jit(solution)/shard_map/ppermute | solution.py:338
  16.0 7.2 %collective-permute-start.4 = (bf16[544,256]{1,0:T(8,128)(2,1)S(1)}, bf16[544,256]{1,0:T(8,128)(2,1)S(1)}, u32[]{:S(2)}, u32[]{:S(2)}) collective-permute-start(bf16[544,256]{1,0:T(8,128)(2,1)S(1)} %get-tuple-element.36.refs_2_.refs_4_), channel_id=1, source_target_pairs={{0,2},{1,3},{2,0},{3,1},{4,6},{5,7},{6,4},{7,5},{8,10},{9,11},{10,... | collective-permute-start | bytes 835592 | tf_op jit(solution)/shard_map/ppermute | solution.py:338
  16.6 5.1 %collective-permute-start.5 = (bf16[272,256]{1,0:T(8,128)(2,1)S(1)}, bf16[272,256]{1,0:T(8,128)(2,1)S(1)}, u32[]{:S(2)}, u32[]{:S(2)}) collective-permute-start(bf16[272,256]{1,0:T(8,128)(2,1)S(1)} %collective-permute-done.2.two_ref), channel_id=1, source_target_pairs={{0,4},{1,5},{2,6},{3,7},{4,0},{5,1},{6,2},{7,3},{8,12},{9,13},{10,... | collective-permute-start | bytes 417800 | tf_op jit(solution)/shard_map/ppermute | solution.py:338
  17.0 13.6 %collective-permute-start.7 = (bf16[512,256]{1,0:T(8,128)(2,1)S(1)}, bf16[512,256]{1,0:T(8,128)(2,1)S(1)}, u32[]{:S(2)}, u32[]{:S(2)}) collective-permute-start(bf16[512,256]{1,0:T(8,128)(2,1)S(1)} %get-tuple-element.37), channel_id=1, source_target_pairs={{0,16},{1,17},{2,18},{3,19},{4,20},{5,21},{6,22},{7,23},{8,24},{9,... | collective-permute-start | bytes 786440 | tf_op jit(solution)/shard_map/ppermute | solution.py:338
  21.7 7.4 %collective-permute-start.8 = (bf16[256,256]{1,0:T(8,128)(2,1)S(1)}, bf16[256,256]{1,0:T(8,128)(2,1)S(1)}, u32[]{:S(2)}, u32[]{:S(2)}) collective-permute-start(bf16[256,256]{1,0:T(8,128)(2,1)S(1)} %copy_piece.4), channel_id=1, source_target_pairs={{0,16},{1,17},{2,18},{3,19},{4,20},{5,21},{6,22},{7,23},{8,24},{9,... | collective-permute-start | bytes 393224 | tf_op jit(solution)/shard_map/ppermute | solution.py:338
  23.2 10.8 %collective-permute-start.11 = (bf16[512,256]{1,0:T(8,128)(2,1)S(1)}, bf16[512,256]{1,0:T(8,128)(2,1)S(1)}, u32[]{:S(2)}, u32[]{:S(2)}) collective-permute-start(bf16[512,256]{1,0:T(8,128)(2,1)S(1)} %copy_piece.5), channel_id=1, source_target_pairs={{0,16},{1,17},{2,18},{3,19},{4,20},{5,21},{6,22},{7,23},{8,24},{9,... | collective-permute-start | bytes 786440 | tf_op jit(solution)/shard_map/ppermute | solution.py:338
  24.3 6.3 %collective-permute-start.6 = (bf16[272,256]{1,0:T(8,128)(2,1)S(1)}, bf16[272,256]{1,0:T(8,128)(2,1)S(1)}, u32[]{:S(2)}, u32[]{:S(2)}) collective-permute-start(bf16[272,256]{1,0:T(8,128)(2,1)S(1)} %copy_piece.3), channel_id=1, source_target_pairs={{0,2},{1,3},{2,0},{3,1},{4,6},{5,7},{6,4},{7,5},{8,10},{9,11},{10,... | collective-permute-start | bytes 417800 | tf_op jit(solution)/shard_map/ppermute | solution.py:338
  29.1 5.0 %collective-permute-start.10 = (bf16[256,256]{1,0:T(8,128)(2,1)S(1)}, bf16[256,256]{1,0:T(8,128)(2,1)S(1)}, u32[]{:S(2)}, u32[]{:S(2)}) collective-permute-start(bf16[256,256]{1,0:T(8,128)(2,1)S(1)} %collective-permute-done.8.refs_9_.refs_4_), channel_id=1, source_target_pairs={{0,2},{1,3},{2,0},{3,1},{4,6},{5,7},{6,4},{7,5},{8,10},{9,11},{10,... | collective-permute-start | bytes 393224 | tf_op jit(solution)/shard_map/ppermute | solution.py:338
  30.6 1.3 %collective-permute-start.9 = (bf16[16,2176]{1,0:T(8,128)(2,1)S(1)}, bf16[16,2176]{1,0:T(8,128)(2,1)S(1)}, u32[]{:S(2)}, u32[]{:S(2)}) collective-permute-start(bf16[16,2176]{1,0:T(8,128)(2,1)S(1)} %pack_rows.1.mine_ref), channel_id=1, source_target_pairs={{0,1},{1,0},{2,3},{3,2},{4,5},{5,4},{6,7},{7,6},{8,9},{9,8},{10,11... | collective-permute-start | bytes 208904 | tf_op jit(solution)/shard_map/ppermute | solution.py:338
  35.0 1.6 %collective-permute-start.12 = (f32[264,256]{1,0:T(8,128)S(1)}, f32[264,256]{1,0:T(8,128)S(1)}, u32[]{:S(2)}, u32[]{:S(2)}) collective-permute-start(f32[264,256]{1,0:T(8,128)S(1)} %get-tuple-element.46), channel_id=1, source_target_pairs={{0,1},{1,0},{2,3},{3,2},{4,5},{5,4},{6,7},{7,6},{8,9},{9,8},{10,11... | collective-permute-start | bytes 811016 | tf_op jit(solution)/shard_map/ppermute | solution.py:338
  36.6 14.7 %copy-start = (bf16[256,1024]{1,0:T(8,128)(2,1)S(1)}, bf16[256,1024]{1,0:T(8,128)(2,1)}, u32[]{:S(2)}) copy-start(bf16[256,1024]{1,0:T(8,128)(2,1)} %value_up_ref.1) | copy-start | bytes 1572868
  36.7 4.3 %collective-permute-start.13 = (bf16[128,256]{1,0:T(8,128)(2,1)S(1)}, bf16[128,256]{1,0:T(8,128)(2,1)S(1)}, u32[]{:S(2)}, u32[]{:S(2)}) collective-permute-start(bf16[128,256]{1,0:T(8,128)(2,1)S(1)} %get-tuple-element.52), channel_id=1, source_target_pairs={{0,2},{1,3},{2,0},{3,1},{4,6},{5,7},{6,4},{7,5},{8,10},{9,11},{10,... | collective-permute-start | bytes 196616 | tf_op jit(solution)/shard_map/ppermute | solution.py:338
  41.0 5.9 %collective-permute-start.14 = (bf16[128,256]{1,0:T(8,128)(2,1)S(1)}, bf16[128,256]{1,0:T(8,128)(2,1)S(1)}, u32[]{:S(2)}, u32[]{:S(2)}) collective-permute-start(bf16[128,256]{1,0:T(8,128)(2,1)S(1)} %get-tuple-element.54), channel_id=1, source_target_pairs={{0,8},{1,9},{2,10},{3,11},{4,12},{5,13},{6,14},{7,15},{8,0},{9,1},... | collective-permute-start | bytes 196616 | tf_op jit(solution)/shard_map/ppermute | solution.py:338
  47.0 4.3 %collective-permute-start.15 = (bf16[128,256]{1,0:T(8,128)(2,1)S(1)}, bf16[128,256]{1,0:T(8,128)(2,1)S(1)}, u32[]{:S(2)}, u32[]{:S(2)}) collective-permute-start(bf16[128,256]{1,0:T(8,128)(2,1)S(1)} %get-tuple-element.56), channel_id=1, source_target_pairs={{0,4},{1,5},{2,6},{3,7},{4,0},{5,1},{6,2},{7,3},{8,12},{9,13},{10,... | collective-permute-start | bytes 196616 | tf_op jit(solution)/shard_map/ppermute | solution.py:338

commit v9 on v8

--- a/solution.py
+++ b/solution.py
@@ -33,63 +33,55 @@
 
 
 def held_kernel(
-    arrived, context_ref, query_hbm, key_up_hbm, cache_hbm, turned_ref, peak_ref, total_ref, mixed_ref, window_ref,
+    slot, arrived, context_ref, query_hbm, key_up_hbm, cache_hbm, tie_ref,
+    turned_ref, peak_ref, total_ref, mixed_ref, window_ref,
     query_ref, key_up_ref, cache_ref, float_ref, scores_ref, sems,
 ):
     copies = [
         pltpu.make_async_copy(source, target, sems.at[n])
         for n, (source, target) in enumerate(
-            [(query_hbm, query_ref), (key_up_hbm, key_up_ref), (cache_hbm, cache_ref)]
+            [(query_hbm.at[slot], query_ref), (key_up_hbm, key_up_ref), (cache_hbm.at[slot], cache_ref)]
         )
     ]
     for copy in copies:
         copy.start()
-    slot_count, span_rows, _ = cache_ref.shape
-    draft_count = query_ref.shape[1]
+    span_rows = cache_ref.shape[0]
     heads_kv = key_up_ref.shape[1] // HEAD_SIZE
     group_size = QUERY_HEADS // heads_kv
-    rows = group_size * draft_count
+    rows = group_size * query_ref.shape[0]
     scale = math.log2(math.e) / math.sqrt(HEAD_SIZE)
     step = 256
     copies[0].wait()
     copies[1].wait()
     for k in range(heads_kv):
-        pieces = []
-        for b in range(slot_count):
-            for g in range(group_size):
-                lane = (k * group_size + g) * HEAD_SIZE
-                pieces.append(query_ref[b, :, lane : lane + HEAD_SIZE].astype(jnp.float32))
-        query = jnp.concatenate(pieces, 0).astype(jnp.bfloat16)
+        lanes = [slice(h * HEAD_SIZE, (h + 1) * HEAD_SIZE) for h in range(k * group_size, (k + 1) * group_size)]
+        query = jnp.concatenate([query_ref[:, lane].astype(jnp.float32) for lane in lanes], 0).astype(jnp.bfloat16)
         key_up = key_up_ref[:, k * HEAD_SIZE : (k + 1) * HEAD_SIZE]
-        turned = lax.dot_general(query, key_up, NT, preferred_element_type=jnp.float32) * scale
-        for b in range(slot_count):
-            float_ref[b, k * rows : (k + 1) * rows, :] = turned[b * rows : (b + 1) * rows]
+        turned = lax.dot_general(query, key_up, NT, preferred_element_type=jnp.float32)
+        float_ref[k * rows : (k + 1) * rows, :] = turned * scale
     copies[2].wait()
-    for b in range(slot_count):
-        first = pl.multiple_of(window_start(context_ref[b], arrived, window_ref.shape[1], span_rows), 128)
-        window_ref[b] = cache_ref[b, pl.ds(first, window_ref.shape[1]), :]
-        turned_ref[b] = split_rows(float_ref[b])
-        peak = None
-        for c in range(0, span_rows, step):
-            scores = join_rows(
-                lax.dot_general(turned_ref[b], cache_ref[b, c : c + step], NT, preferred_element_type=jnp.float32)
-            )
-            column = lax.broadcasted_iota(jnp.int32, (1, step), 1) + c
-            scores = jnp.where(column < context_ref[b] - arrived, scores, FAR)
-            scores_ref[:, c : c + step] = scores
-            top = jnp.max(scores, 1, keepdims=True)
-            peak = top if peak is None else jnp.maximum(peak, top)
-        peak_ref[b] = peak
-        total = jnp.zeros_like(peak)
-        mixed = jnp.zeros(mixed_ref.shape[1:], jnp.float32)
-        for c in range(0, span_rows, step):
-            weights = jnp.exp2(scores_ref[:, c : c + step] - peak)
-            total += jnp.sum(weights, 1, keepdims=True)
-            mixed += join_rows(
-                jnp.dot(split_rows(weights), cache_ref[b, c : c + step], preferred_element_type=jnp.float32)
-            )
-        total_ref[b] = total
-        mixed_ref[b] = mixed
+    first = pl.multiple_of(window_start(context_ref[slot], arrived, window_ref.shape[0], span_rows), 128)
+    window_ref[...] = cache_ref[pl.ds(first, window_ref.shape[0]), :]
+    turned_ref[...] = split_rows(float_ref[...])
+    peak = None
+    for c in range(0, span_rows, step):
+        scores = join_rows(
+            lax.dot_general(turned_ref[...], cache_ref[c : c + step], NT, preferred_element_type=jnp.float32)
+        )
+        column = lax.broadcasted_iota(jnp.int32, (1, step), 1) + c
+        scores = jnp.where(column < context_ref[slot] - arrived, scores, FAR)
+        scores_ref[:, c : c + step] = scores
+        top = jnp.max(scores, 1, keepdims=True)
+        peak = top if peak is None else jnp.maximum(peak, top)
+    peak_ref[...] = peak
+    total = jnp.zeros_like(peak)
+    mixed = jnp.zeros(mixed_ref.shape, jnp.float32)
+    for c in range(0, span_rows, step):
+        weights = jnp.exp2(scores_ref[:, c : c + step] - peak)
+        total += jnp.sum(weights, 1, keepdims=True)
+        mixed += join_rows(jnp.dot(split_rows(weights), cache_ref[c : c + step], preferred_element_type=jnp.float32))
+    total_ref[...] = total
+    mixed_ref[...] = mixed
 
 
 def window_start(context, arrived, size, span_rows):
@@ -97,34 +89,35 @@
 
 
 def window_kernel(
-    arrived, span_rows, draft_count, context_ref, limit_ref, turned_ref, peak_ref, total_ref, mixed_ref, window_ref,
-    draft_latent_ref, new_peak_ref, new_total_ref, new_mixed_ref,
+    arrived, span_rows, draft_count, context_ref, limit_ref, draft_latent_ref, *refs
 ):
-    slot_count, size, width = window_ref.shape
-    rows = peak_ref.shape[1]
+    held_refs, (new_peak_ref, new_total_ref, new_mixed_ref) = refs[:-3], refs[-3:]
+    slot_count, rows, width = new_mixed_ref.shape
     drafts = draft_latent_ref[...]
     drafts = jnp.concatenate([drafts, jnp.zeros((128 - drafts.shape[0], width), jnp.float32)], 0).astype(jnp.bfloat16)
     token = lax.broadcasted_iota(jnp.int32, (rows, 1), 0) % draft_count
     spot = lax.broadcasted_iota(jnp.int32, (rows, 128), 1)
     for b in range(slot_count):
+        turned_ref, peak_ref, total_ref, mixed_ref, window_ref = held_refs[5 * b : 5 * b + 5]
+        size = window_ref.shape[0]
         first = window_start(context_ref[b], arrived, size, span_rows)
-        scores = join_rows(lax.dot_general(turned_ref[b], window_ref[b], NT, preferred_element_type=jnp.float32))
+        scores = join_rows(lax.dot_general(turned_ref[...], window_ref[...], NT, preferred_element_type=jnp.float32))
         column = lax.broadcasted_iota(jnp.int32, (1, size), 1) + first
         seen = (column >= context_ref[b] - arrived) & (column < limit_ref[b : b + 1, 0:1])
         scores = jnp.where(seen, scores, FAR)
-        draft_scores = join_rows(lax.dot_general(turned_ref[b], drafts, NT, preferred_element_type=jnp.float32))
+        draft_scores = join_rows(lax.dot_general(turned_ref[...], drafts, NT, preferred_element_type=jnp.float32))
         draft_seen = (spot >= b * draft_count) & (spot <= b * draft_count + token)
         draft_scores = jnp.where(draft_seen, draft_scores, FAR)
         peak = jnp.maximum(jnp.max(scores, 1, keepdims=True), jnp.max(draft_scores, 1, keepdims=True))
-        peak = jnp.maximum(peak, peak_ref[b])
+        peak = jnp.maximum(peak, peak_ref[...])
         weights, draft_weights = jnp.exp2(scores - peak), jnp.exp2(draft_scores - peak)
-        fade = jnp.exp2(peak_ref[b] - peak)
+        fade = jnp.exp2(peak_ref[...] - peak)
         new_peak_ref[b] = peak
         total = jnp.sum(weights, 1, keepdims=True) + jnp.sum(draft_weights, 1, keepdims=True)
-        new_total_ref[b] = total_ref[b] * fade + total
-        mixed = jnp.dot(split_rows(weights), window_ref[b], preferred_element_type=jnp.float32)
+        new_total_ref[b] = total_ref[...] * fade + total
+        mixed = jnp.dot(split_rows(weights), window_ref[...], preferred_element_type=jnp.float32)
         mixed += jnp.dot(split_rows(draft_weights), drafts, preferred_element_type=jnp.float32)
-        new_mixed_ref[b] = mixed_ref[b] * fade + join_rows(mixed)
+        new_mixed_ref[b] = mixed_ref[...] * fade + join_rows(mixed)
 
 
 def piece_sums(starts, spans, row_refs, refs):
@@ -139,20 +132,19 @@
 
 
 def down_kernel(starts_of, spans, first, *refs):
-    row_refs, refs, out_ref = refs[:2], refs[2:-1], refs[-1]
+    row_refs, refs, out_ref = refs[:4], refs[4:-1], refs[-1]
     total = piece_sums(starts_of(), spans, row_refs, refs)
     out_ref[...] = total if first else total + refs[-1][...]
 
 
 def down_place_kernel(starts_of, spans, *refs):
-    row_refs, refs, (keep_ref, send_ref) = refs[:2], refs[2:-2], refs[-2:]
+    row_refs, refs, (keep_ref, send_ref) = refs[:4], refs[4:-2], refs[-2:]
     place_ref, sum_ref, refs = refs[0], refs[1], refs[2:]
     total = piece_sums(starts_of(), spans, row_refs, refs) + sum_ref[...]
     slots, width = keep_ref.shape[0] - 8, keep_ref.shape[1]
     count = place_ref.shape[1]
-    mine, both = count // 2, row_refs[0].shape[0]
     parts = []
-    left = jnp.concatenate([total[:mine], total[both : both + mine]], 0)
+    left = total[:count]
     for _ in range(3):
         part = left.astype(jnp.bfloat16)
         parts.append(part)
@@ -160,7 +152,7 @@
     parts = jnp.concatenate(parts, 1)
     core = lax.axis_index("wide") % 2
     spot = lax.broadcasted_iota(jnp.int32, (slots, count), 0)
-    for ref, target, draft in ((keep_ref, core, mine), (send_ref, 1 - core, both + mine)):
+    for ref, target, draft in ((keep_ref, core, count), (send_ref, 1 - core, count + 16)):
         chosen = jnp.where(spot + target * slots == place_ref[...], 1.0, 0.0).astype(jnp.bfloat16)
         moved = jnp.dot(chosen, parts, preferred_element_type=jnp.float32)
         ref[:slots, :] = moved[:, :width] + moved[:, width : 2 * width] + moved[:, 2 * width :]
@@ -192,9 +184,7 @@
                 ref[spot : spot + size, :] = source[first + n * size : first + (n + 1) * size, :]
 
 
-def start_kernel(
-    target_hbm, shard_hbm, prompt_hbm, draft_hbm, half_ref, full_ref, target_ref, rows_ref, draft_ref, sems
-):
+def start_kernel(target_hbm, shard_hbm, draft_hbm, half_ref, full_ref, target_ref, rows_ref, draft_ref, sems):
     half_rows, shard_rows = half_ref.shape[0] - 16, full_ref.shape[0] - 16
     mine = pl.ds(pl.multiple_of(lax.axis_index("rep") * half_rows, half_rows), half_rows)
     copies = [
@@ -202,7 +192,6 @@
         pltpu.make_async_copy(shard_hbm.at[mine], half_ref.at[:half_rows], sems.at[1]),
         pltpu.make_async_copy(shard_hbm, full_ref.at[:shard_rows], sems.at[2]),
         pltpu.make_async_copy(draft_hbm, draft_ref, sems.at[3]),
-        pltpu.make_async_copy(prompt_hbm, rows_ref.at[: prompt_hbm.shape[0]], sems.at[4]),
     ]
     for copy in copies:
         copy.start()
@@ -216,9 +205,9 @@
     copies[3].wait()
     rows = [draft_ref[b].astype(jnp.float32) for b in range(draft_ref.shape[0])]
     rows.append(jnp.zeros((8, rows_ref.shape[1]), jnp.float32))
-    rows_ref[count:, :] = jnp.concatenate(rows, 0).astype(jnp.bfloat16)
-    for n in (1, 2, 4):
-        copies[n].wait()
+    rows_ref[...] = jnp.concatenate(rows, 0).astype(jnp.bfloat16)
+    for copy in copies[1:3]:
+        copy.wait()
 
 
 def join_kernel(one_ref, two_ref, *refs):
@@ -227,6 +216,12 @@
     out_ref[rows:, :] = two_ref[...]
     bare_ref[: rows - 16, :] = one_ref[: rows - 16, :]
     bare_ref[rows - 16 :, :] = two_ref[: rows - 16, :]
+
+
+def tail_kernel(one_ref, two_ref, out_ref):
+    rest = out_ref.shape[0] - two_ref.shape[0]
+    out_ref[:rest, :] = one_ref[one_ref.shape[0] - rest :, :]
+    out_ref[rest:, :] = two_ref[...]
 
 
 def copy_kernel(spans, one_ref, *refs):
@@ -289,9 +284,10 @@
     outgoing_ref[...] = jnp.dot(chosen, latent, preferred_element_type=jnp.float32).astype(jnp.bfloat16)
 
 
-def late_kernel(column_slot_ref, turned_ref, peak_ref, total_ref, mixed_ref, value_up_ref, *refs):
-    incoming_refs, (out_ref, rows_ref, parted_ref) = refs[:-3], refs[-3:]
+def late_kernel(column_slot_ref, peak_ref, total_ref, mixed_ref, value_up_ref, *refs):
+    refs, (out_ref, rows_ref, parted_ref) = refs[:-3], refs[-3:]
     slot_count, draft_count, _ = out_ref.shape
+    turned_refs, incoming_refs = refs[:slot_count], refs[slot_count:]
     heads_kv = value_up_ref.shape[1] // HEAD_SIZE
     group_size = QUERY_HEADS // heads_kv
     head_rows = group_size * draft_count
@@ -300,7 +296,7 @@
     for n, ref in enumerate(incoming_refs):
         rows_ref[n * block : (n + 1) * block, :] = ref[...]
     for b in range(slot_count):
-        scores = join_rows(lax.dot_general(turned_ref[b], rows_ref[...], NT, preferred_element_type=jnp.float32))
+        scores = join_rows(lax.dot_general(turned_refs[b][...], rows_ref[...], NT, preferred_element_type=jnp.float32))
         scores = jnp.where(column_slot_ref[...] == b, scores, FAR)
         peak = jnp.maximum(jnp.max(scores, 1, keepdims=True), peak_ref[b])
         weights = jnp.exp2(scores - peak)
@@ -355,32 +351,22 @@
     hbm = pl.BlockSpec(memory_space=pltpu.HBM)
     half_rows = shard_rows // 2
     ext = half_rows + 16
-    padded = (count + 16, prompt_hidden.shape[1])
-    half, full, target, rows = call(
+    half, full, target, draft_rows = call(
         start_kernel,
         [
             array(ext),
             array(shard_rows + 16),
             jax.ShapeDtypeStruct((1, count), jnp.int32),
-            jax.ShapeDtypeStruct(padded, bf16),
+            jax.ShapeDtypeStruct((16, draft_hidden.shape[2]), bf16),
         ],
         "start_rows",
-        *(
-            pltpu.with_memory_space_constraint(x, pltpu.HBM)
-            for x in (row_target.reshape(1, count), shard, prompt_hidden, draft_hidden)
-        ),
-        specs=[hbm] * 4,
-        scratch_shapes=[pltpu.VMEM(draft_hidden.shape, bf16), pltpu.SemaphoreType.DMA((5,))],
+        *(pltpu.with_memory_space_constraint(x, pltpu.HBM) for x in (row_target.reshape(1, count), shard, draft_hidden)),
+        specs=[hbm] * 3,
+        scratch_shapes=[pltpu.VMEM(draft_hidden.shape, bf16), pltpu.SemaphoreType.DMA((4,))],
     )
     za, zb = swap(half, z=1), swap(half, z=2)
     y0 = swap(full, y=1)
-    rows = [rows, swap(rows, c=1)]
-    zab, bare = call(
-        join_kernel, [array(2 * ext), array(2 * half_rows)], "join_pieces", za, zb, y0, rows[1], held,
-        specs=[WHOLE] * 2 + [UNREAD] * 3,
-    )
-    yab, xab = swap(zab, y=1), swap(bare, r=1)
-    zc = swap(zb, z=1)
+    other_prompt, other_drafts = swap(prompt_hidden, c=1), swap(draft_rows, c=1)
 
     def copy(x, spans, *ties):
         return call(
@@ -388,10 +374,18 @@
             specs=[WHOLE] + [UNREAD] * len(ties),
         )
 
+    held_rows = [held(b, half) for b in range(2)]
+    zab, bare = call(
+        join_kernel, [array(2 * ext), array(2 * half_rows)], "join_pieces", za, zb, y0, other_drafts,
+        *(x[1] for x in held_rows), specs=[WHOLE] * 2 + [UNREAD] * 4,
+    )
+    yab, xab = swap(zab, y=1), swap(bare, r=1)
+    zc = swap(zb, z=1)
     xc = swap(copy(zc, [(0, half_rows)]), r=1)
-    xyab = swap(copy(yab, [(0, half_rows), (ext, half_rows)]), r=1)
+    quarter = half_rows // 2
+    xy = swap(copy(yab, [(0, half_rows), (ext, quarter)]), r=1)
     yc = swap(copy(zc, [(0, ext)], yab), y=1)
-    yxc = swap(xc, y=1)
+    yx = swap(call(tail_kernel, array(quarter + half_rows), "tail_piece", xab, xc), y=1)
 
     order = [
         (half, half_rows), (y0, shard_rows), (zab, ext + half_rows), (yab, ext + half_rows),
@@ -400,8 +394,8 @@
     pack = call(
         functools.partial(pack_kernel, [(n, first) for n, (_, first) in enumerate(order)]),
         jax.ShapeDtypeStruct((16, len(order) * width + count), bf16), "pack_rows",
-        target, *(x for x, _ in order), xab, xc,
-        specs=[WHOLE] * (1 + len(order)) + [UNREAD] * 2,
+        target, *(x for x, _ in order), xab, xc, other_prompt,
+        specs=[WHOLE] * (1 + len(order)) + [UNREAD] * 3,
     )
     other_pack = swap(pack, c=1)
     limit, column_slot, place = call(
@@ -420,14 +414,16 @@
             rep, wide = lax.axis_index("rep"), lax.axis_index("wide")
             z, y, c = wide // 4, wide // 2 % 2, wide % 2
             found = []
-            for _, _, _, (x_step, z_step, y_step) in uses:
+            for _, _, _, (x_step, z_step, y_step), *further in uses:
                 owner_z = (z // 2 + z_step // 2) % 2 * 2 + (z + z_step) % 2
                 owner = (owner_z * 2 + (y + y_step) % 2) * 2 + c
-                found.append(owner * shard_rows + (0 if x_step is None else (rep + x_step) % 2 * half_rows))
+                start = owner * shard_rows + (0 if x_step is None else (rep + x_step) % 2 * half_rows)
+                found.append(start + sum(further))
             return found
 
         return starts
 
+    rows = [prompt_hidden, other_prompt, draft_rows, other_drafts]
     stages = [
         ([full, y0], [(0, 0, shard_rows, (None, 0, 0)), (1, 0, shard_rows, (None, 0, 1))]),
         (
@@ -441,13 +437,13 @@
              (1, 0, half_rows, (0, 3, 0)), (2, 0, half_rows, (0, 3, 1))],
         ),
         (
-            [xc, yxc, xyab],
-            [(0, 0, half_rows, (1, 3, 0)), (1, 0, half_rows, (1, 3, 1)),
-             (2, 0, half_rows, (1, 1, 1)), (2, half_rows, half_rows, (1, 2, 1))],
+            [xc, yx, xy],
+            [(0, 0, half_rows, (1, 3, 0)), (1, quarter, half_rows, (1, 3, 1)), (2, 0, half_rows, (1, 1, 1)),
+             (2, half_rows, quarter, (1, 2, 1)), (1, 0, quarter, (1, 2, 1), quarter)],
         ),
     ]
     sums = []
-    total_rows = 2 * padded[0]
+    total_rows = 2 * count + 32
     for n, (pieces, uses) in enumerate(stages[:-1]):
         sums = [
             call(
@@ -474,7 +470,7 @@
         stay, send = call(functools.partial(mix_kernel, 1), [block, block], "mix_rows", stay, came)
         return draft_latent, [stay, swap(send, z=1)]
 
-    return limit, column_slot, finish
+    return limit, column_slot, finish, held_rows
 
 
 def deliver_plain(prompt_hidden, draft_hidden, shard, row_target, context_len, held):
@@ -519,7 +515,7 @@
         )
         return draft_latent, [incoming.reshape(arrived, latent_width)]
 
-    return limit, column_slot, finish
+    return limit, column_slot, finish, [held(b, context_len) for b in range(slot_count)]
 
 
 def local(
@@ -547,45 +543,52 @@
         jax.ShapeDtypeStruct((slot_count, rows, 1), f32),
         jax.ShapeDtypeStruct((slot_count, rows, latent_width), f32),
     ]
-    turned, peak, total, mixed, edge = pl.pallas_call(
-        functools.partial(held_kernel, arrived),
-        out_shape=[
-            jax.ShapeDtypeStruct((slot_count, 2 * rows, latent_width), bf16),
-            *stats,
-            jax.ShapeDtypeStruct((slot_count, window, latent_width), bf16),
-        ],
-        in_specs=[SCALARS, hbm, hbm, hbm],
-        out_specs=[WHOLE] * 5,
-        scratch_shapes=[
-            pltpu.VMEM(draft_query_heads.shape, bf16),
-            pltpu.VMEM(key_up_weight.shape, bf16),
-            pltpu.VMEM(resident_latent.shape, bf16),
-            pltpu.VMEM((slot_count, rows, latent_width), f32),
-            pltpu.VMEM((rows, span_rows), f32),
-            pltpu.SemaphoreType.DMA((3,)),
-        ],
-        compiler_params=params(16),
-        cost_estimate=pl.CostEstimate(flops=2**31, bytes_accessed=2**21, transcendentals=0),
-        name="held_rows",
-    )(context_len, *(pltpu.with_memory_space_constraint(x, pltpu.HBM) for x in (draft_query_heads, key_up_weight, resident_latent)))
+    held_rows = [
+        jax.ShapeDtypeStruct((2 * rows, latent_width), bf16),
+        *(jax.ShapeDtypeStruct(x.shape[1:], f32) for x in stats),
+        jax.ShapeDtypeStruct((window, latent_width), bf16),
+    ]
+    sources = [
+        pltpu.with_memory_space_constraint(x, pltpu.HBM) for x in (draft_query_heads, key_up_weight, resident_latent)
+    ]
+
+    def held(slot, tie):
+        return pl.pallas_call(
+            functools.partial(held_kernel, slot, arrived),
+            out_shape=held_rows,
+            in_specs=[SCALARS, hbm, hbm, hbm, UNREAD],
+            out_specs=[WHOLE] * 5,
+            scratch_shapes=[
+                pltpu.VMEM(draft_query_heads.shape[1:], bf16),
+                pltpu.VMEM(key_up_weight.shape, bf16),
+                pltpu.VMEM(resident_latent.shape[1:], bf16),
+                pltpu.VMEM((rows, latent_width), f32),
+                pltpu.VMEM((rows, span_rows), f32),
+                pltpu.SemaphoreType.DMA((3,)),
+            ],
+            compiler_params=params(16),
+            cost_estimate=pl.CostEstimate(flops=2**31, bytes_accessed=2**21, transcendentals=0),
+            name="held_rows",
+        )(context_len, *sources, tie)
+
     known = wide_size == 16 and lax.axis_size("rep") == 2
-    limit, column_slot, finish = (deliver if known else deliver_plain)(
-        prompt_hidden, draft_hidden, down_weight, row_target, context_len, peak
+    limit, column_slot, finish, held = (deliver if known else deliver_plain)(
+        prompt_hidden, draft_hidden, down_weight, row_target, context_len, held
     )
     draft_latent, incoming = finish()
     peak, total, mixed = pl.pallas_call(
         functools.partial(window_kernel, arrived, span_rows, draft_count),
         out_shape=stats,
-        in_specs=[SCALARS] + [WHOLE] * 7,
+        in_specs=[SCALARS] + [WHOLE] * (2 + 5 * slot_count),
         out_specs=[WHOLE] * 3,
         compiler_params=params(16),
         cost_estimate=pl.CostEstimate(flops=2**30, bytes_accessed=2**16, transcendentals=0),
         name="window_rows",
-    )(context_len, limit, turned, peak, total, mixed, edge, draft_latent)
+    )(context_len, limit, draft_latent, *(x for one in held for x in one))
     return pl.pallas_call(
         late_kernel,
         out_shape=jax.ShapeDtypeStruct((slot_count, draft_count, QUERY_HEADS * HEAD_SIZE), bf16),
-        in_specs=[WHOLE] * (6 + len(incoming)),
+        in_specs=[WHOLE] * (5 + slot_count + len(incoming)),
         out_specs=WHOLE,
         scratch_shapes=[
             pltpu.VMEM((arrived, latent_width), bf16),
@@ -593,7 +596,7 @@
         ],
         compiler_params=params(16),
         name="late_rows",
-    )(column_slot, turned, peak, total, mixed, value_up_weight, *incoming)
+    )(column_slot, peak, total, mixed, value_up_weight, *(one[0] for one in held), *incoming)
 
 
 def solution(mesh):

time: 53.7 us -> 54.4 us (1.013)
  local copies, waits for them, and re-layouts: 0.01 us -> 2.45 us
  waiting for transfers between devices: 20.3 us -> 17.9 us
  Pallas kernels: 13.2 us -> 15.2 us
  starting transfers between devices: 19.9 us -> 18.3 us
    pallas_call x1 -> x2, Pallas kernels: 4.01 us -> 6.73 us  [held(): pl.pallas_call(functools.partial(held_kernel, slot, arrived), out_shape=h...]
    unnamed x4 -> x8, local copies, waits for them, and re-layouts: 0.01 us -> 2.45 us
    ppermute x16 -> x17, waiting for transfers between devices: 20.3 us -> 17.9 us  [swap(): return lax.ppermute(x, ('rep', 'wide'), pairs)]
    ppermute x16 -> x17, starting transfers between devices: 19.9 us -> 18.3 us  [swap(): return lax.ppermute(x, ('rep', 'wide'), pairs)]
    pallas_call x14 -> x15, Pallas kernels: 4.7 us -> 4.07 us  [call(): pl.pallas_call(kernel, out_shape=out_shape, in_specs=specs or [WHOLE] * l...]
  transfers between devices with their start and end apart: 16 -> 17, of which waited for: 10 -> 9; matrix products, arithmetic and copies ran while one was open for 0% -> 0% of each run, Pallas kernels for 15% -> 22%
where the time goes in v9:
time: 54.4 us; the launch traced here: 54.1 us
  starting transfers between devices  18.3 us (34%)
  waiting for transfers between devices  17.9 us (33%)
  Pallas kernels  15.2 us (28%)
  local copies, waits for them, and re-layouts  2.45 us (5%)
    ppermute x17, starting transfers between devices, swap(): return lax.ppermute(x, ('rep', 'wide'), pairs)  18.3 us
    ppermute x17, waiting for transfers between devices, swap(): return lax.ppermute(x, ('rep', 'wide'), pairs)  17.9 us
    pallas_call x2, Pallas kernels, held(): pl.pallas_call(functools.partial(held_kernel, slot, arrived), out_shape=h...  6.73 us
    pallas_call x15, Pallas kernels, call(): pl.pallas_call(kernel, out_shape=out_shape, in_specs=specs or [WHOLE] * l...  4.07 us
    unnamed x8, local copies, waits for them, and re-layouts  2.45 us
    pallas_call x1, Pallas kernels, local(): pl.pallas_call(late_kernel, out_shape=jax.ShapeDtypeStruct((slot_count, d...  2.23 us
    pallas_call x1, Pallas kernels, local(): pl.pallas_call(functools.partial(window_kernel, arrived, span_rows, draft...  2.21 us
  transfers between devices with their start and end apart: 17, of which 9 were waited for; matrix products, arithmetic and copies ran while one was open for 0% of the time, Pallas kernels for 22%

profile of v9, /device:TPU:0, one launch (start us, length us, event | category | flops | bytes accessed | tf_op | source)
XLA Modules:
  0.0 54.1 jit_solution(13159282942871039744)
XLA Ops:
  0.0 0.5 collective-permute-start.9
  0.5 1.1 %start_rows.1 = (bf16[272,256]{1,0:T(8,128)(2,1)S(1)}, bf16[528,256]{1,0:T(8,128)(2,1)S(1)}, s32[1,128]{1,0:T(1,128)S(1)}, bf16[16,8192]{1,0:T(8,128)(2,1)S(1)}) custom-call(s32[1,128]{1,0:T(1,128)} %bitcast.1, bf16[512,256]{1,0:T(8,128)(2,1)} %shard_hbm.1, bf16[2,4,8192]{2,1,0:T(4,128)(2,1)} %draft_hbm.1), custom_call_target="tpu_custom_call" | custom-call | flops 1048576 | bytes 65536 | tf_op jit(solution)/shard_map/start_rows/pallas_call | solution.py:340
  1.6 2.6 %collective-permute-start.1 = (bf16[272,256]{1,0:T(8,128)(2,1)S(1)}, bf16[272,256]{1,0:T(8,128)(2,1)S(1)}, u32[]{:S(2)}, u32[]{:S(2)}) collective-permute-start(bf16[272,256]{1,0:T(8,128)(2,1)S(1)} %get-tuple-element.37.tie_ref.refs_0_), channel_id=1, source_target_pairs={{0,4},{1,5},{2,6},{3,7},{4,0},{5,1},{6,2},{7,3},{8,12},{9,13},{10,... | collective-permute-start | bytes 417800 | tf_op jit(solution)/shard_map/ppermute | solution.py:334
  4.2 2.6 %collective-permute-start.2 = (bf16[272,256]{1,0:T(8,128)(2,1)S(1)}, bf16[272,256]{1,0:T(8,128)(2,1)S(1)}, u32[]{:S(2)}, u32[]{:S(2)}) collective-permute-start(bf16[272,256]{1,0:T(8,128)(2,1)S(1)} %get-tuple-element.37.tie_ref.refs_0_), channel_id=1, source_target_pairs={{0,8},{1,9},{2,10},{3,11},{4,12},{5,13},{6,14},{7,15},{8,0},{9,1},... | collective-permute-start | bytes 417800 | tf_op jit(solution)/shard_map/ppermute | solution.py:334
  6.8 1.5 %collective-permute-start = (bf16[528,256]{1,0:T(8,128)(2,1)S(1)}, bf16[528,256]{1,0:T(8,128)(2,1)S(1)}, u32[]{:S(2)}, u32[]{:S(2)}) collective-permute-start(bf16[528,256]{1,0:T(8,128)(2,1)S(1)} %get-tuple-element.38.refs_4_), channel_id=1, source_target_pairs={{0,2},{1,3},{2,0},{3,1},{4,6},{5,7},{6,4},{7,5},{8,10},{9,11},{10,... | collective-permute-start | bytes 811016 | tf_op jit(solution)/shard_map/ppermute | solution.py:334
  8.3 0.7 %copy-done.2 = s32[2]{0:T(128)S(1)} copy-done((s32[2]{0:T(128)S(1)}, s32[2]{0:T(128)}, u32[]{:S(2)}) %copy-start.2) | copy-done | bytes 32
  9.0 3.4 %held_rows.2 = (bf16[512,256]{1,0:T(8,128)(2,1)S(1)}, f32[256,1]{1,0:T(8,128)S(1)}, f32[256,1]{1,0:T(8,128)S(1)}, f32[256,256]{1,0:T(8,128)S(1)}, bf16[384,256]{1,0:T(8,128)(2,1)S(1)}) custom-call(s32[2]{0:T(128)S(1)} %copy-done.2, bf16[2,4,8192]{2,1,0:T(4,128)(2,1)} %query_hbm.3, bf16[256,1024]{1,0:T(8,128)(2,1)} %key_up_hbm.3, ...), custom_call_target="tpu_custom_call" | custom-call | flops 2147483648 | bytes 2097152 | tf_op jit(solution)/shard_map/held_rows/pallas_call | solution.py:556
  12.4 3.4 %held_rows.3 = (bf16[512,256]{1,0:T(8,128)(2,1)S(1)}, f32[256,1]{1,0:T(8,128)S(1)}, f32[256,1]{1,0:T(8,128)S(1)}, f32[256,256]{1,0:T(8,128)S(1)}, bf16[384,256]{1,0:T(8,128)(2,1)S(1)}) custom-call(s32[2]{0:T(128)S(1)} %copy-done.2, bf16[2,4,8192]{2,1,0:T(4,128)(2,1)} %query_hbm.3, bf16[256,1024]{1,0:T(8,128)(2,1)} %key_up_hbm.3, ...), custom_call_target="tpu_custom_call" | custom-call | flops 2147483648 | bytes 2097152 | tf_op jit(solution)/shard_map/held_rows/pallas_call | solution.py:556
  15.8 0.9 %collective-permute-start.4 = (bf16[544,256]{1,0:T(8,128)(2,1)S(1)}, bf16[544,256]{1,0:T(8,128)(2,1)S(1)}, u32[]{:S(2)}, u32[]{:S(2)}) collective-permute-start(bf16[544,256]{1,0:T(8,128)(2,1)S(1)} %get-tuple-element.42.refs_2_.refs_4_), channel_id=1, source_target_pairs={{0,2},{1,3},{2,0},{3,1},{4,6},{5,7},{6,4},{7,5},{8,10},{9,11},{10,... | collective-permute-start | bytes 835592 | tf_op jit(solution)/shard_map/ppermute | solution.py:334
  16.8 0.4 collective-permute-start.5
  17.2 1.5 %collective-permute-start.7 = (bf16[512,256]{1,0:T(8,128)(2,1)S(1)}, bf16[512,256]{1,0:T(8,128)(2,1)S(1)}, u32[]{:S(2)}, u32[]{:S(2)}) collective-permute-start(bf16[512,256]{1,0:T(8,128)(2,1)S(1)} %get-tuple-element.43), channel_id=1, source_target_pairs={{0,16},{1,17},{2,18},{3,19},{4,20},{5,21},{6,22},{7,23},{8,24},{9,... | collective-permute-start | bytes 786440 | tf_op jit(solution)/shard_map/ppermute | solution.py:334
  18.7 3.5 %collective-permute-done.5.one_ref.refs_6_.refs_5_ = bf16[272,256]{1,0:T(8,128)(2,1)S(1)} collective-permute-done((bf16[272,256]{1,0:T(8,128)(2,1)S(1)}, bf16[272,256]{1,0:T(8,128)(2,1)S(1)}, u32[]{:S(2)}, u32[]{:S(2)}) %collective-permute-start.5) | collective-permute-done | bytes 139296 | tf_op jit(solution)/shard_map/ppermute | solution.py:334
  22.2 1.6 %collective-permute-start.8 = (bf16[256,256]{1,0:T(8,128)(2,1)S(1)}, bf16[256,256]{1,0:T(8,128)(2,1)S(1)}, u32[]{:S(2)}, u32[]{:S(2)}) collective-permute-start(bf16[256,256]{1,0:T(8,128)(2,1)S(1)} %copy_piece.4), channel_id=1, source_target_pairs={{0,16},{1,17},{2,18},{3,19},{4,20},{5,21},{6,22},{7,23},{8,24},{9,... | collective-permute-start | bytes 393224 | tf_op jit(solution)/shard_map/ppermute | solution.py:334
  23.8 1.2 %collective-permute-done.4.refs_0_.refs_3_.refs_5_.one_ref = bf16[544,256]{1,0:T(8,128)(2,1)S(1)} collective-permute-done((bf16[544,256]{1,0:T(8,128)(2,1)S(1)}, bf16[544,256]{1,0:T(8,128)(2,1)S(1)}, u32[]{:S(2)}, u32[]{:S(2)}) %collective-permute-start.4) | collective-permute-done | bytes 278560 | tf_op jit(solution)/shard_map/ppermute | solution.py:334
  25.0 0.6 %collective-permute-start.6 = (bf16[272,256]{1,0:T(8,128)(2,1)S(1)}, bf16[272,256]{1,0:T(8,128)(2,1)S(1)}, u32[]{:S(2)}, u32[]{:S(2)}) collective-permute-start(bf16[272,256]{1,0:T(8,128)(2,1)S(1)} %copy_piece.3), channel_id=1, source_target_pairs={{0,2},{1,3},{2,0},{3,1},{4,6},{5,7},{6,4},{7,5},{8,10},{9,11},{10,... | collective-permute-start | bytes 417800 | tf_op jit(solution)/shard_map/ppermute | solution.py:334
  25.6 2.3 %collective-permute-done.8.refs_9_.two_ref.refs_6_ = bf16[256,256]{1,0:T(8,128)(2,1)S(1)} collective-permute-done((bf16[256,256]{1,0:T(8,128)(2,1)S(1)}, bf16[256,256]{1,0:T(8,128)(2,1)S(1)}, u32[]{:S(2)}, u32[]{:S(2)}) %collective-permute-start.8) | collective-permute-done | bytes 131104 | tf_op jit(solution)/shard_map/ppermute | solution.py:334
  27.8 1.6 %collective-permute-start.11 = (bf16[384,256]{1,0:T(8,128)(2,1)S(1)}, bf16[384,256]{1,0:T(8,128)(2,1)S(1)}, u32[]{:S(2)}, u32[]{:S(2)}) collective-permute-start(bf16[384,256]{1,0:T(8,128)(2,1)S(1)} %tail_piece.1), channel_id=1, source_target_pairs={{0,2},{1,3},{2,0},{3,1},{4,6},{5,7},{6,4},{7,5},{8,10},{9,11},{10,... | collective-permute-start | bytes 589832 | tf_op jit(solution)/shard_map/ppermute | solution.py:334
  29.4 1.6 %collective-permute-start.12 = (bf16[384,256]{1,0:T(8,128)(2,1)S(1)}, bf16[384,256]{1,0:T(8,128)(2,1)S(1)}, u32[]{:S(2)}, u32[]{:S(2)}) collective-permute-start(bf16[384,256]{1,0:T(8,128)(2,1)S(1)} %copy_piece.5), channel_id=1, source_target_pairs={{0,16},{1,17},{2,18},{3,19},{4,20},{5,21},{6,22},{7,23},{8,24},{9,... | collective-permute-start | bytes 589832 | tf_op jit(solution)/shard_map/ppermute | solution.py:334
  31.3 1.5 %copy-done = bf16[128,8192]{1,0:T(8,128)(2,1)S(1)} copy-done((bf16[128,8192]{1,0:T(8,128)(2,1)S(1)}, bf16[128,8192]{1,0:T(8,128)(2,1)}, u32[]{:S(2)}) %copy-start) | copy-done | bytes 2097176
  33.1 0.4 down_rows.4.refs_7_
  33.5 0.3 down_rows.5.refs_5_
  34.1 0.7 %count_rows.1 = (s32[2,128]{1,0:T(2,128)S(1)}, s32[1,256]{1,0:T(1,128)S(1)}, s32[1,256]{1,0:T(1,128)S(1)}) custom-call(s32[2]{0:T(128)S(1)} %copy-done.3, bf16[16,2176]{1,0:T(8,128)(2,1)S(1)} %pack_rows.1.mine_ref, bf16[16,2176]{1,0:T(8,128)(2,1)S(1)} %collective-permute-done.10.other_ref), custom_call_target="tpu_custom_call" | custom-call | flops 1048576 | bytes 65536 | tf_op jit(solution)/shard_map/count_rows/pallas_call | solution.py:340
  34.9 0.4 collective-permute-done.12.refs_8_
  35.3 1.0 %down_place_rows.1 = (f32[264,256]{1,0:T(8,128)S(1)}, f32[264,256]{1,0:T(8,128)S(1)}) custom-call(bf16[128,8192]{1,0:T(8,128)(2,1)S(1)} %copy-done, bf16[128,8192]{1,0:T(8,128)(2,1)S(1)} %collective-permute-done.9.refs_10_.refs_1_, bf16[16,8192]{1,0:T(8,128)(2,1)S(1)} %get-tuple-element.39.refs_2_, ...), custom_call_target="tpu_custom_call" | custom-call | flops 67108864 | bytes 65536 | tf_op jit(solution)/shard_map/down_place_rows/pallas_call | solution.py:340
  36.4 1.5 %collective-permute-done.13.came_ref = f32[264,256]{1,0:T(8,128)S(1)} collective-permute-done((f32[264,256]{1,0:T(8,128)S(1)}, f32[264,256]{1,0:T(8,128)S(1)}, u32[]{:S(2)}, u32[]{:S(2)}) %collective-permute-start.13) | collective-permute-done | bytes 270368 | tf_op jit(solution)/shard_map/ppermute | solution.py:334
  38.0 0.5 collective-permute-start.14
  38.5 3.8 %collective-permute-done.14.came_ref = bf16[128,256]{1,0:T(8,128)(2,1)S(1)} collective-permute-done((bf16[128,256]{1,0:T(8,128)(2,1)S(1)}, bf16[128,256]{1,0:T(8,128)(2,1)S(1)}, u32[]{:S(2)}, u32[]{:S(2)}) %collective-permute-start.14) | collective-permute-done | bytes 65568 | tf_op jit(solution)/shard_map/ppermute | solution.py:334
  42.3 0.4 collective-permute-start.15
  42.7 4.8 %collective-permute-done.15.came_ref = bf16[128,256]{1,0:T(8,128)(2,1)S(1)} collective-permute-done((bf16[128,256]{1,0:T(8,128)(2,1)S(1)}, bf16[128,256]{1,0:T(8,128)(2,1)S(1)}, u32[]{:S(2)}, u32[]{:S(2)}) %collective-permute-start.15) | collective-permute-done | bytes 65568 | tf_op jit(solution)/shard_map/ppermute | solution.py:334
  47.6 1.9 %collective-permute-start.16 = (bf16[128,256]{1,0:T(8,128)(2,1)S(1)}, bf16[128,256]{1,0:T(8,128)(2,1)S(1)}, u32[]{:S(2)}, u32[]{:S(2)}) collective-permute-start(bf16[128,256]{1,0:T(8,128)(2,1)S(1)} %get-tuple-element.66), channel_id=1, source_target_pairs={{0,4},{1,5},{2,6},{3,7},{4,0},{5,1},{6,2},{7,3},{8,12},{9,13},{10,... | collective-permute-start | bytes 196616 | tf_op jit(solution)/shard_map/ppermute | solution.py:334
  49.5 2.2 %window_rows.1 = (f32[2,256,1]{2,1,0:T(8,128)S(1)}, f32[2,256,1]{2,1,0:T(8,128)S(1)}, f32[2,256,256]{2,1,0:T(8,128)S(1)}) custom-call(s32[2]{0:T(128)S(1)} %copy-done.3, s32[2,128]{1,0:T(2,128)S(1)} %get-tuple-element.45.limit_ref, f32[8,256]{1,0:T(8,128)S(1)} %get-tuple-element.49.draft_latent_ref, bf16[512,256]{1,0:T(8,128)(2,1)S(1)} %get-tuple-element.50.refs_0_, ...), custom_call_target="tpu_custom_call" | custom-call | flops 1073741824 | bytes 65536 | tf_op jit(solution)/shard_map/window_rows/pallas_call | solution.py:579
  51.9 2.2 %late_rows.1 = bf16[2,4,8192]{2,1,0:T(4,128)(2,1)} custom-call(s32[1,256]{1,0:T(1,128)S(1)} %get-tuple-element.44.column_slot_ref, f32[2,256,1]{2,1,0:T(8,128)S(1)} %get-tuple-element.58.peak_ref, f32[2,256,1]{2,1,0:T(8,128)S(1)} %get-tuple-element.59.total_ref, f32[2,256,256]{2,1,0:T(8,128)S(1)} %get-tuple-element.60.mixed_ref, ...), custom_call_target="tpu_custom_call" | custom-call | tf_op jit(solution)/shard_map/late_rows/pallas_call | solution.py:588
  (29 shorter events, 1.3 us)
Async XLA Ops:
  0.0 31.2 %collective-permute-start.9 = (bf16[128,8192]{1,0:T(8,128)(2,1)}, bf16[128,8192]{1,0:T(8,128)(2,1)S(1)}, u32[]{:S(2)}, u32[]{:S(2)}) collective-permute-start(bf16[128,8192]{1,0:T(8,128)(2,1)} %refs_0_.7), channel_id=1, source_target_pairs={{0,1},{1,0},{2,3},{3,2},{4,5},{5,4},{6,7},{7,6},{8,9},{9,8},{10,11... | collective-permute-start | bytes 6291464 | tf_op jit(solution)/shard_map/ppermute | solution.py:334
  1.6 14.2 %collective-permute-start.1 = (bf16[272,256]{1,0:T(8,128)(2,1)S(1)}, bf16[272,256]{1,0:T(8,128)(2,1)S(1)}, u32[]{:S(2)}, u32[]{:S(2)}) collective-permute-start(bf16[272,256]{1,0:T(8,128)(2,1)S(1)} %get-tuple-element.37.tie_ref.refs_0_), channel_id=1, source_target_pairs={{0,4},{1,5},{2,6},{3,7},{4,0},{5,1},{6,2},{7,3},{8,12},{9,13},{10,... | collective-permute-start | bytes 417800 | tf_op jit(solution)/shard_map/ppermute | solution.py:334
  4.2 11.5 %collective-permute-start.2 = (bf16[272,256]{1,0:T(8,128)(2,1)S(1)}, bf16[272,256]{1,0:T(8,128)(2,1)S(1)}, u32[]{:S(2)}, u32[]{:S(2)}) collective-permute-start(bf16[272,256]{1,0:T(8,128)(2,1)S(1)} %get-tuple-element.37.tie_ref.refs_0_), channel_id=1, source_target_pairs={{0,8},{1,9},{2,10},{3,11},{4,12},{5,13},{6,14},{7,15},{8,0},{9,1},... | collective-permute-start | bytes 417800 | tf_op jit(solution)/shard_map/ppermute | solution.py:334
  6.8 9.0 %collective-permute-start = (bf16[528,256]{1,0:T(8,128)(2,1)S(1)}, bf16[528,256]{1,0:T(8,128)(2,1)S(1)}, u32[]{:S(2)}, u32[]{:S(2)}) collective-permute-start(bf16[528,256]{1,0:T(8,128)(2,1)S(1)} %get-tuple-element.38.refs_4_), channel_id=1, source_target_pairs={{0,2},{1,3},{2,0},{3,1},{4,6},{5,7},{6,4},{7,5},{8,10},{9,11},{10,... | collective-permute-start | bytes 811016 | tf_op jit(solution)/shard_map/ppermute | solution.py:334
  8.3 7.4 %collective-permute-start.3 = (bf16[16,8192]{1,0:T(8,128)(2,1)S(1)}, bf16[16,8192]{1,0:T(8,128)(2,1)S(1)}, u32[]{:S(2)}, u32[]{:S(2)}) collective-permute-start(bf16[16,8192]{1,0:T(8,128)(2,1)S(1)} %get-tuple-element.39.refs_2_), channel_id=1, source_target_pairs={{0,1},{1,0},{2,3},{3,2},{4,5},{5,4},{6,7},{7,6},{8,9},{9,8},{10,11... | collective-permute-start | bytes 786440 | tf_op jit(solution)/shard_map/ppermute | solution.py:334
  8.3 0.7 %copy-start.2 = (s32[2]{0:T(128)S(1)}, s32[2]{0:T(128)}, u32[]{:S(2)}) copy-start(s32[2]{0:T(128)} %context_ref.7) | copy-start | bytes 28
  15.8 9.1 %collective-permute-start.4 = (bf16[544,256]{1,0:T(8,128)(2,1)S(1)}, bf16[544,256]{1,0:T(8,128)(2,1)S(1)}, u32[]{:S(2)}, u32[]{:S(2)}) collective-permute-start(bf16[544,256]{1,0:T(8,128)(2,1)S(1)} %get-tuple-element.42.refs_2_.refs_4_), channel_id=1, source_target_pairs={{0,2},{1,3},{2,0},{3,1},{4,6},{5,7},{6,4},{7,5},{8,10},{9,11},{10,... | collective-permute-start | bytes 835592 | tf_op jit(solution)/shard_map/ppermute | solution.py:334
  16.8 5.4 %collective-permute-start.5 = (bf16[272,256]{1,0:T(8,128)(2,1)S(1)}, bf16[272,256]{1,0:T(8,128)(2,1)S(1)}, u32[]{:S(2)}, u32[]{:S(2)}) collective-permute-start(bf16[272,256]{1,0:T(8,128)(2,1)S(1)} %collective-permute-done.2.two_ref), channel_id=1, source_target_pairs={{0,4},{1,5},{2,6},{3,7},{4,0},{5,1},{6,2},{7,3},{8,12},{9,13},{10,... | collective-permute-start | bytes 417800 | tf_op jit(solution)/shard_map/ppermute | solution.py:334
  17.2 10.6 %collective-permute-start.7 = (bf16[512,256]{1,0:T(8,128)(2,1)S(1)}, bf16[512,256]{1,0:T(8,128)(2,1)S(1)}, u32[]{:S(2)}, u32[]{:S(2)}) collective-permute-start(bf16[512,256]{1,0:T(8,128)(2,1)S(1)} %get-tuple-element.43), channel_id=1, source_target_pairs={{0,16},{1,17},{2,18},{3,19},{4,20},{5,21},{6,22},{7,23},{8,24},{9,... | collective-permute-start | bytes 786440 | tf_op jit(solution)/shard_map/ppermute | solution.py:334
  22.2 5.6 %collective-permute-start.8 = (bf16[256,256]{1,0:T(8,128)(2,1)S(1)}, bf16[256,256]{1,0:T(8,128)(2,1)S(1)}, u32[]{:S(2)}, u32[]{:S(2)}) collective-permute-start(bf16[256,256]{1,0:T(8,128)(2,1)S(1)} %copy_piece.4), channel_id=1, source_target_pairs={{0,16},{1,17},{2,18},{3,19},{4,20},{5,21},{6,22},{7,23},{8,24},{9,... | collective-permute-start | bytes 393224 | tf_op jit(solution)/shard_map/ppermute | solution.py:334
  25.0 6.2 %collective-permute-start.6 = (bf16[272,256]{1,0:T(8,128)(2,1)S(1)}, bf16[272,256]{1,0:T(8,128)(2,1)S(1)}, u32[]{:S(2)}, u32[]{:S(2)}) collective-permute-start(bf16[272,256]{1,0:T(8,128)(2,1)S(1)} %copy_piece.3), channel_id=1, source_target_pairs={{0,2},{1,3},{2,0},{3,1},{4,6},{5,7},{6,4},{7,5},{8,10},{9,11},{10,... | collective-permute-start | bytes 417800 | tf_op jit(solution)/shard_map/ppermute | solution.py:334
  27.8 7.0 %collective-permute-start.11 = (bf16[384,256]{1,0:T(8,128)(2,1)S(1)}, bf16[384,256]{1,0:T(8,128)(2,1)S(1)}, u32[]{:S(2)}, u32[]{:S(2)}) collective-permute-start(bf16[384,256]{1,0:T(8,128)(2,1)S(1)} %tail_piece.1), channel_id=1, source_target_pairs={{0,2},{1,3},{2,0},{3,1},{4,6},{5,7},{6,4},{7,5},{8,10},{9,11},{10,... | collective-permute-start | bytes 589832 | tf_op jit(solution)/shard_map/ppermute | solution.py:334
  29.4 5.8 %collective-permute-start.12 = (bf16[384,256]{1,0:T(8,128)(2,1)S(1)}, bf16[384,256]{1,0:T(8,128)(2,1)S(1)}, u32[]{:S(2)}, u32[]{:S(2)}) collective-permute-start(bf16[384,256]{1,0:T(8,128)(2,1)S(1)} %copy_piece.5), channel_id=1, source_target_pairs={{0,16},{1,17},{2,18},{3,19},{4,20},{5,21},{6,22},{7,23},{8,24},{9,... | collective-permute-start | bytes 589832 | tf_op jit(solution)/shard_map/ppermute | solution.py:334
  31.2 1.6 %copy-start = (bf16[128,8192]{1,0:T(8,128)(2,1)S(1)}, bf16[128,8192]{1,0:T(8,128)(2,1)}, u32[]{:S(2)}) copy-start(bf16[128,8192]{1,0:T(8,128)(2,1)} %refs_0_.7) | copy-start | bytes 6291460
  31.2 2.7 %collective-permute-start.10 = (bf16[16,2176]{1,0:T(8,128)(2,1)S(1)}, bf16[16,2176]{1,0:T(8,128)(2,1)S(1)}, u32[]{:S(2)}, u32[]{:S(2)}) collective-permute-start(bf16[16,2176]{1,0:T(8,128)(2,1)S(1)} %pack_rows.1.mine_ref), channel_id=1, source_target_pairs={{0,1},{1,0},{2,3},{3,2},{4,5},{5,4},{6,7},{7,6},{8,9},{9,8},{10,11... | collective-permute-start | bytes 208904 | tf_op jit(solution)/shard_map/ppermute | solution.py:334
  33.5 0.7 %copy-start.3 = (s32[2]{0:T(128)S(1)}, s32[2]{0:T(128)}, u32[]{:S(2)}) copy-start(s32[2]{0:T(128)} %context_ref.7) | copy-start | bytes 28
  36.3 1.6 %collective-permute-start.13 = (f32[264,256]{1,0:T(8,128)S(1)}, f32[264,256]{1,0:T(8,128)S(1)}, u32[]{:S(2)}, u32[]{:S(2)}) collective-permute-start(f32[264,256]{1,0:T(8,128)S(1)} %get-tuple-element.48), channel_id=1, source_target_pairs={{0,1},{1,0},{2,3},{3,2},{4,5},{5,4},{6,7},{7,6},{8,9},{9,8},{10,11... | collective-permute-start | bytes 811016 | tf_op jit(solution)/shard_map/ppermute | solution.py:334
  38.0 4.3 %collective-permute-start.14 = (bf16[128,256]{1,0:T(8,128)(2,1)S(1)}, bf16[128,256]{1,0:T(8,128)(2,1)S(1)}, u32[]{:S(2)}, u32[]{:S(2)}) collective-permute-start(bf16[128,256]{1,0:T(8,128)(2,1)S(1)} %get-tuple-element.62), channel_id=1, source_target_pairs={{0,2},{1,3},{2,0},{3,1},{4,6},{5,7},{6,4},{7,5},{8,10},{9,11},{10,... | collective-permute-start | bytes 196616 | tf_op jit(solution)/shard_map/ppermute | solution.py:334
  42.3 9.6 %copy-start.1 = (bf16[256,1024]{1,0:T(8,128)(2,1)S(1)}, bf16[256,1024]{1,0:T(8,128)(2,1)}, u32[]{:S(2)}) copy-start(bf16[256,1024]{1,0:T(8,128)(2,1)} %value_up_ref.1) | copy-start | bytes 1572868
  42.3 5.2 %collective-permute-start.15 = (bf16[128,256]{1,0:T(8,128)(2,1)S(1)}, bf16[128,256]{1,0:T(8,128)(2,1)S(1)}, u32[]{:S(2)}, u32[]{:S(2)}) collective-permute-start(bf16[128,256]{1,0:T(8,128)(2,1)S(1)} %get-tuple-element.64), channel_id=1, source_target_pairs={{0,8},{1,9},{2,10},{3,11},{4,12},{5,13},{6,14},{7,15},{8,0},{9,1},... | collective-permute-start | bytes 196616 | tf_op jit(solution)/shard_map/ppermute | solution.py:334
  47.6 4.3 %collective-permute-start.16 = (bf16[128,256]{1,0:T(8,128)(2,1)S(1)}, bf16[128,256]{1,0:T(8,128)(2,1)S(1)}, u32[]{:S(2)}, u32[]{:S(2)}) collective-permute-start(bf16[128,256]{1,0:T(8,128)(2,1)S(1)} %get-tuple-element.66), channel_id=1, source_target_pairs={{0,4},{1,5},{2,6},{3,7},{4,0},{5,1},{6,2},{7,3},{8,12},{9,13},{10,... | collective-permute-start | bytes 196616 | tf_op jit(solution)/shard_map/ppermute | solution.py:334

commit v10 on v8

--- a/solution.py
+++ b/solution.py
@@ -139,20 +139,19 @@
 
 
 def down_kernel(starts_of, spans, first, *refs):
-    row_refs, refs, out_ref = refs[:2], refs[2:-1], refs[-1]
+    row_refs, refs, out_ref = refs[:4], refs[4:-1], refs[-1]
     total = piece_sums(starts_of(), spans, row_refs, refs)
     out_ref[...] = total if first else total + refs[-1][...]
 
 
 def down_place_kernel(starts_of, spans, *refs):
-    row_refs, refs, (keep_ref, send_ref) = refs[:2], refs[2:-2], refs[-2:]
+    row_refs, refs, (keep_ref, send_ref) = refs[:4], refs[4:-2], refs[-2:]
     place_ref, sum_ref, refs = refs[0], refs[1], refs[2:]
     total = piece_sums(starts_of(), spans, row_refs, refs) + sum_ref[...]
     slots, width = keep_ref.shape[0] - 8, keep_ref.shape[1]
     count = place_ref.shape[1]
-    mine, both = count // 2, row_refs[0].shape[0]
     parts = []
-    left = jnp.concatenate([total[:mine], total[both : both + mine]], 0)
+    left = total[:count]
     for _ in range(3):
         part = left.astype(jnp.bfloat16)
         parts.append(part)
@@ -160,7 +159,7 @@
     parts = jnp.concatenate(parts, 1)
     core = lax.axis_index("wide") % 2
     spot = lax.broadcasted_iota(jnp.int32, (slots, count), 0)
-    for ref, target, draft in ((keep_ref, core, mine), (send_ref, 1 - core, both + mine)):
+    for ref, target, draft in ((keep_ref, core, count), (send_ref, 1 - core, count + 16)):
         chosen = jnp.where(spot + target * slots == place_ref[...], 1.0, 0.0).astype(jnp.bfloat16)
         moved = jnp.dot(chosen, parts, preferred_element_type=jnp.float32)
         ref[:slots, :] = moved[:, :width] + moved[:, width : 2 * width] + moved[:, 2 * width :]
@@ -192,9 +191,7 @@
                 ref[spot : spot + size, :] = source[first + n * size : first + (n + 1) * size, :]
 
 
-def start_kernel(
-    target_hbm, shard_hbm, prompt_hbm, draft_hbm, half_ref, full_ref, target_ref, rows_ref, draft_ref, sems
-):
+def start_kernel(target_hbm, shard_hbm, draft_hbm, half_ref, full_ref, rows_ref, target_ref, draft_ref, sems):
     half_rows, shard_rows = half_ref.shape[0] - 16, full_ref.shape[0] - 16
     mine = pl.ds(pl.multiple_of(lax.axis_index("rep") * half_rows, half_rows), half_rows)
     copies = [
@@ -202,7 +199,6 @@
         pltpu.make_async_copy(shard_hbm.at[mine], half_ref.at[:half_rows], sems.at[1]),
         pltpu.make_async_copy(shard_hbm, full_ref.at[:shard_rows], sems.at[2]),
         pltpu.make_async_copy(draft_hbm, draft_ref, sems.at[3]),
-        pltpu.make_async_copy(prompt_hbm, rows_ref.at[: prompt_hbm.shape[0]], sems.at[4]),
     ]
     for copy in copies:
         copy.start()
@@ -215,10 +211,11 @@
     full_ref[shard_rows:, :] = block.astype(jnp.bfloat16)
     copies[3].wait()
     rows = [draft_ref[b].astype(jnp.float32) for b in range(draft_ref.shape[0])]
-    rows.append(jnp.zeros((8, rows_ref.shape[1]), jnp.float32))
-    rows_ref[count:, :] = jnp.concatenate(rows, 0).astype(jnp.bfloat16)
-    for n in (1, 2, 4):
-        copies[n].wait()
+    target = jnp.broadcast_to(target_ref[...].astype(jnp.float32), (8, count))
+    rows.append(jnp.concatenate([target, jnp.zeros((8, rows_ref.shape[1] - count), jnp.float32)], 1))
+    rows_ref[...] = jnp.concatenate(rows, 0).astype(jnp.bfloat16)
+    for copy in copies[1:3]:
+        copy.wait()
 
 
 def join_kernel(one_ref, two_ref, *refs):
@@ -229,6 +226,12 @@
     bare_ref[rows - 16 :, :] = two_ref[: rows - 16, :]
 
 
+def append_kernel(one_ref, two_ref, out_ref):
+    rows = one_ref.shape[0]
+    out_ref[:rows, :] = one_ref[...]
+    out_ref[rows:, :] = two_ref[...]
+
+
 def copy_kernel(spans, one_ref, *refs):
     done = 0
     for first, count in spans:
@@ -236,17 +239,21 @@
         done += count
 
 
-def pack_kernel(spans, target_ref, *refs):
+def other_half_kernel(shard_ref, out_ref):
+    rows = out_ref.shape[0]
+    first = pl.multiple_of((1 - lax.axis_index("rep")) * rows, rows)
+    out_ref[...] = shard_ref[pl.ds(first, rows), :]
+
+
+def pack_kernel(spans, *refs):
     out_ref, width = refs[-1], refs[0].shape[1]
     for m, (n, first) in enumerate(spans):
         out_ref[:, m * width : (m + 1) * width] = refs[n][first : first + 16, :]
-    target = jnp.broadcast_to(target_ref[...].astype(jnp.float32), (16, target_ref.shape[1]))
-    out_ref[:, len(spans) * width :] = target.astype(jnp.bfloat16)
-
-
-def count_kernel(most_rows, context_ref, mine_ref, other_ref, limit_ref, column_slot_ref, place_ref):
-    f32, bf16 = jnp.float32, jnp.bfloat16
-    count, width = place_ref.shape[1] // 2, 256
+
+
+def count_kernel(most_rows, context_ref, mine_ref, other_ref, limit_ref, column_slot_ref):
+    f32 = jnp.float32
+    width = mine_ref.shape[1] // 8
     wide = lax.axis_index("wide")
     core = wide % 2
     mine, other = mine_ref[...].astype(f32), other_ref[...].astype(f32)
@@ -266,10 +273,16 @@
         spread.append(jnp.sum(jnp.where(lane // most_rows == row, number, 0.0), 0, keepdims=True).astype(jnp.int32))
     spot = lax.broadcasted_iota(jnp.int32, column_slot_ref.shape, 1) % most_rows
     column_slot_ref[...] = jnp.where(spot < spread[0], 0, jnp.where(spot >= most_rows - spread[1], 1, -1))
+
+
+def place_kernel(most_rows, mine_ref, other_ref, place_ref):
+    f32, bf16 = jnp.float32, jnp.bfloat16
+    count = place_ref.shape[1] // 2
+    core = lax.axis_index("wide") % 2
     earlier = lax.broadcasted_iota(jnp.int32, (count, count), 0) < lax.broadcasted_iota(jnp.int32, (count, count), 1)
     earlier = jnp.where(earlier, 1.0, 0.0).astype(bf16)
-    for n, (rows, owner) in enumerate(((mine, core), (other, 1 - core))):
-        target = rows[:1, 8 * width : 8 * width + count].astype(jnp.int32)
+    for n, (ref, owner) in enumerate(((mine_ref, core), (other_ref, 1 - core))):
+        target = ref[:, :count].astype(f32)[8:9].astype(jnp.int32)
         hit = jnp.where(lax.broadcasted_iota(jnp.int32, (64, count), 0) == target, 1.0, 0.0)
         before = jnp.dot(hit.astype(bf16), earlier, preferred_element_type=f32)
         rank = jnp.sum(hit * before, 0, keepdims=True).astype(jnp.int32)
@@ -355,32 +368,23 @@
     hbm = pl.BlockSpec(memory_space=pltpu.HBM)
     half_rows = shard_rows // 2
     ext = half_rows + 16
-    padded = (count + 16, prompt_hidden.shape[1])
-    half, full, target, rows = call(
+    half, full, draft_rows = call(
         start_kernel,
         [
             array(ext),
             array(shard_rows + 16),
-            jax.ShapeDtypeStruct((1, count), jnp.int32),
-            jax.ShapeDtypeStruct(padded, bf16),
+            jax.ShapeDtypeStruct((16, draft_hidden.shape[2]), bf16),
         ],
         "start_rows",
-        *(
-            pltpu.with_memory_space_constraint(x, pltpu.HBM)
-            for x in (row_target.reshape(1, count), shard, prompt_hidden, draft_hidden)
-        ),
-        specs=[hbm] * 4,
-        scratch_shapes=[pltpu.VMEM(draft_hidden.shape, bf16), pltpu.SemaphoreType.DMA((5,))],
+        *(pltpu.with_memory_space_constraint(x, pltpu.HBM) for x in (row_target.reshape(1, count), shard, draft_hidden)),
+        specs=[hbm] * 3,
+        scratch_shapes=[
+            pltpu.VMEM((1, count), jnp.int32), pltpu.VMEM(draft_hidden.shape, bf16), pltpu.SemaphoreType.DMA((4,))
+        ],
     )
     za, zb = swap(half, z=1), swap(half, z=2)
     y0 = swap(full, y=1)
-    rows = [rows, swap(rows, c=1)]
-    zab, bare = call(
-        join_kernel, [array(2 * ext), array(2 * half_rows)], "join_pieces", za, zb, y0, rows[1], held,
-        specs=[WHOLE] * 2 + [UNREAD] * 3,
-    )
-    yab, xab = swap(zab, y=1), swap(bare, r=1)
-    zc = swap(zb, z=1)
+    other_prompt, other_drafts = swap(prompt_hidden, c=1), swap(draft_rows, c=1)
 
     def copy(x, spans, *ties):
         return call(
@@ -388,31 +392,36 @@
             specs=[WHOLE] + [UNREAD] * len(ties),
         )
 
-    xc = swap(copy(zc, [(0, half_rows)]), r=1)
-    xyab = swap(copy(yab, [(0, half_rows), (ext, half_rows)]), r=1)
-    yc = swap(copy(zc, [(0, ext)], yab), y=1)
-    yxc = swap(xc, y=1)
+    rest = call(other_half_kernel, array(half_rows), "other_half", y0)
+    db = swap(rest, z=2)
+    zab, bare = call(
+        join_kernel, [array(2 * ext), array(2 * half_rows)], "join_pieces", za, zb, other_drafts, held,
+        specs=[WHOLE] * 2 + [UNREAD] * 2,
+    )
+    yab, xab = swap(zab, y=1), swap(bare, r=1)
+    zc_da = swap(call(append_kernel, array(ext + half_rows), "append_piece", zb, rest), z=1)
+    dc = swap(db, z=1)
+    xc = swap(copy(zc_da, [(0, half_rows)]), r=1)
+    yc = swap(copy(zc_da, [(0, ext)], yab), y=1)
 
     order = [
         (half, half_rows), (y0, shard_rows), (zab, ext + half_rows), (yab, ext + half_rows),
-        (zab, half_rows), (yab, half_rows), (zc, half_rows), (yc, half_rows),
+        (zab, half_rows), (yab, half_rows), (zc_da, half_rows), (yc, half_rows),
     ]
     pack = call(
         functools.partial(pack_kernel, [(n, first) for n, (_, first) in enumerate(order)]),
-        jax.ShapeDtypeStruct((16, len(order) * width + count), bf16), "pack_rows",
-        target, *(x for x, _ in order), xab, xc,
-        specs=[WHOLE] * (1 + len(order)) + [UNREAD] * 2,
+        jax.ShapeDtypeStruct((16, len(order) * width), bf16), "pack_rows", *(x for x, _ in order),
     )
     other_pack = swap(pack, c=1)
-    limit, column_slot, place = call(
+    limit, column_slot = call(
         functools.partial(count_kernel, most_rows),
-        [
-            jax.ShapeDtypeStruct((2, 128), jnp.int32),
-            jax.ShapeDtypeStruct((1, 2 * count), jnp.int32),
-            jax.ShapeDtypeStruct((1, 2 * count), jnp.int32),
-        ],
+        [jax.ShapeDtypeStruct((2, 128), jnp.int32), jax.ShapeDtypeStruct((1, 2 * count), jnp.int32)],
         "count_rows", context_len, pack, other_pack,
         specs=[SCALARS, WHOLE, WHOLE],
+    )
+    place = call(
+        functools.partial(place_kernel, most_rows), jax.ShapeDtypeStruct((1, 2 * count), jnp.int32), "place_rows",
+        draft_rows, other_drafts,
     )
 
     def starts_of(uses):
@@ -420,14 +429,16 @@
             rep, wide = lax.axis_index("rep"), lax.axis_index("wide")
             z, y, c = wide // 4, wide // 2 % 2, wide % 2
             found = []
-            for _, _, _, (x_step, z_step, y_step) in uses:
+            for _, _, _, (x_step, z_step, y_step), *further in uses:
                 owner_z = (z // 2 + z_step // 2) % 2 * 2 + (z + z_step) % 2
                 owner = (owner_z * 2 + (y + y_step) % 2) * 2 + c
-                found.append(owner * shard_rows + (0 if x_step is None else (rep + x_step) % 2 * half_rows))
+                start = owner * shard_rows + (0 if x_step is None else (rep + x_step) % 2 * half_rows)
+                found.append(start + sum(further))
             return found
 
         return starts
 
+    rows = [prompt_hidden, other_prompt, draft_rows, other_drafts]
     stages = [
         ([full, y0], [(0, 0, shard_rows, (None, 0, 0)), (1, 0, shard_rows, (None, 0, 1))]),
         (
@@ -436,18 +447,18 @@
              (1, 0, half_rows, (0, 1, 1)), (1, ext, half_rows, (0, 2, 1))],
         ),
         (
-            [xab, zc, yc],
+            [xab, zc_da],
             [(0, 0, half_rows, (1, 1, 0)), (0, half_rows, half_rows, (1, 2, 0)),
-             (1, 0, half_rows, (0, 3, 0)), (2, 0, half_rows, (0, 3, 1))],
+             (1, 0, half_rows, (0, 3, 0)), (1, ext, half_rows, (1, 1, 1))],
         ),
         (
-            [xc, yxc, xyab],
-            [(0, 0, half_rows, (1, 3, 0)), (1, 0, half_rows, (1, 3, 1)),
-             (2, 0, half_rows, (1, 1, 1)), (2, half_rows, half_rows, (1, 2, 1))],
+            [xc, yc, db, dc],
+            [(0, 0, half_rows, (1, 3, 0)), (1, 0, half_rows, (0, 3, 1)),
+             (2, 0, half_rows, (1, 2, 1)), (3, 0, half_rows, (1, 3, 1))],
         ),
     ]
     sums = []
-    total_rows = 2 * padded[0]
+    total_rows = 2 * count + 32
     for n, (pieces, uses) in enumerate(stages[:-1]):
         sums = [
             call(

time: 53.7 us -> 51.6 us (0.961)
  waiting for transfers between devices: 20.3 us -> 18.6 us
  Pallas kernels: 13.2 us -> 12.5 us
  local copies, waits for them, and re-layouts: 0.01 us -> 0.67 us
    ppermute x16 -> x17, waiting for transfers between devices: 20.3 us -> 18.6 us  [swap(): return lax.ppermute(x, ('rep', 'wide'), pairs)]
    unnamed x4 -> x8, local copies, waits for them, and re-layouts: 0.01 us -> 0.67 us
    pallas_call x14 -> x16, Pallas kernels: 4.7 us -> 4.06 us  [call(): pl.pallas_call(kernel, out_shape=out_shape, in_specs=specs or [WHOLE] * l...]
    ppermute x16 -> x17, starting transfers between devices: 19.9 us -> 19.5 us  [swap(): return lax.ppermute(x, ('rep', 'wide'), pairs)]
  transfers between devices with their start and end apart: 16 -> 17, of which waited for: 10 -> 9; matrix products, arithmetic and copies ran while one was open for 0% -> 0% of each run, Pallas kernels for 15% -> 18%
where the time goes in v10:
time: 51.6 us; the launch traced here: 51.4 us
  starting transfers between devices  19.5 us (38%)
  waiting for transfers between devices  18.6 us (36%)
  Pallas kernels  12.5 us (24%)
  local copies, waits for them, and re-layouts  0.67 us (1%)
    ppermute x17, starting transfers between devices, swap(): return lax.ppermute(x, ('rep', 'wide'), pairs)  19.5 us
    ppermute x17, waiting for transfers between devices, swap(): return lax.ppermute(x, ('rep', 'wide'), pairs)  18.6 us
    pallas_call x16, Pallas kernels, call(): pl.pallas_call(kernel, out_shape=out_shape, in_specs=specs or [WHOLE] * l...  4.06 us
    pallas_call x1, Pallas kernels, local(): pl.pallas_call(functools.partial(held_kernel, arrived), out_shape=[jax.Sh...  3.99 us
    pallas_call x1, Pallas kernels, local(): pl.pallas_call(late_kernel, out_shape=jax.ShapeDtypeStruct((slot_count, d...  2.23 us
    pallas_call x1, Pallas kernels, local(): pl.pallas_call(functools.partial(window_kernel, arrived, span_rows, draft...  2.23 us
  transfers between devices with their start and end apart: 17, of which 9 were waited for; matrix products, arithmetic and copies ran while one was open for 0% of the time, Pallas kernels for 18%

profile of v10, /device:TPU:0, one launch (start us, length us, event | category | flops | bytes accessed | tf_op | source)
XLA Modules:
  0.0 51.4 jit_solution(4993877392585955390)
XLA Ops:
  0.0 0.5 collective-permute-start.8
  0.5 1.1 %start_rows.1 = (bf16[272,256]{1,0:T(8,128)(2,1)S(1)}, bf16[528,256]{1,0:T(8,128)(2,1)S(1)}, bf16[16,8192]{1,0:T(8,128)(2,1)S(1)}) custom-call(s32[1,128]{1,0:T(1,128)} %bitcast.1, bf16[512,256]{1,0:T(8,128)(2,1)} %shard_hbm.1, bf16[2,4,8192]{2,1,0:T(4,128)(2,1)} %draft_hbm.1), custom_call_target="tpu_custom_call" | custom-call | flops 1048576 | bytes 65536 | tf_op jit(solution)/shard_map/start_rows/pallas_call | solution.py:357
  1.7 3.0 %collective-permute-start = (bf16[528,256]{1,0:T(8,128)(2,1)S(1)}, bf16[528,256]{1,0:T(8,128)(2,1)S(1)}, u32[]{:S(2)}, u32[]{:S(2)}) collective-permute-start(bf16[528,256]{1,0:T(8,128)(2,1)S(1)} %get-tuple-element.30.refs_4_), channel_id=1, source_target_pairs={{0,2},{1,3},{2,0},{3,1},{4,6},{5,7},{6,4},{7,5},{8,10},{9,11},{10,... | collective-permute-start | bytes 811016 | tf_op jit(solution)/shard_map/ppermute | solution.py:351
  4.7 1.6 %collective-permute-start.1 = (bf16[272,256]{1,0:T(8,128)(2,1)S(1)}, bf16[272,256]{1,0:T(8,128)(2,1)S(1)}, u32[]{:S(2)}, u32[]{:S(2)}) collective-permute-start(bf16[272,256]{1,0:T(8,128)(2,1)S(1)} %get-tuple-element.29.refs_0_), channel_id=1, source_target_pairs={{0,4},{1,5},{2,6},{3,7},{4,0},{5,1},{6,2},{7,3},{8,12},{9,13},{10,... | collective-permute-start | bytes 417800 | tf_op jit(solution)/shard_map/ppermute | solution.py:351
  6.3 2.6 %collective-permute-start.2 = (bf16[272,256]{1,0:T(8,128)(2,1)S(1)}, bf16[272,256]{1,0:T(8,128)(2,1)S(1)}, u32[]{:S(2)}, u32[]{:S(2)}) collective-permute-start(bf16[272,256]{1,0:T(8,128)(2,1)S(1)} %get-tuple-element.29.refs_0_), channel_id=1, source_target_pairs={{0,8},{1,9},{2,10},{3,11},{4,12},{5,13},{6,14},{7,15},{8,0},{9,1},... | collective-permute-start | bytes 417800 | tf_op jit(solution)/shard_map/ppermute | solution.py:351
  8.9 0.7 %copy-done.2 = s32[2]{0:T(128)S(1)} copy-done((s32[2]{0:T(128)S(1)}, s32[2]{0:T(128)}, u32[]{:S(2)}) %copy-start.2) | copy-done | bytes 32
  9.5 4.0 %held_rows.1 = (bf16[2,512,256]{2,1,0:T(8,128)(2,1)S(1)}, f32[2,256,1]{2,1,0:T(8,128)S(1)}, f32[2,256,1]{2,1,0:T(8,128)S(1)}, f32[2,256,256]{2,1,0:T(8,128)S(1)}, bf16[2,384,256]{2,1,0:T(8,128)(2,1)S(1)}) custom-call(s32[2]{0:T(128)S(1)} %copy-done.2, bf16[2,4,8192]{2,1,0:T(4,128)(2,1)} %query_hbm.1, bf16[256,1024]{1,0:T(8,128)(2,1)} %key_up_hbm.1, ...), custom_call_target="tpu_custom_call" | custom-call | flops 2147483648 | bytes 2097152 | tf_op jit(solution)/shard_map/held_rows/pallas_call | solution.py:561
  13.5 1.8 %collective-permute-done.2.two_ref.one_ref = bf16[272,256]{1,0:T(8,128)(2,1)S(1)} collective-permute-done((bf16[272,256]{1,0:T(8,128)(2,1)S(1)}, bf16[272,256]{1,0:T(8,128)(2,1)S(1)}, u32[]{:S(2)}, u32[]{:S(2)}) %collective-permute-start.2) | collective-permute-done | bytes 139296 | tf_op jit(solution)/shard_map/ppermute | solution.py:351
  15.3 0.6 %collective-permute-start.4 = (bf16[544,256]{1,0:T(8,128)(2,1)S(1)}, bf16[544,256]{1,0:T(8,128)(2,1)S(1)}, u32[]{:S(2)}, u32[]{:S(2)}) collective-permute-start(bf16[544,256]{1,0:T(8,128)(2,1)S(1)} %get-tuple-element.33.refs_2_.refs_4_), channel_id=1, source_target_pairs={{0,2},{1,3},{2,0},{3,1},{4,6},{5,7},{6,4},{7,5},{8,10},{9,11},{10,... | collective-permute-start | bytes 835592 | tf_op jit(solution)/shard_map/ppermute | solution.py:351
  15.9 0.5 collective-permute-start.5
  16.5 1.5 %collective-permute-start.9 = (bf16[512,256]{1,0:T(8,128)(2,1)S(1)}, bf16[512,256]{1,0:T(8,128)(2,1)S(1)}, u32[]{:S(2)}, u32[]{:S(2)}) collective-permute-start(bf16[512,256]{1,0:T(8,128)(2,1)S(1)} %get-tuple-element.40), channel_id=1, source_target_pairs={{0,16},{1,17},{2,18},{3,19},{4,20},{5,21},{6,22},{7,23},{8,24},{9,... | collective-permute-start | bytes 786440 | tf_op jit(solution)/shard_map/ppermute | solution.py:351
  18.0 2.6 %collective-permute-start.11 = (bf16[256,256]{1,0:T(8,128)(2,1)S(1)}, bf16[256,256]{1,0:T(8,128)(2,1)S(1)}, u32[]{:S(2)}, u32[]{:S(2)}) collective-permute-start(bf16[256,256]{1,0:T(8,128)(2,1)S(1)} %other_half.1.two_ref), channel_id=1, source_target_pairs={{0,8},{1,9},{2,10},{3,11},{4,12},{5,13},{6,14},{7,15},{8,0},{9,1},... | collective-permute-start | bytes 393224 | tf_op jit(solution)/shard_map/ppermute | solution.py:351
  20.5 2.0 %collective-permute-done.4.refs_0_.refs_3_.refs_5_ = bf16[544,256]{1,0:T(8,128)(2,1)S(1)} collective-permute-done((bf16[544,256]{1,0:T(8,128)(2,1)S(1)}, bf16[544,256]{1,0:T(8,128)(2,1)S(1)}, u32[]{:S(2)}, u32[]{:S(2)}) %collective-permute-start.4) | collective-permute-done | bytes 278560 | tf_op jit(solution)/shard_map/ppermute | solution.py:351
  22.5 3.3 %collective-permute-done.5.one_ref.refs_6_.refs_5_ = bf16[528,256]{1,0:T(8,128)(2,1)S(1)} collective-permute-done((bf16[528,256]{1,0:T(8,128)(2,1)S(1)}, bf16[528,256]{1,0:T(8,128)(2,1)S(1)}, u32[]{:S(2)}, u32[]{:S(2)}) %collective-permute-start.5) | collective-permute-done | bytes 270368 | tf_op jit(solution)/shard_map/ppermute | solution.py:351
  25.8 1.6 %collective-permute-start.6 = (bf16[272,256]{1,0:T(8,128)(2,1)S(1)}, bf16[272,256]{1,0:T(8,128)(2,1)S(1)}, u32[]{:S(2)}, u32[]{:S(2)}) collective-permute-start(bf16[272,256]{1,0:T(8,128)(2,1)S(1)} %copy_piece.2), channel_id=1, source_target_pairs={{0,2},{1,3},{2,0},{3,1},{4,6},{5,7},{6,4},{7,5},{8,10},{9,11},{10,... | collective-permute-start | bytes 417800 | tf_op jit(solution)/shard_map/ppermute | solution.py:351
  27.4 0.6 %collective-permute-start.10 = (bf16[256,256]{1,0:T(8,128)(2,1)S(1)}, bf16[256,256]{1,0:T(8,128)(2,1)S(1)}, u32[]{:S(2)}, u32[]{:S(2)}) collective-permute-start(bf16[256,256]{1,0:T(8,128)(2,1)S(1)} %copy_piece.3), channel_id=1, source_target_pairs={{0,16},{1,17},{2,18},{3,19},{4,20},{5,21},{6,22},{7,23},{8,24},{9,... | collective-permute-start | bytes 393224 | tf_op jit(solution)/shard_map/ppermute | solution.py:351
  28.1 0.2 place_rows.1.refs_4_
  28.2 0.3 down_rows.3.refs_6_
  28.6 0.4 down_rows.4.refs_6_
  28.9 0.3 down_rows.5.refs_5_
  29.3 3.1 %collective-permute-done.12.refs_9_ = bf16[256,256]{1,0:T(8,128)(2,1)S(1)} collective-permute-done((bf16[256,256]{1,0:T(8,128)(2,1)S(1)}, bf16[256,256]{1,0:T(8,128)(2,1)S(1)}, u32[]{:S(2)}, u32[]{:S(2)}) %collective-permute-start.12) | collective-permute-done | bytes 131104 | tf_op jit(solution)/shard_map/ppermute | solution.py:351
  32.5 0.9 %down_place_rows.1 = (f32[264,256]{1,0:T(8,128)S(1)}, f32[264,256]{1,0:T(8,128)S(1)}) custom-call(bf16[128,8192]{1,0:T(8,128)(2,1)S(1)} %copy-done, bf16[128,8192]{1,0:T(8,128)(2,1)S(1)} %collective-permute-done.8.refs_1_, bf16[16,8192]{1,0:T(8,128)(2,1)S(1)} %get-tuple-element.31.mine_ref.refs_2_, ...), custom_call_target="tpu_custom_call" | custom-call | flops 67108864 | bytes 65536 | tf_op jit(solution)/shard_map/down_place_rows/pallas_call | solution.py:357
  33.5 1.5 %collective-permute-done.13.came_ref = f32[264,256]{1,0:T(8,128)S(1)} collective-permute-done((f32[264,256]{1,0:T(8,128)S(1)}, f32[264,256]{1,0:T(8,128)S(1)}, u32[]{:S(2)}, u32[]{:S(2)}) %collective-permute-start.13) | collective-permute-done | bytes 270368 | tf_op jit(solution)/shard_map/ppermute | solution.py:351
  35.1 0.6 %collective-permute-start.14 = (bf16[128,256]{1,0:T(8,128)(2,1)S(1)}, bf16[128,256]{1,0:T(8,128)(2,1)S(1)}, u32[]{:S(2)}, u32[]{:S(2)}) collective-permute-start(bf16[128,256]{1,0:T(8,128)(2,1)S(1)} %get-tuple-element.48), channel_id=1, source_target_pairs={{0,2},{1,3},{2,0},{3,1},{4,6},{5,7},{6,4},{7,5},{8,10},{9,11},{10,... | collective-permute-start | bytes 196616 | tf_op jit(solution)/shard_map/ppermute | solution.py:351
  35.7 3.7 %collective-permute-done.14.came_ref = bf16[128,256]{1,0:T(8,128)(2,1)S(1)} collective-permute-done((bf16[128,256]{1,0:T(8,128)(2,1)S(1)}, bf16[128,256]{1,0:T(8,128)(2,1)S(1)}, u32[]{:S(2)}, u32[]{:S(2)}) %collective-permute-start.14) | collective-permute-done | bytes 65568 | tf_op jit(solution)/shard_map/ppermute | solution.py:351
  39.4 1.8 %collective-permute-start.15 = (bf16[128,256]{1,0:T(8,128)(2,1)S(1)}, bf16[128,256]{1,0:T(8,128)(2,1)S(1)}, u32[]{:S(2)}, u32[]{:S(2)}) collective-permute-start(bf16[128,256]{1,0:T(8,128)(2,1)S(1)} %get-tuple-element.50), channel_id=1, source_target_pairs={{0,8},{1,9},{2,10},{3,11},{4,12},{5,13},{6,14},{7,15},{8,0},{9,1},... | collective-permute-start | bytes 196616 | tf_op jit(solution)/shard_map/ppermute | solution.py:351
  41.2 0.7 %count_rows.1 = (s32[2,128]{1,0:T(2,128)S(1)}, s32[1,256]{1,0:T(1,128)S(1)}) custom-call(s32[2]{0:T(128)S(1)} %copy-done.2, bf16[16,2048]{1,0:T(8,128)(2,1)S(1)} %pack_rows.1.mine_ref, bf16[16,2048]{1,0:T(8,128)(2,1)S(1)} %collective-permute-done.7.other_ref), custom_call_target="tpu_custom_call" | custom-call | flops 1048576 | bytes 65536 | tf_op jit(solution)/shard_map/count_rows/pallas_call | solution.py:357
  41.9 3.0 %collective-permute-done.15.came_ref = bf16[128,256]{1,0:T(8,128)(2,1)S(1)} collective-permute-done((bf16[128,256]{1,0:T(8,128)(2,1)S(1)}, bf16[128,256]{1,0:T(8,128)(2,1)S(1)}, u32[]{:S(2)}, u32[]{:S(2)}) %collective-permute-start.15) | collective-permute-done | bytes 65568 | tf_op jit(solution)/shard_map/ppermute | solution.py:351
  44.9 1.9 %collective-permute-start.16 = (bf16[128,256]{1,0:T(8,128)(2,1)S(1)}, bf16[128,256]{1,0:T(8,128)(2,1)S(1)}, u32[]{:S(2)}, u32[]{:S(2)}) collective-permute-start(bf16[128,256]{1,0:T(8,128)(2,1)S(1)} %get-tuple-element.52), channel_id=1, source_target_pairs={{0,4},{1,5},{2,6},{3,7},{4,0},{5,1},{6,2},{7,3},{8,12},{9,13},{10,... | collective-permute-start | bytes 196616 | tf_op jit(solution)/shard_map/ppermute | solution.py:351
  46.8 2.2 %window_rows.1 = (f32[2,256,1]{2,1,0:T(8,128)S(1)}, f32[2,256,1]{2,1,0:T(8,128)S(1)}, f32[2,256,256]{2,1,0:T(8,128)S(1)}) custom-call(s32[2]{0:T(128)S(1)} %copy-done.3, s32[2,128]{1,0:T(2,128)S(1)} %get-tuple-element.36.limit_ref, bf16[2,512,256]{2,1,0:T(8,128)(2,1)S(1)} %get-tuple-element.35.turned_ref, ...), custom_call_target="tpu_custom_call" | custom-call | flops 1073741824 | bytes 65536 | tf_op jit(solution)/shard_map/window_rows/pallas_call | solution.py:587
  49.0 0.2 collective-permute-done.16.refs_1_
  49.2 2.2 %late_rows.1 = bf16[2,4,8192]{2,1,0:T(4,128)(2,1)} custom-call(s32[1,256]{1,0:T(1,128)S(1)} %get-tuple-element.34.column_slot_ref, bf16[2,512,256]{2,1,0:T(8,128)(2,1)S(1)} %get-tuple-element.35.turned_ref, f32[2,256,1]{2,1,0:T(8,128)S(1)} %get-tuple-element.44.peak_ref, f32[2,256,1]{2,1,0:T(8,128)S(1)} %get-tuple-element.45.total_ref, ...), custom_call_target="tpu_custom_call" | custom-call | tf_op jit(solution)/shard_map/late_rows/pallas_call | solution.py:596
  (29 shorter events, 0.5 us)
Async XLA Ops:
  0.0 28.2 %collective-permute-start.8 = (bf16[128,8192]{1,0:T(8,128)(2,1)}, bf16[128,8192]{1,0:T(8,128)(2,1)S(1)}, u32[]{:S(2)}, u32[]{:S(2)}) collective-permute-start(bf16[128,8192]{1,0:T(8,128)(2,1)} %refs_0_.7), channel_id=1, source_target_pairs={{0,1},{1,0},{2,3},{3,2},{4,5},{5,4},{6,7},{7,6},{8,9},{9,8},{10,11... | collective-permute-start | bytes 6291464 | tf_op jit(solution)/shard_map/ppermute | solution.py:351
  1.6 13.7 %collective-permute-start.3 = (bf16[16,8192]{1,0:T(8,128)(2,1)S(1)}, bf16[16,8192]{1,0:T(8,128)(2,1)S(1)}, u32[]{:S(2)}, u32[]{:S(2)}) collective-permute-start(bf16[16,8192]{1,0:T(8,128)(2,1)S(1)} %get-tuple-element.31.mine_ref.refs_2_), channel_id=1, source_target_pairs={{0,1},{1,0},{2,3},{3,2},{4,5},{5,4},{6,7},{7,6},{8,9},{9,8},{10,11... | collective-permute-start | bytes 786440 | tf_op jit(solution)/shard_map/ppermute | solution.py:351
  1.7 14.2 %collective-permute-start = (bf16[528,256]{1,0:T(8,128)(2,1)S(1)}, bf16[528,256]{1,0:T(8,128)(2,1)S(1)}, u32[]{:S(2)}, u32[]{:S(2)}) collective-permute-start(bf16[528,256]{1,0:T(8,128)(2,1)S(1)} %get-tuple-element.30.refs_4_), channel_id=1, source_target_pairs={{0,2},{1,3},{2,0},{3,1},{4,6},{5,7},{6,4},{7,5},{8,10},{9,11},{10,... | collective-permute-start | bytes 811016 | tf_op jit(solution)/shard_map/ppermute | solution.py:351
  4.7 8.8 %collective-permute-start.1 = (bf16[272,256]{1,0:T(8,128)(2,1)S(1)}, bf16[272,256]{1,0:T(8,128)(2,1)S(1)}, u32[]{:S(2)}, u32[]{:S(2)}) collective-permute-start(bf16[272,256]{1,0:T(8,128)(2,1)S(1)} %get-tuple-element.29.refs_0_), channel_id=1, source_target_pairs={{0,4},{1,5},{2,6},{3,7},{4,0},{5,1},{6,2},{7,3},{8,12},{9,13},{10,... | collective-permute-start | bytes 417800 | tf_op jit(solution)/shard_map/ppermute | solution.py:351
  6.3 9.0 %collective-permute-start.2 = (bf16[272,256]{1,0:T(8,128)(2,1)S(1)}, bf16[272,256]{1,0:T(8,128)(2,1)S(1)}, u32[]{:S(2)}, u32[]{:S(2)}) collective-permute-start(bf16[272,256]{1,0:T(8,128)(2,1)S(1)} %get-tuple-element.29.refs_0_), channel_id=1, source_target_pairs={{0,8},{1,9},{2,10},{3,11},{4,12},{5,13},{6,14},{7,15},{8,0},{9,1},... | collective-permute-start | bytes 417800 | tf_op jit(solution)/shard_map/ppermute | solution.py:351
  8.8 0.7 %copy-start.2 = (s32[2]{0:T(128)S(1)}, s32[2]{0:T(128)}, u32[]{:S(2)}) copy-start(s32[2]{0:T(128)} %context_ref.5) | copy-start | bytes 28
  13.5 14.7 %copy-start = (bf16[128,8192]{1,0:T(8,128)(2,1)S(1)}, bf16[128,8192]{1,0:T(8,128)(2,1)}, u32[]{:S(2)}) copy-start(bf16[128,8192]{1,0:T(8,128)(2,1)} %refs_0_.7) | copy-start | bytes 6291460
  15.3 7.2 %collective-permute-start.4 = (bf16[544,256]{1,0:T(8,128)(2,1)S(1)}, bf16[544,256]{1,0:T(8,128)(2,1)S(1)}, u32[]{:S(2)}, u32[]{:S(2)}) collective-permute-start(bf16[544,256]{1,0:T(8,128)(2,1)S(1)} %get-tuple-element.33.refs_2_.refs_4_), channel_id=1, source_target_pairs={{0,2},{1,3},{2,0},{3,1},{4,6},{5,7},{6,4},{7,5},{8,10},{9,11},{10,... | collective-permute-start | bytes 835592 | tf_op jit(solution)/shard_map/ppermute | solution.py:351
  15.9 9.9 %collective-permute-start.5 = (bf16[528,256]{1,0:T(8,128)(2,1)S(1)}, bf16[528,256]{1,0:T(8,128)(2,1)S(1)}, u32[]{:S(2)}, u32[]{:S(2)}) collective-permute-start(bf16[528,256]{1,0:T(8,128)(2,1)S(1)} %append_piece.1), channel_id=1, source_target_pairs={{0,4},{1,5},{2,6},{3,7},{4,0},{5,1},{6,2},{7,3},{8,12},{9,13},{10,... | collective-permute-start | bytes 811016 | tf_op jit(solution)/shard_map/ppermute | solution.py:351
  16.5 12.5 %collective-permute-start.9 = (bf16[512,256]{1,0:T(8,128)(2,1)S(1)}, bf16[512,256]{1,0:T(8,128)(2,1)S(1)}, u32[]{:S(2)}, u32[]{:S(2)}) collective-permute-start(bf16[512,256]{1,0:T(8,128)(2,1)S(1)} %get-tuple-element.40), channel_id=1, source_target_pairs={{0,16},{1,17},{2,18},{3,19},{4,20},{5,21},{6,22},{7,23},{8,24},{9,... | collective-permute-start | bytes 786440 | tf_op jit(solution)/shard_map/ppermute | solution.py:351
  18.0 9.5 %collective-permute-start.11 = (bf16[256,256]{1,0:T(8,128)(2,1)S(1)}, bf16[256,256]{1,0:T(8,128)(2,1)S(1)}, u32[]{:S(2)}, u32[]{:S(2)}) collective-permute-start(bf16[256,256]{1,0:T(8,128)(2,1)S(1)} %other_half.1.two_ref), channel_id=1, source_target_pairs={{0,8},{1,9},{2,10},{3,11},{4,12},{5,13},{6,14},{7,15},{8,0},{9,1},... | collective-permute-start | bytes 393224 | tf_op jit(solution)/shard_map/ppermute | solution.py:351
  25.8 6.7 %collective-permute-start.6 = (bf16[272,256]{1,0:T(8,128)(2,1)S(1)}, bf16[272,256]{1,0:T(8,128)(2,1)S(1)}, u32[]{:S(2)}, u32[]{:S(2)}) collective-permute-start(bf16[272,256]{1,0:T(8,128)(2,1)S(1)} %copy_piece.2), channel_id=1, source_target_pairs={{0,2},{1,3},{2,0},{3,1},{4,6},{5,7},{6,4},{7,5},{8,10},{9,11},{10,... | collective-permute-start | bytes 417800 | tf_op jit(solution)/shard_map/ppermute | solution.py:351
  27.4 5.0 %collective-permute-start.12 = (bf16[256,256]{1,0:T(8,128)(2,1)S(1)}, bf16[256,256]{1,0:T(8,128)(2,1)S(1)}, u32[]{:S(2)}, u32[]{:S(2)}) collective-permute-start(bf16[256,256]{1,0:T(8,128)(2,1)S(1)} %collective-permute-done.11.refs_8_), channel_id=1, source_target_pairs={{0,4},{1,5},{2,6},{3,7},{4,0},{5,1},{6,2},{7,3},{8,12},{9,13},{10,... | collective-permute-start | bytes 393224 | tf_op jit(solution)/shard_map/ppermute | solution.py:351
  27.4 5.0 %collective-permute-start.10 = (bf16[256,256]{1,0:T(8,128)(2,1)S(1)}, bf16[256,256]{1,0:T(8,128)(2,1)S(1)}, u32[]{:S(2)}, u32[]{:S(2)}) collective-permute-start(bf16[256,256]{1,0:T(8,128)(2,1)S(1)} %copy_piece.3), channel_id=1, source_target_pairs={{0,16},{1,17},{2,18},{3,19},{4,20},{5,21},{6,22},{7,23},{8,24},{9,... | collective-permute-start | bytes 393224 | tf_op jit(solution)/shard_map/ppermute | solution.py:351
  33.4 13.4 %copy-start.3 = (s32[2]{0:T(128)S(1)}, s32[2]{0:T(128)}, u32[]{:S(2)}) copy-start(s32[2]{0:T(128)} %context_ref.5) | copy-start | bytes 28
  33.4 1.6 %collective-permute-start.13 = (f32[264,256]{1,0:T(8,128)S(1)}, f32[264,256]{1,0:T(8,128)S(1)}, u32[]{:S(2)}, u32[]{:S(2)}) collective-permute-start(f32[264,256]{1,0:T(8,128)S(1)} %get-tuple-element.42), channel_id=1, source_target_pairs={{0,1},{1,0},{2,3},{3,2},{4,5},{5,4},{6,7},{7,6},{8,9},{9,8},{10,11... | collective-permute-start | bytes 811016 | tf_op jit(solution)/shard_map/ppermute | solution.py:351
  35.1 4.3 %collective-permute-start.14 = (bf16[128,256]{1,0:T(8,128)(2,1)S(1)}, bf16[128,256]{1,0:T(8,128)(2,1)S(1)}, u32[]{:S(2)}, u32[]{:S(2)}) collective-permute-start(bf16[128,256]{1,0:T(8,128)(2,1)S(1)} %get-tuple-element.48), channel_id=1, source_target_pairs={{0,2},{1,3},{2,0},{3,1},{4,6},{5,7},{6,4},{7,5},{8,10},{9,11},{10,... | collective-permute-start | bytes 196616 | tf_op jit(solution)/shard_map/ppermute | solution.py:351
  35.7 5.5 %collective-permute-start.7 = (bf16[16,2048]{1,0:T(8,128)(2,1)S(1)}, bf16[16,2048]{1,0:T(8,128)(2,1)S(1)}, u32[]{:S(2)}, u32[]{:S(2)}) collective-permute-start(bf16[16,2048]{1,0:T(8,128)(2,1)S(1)} %pack_rows.1.mine_ref), channel_id=1, source_target_pairs={{0,1},{1,0},{2,3},{3,2},{4,5},{5,4},{6,7},{7,6},{8,9},{9,8},{10,11... | collective-permute-start | bytes 196616 | tf_op jit(solution)/shard_map/ppermute | solution.py:351
  39.4 5.4 %collective-permute-start.15 = (bf16[128,256]{1,0:T(8,128)(2,1)S(1)}, bf16[128,256]{1,0:T(8,128)(2,1)S(1)}, u32[]{:S(2)}, u32[]{:S(2)}) collective-permute-start(bf16[128,256]{1,0:T(8,128)(2,1)S(1)} %get-tuple-element.50), channel_id=1, source_target_pairs={{0,8},{1,9},{2,10},{3,11},{4,12},{5,13},{6,14},{7,15},{8,0},{9,1},... | collective-permute-start | bytes 196616 | tf_op jit(solution)/shard_map/ppermute | solution.py:351
  41.9 7.3 %copy-start.1 = (bf16[256,1024]{1,0:T(8,128)(2,1)S(1)}, bf16[256,1024]{1,0:T(8,128)(2,1)}, u32[]{:S(2)}) copy-start(bf16[256,1024]{1,0:T(8,128)(2,1)} %value_up_ref.1) | copy-start | bytes 1572868
  44.9 4.3 %collective-permute-start.16 = (bf16[128,256]{1,0:T(8,128)(2,1)S(1)}, bf16[128,256]{1,0:T(8,128)(2,1)S(1)}, u32[]{:S(2)}, u32[]{:S(2)}) collective-permute-start(bf16[128,256]{1,0:T(8,128)(2,1)S(1)} %get-tuple-element.52), channel_id=1, source_target_pairs={{0,4},{1,5},{2,6},{3,7},{4,0},{5,1},{6,2},{7,3},{8,12},{9,13},{10,... | collective-permute-start | bytes 196616 | tf_op jit(solution)/shard_map/ppermute | solution.py:351

commit v11 on v10

--- a/solution.py
+++ b/solution.py
@@ -226,12 +226,6 @@
     bare_ref[rows - 16 :, :] = two_ref[: rows - 16, :]
 
 
-def append_kernel(one_ref, two_ref, out_ref):
-    rows = one_ref.shape[0]
-    out_ref[:rows, :] = one_ref[...]
-    out_ref[rows:, :] = two_ref[...]
-
-
 def copy_kernel(spans, one_ref, *refs):
     done = 0
     for first, count in spans:
@@ -399,14 +393,14 @@
         specs=[WHOLE] * 2 + [UNREAD] * 2,
     )
     yab, xab = swap(zab, y=1), swap(bare, r=1)
-    zc_da = swap(call(append_kernel, array(ext + half_rows), "append_piece", zb, rest), z=1)
-    dc = swap(db, z=1)
-    xc = swap(copy(zc_da, [(0, half_rows)]), r=1)
-    yc = swap(copy(zc_da, [(0, ext)], yab), y=1)
+    zc, dc = swap(zb, z=1), swap(db, z=1)
+    xc = swap(copy(zc, [(0, half_rows)]), r=1)
+    xya = swap(copy(yab, [(0, half_rows)]), r=1)
+    yc = swap(copy(zc, [(0, ext)], yab), y=1)
 
     order = [
         (half, half_rows), (y0, shard_rows), (zab, ext + half_rows), (yab, ext + half_rows),
-        (zab, half_rows), (yab, half_rows), (zc_da, half_rows), (yc, half_rows),
+        (zab, half_rows), (yab, half_rows), (zc, half_rows), (yc, half_rows),
     ]
     pack = call(
         functools.partial(pack_kernel, [(n, first) for n, (_, first) in enumerate(order)]),
@@ -447,14 +441,13 @@
              (1, 0, half_rows, (0, 1, 1)), (1, ext, half_rows, (0, 2, 1))],
         ),
         (
-            [xab, zc_da],
-            [(0, 0, half_rows, (1, 1, 0)), (0, half_rows, half_rows, (1, 2, 0)),
-             (1, 0, half_rows, (0, 3, 0)), (1, ext, half_rows, (1, 1, 1))],
+            [xab, zc],
+            [(0, 0, half_rows, (1, 1, 0)), (0, half_rows, half_rows, (1, 2, 0)), (1, 0, half_rows, (0, 3, 0))],
         ),
         (
-            [xc, yc, db, dc],
-            [(0, 0, half_rows, (1, 3, 0)), (1, 0, half_rows, (0, 3, 1)),
-             (2, 0, half_rows, (1, 2, 1)), (3, 0, half_rows, (1, 3, 1))],
+            [xc, yc, xya, db, dc],
+            [(0, 0, half_rows, (1, 3, 0)), (1, 0, half_rows, (0, 3, 1)), (2, 0, half_rows, (1, 1, 1)),
+             (3, 0, half_rows, (1, 2, 1)), (4, 0, half_rows, (1, 3, 1))],
         ),
     ]
     sums = []

time: 51.6 us -> 49.6 us (0.961)
  waiting for transfers between devices: 18.6 us -> 14.1 us
  starting transfers between devices: 19.5 us -> 21.9 us
    ppermute x17 -> x18, waiting for transfers between devices: 18.6 us -> 14.1 us  [swap(): return lax.ppermute(x, ('rep', 'wide'), pairs)]
    ppermute x17 -> x18, starting transfers between devices: 19.5 us -> 21.9 us  [swap(): return lax.ppermute(x, ('rep', 'wide'), pairs)]
  transfers between devices with their start and end apart: 17 -> 18, of which waited for: 9 -> 10; matrix products, arithmetic and copies ran while one was open for 0% -> 0% of each run, Pallas kernels for 18% -> 19%
where the time goes in v11:
time: 49.6 us; the launch traced here: 49.5 us
  starting transfers between devices  21.9 us (44%)
  waiting for transfers between devices  14.1 us (28%)
  Pallas kernels  12.6 us (25%)
  local copies, waits for them, and re-layouts  0.67 us (1%)
    ppermute x18, starting transfers between devices, swap(): return lax.ppermute(x, ('rep', 'wide'), pairs)  21.9 us
    ppermute x18, waiting for transfers between devices, swap(): return lax.ppermute(x, ('rep', 'wide'), pairs)  14.1 us
    pallas_call x16, Pallas kernels, call(): pl.pallas_call(kernel, out_shape=out_shape, in_specs=specs or [WHOLE] * l...  4.12 us
    pallas_call x1, Pallas kernels, local(): pl.pallas_call(functools.partial(held_kernel, arrived), out_shape=[jax.Sh...  3.99 us
    pallas_call x1, Pallas kernels, local(): pl.pallas_call(functools.partial(window_kernel, arrived, span_rows, draft...  2.23 us
    pallas_call x1, Pallas kernels, local(): pl.pallas_call(late_kernel, out_shape=jax.ShapeDtypeStruct((slot_count, d...  2.23 us
  transfers between devices with their start and end apart: 18, of which 10 were waited for; matrix products, arithmetic and copies ran while one was open for 0% of the time, Pallas kernels for 19%

profile of v11, /device:TPU:0, one launch (start us, length us, event | category | flops | bytes accessed | tf_op | source)
XLA Modules:
  0.0 49.5 jit_solution(6904223418295986662)
XLA Ops:
  0.0 0.5 collective-permute-start.8
  0.5 1.1 %start_rows.1 = (bf16[272,256]{1,0:T(8,128)(2,1)S(1)}, bf16[528,256]{1,0:T(8,128)(2,1)S(1)}, bf16[16,8192]{1,0:T(8,128)(2,1)S(1)}) custom-call(s32[1,128]{1,0:T(1,128)} %bitcast.1, bf16[512,256]{1,0:T(8,128)(2,1)} %shard_hbm.1, bf16[2,4,8192]{2,1,0:T(4,128)(2,1)} %draft_hbm.1), custom_call_target="tpu_custom_call" | custom-call | flops 1048576 | bytes 65536 | tf_op jit(solution)/shard_map/start_rows/pallas_call | solution.py:351
  1.7 3.0 %collective-permute-start.1 = (bf16[272,256]{1,0:T(8,128)(2,1)S(1)}, bf16[272,256]{1,0:T(8,128)(2,1)S(1)}, u32[]{:S(2)}, u32[]{:S(2)}) collective-permute-start(bf16[272,256]{1,0:T(8,128)(2,1)S(1)} %get-tuple-element.29.refs_0_), channel_id=1, source_target_pairs={{0,4},{1,5},{2,6},{3,7},{4,0},{5,1},{6,2},{7,3},{8,12},{9,13},{10,... | collective-permute-start | bytes 417800 | tf_op jit(solution)/shard_map/ppermute | solution.py:345
  4.7 2.6 %collective-permute-start.2 = (bf16[272,256]{1,0:T(8,128)(2,1)S(1)}, bf16[272,256]{1,0:T(8,128)(2,1)S(1)}, u32[]{:S(2)}, u32[]{:S(2)}) collective-permute-start(bf16[272,256]{1,0:T(8,128)(2,1)S(1)} %get-tuple-element.29.refs_0_), channel_id=1, source_target_pairs={{0,8},{1,9},{2,10},{3,11},{4,12},{5,13},{6,14},{7,15},{8,0},{9,1},... | collective-permute-start | bytes 417800 | tf_op jit(solution)/shard_map/ppermute | solution.py:345
  7.3 1.5 %collective-permute-start = (bf16[528,256]{1,0:T(8,128)(2,1)S(1)}, bf16[528,256]{1,0:T(8,128)(2,1)S(1)}, u32[]{:S(2)}, u32[]{:S(2)}) collective-permute-start(bf16[528,256]{1,0:T(8,128)(2,1)S(1)} %get-tuple-element.30.refs_4_), channel_id=1, source_target_pairs={{0,2},{1,3},{2,0},{3,1},{4,6},{5,7},{6,4},{7,5},{8,10},{9,11},{10,... | collective-permute-start | bytes 811016 | tf_op jit(solution)/shard_map/ppermute | solution.py:345
  8.9 0.7 %copy-done.2 = s32[2]{0:T(128)S(1)} copy-done((s32[2]{0:T(128)S(1)}, s32[2]{0:T(128)}, u32[]{:S(2)}) %copy-start.2) | copy-done | bytes 32
  9.5 4.0 %held_rows.1 = (bf16[2,512,256]{2,1,0:T(8,128)(2,1)S(1)}, f32[2,256,1]{2,1,0:T(8,128)S(1)}, f32[2,256,1]{2,1,0:T(8,128)S(1)}, f32[2,256,256]{2,1,0:T(8,128)S(1)}, bf16[2,384,256]{2,1,0:T(8,128)(2,1)S(1)}) custom-call(s32[2]{0:T(128)S(1)} %copy-done.2, bf16[2,4,8192]{2,1,0:T(4,128)(2,1)} %query_hbm.1, bf16[256,1024]{1,0:T(8,128)(2,1)} %key_up_hbm.1, ...), custom_call_target="tpu_custom_call" | custom-call | flops 2147483648 | bytes 2097152 | tf_op jit(solution)/shard_map/held_rows/pallas_call | solution.py:554
  13.5 0.5 %collective-permute-done.2.two_ref = bf16[272,256]{1,0:T(8,128)(2,1)S(1)} collective-permute-done((bf16[272,256]{1,0:T(8,128)(2,1)S(1)}, bf16[272,256]{1,0:T(8,128)(2,1)S(1)}, u32[]{:S(2)}, u32[]{:S(2)}) %collective-permute-start.2) | collective-permute-done | bytes 139296 | tf_op jit(solution)/shard_map/ppermute | solution.py:345
  14.1 1.6 %collective-permute-start.4 = (bf16[544,256]{1,0:T(8,128)(2,1)S(1)}, bf16[544,256]{1,0:T(8,128)(2,1)S(1)}, u32[]{:S(2)}, u32[]{:S(2)}) collective-permute-start(bf16[544,256]{1,0:T(8,128)(2,1)S(1)} %get-tuple-element.33.refs_2_.refs_4_), channel_id=1, source_target_pairs={{0,2},{1,3},{2,0},{3,1},{4,6},{5,7},{6,4},{7,5},{8,10},{9,11},{10,... | collective-permute-start | bytes 835592 | tf_op jit(solution)/shard_map/ppermute | solution.py:345
  15.7 0.4 collective-permute-start.5
  16.1 1.5 %collective-permute-start.9 = (bf16[512,256]{1,0:T(8,128)(2,1)S(1)}, bf16[512,256]{1,0:T(8,128)(2,1)S(1)}, u32[]{:S(2)}, u32[]{:S(2)}) collective-permute-start(bf16[512,256]{1,0:T(8,128)(2,1)S(1)} %get-tuple-element.40), channel_id=1, source_target_pairs={{0,16},{1,17},{2,18},{3,19},{4,20},{5,21},{6,22},{7,23},{8,24},{9,... | collective-permute-start | bytes 786440 | tf_op jit(solution)/shard_map/ppermute | solution.py:345
  17.6 2.7 %collective-permute-start.12 = (bf16[256,256]{1,0:T(8,128)(2,1)S(1)}, bf16[256,256]{1,0:T(8,128)(2,1)S(1)}, u32[]{:S(2)}, u32[]{:S(2)}) collective-permute-start(bf16[256,256]{1,0:T(8,128)(2,1)S(1)} %other_half.1), channel_id=1, source_target_pairs={{0,8},{1,9},{2,10},{3,11},{4,12},{5,13},{6,14},{7,15},{8,0},{9,1},... | collective-permute-start | bytes 393224 | tf_op jit(solution)/shard_map/ppermute | solution.py:345
  20.3 1.9 %collective-permute-done.5.one_ref.refs_6_.refs_5_ = bf16[272,256]{1,0:T(8,128)(2,1)S(1)} collective-permute-done((bf16[272,256]{1,0:T(8,128)(2,1)S(1)}, bf16[272,256]{1,0:T(8,128)(2,1)S(1)}, u32[]{:S(2)}, u32[]{:S(2)}) %collective-permute-start.5) | collective-permute-done | bytes 139296 | tf_op jit(solution)/shard_map/ppermute | solution.py:345
  22.2 0.6 %collective-permute-start.6 = (bf16[272,256]{1,0:T(8,128)(2,1)S(1)}, bf16[272,256]{1,0:T(8,128)(2,1)S(1)}, u32[]{:S(2)}, u32[]{:S(2)}) collective-permute-start(bf16[272,256]{1,0:T(8,128)(2,1)S(1)} %copy_piece.3), channel_id=1, source_target_pairs={{0,2},{1,3},{2,0},{3,1},{4,6},{5,7},{6,4},{7,5},{8,10},{9,11},{10,... | collective-permute-start | bytes 417800 | tf_op jit(solution)/shard_map/ppermute | solution.py:345
  22.8 1.6 %collective-permute-start.10 = (bf16[256,256]{1,0:T(8,128)(2,1)S(1)}, bf16[256,256]{1,0:T(8,128)(2,1)S(1)}, u32[]{:S(2)}, u32[]{:S(2)}) collective-permute-start(bf16[256,256]{1,0:T(8,128)(2,1)S(1)} %copy_piece.4), channel_id=1, source_target_pairs={{0,16},{1,17},{2,18},{3,19},{4,20},{5,21},{6,22},{7,23},{8,24},{9,... | collective-permute-start | bytes 393224 | tf_op jit(solution)/shard_map/ppermute | solution.py:345
  24.4 0.7 %collective-permute-done.12.refs_9_ = bf16[256,256]{1,0:T(8,128)(2,1)S(1)} collective-permute-done((bf16[256,256]{1,0:T(8,128)(2,1)S(1)}, bf16[256,256]{1,0:T(8,128)(2,1)S(1)}, u32[]{:S(2)}, u32[]{:S(2)}) %collective-permute-start.12) | collective-permute-done | bytes 131104 | tf_op jit(solution)/shard_map/ppermute | solution.py:345
  25.1 0.4 collective-permute-start.13
  25.5 0.6 %collective-permute-start.11 = (bf16[256,256]{1,0:T(8,128)(2,1)S(1)}, bf16[256,256]{1,0:T(8,128)(2,1)S(1)}, u32[]{:S(2)}, u32[]{:S(2)}) collective-permute-start(bf16[256,256]{1,0:T(8,128)(2,1)S(1)} %copy_piece.5), channel_id=1, source_target_pairs={{0,16},{1,17},{2,18},{3,19},{4,20},{5,21},{6,22},{7,23},{8,24},{9,... | collective-permute-start | bytes 393224 | tf_op jit(solution)/shard_map/ppermute | solution.py:345
  27.3 1.1 %collective-permute-done.10.refs_6_ = bf16[256,256]{1,0:T(8,128)(2,1)S(1)} collective-permute-done((bf16[256,256]{1,0:T(8,128)(2,1)S(1)}, bf16[256,256]{1,0:T(8,128)(2,1)S(1)}, u32[]{:S(2)}, u32[]{:S(2)}) %collective-permute-start.10) | collective-permute-done | bytes 131104 | tf_op jit(solution)/shard_map/ppermute | solution.py:345
  28.4 1.6 %collective-permute-done.13.refs_10_ = bf16[256,256]{1,0:T(8,128)(2,1)S(1)} collective-permute-done((bf16[256,256]{1,0:T(8,128)(2,1)S(1)}, bf16[256,256]{1,0:T(8,128)(2,1)S(1)}, u32[]{:S(2)}, u32[]{:S(2)}) %collective-permute-start.13) | collective-permute-done | bytes 131104 | tf_op jit(solution)/shard_map/ppermute | solution.py:345
  30.0 0.5 %collective-permute-done.11.refs_8_ = bf16[256,256]{1,0:T(8,128)(2,1)S(1)} collective-permute-done((bf16[256,256]{1,0:T(8,128)(2,1)S(1)}, bf16[256,256]{1,0:T(8,128)(2,1)S(1)}, u32[]{:S(2)}, u32[]{:S(2)}) %collective-permute-start.11) | collective-permute-done | bytes 131104 | tf_op jit(solution)/shard_map/ppermute | solution.py:345
  30.6 1.0 %down_place_rows.1 = (f32[264,256]{1,0:T(8,128)S(1)}, f32[264,256]{1,0:T(8,128)S(1)}) custom-call(bf16[128,8192]{1,0:T(8,128)(2,1)S(1)} %copy-done, bf16[128,8192]{1,0:T(8,128)(2,1)S(1)} %collective-permute-done.8.refs_1_, bf16[16,8192]{1,0:T(8,128)(2,1)S(1)} %get-tuple-element.31.mine_ref.refs_2_, ...), custom_call_target="tpu_custom_call" | custom-call | flops 67108864 | bytes 65536 | tf_op jit(solution)/shard_map/down_place_rows/pallas_call | solution.py:351
  31.7 1.5 %collective-permute-done.14.came_ref = f32[264,256]{1,0:T(8,128)S(1)} collective-permute-done((f32[264,256]{1,0:T(8,128)S(1)}, f32[264,256]{1,0:T(8,128)S(1)}, u32[]{:S(2)}, u32[]{:S(2)}) %collective-permute-start.14) | collective-permute-done | bytes 270368 | tf_op jit(solution)/shard_map/ppermute | solution.py:345
  33.3 0.6 %collective-permute-start.15 = (bf16[128,256]{1,0:T(8,128)(2,1)S(1)}, bf16[128,256]{1,0:T(8,128)(2,1)S(1)}, u32[]{:S(2)}, u32[]{:S(2)}) collective-permute-start(bf16[128,256]{1,0:T(8,128)(2,1)S(1)} %get-tuple-element.48), channel_id=1, source_target_pairs={{0,2},{1,3},{2,0},{3,1},{4,6},{5,7},{6,4},{7,5},{8,10},{9,11},{10,... | collective-permute-start | bytes 196616 | tf_op jit(solution)/shard_map/ppermute | solution.py:345
  33.9 3.7 %collective-permute-done.15.came_ref = bf16[128,256]{1,0:T(8,128)(2,1)S(1)} collective-permute-done((bf16[128,256]{1,0:T(8,128)(2,1)S(1)}, bf16[128,256]{1,0:T(8,128)(2,1)S(1)}, u32[]{:S(2)}, u32[]{:S(2)}) %collective-permute-start.15) | collective-permute-done | bytes 65568 | tf_op jit(solution)/shard_map/ppermute | solution.py:345
  37.7 2.5 %collective-permute-start.16 = (bf16[128,256]{1,0:T(8,128)(2,1)S(1)}, bf16[128,256]{1,0:T(8,128)(2,1)S(1)}, u32[]{:S(2)}, u32[]{:S(2)}) collective-permute-start(bf16[128,256]{1,0:T(8,128)(2,1)S(1)} %get-tuple-element.50), channel_id=1, source_target_pairs={{0,8},{1,9},{2,10},{3,11},{4,12},{5,13},{6,14},{7,15},{8,0},{9,1},... | collective-permute-start | bytes 196616 | tf_op jit(solution)/shard_map/ppermute | solution.py:345
  40.1 0.7 %count_rows.1 = (s32[2,128]{1,0:T(2,128)S(1)}, s32[1,256]{1,0:T(1,128)S(1)}) custom-call(s32[2]{0:T(128)S(1)} %copy-done.3, bf16[16,2048]{1,0:T(8,128)(2,1)S(1)} %pack_rows.1.mine_ref, bf16[16,2048]{1,0:T(8,128)(2,1)S(1)} %collective-permute-done.7.other_ref), custom_call_target="tpu_custom_call" | custom-call | flops 1048576 | bytes 65536 | tf_op jit(solution)/shard_map/count_rows/pallas_call | solution.py:351
  40.8 2.1 %collective-permute-done.16.came_ref = bf16[128,256]{1,0:T(8,128)(2,1)S(1)} collective-permute-done((bf16[128,256]{1,0:T(8,128)(2,1)S(1)}, bf16[128,256]{1,0:T(8,128)(2,1)S(1)}, u32[]{:S(2)}, u32[]{:S(2)}) %collective-permute-start.16) | collective-permute-done | bytes 65568 | tf_op jit(solution)/shard_map/ppermute | solution.py:345
  42.9 1.6 %collective-permute-start.17 = (bf16[128,256]{1,0:T(8,128)(2,1)S(1)}, bf16[128,256]{1,0:T(8,128)(2,1)S(1)}, u32[]{:S(2)}, u32[]{:S(2)}) collective-permute-start(bf16[128,256]{1,0:T(8,128)(2,1)S(1)} %get-tuple-element.52), channel_id=1, source_target_pairs={{0,4},{1,5},{2,6},{3,7},{4,0},{5,1},{6,2},{7,3},{8,12},{9,13},{10,... | collective-permute-start | bytes 196616 | tf_op jit(solution)/shard_map/ppermute | solution.py:345
  44.5 2.2 %window_rows.1 = (f32[2,256,1]{2,1,0:T(8,128)S(1)}, f32[2,256,1]{2,1,0:T(8,128)S(1)}, f32[2,256,256]{2,1,0:T(8,128)S(1)}) custom-call(s32[2]{0:T(128)S(1)} %copy-done.3, s32[2,128]{1,0:T(2,128)S(1)} %get-tuple-element.36.limit_ref, bf16[2,512,256]{2,1,0:T(8,128)(2,1)S(1)} %get-tuple-element.35.turned_ref, ...), custom_call_target="tpu_custom_call" | custom-call | flops 1073741824 | bytes 65536 | tf_op jit(solution)/shard_map/window_rows/pallas_call | solution.py:580
  46.8 0.4 collective-permute-done.17.refs_1_
  47.2 2.2 %late_rows.1 = bf16[2,4,8192]{2,1,0:T(4,128)(2,1)} custom-call(s32[1,256]{1,0:T(1,128)S(1)} %get-tuple-element.34.column_slot_ref, bf16[2,512,256]{2,1,0:T(8,128)(2,1)S(1)} %get-tuple-element.35.turned_ref, f32[2,256,1]{2,1,0:T(8,128)S(1)} %get-tuple-element.44.peak_ref, f32[2,256,1]{2,1,0:T(8,128)S(1)} %get-tuple-element.45.total_ref, ...), custom_call_target="tpu_custom_call" | custom-call | tf_op jit(solution)/shard_map/late_rows/pallas_call | solution.py:589
  (31 shorter events, 1.5 us)
Async XLA Ops:
  0.0 25.5 %collective-permute-start.8 = (bf16[128,8192]{1,0:T(8,128)(2,1)}, bf16[128,8192]{1,0:T(8,128)(2,1)S(1)}, u32[]{:S(2)}, u32[]{:S(2)}) collective-permute-start(bf16[128,8192]{1,0:T(8,128)(2,1)} %refs_0_.7), channel_id=1, source_target_pairs={{0,1},{1,0},{2,3},{3,2},{4,5},{5,4},{6,7},{7,6},{8,9},{9,8},{10,11... | collective-permute-start | bytes 6291464 | tf_op jit(solution)/shard_map/ppermute | solution.py:345
  1.6 12.5 %collective-permute-start.3 = (bf16[16,8192]{1,0:T(8,128)(2,1)S(1)}, bf16[16,8192]{1,0:T(8,128)(2,1)S(1)}, u32[]{:S(2)}, u32[]{:S(2)}) collective-permute-start(bf16[16,8192]{1,0:T(8,128)(2,1)S(1)} %get-tuple-element.31.mine_ref.refs_2_), channel_id=1, source_target_pairs={{0,1},{1,0},{2,3},{3,2},{4,5},{5,4},{6,7},{7,6},{8,9},{9,8},{10,11... | collective-permute-start | bytes 786440 | tf_op jit(solution)/shard_map/ppermute | solution.py:345
  1.7 11.8 %collective-permute-start.1 = (bf16[272,256]{1,0:T(8,128)(2,1)S(1)}, bf16[272,256]{1,0:T(8,128)(2,1)S(1)}, u32[]{:S(2)}, u32[]{:S(2)}) collective-permute-start(bf16[272,256]{1,0:T(8,128)(2,1)S(1)} %get-tuple-element.29.refs_0_), channel_id=1, source_target_pairs={{0,4},{1,5},{2,6},{3,7},{4,0},{5,1},{6,2},{7,3},{8,12},{9,13},{10,... | collective-permute-start | bytes 417800 | tf_op jit(solution)/shard_map/ppermute | solution.py:345
  4.7 9.3 %collective-permute-start.2 = (bf16[272,256]{1,0:T(8,128)(2,1)S(1)}, bf16[272,256]{1,0:T(8,128)(2,1)S(1)}, u32[]{:S(2)}, u32[]{:S(2)}) collective-permute-start(bf16[272,256]{1,0:T(8,128)(2,1)S(1)} %get-tuple-element.29.refs_0_), channel_id=1, source_target_pairs={{0,8},{1,9},{2,10},{3,11},{4,12},{5,13},{6,14},{7,15},{8,0},{9,1},... | collective-permute-start | bytes 417800 | tf_op jit(solution)/shard_map/ppermute | solution.py:345
  7.3 10.3 %collective-permute-start = (bf16[528,256]{1,0:T(8,128)(2,1)S(1)}, bf16[528,256]{1,0:T(8,128)(2,1)S(1)}, u32[]{:S(2)}, u32[]{:S(2)}) collective-permute-start(bf16[528,256]{1,0:T(8,128)(2,1)S(1)} %get-tuple-element.30.refs_4_), channel_id=1, source_target_pairs={{0,2},{1,3},{2,0},{3,1},{4,6},{5,7},{6,4},{7,5},{8,10},{9,11},{10,... | collective-permute-start | bytes 811016 | tf_op jit(solution)/shard_map/ppermute | solution.py:345
  8.8 0.7 %copy-start.2 = (s32[2]{0:T(128)S(1)}, s32[2]{0:T(128)}, u32[]{:S(2)}) copy-start(s32[2]{0:T(128)} %context_ref.5) | copy-start | bytes 28
  13.5 12.8 %copy-start = (bf16[128,8192]{1,0:T(8,128)(2,1)S(1)}, bf16[128,8192]{1,0:T(8,128)(2,1)}, u32[]{:S(2)}) copy-start(bf16[128,8192]{1,0:T(8,128)(2,1)} %refs_0_.7) | copy-start | bytes 6291460
  14.1 8.0 %collective-permute-start.4 = (bf16[544,256]{1,0:T(8,128)(2,1)S(1)}, bf16[544,256]{1,0:T(8,128)(2,1)S(1)}, u32[]{:S(2)}, u32[]{:S(2)}) collective-permute-start(bf16[544,256]{1,0:T(8,128)(2,1)S(1)} %get-tuple-element.33.refs_2_.refs_4_), channel_id=1, source_target_pairs={{0,2},{1,3},{2,0},{3,1},{4,6},{5,7},{6,4},{7,5},{8,10},{9,11},{10,... | collective-permute-start | bytes 835592 | tf_op jit(solution)/shard_map/ppermute | solution.py:345
  15.7 6.5 %collective-permute-start.5 = (bf16[272,256]{1,0:T(8,128)(2,1)S(1)}, bf16[272,256]{1,0:T(8,128)(2,1)S(1)}, u32[]{:S(2)}, u32[]{:S(2)}) collective-permute-start(bf16[272,256]{1,0:T(8,128)(2,1)S(1)} %collective-permute-done.2.two_ref), channel_id=1, source_target_pairs={{0,4},{1,5},{2,6},{3,7},{4,0},{5,1},{6,2},{7,3},{8,12},{9,13},{10,... | collective-permute-start | bytes 417800 | tf_op jit(solution)/shard_map/ppermute | solution.py:345
  16.1 10.9 %collective-permute-start.9 = (bf16[512,256]{1,0:T(8,128)(2,1)S(1)}, bf16[512,256]{1,0:T(8,128)(2,1)S(1)}, u32[]{:S(2)}, u32[]{:S(2)}) collective-permute-start(bf16[512,256]{1,0:T(8,128)(2,1)S(1)} %get-tuple-element.40), channel_id=1, source_target_pairs={{0,16},{1,17},{2,18},{3,19},{4,20},{5,21},{6,22},{7,23},{8,24},{9,... | collective-permute-start | bytes 786440 | tf_op jit(solution)/shard_map/ppermute | solution.py:345
  17.6 7.4 %collective-permute-start.12 = (bf16[256,256]{1,0:T(8,128)(2,1)S(1)}, bf16[256,256]{1,0:T(8,128)(2,1)S(1)}, u32[]{:S(2)}, u32[]{:S(2)}) collective-permute-start(bf16[256,256]{1,0:T(8,128)(2,1)S(1)} %other_half.1), channel_id=1, source_target_pairs={{0,8},{1,9},{2,10},{3,11},{4,12},{5,13},{6,14},{7,15},{8,0},{9,1},... | collective-permute-start | bytes 393224 | tf_op jit(solution)/shard_map/ppermute | solution.py:345
  22.2 8.4 %collective-permute-start.6 = (bf16[272,256]{1,0:T(8,128)(2,1)S(1)}, bf16[272,256]{1,0:T(8,128)(2,1)S(1)}, u32[]{:S(2)}, u32[]{:S(2)}) collective-permute-start(bf16[272,256]{1,0:T(8,128)(2,1)S(1)} %copy_piece.3), channel_id=1, source_target_pairs={{0,2},{1,3},{2,0},{3,1},{4,6},{5,7},{6,4},{7,5},{8,10},{9,11},{10,... | collective-permute-start | bytes 417800 | tf_op jit(solution)/shard_map/ppermute | solution.py:345
  22.8 5.6 %collective-permute-start.10 = (bf16[256,256]{1,0:T(8,128)(2,1)S(1)}, bf16[256,256]{1,0:T(8,128)(2,1)S(1)}, u32[]{:S(2)}, u32[]{:S(2)}) collective-permute-start(bf16[256,256]{1,0:T(8,128)(2,1)S(1)} %copy_piece.4), channel_id=1, source_target_pairs={{0,16},{1,17},{2,18},{3,19},{4,20},{5,21},{6,22},{7,23},{8,24},{9,... | collective-permute-start | bytes 393224 | tf_op jit(solution)/shard_map/ppermute | solution.py:345
  25.1 5.0 %collective-permute-start.13 = (bf16[256,256]{1,0:T(8,128)(2,1)S(1)}, bf16[256,256]{1,0:T(8,128)(2,1)S(1)}, u32[]{:S(2)}, u32[]{:S(2)}) collective-permute-start(bf16[256,256]{1,0:T(8,128)(2,1)S(1)} %collective-permute-done.12.refs_9_), channel_id=1, source_target_pairs={{0,4},{1,5},{2,6},{3,7},{4,0},{5,1},{6,2},{7,3},{8,12},{9,13},{10,... | collective-permute-start | bytes 393224 | tf_op jit(solution)/shard_map/ppermute | solution.py:345
  25.5 5.0 %collective-permute-start.11 = (bf16[256,256]{1,0:T(8,128)(2,1)S(1)}, bf16[256,256]{1,0:T(8,128)(2,1)S(1)}, u32[]{:S(2)}, u32[]{:S(2)}) collective-permute-start(bf16[256,256]{1,0:T(8,128)(2,1)S(1)} %copy_piece.5), channel_id=1, source_target_pairs={{0,16},{1,17},{2,18},{3,19},{4,20},{5,21},{6,22},{7,23},{8,24},{9,... | collective-permute-start | bytes 393224 | tf_op jit(solution)/shard_map/ppermute | solution.py:345
  31.6 8.5 %copy-start.3 = (s32[2]{0:T(128)S(1)}, s32[2]{0:T(128)}, u32[]{:S(2)}) copy-start(s32[2]{0:T(128)} %context_ref.5) | copy-start | bytes 28
  31.6 1.6 %collective-permute-start.14 = (f32[264,256]{1,0:T(8,128)S(1)}, f32[264,256]{1,0:T(8,128)S(1)}, u32[]{:S(2)}, u32[]{:S(2)}) collective-permute-start(f32[264,256]{1,0:T(8,128)S(1)} %get-tuple-element.42), channel_id=1, source_target_pairs={{0,1},{1,0},{2,3},{3,2},{4,5},{5,4},{6,7},{7,6},{8,9},{9,8},{10,11... | collective-permute-start | bytes 811016 | tf_op jit(solution)/shard_map/ppermute | solution.py:345
  33.3 4.3 %collective-permute-start.15 = (bf16[128,256]{1,0:T(8,128)(2,1)S(1)}, bf16[128,256]{1,0:T(8,128)(2,1)S(1)}, u32[]{:S(2)}, u32[]{:S(2)}) collective-permute-start(bf16[128,256]{1,0:T(8,128)(2,1)S(1)} %get-tuple-element.48), channel_id=1, source_target_pairs={{0,2},{1,3},{2,0},{3,1},{4,6},{5,7},{6,4},{7,5},{8,10},{9,11},{10,... | collective-permute-start | bytes 196616 | tf_op jit(solution)/shard_map/ppermute | solution.py:345
  33.9 6.3 %collective-permute-start.7 = (bf16[16,2048]{1,0:T(8,128)(2,1)S(1)}, bf16[16,2048]{1,0:T(8,128)(2,1)S(1)}, u32[]{:S(2)}, u32[]{:S(2)}) collective-permute-start(bf16[16,2048]{1,0:T(8,128)(2,1)S(1)} %pack_rows.1.mine_ref), channel_id=1, source_target_pairs={{0,1},{1,0},{2,3},{3,2},{4,5},{5,4},{6,7},{7,6},{8,9},{9,8},{10,11... | collective-permute-start | bytes 196616 | tf_op jit(solution)/shard_map/ppermute | solution.py:345
  37.7 5.2 %collective-permute-start.16 = (bf16[128,256]{1,0:T(8,128)(2,1)S(1)}, bf16[128,256]{1,0:T(8,128)(2,1)S(1)}, u32[]{:S(2)}, u32[]{:S(2)}) collective-permute-start(bf16[128,256]{1,0:T(8,128)(2,1)S(1)} %get-tuple-element.50), channel_id=1, source_target_pairs={{0,8},{1,9},{2,10},{3,11},{4,12},{5,13},{6,14},{7,15},{8,0},{9,1},... | collective-permute-start | bytes 196616 | tf_op jit(solution)/shard_map/ppermute | solution.py:345
  40.8 6.4 %copy-start.1 = (bf16[256,1024]{1,0:T(8,128)(2,1)S(1)}, bf16[256,1024]{1,0:T(8,128)(2,1)}, u32[]{:S(2)}) copy-start(bf16[256,1024]{1,0:T(8,128)(2,1)} %value_up_ref.1) | copy-start | bytes 1572868
  42.9 4.3 %collective-permute-start.17 = (bf16[128,256]{1,0:T(8,128)(2,1)S(1)}, bf16[128,256]{1,0:T(8,128)(2,1)S(1)}, u32[]{:S(2)}, u32[]{:S(2)}) collective-permute-start(bf16[128,256]{1,0:T(8,128)(2,1)S(1)} %get-tuple-element.52), channel_id=1, source_target_pairs={{0,4},{1,5},{2,6},{3,7},{4,0},{5,1},{6,2},{7,3},{8,12},{9,13},{10,... | collective-permute-start | bytes 196616 | tf_op jit(solution)/shard_map/ppermute | solution.py:345

commit v12 on v11

--- a/solution.py
+++ b/solution.py
@@ -166,29 +166,11 @@
         ref[slots:, :] = total[draft : draft + 8]
 
 
-def route_kernel(keep_ref, came_ref, draft_latent_ref, stay_ref, send_ref, float_ref):
-    float_ref[...] = keep_ref[...] + came_ref[...]
-    slots = float_ref.shape[0] - 8
-    draft_latent_ref[...] = float_ref[slots:, :].astype(jnp.bfloat16).astype(jnp.float32)
-    size = slots // 8
-    wide = lax.axis_index("wide")
-    z, y = wide // 4, wide // 2 % 2
-    for other, ref in ((0, stay_ref), (1, send_ref)):
-        for n, (high, low) in enumerate(((0, 0), (0, 1), (1, 0), (1, 1))):
-            there = (z // 2 + high) % 2 * 2 + (z + low) % 2
-            block = there * 2 + (y + other) % 2
-            rows = pl.ds(pl.multiple_of(block * size, size), size)
-            ref[n * size : (n + 1) * size, :] = float_ref[rows, :].astype(jnp.bfloat16)
-
-
-def mix_kernel(outer, keep_ref, came_ref, stay_ref, send_ref):
-    half = keep_ref.shape[0] // 2
-    size = half // outer
-    for ref, first in ((stay_ref, 0), (send_ref, half)):
-        for n in range(outer):
-            for m, source in enumerate((keep_ref, came_ref)):
-                spot = (n * 2 + m) * size
-                ref[spot : spot + size, :] = source[first + n * size : first + (n + 1) * size, :]
+def route_kernel(keep_ref, came_ref, draft_latent_ref, out_ref):
+    slots = out_ref.shape[0]
+    out_ref[...] = (keep_ref[:slots, :] + came_ref[:slots, :]).astype(jnp.bfloat16)
+    drafts = keep_ref[slots:, :] + came_ref[slots:, :]
+    draft_latent_ref[...] = drafts.astype(jnp.bfloat16).astype(jnp.float32)
 
 
 def start_kernel(target_hbm, shard_hbm, draft_hbm, half_ref, full_ref, rows_ref, target_ref, draft_ref, sems):
@@ -259,12 +241,16 @@
     counts = jnp.concatenate(counts, 0)
     lane = lax.broadcasted_iota(jnp.int32, counts.shape, 1)
     row = lax.broadcasted_iota(jnp.int32, counts.shape, 0)
+    z, y = wide // 4, wide // 2 % 2
+    chip = lane // (2 * most_rows)
+    near, far, side = (chip // 2 + z) % 2, (chip // 4 + z // 2) % 2, (chip + y) % 2
+    source = (near * 4 + far * 2 + side) * 2 + lane // most_rows % 2
     spread = []
     for b in range(2):
         number = jnp.sum(jnp.where(lane == wide * 2 + b, counts, 0.0), 1, keepdims=True)
         limit = context_ref[b] - jnp.sum(number, 0, keepdims=True).astype(jnp.int32)
         limit_ref[b : b + 1, :] = jnp.broadcast_to(limit, (1, limit_ref.shape[1]))
-        spread.append(jnp.sum(jnp.where(lane // most_rows == row, number, 0.0), 0, keepdims=True).astype(jnp.int32))
+        spread.append(jnp.sum(jnp.where(source == row, number, 0.0), 0, keepdims=True).astype(jnp.int32))
     spot = lax.broadcasted_iota(jnp.int32, column_slot_ref.shape, 1) % most_rows
     column_slot_ref[...] = jnp.where(spot < spread[0], 0, jnp.where(spot >= most_rows - spread[1], 1, -1))
 
@@ -467,16 +453,12 @@
             [array(2 * count + 8, f32)] * 2, "down_place_rows", *rows, place, *sums, *pieces, flops=2**26,
         )
         came = swap(send, c=1)
-        block = array(count)
-        draft_latent, stay, send = call(
-            route_kernel, [array(8, f32), block, block], "route_rows", keep, came,
-            scratch_shapes=[pltpu.VMEM((2 * count + 8, width), f32)],
+        draft_latent, outgoing = call(route_kernel, [array(8, f32), array(2 * count)], "route_rows", keep, came)
+        incoming = lax.all_to_all(
+            outgoing.reshape(8, 2 * most_rows, width), "wide", split_axis=0, concat_axis=0, tiled=True,
+            axis_index_groups=[list(range(c, 16, 2)) for c in range(2)],
         )
-        came = swap(send, y=1)
-        stay, send = call(functools.partial(mix_kernel, 2), [block, block], "mix_rows", stay, came)
-        came = swap(send, z=2)
-        stay, send = call(functools.partial(mix_kernel, 1), [block, block], "mix_rows", stay, came)
-        return draft_latent, [stay, swap(send, z=1)]
+        return draft_latent, [incoming.reshape(2 * count, width)]
 
     return limit, column_slot, finish
 

time: 49.6 us -> 47.6 us (0.960)
  waiting for transfers between devices: 14.1 us -> 11.2 us
  local copies, waits for them, and re-layouts: 0.67 us -> 1.62 us
  starting transfers between devices: 21.9 us -> 21 us
  Pallas kernels: 12.6 us -> 13.2 us
    ppermute x18 -> x15, waiting for transfers between devices: 14.1 us -> 9.08 us  [swap(): return lax.ppermute(x, ('rep', 'wide'), pairs)]
    ppermute x18 -> x15, starting transfers between devices: 21.9 us -> 17.3 us  [swap(): return lax.ppermute(x, ('rep', 'wide'), pairs)]
    all_to_all x0 -> x1, starting transfers between devices: none -> 3.76 us  [finish(): lax.all_to_all(outgoing.reshape(8, 2 * most_rows, width), 'wide', split_a...]
    all_to_all x0 -> x1, waiting for transfers between devices: none -> 2.13 us  [finish(): lax.all_to_all(outgoing.reshape(8, 2 * most_rows, width), 'wide', split_a...]
    unnamed x8 -> x12, local copies, waits for them, and re-layouts: 0.67 us -> 1.62 us
    pallas_call x16 -> x14, Pallas kernels: 4.12 us -> 4.76 us  [call(): pl.pallas_call(kernel, out_shape=out_shape, in_specs=specs or [WHOLE] * l...]
  transfers between devices with their start and end apart: 18 -> 16, of which waited for: 10 -> 9; matrix products, arithmetic and copies ran while one was open for 0% -> 0% of each run, Pallas kernels for 19% -> 20%
where the time goes in v12:
time: 47.6 us; the launch traced here: 47.3 us
  starting transfers between devices  21 us (44%)
  Pallas kernels  13.2 us (28%)
  waiting for transfers between devices  11.2 us (24%)
  local copies, waits for them, and re-layouts  1.62 us (3%)
    ppermute x15, starting transfers between devices, swap(): return lax.ppermute(x, ('rep', 'wide'), pairs)  17.3 us
    ppermute x15, waiting for transfers between devices, swap(): return lax.ppermute(x, ('rep', 'wide'), pairs)  9.08 us
    pallas_call x14, Pallas kernels, call(): pl.pallas_call(kernel, out_shape=out_shape, in_specs=specs or [WHOLE] * l...  4.76 us
    pallas_call x1, Pallas kernels, local(): pl.pallas_call(functools.partial(held_kernel, arrived), out_shape=[jax.Sh...  4.01 us
    all_to_all x1, starting transfers between devices, finish(): lax.all_to_all(outgoing.reshape(8, 2 * most_rows, width), 'wide', split_a...  3.76 us
    pallas_call x1, Pallas kernels, local(): pl.pallas_call(functools.partial(window_kernel, arrived, span_rows, draft...  2.24 us
    pallas_call x1, Pallas kernels, local(): pl.pallas_call(late_kernel, out_shape=jax.ShapeDtypeStruct((slot_count, d...  2.23 us
    all_to_all x1, waiting for transfers between devices, finish(): lax.all_to_all(outgoing.reshape(8, 2 * most_rows, width), 'wide', split_a...  2.13 us
  transfers between devices with their start and end apart: 16, of which 9 were waited for; matrix products, arithmetic and copies ran while one was open for 0% of the time, Pallas kernels for 20%

profile of v12, /device:TPU:0, one launch (start us, length us, event | category | flops | bytes accessed | tf_op | source)
XLA Modules:
  0.0 47.3 jit_solution(4606749098006615596)
XLA Ops:
  0.0 0.5 collective-permute-start.8
  0.5 1.1 %start_rows.1 = (bf16[272,256]{1,0:T(8,128)(2,1)S(1)}, bf16[528,256]{1,0:T(8,128)(2,1)S(1)}, bf16[16,8192]{1,0:T(8,128)(2,1)S(1)}) custom-call(s32[1,128]{1,0:T(1,128)} %bitcast.4, bf16[512,256]{1,0:T(8,128)(2,1)} %shard_hbm.1, bf16[2,4,8192]{2,1,0:T(4,128)(2,1)} %draft_hbm.1), custom_call_target="tpu_custom_call" | custom-call | flops 1048576 | bytes 65536 | tf_op jit(solution)/shard_map/start_rows/pallas_call | solution.py:337
  1.7 3.0 %collective-permute-start.1 = (bf16[272,256]{1,0:T(8,128)(2,1)S(1)}, bf16[272,256]{1,0:T(8,128)(2,1)S(1)}, u32[]{:S(2)}, u32[]{:S(2)}) collective-permute-start(bf16[272,256]{1,0:T(8,128)(2,1)S(1)} %get-tuple-element.24.refs_0_), channel_id=1, source_target_pairs={{0,4},{1,5},{2,6},{3,7},{4,0},{5,1},{6,2},{7,3},{8,12},{9,13},{10,... | collective-permute-start | bytes 417800 | tf_op jit(solution)/shard_map/ppermute | solution.py:331
  4.7 2.6 %collective-permute-start.2 = (bf16[272,256]{1,0:T(8,128)(2,1)S(1)}, bf16[272,256]{1,0:T(8,128)(2,1)S(1)}, u32[]{:S(2)}, u32[]{:S(2)}) collective-permute-start(bf16[272,256]{1,0:T(8,128)(2,1)S(1)} %get-tuple-element.24.refs_0_), channel_id=1, source_target_pairs={{0,8},{1,9},{2,10},{3,11},{4,12},{5,13},{6,14},{7,15},{8,0},{9,1},... | collective-permute-start | bytes 417800 | tf_op jit(solution)/shard_map/ppermute | solution.py:331
  7.3 1.5 %collective-permute-start = (bf16[528,256]{1,0:T(8,128)(2,1)S(1)}, bf16[528,256]{1,0:T(8,128)(2,1)S(1)}, u32[]{:S(2)}, u32[]{:S(2)}) collective-permute-start(bf16[528,256]{1,0:T(8,128)(2,1)S(1)} %get-tuple-element.25.refs_4_), channel_id=1, source_target_pairs={{0,2},{1,3},{2,0},{3,1},{4,6},{5,7},{6,4},{7,5},{8,10},{9,11},{10,... | collective-permute-start | bytes 811016 | tf_op jit(solution)/shard_map/ppermute | solution.py:331
  8.9 0.7 %copy-done.2 = s32[2]{0:T(128)S(1)} copy-done((s32[2]{0:T(128)S(1)}, s32[2]{0:T(128)}, u32[]{:S(2)}) %copy-start.2) | copy-done | bytes 32
  9.5 4.0 %held_rows.1 = (bf16[2,512,256]{2,1,0:T(8,128)(2,1)S(1)}, f32[2,256,1]{2,1,0:T(8,128)S(1)}, f32[2,256,1]{2,1,0:T(8,128)S(1)}, f32[2,256,256]{2,1,0:T(8,128)S(1)}, bf16[2,384,256]{2,1,0:T(8,128)(2,1)S(1)}) custom-call(s32[2]{0:T(128)S(1)} %copy-done.2, bf16[2,4,8192]{2,1,0:T(4,128)(2,1)} %query_hbm.1, bf16[256,1024]{1,0:T(8,128)(2,1)} %key_up_hbm.1, ...), custom_call_target="tpu_custom_call" | custom-call | flops 2147483648 | bytes 2097152 | tf_op jit(solution)/shard_map/held_rows/pallas_call | solution.py:536
  13.6 0.5 %collective-permute-done.2.two_ref = bf16[272,256]{1,0:T(8,128)(2,1)S(1)} collective-permute-done((bf16[272,256]{1,0:T(8,128)(2,1)S(1)}, bf16[272,256]{1,0:T(8,128)(2,1)S(1)}, u32[]{:S(2)}, u32[]{:S(2)}) %collective-permute-start.2) | collective-permute-done | bytes 139296 | tf_op jit(solution)/shard_map/ppermute | solution.py:331
  14.1 1.6 %collective-permute-start.4 = (bf16[544,256]{1,0:T(8,128)(2,1)S(1)}, bf16[544,256]{1,0:T(8,128)(2,1)S(1)}, u32[]{:S(2)}, u32[]{:S(2)}) collective-permute-start(bf16[544,256]{1,0:T(8,128)(2,1)S(1)} %get-tuple-element.28.refs_2_.refs_4_), channel_id=1, source_target_pairs={{0,2},{1,3},{2,0},{3,1},{4,6},{5,7},{6,4},{7,5},{8,10},{9,11},{10,... | collective-permute-start | bytes 835592 | tf_op jit(solution)/shard_map/ppermute | solution.py:331
  15.7 0.4 collective-permute-start.5
  16.1 1.5 %collective-permute-start.9 = (bf16[512,256]{1,0:T(8,128)(2,1)S(1)}, bf16[512,256]{1,0:T(8,128)(2,1)S(1)}, u32[]{:S(2)}, u32[]{:S(2)}) collective-permute-start(bf16[512,256]{1,0:T(8,128)(2,1)S(1)} %get-tuple-element.35), channel_id=1, source_target_pairs={{0,16},{1,17},{2,18},{3,19},{4,20},{5,21},{6,22},{7,23},{8,24},{9,... | collective-permute-start | bytes 786440 | tf_op jit(solution)/shard_map/ppermute | solution.py:331
  17.6 2.7 %collective-permute-start.12 = (bf16[256,256]{1,0:T(8,128)(2,1)S(1)}, bf16[256,256]{1,0:T(8,128)(2,1)S(1)}, u32[]{:S(2)}, u32[]{:S(2)}) collective-permute-start(bf16[256,256]{1,0:T(8,128)(2,1)S(1)} %other_half.1), channel_id=1, source_target_pairs={{0,8},{1,9},{2,10},{3,11},{4,12},{5,13},{6,14},{7,15},{8,0},{9,1},... | collective-permute-start | bytes 393224 | tf_op jit(solution)/shard_map/ppermute | solution.py:331
  20.3 1.9 %collective-permute-done.5.one_ref.refs_6_.refs_5_ = bf16[272,256]{1,0:T(8,128)(2,1)S(1)} collective-permute-done((bf16[272,256]{1,0:T(8,128)(2,1)S(1)}, bf16[272,256]{1,0:T(8,128)(2,1)S(1)}, u32[]{:S(2)}, u32[]{:S(2)}) %collective-permute-start.5) | collective-permute-done | bytes 139296 | tf_op jit(solution)/shard_map/ppermute | solution.py:331
  22.2 0.6 %collective-permute-start.6 = (bf16[272,256]{1,0:T(8,128)(2,1)S(1)}, bf16[272,256]{1,0:T(8,128)(2,1)S(1)}, u32[]{:S(2)}, u32[]{:S(2)}) collective-permute-start(bf16[272,256]{1,0:T(8,128)(2,1)S(1)} %copy_piece.3), channel_id=1, source_target_pairs={{0,2},{1,3},{2,0},{3,1},{4,6},{5,7},{6,4},{7,5},{8,10},{9,11},{10,... | collective-permute-start | bytes 417800 | tf_op jit(solution)/shard_map/ppermute | solution.py:331
  22.8 1.6 %collective-permute-start.10 = (bf16[256,256]{1,0:T(8,128)(2,1)S(1)}, bf16[256,256]{1,0:T(8,128)(2,1)S(1)}, u32[]{:S(2)}, u32[]{:S(2)}) collective-permute-start(bf16[256,256]{1,0:T(8,128)(2,1)S(1)} %copy_piece.4), channel_id=1, source_target_pairs={{0,16},{1,17},{2,18},{3,19},{4,20},{5,21},{6,22},{7,23},{8,24},{9,... | collective-permute-start | bytes 393224 | tf_op jit(solution)/shard_map/ppermute | solution.py:331
  24.4 0.7 %collective-permute-done.12.refs_9_ = bf16[256,256]{1,0:T(8,128)(2,1)S(1)} collective-permute-done((bf16[256,256]{1,0:T(8,128)(2,1)S(1)}, bf16[256,256]{1,0:T(8,128)(2,1)S(1)}, u32[]{:S(2)}, u32[]{:S(2)}) %collective-permute-start.12) | collective-permute-done | bytes 131104 | tf_op jit(solution)/shard_map/ppermute | solution.py:331
  25.1 0.4 collective-permute-start.13
  25.5 0.6 %collective-permute-start.11 = (bf16[256,256]{1,0:T(8,128)(2,1)S(1)}, bf16[256,256]{1,0:T(8,128)(2,1)S(1)}, u32[]{:S(2)}, u32[]{:S(2)}) collective-permute-start(bf16[256,256]{1,0:T(8,128)(2,1)S(1)} %copy_piece.5), channel_id=1, source_target_pairs={{0,16},{1,17},{2,18},{3,19},{4,20},{5,21},{6,22},{7,23},{8,24},{9,... | collective-permute-start | bytes 393224 | tf_op jit(solution)/shard_map/ppermute | solution.py:331
  26.7 0.4 down_rows.4.refs_6_
  27.3 1.1 %collective-permute-done.10.refs_6_ = bf16[256,256]{1,0:T(8,128)(2,1)S(1)} collective-permute-done((bf16[256,256]{1,0:T(8,128)(2,1)S(1)}, bf16[256,256]{1,0:T(8,128)(2,1)S(1)}, u32[]{:S(2)}, u32[]{:S(2)}) %collective-permute-start.10) | collective-permute-done | bytes 131104 | tf_op jit(solution)/shard_map/ppermute | solution.py:331
  28.4 1.6 %collective-permute-done.13.refs_10_ = bf16[256,256]{1,0:T(8,128)(2,1)S(1)} collective-permute-done((bf16[256,256]{1,0:T(8,128)(2,1)S(1)}, bf16[256,256]{1,0:T(8,128)(2,1)S(1)}, u32[]{:S(2)}, u32[]{:S(2)}) %collective-permute-start.13) | collective-permute-done | bytes 131104 | tf_op jit(solution)/shard_map/ppermute | solution.py:331
  30.0 0.5 %collective-permute-done.11.refs_8_ = bf16[256,256]{1,0:T(8,128)(2,1)S(1)} collective-permute-done((bf16[256,256]{1,0:T(8,128)(2,1)S(1)}, bf16[256,256]{1,0:T(8,128)(2,1)S(1)}, u32[]{:S(2)}, u32[]{:S(2)}) %collective-permute-start.11) | collective-permute-done | bytes 131104 | tf_op jit(solution)/shard_map/ppermute | solution.py:331
  30.6 1.0 %down_place_rows.1 = (f32[264,256]{1,0:T(8,128)S(1)}, f32[264,256]{1,0:T(8,128)S(1)}) custom-call(bf16[128,8192]{1,0:T(8,128)(2,1)S(1)} %copy-done, bf16[128,8192]{1,0:T(8,128)(2,1)S(1)} %collective-permute-done.8.refs_1_, bf16[16,8192]{1,0:T(8,128)(2,1)S(1)} %get-tuple-element.26.mine_ref.refs_2_, ...), custom_call_target="tpu_custom_call" | custom-call | flops 67108864 | bytes 65536 | tf_op jit(solution)/shard_map/down_place_rows/pallas_call | solution.py:337
  31.7 1.5 %collective-permute-done.14.came_ref = f32[264,256]{1,0:T(8,128)S(1)} collective-permute-done((f32[264,256]{1,0:T(8,128)S(1)}, f32[264,256]{1,0:T(8,128)S(1)}, u32[]{:S(2)}, u32[]{:S(2)}) %collective-permute-start.14) | collective-permute-done | bytes 270368 | tf_op jit(solution)/shard_map/ppermute | solution.py:331
  33.3 0.7 %route_rows.1 = (f32[8,256]{1,0:T(8,128)S(1)}, bf16[256,256]{1,0:T(8,128)(2,1)}) custom-call(f32[264,256]{1,0:T(8,128)S(1)} %get-tuple-element.36.keep_ref, f32[264,256]{1,0:T(8,128)S(1)} %collective-permute-done.14.came_ref), custom_call_target="tpu_custom_call" | custom-call | flops 1048576 | bytes 65536 | tf_op jit(solution)/shard_map/route_rows/pallas_call | solution.py:337
  34.0 3.8 %all-to-all-start = ((bf16[8,32,256]{2,1,0:T(8,128)(2,1)}), bf16[8,32,256]{2,1,0:T(8,128)(2,1)S(1)}, u32[]{:S(2)}, u32[]{:S(2)}) async-start(bf16[8,32,256]{2,1,0:T(8,128)(2,1)} %bitcast.1), calls=%async_computation | async-start | bytes 262144 | tf_op jit(solution)/shard_map/all_to_all | solution.py:457
  37.8 1.2 %collective-permute-done.7.other_ref = bf16[16,2048]{1,0:T(8,128)(2,1)S(1)} collective-permute-done((bf16[16,2048]{1,0:T(8,128)(2,1)S(1)}, bf16[16,2048]{1,0:T(8,128)(2,1)S(1)}, u32[]{:S(2)}, u32[]{:S(2)}) %collective-permute-start.7) | collective-permute-done | bytes 65568 | tf_op jit(solution)/shard_map/ppermute | solution.py:331
  39.1 0.7 %count_rows.1 = (s32[2,128]{1,0:T(2,128)S(1)}, s32[1,256]{1,0:T(1,128)S(1)}) custom-call(s32[2]{0:T(128)S(1)} %copy-done.3, bf16[16,2048]{1,0:T(8,128)(2,1)S(1)} %pack_rows.1.mine_ref, bf16[16,2048]{1,0:T(8,128)(2,1)S(1)} %collective-permute-done.7.other_ref), custom_call_target="tpu_custom_call" | custom-call | flops 1048576 | bytes 65536 | tf_op jit(solution)/shard_map/count_rows/pallas_call | solution.py:337
  39.7 0.9 %copy-done.5 = f32[2,256,1]{2,1,0:T(8,128)S(1)} copy-done((f32[2,256,1]{2,1,0:T(8,128)S(1)}, f32[2,256,1]{2,1,0:T(8,128)}, u32[]{:S(2)}) %copy-start.5) | copy-done | bytes 2072
  40.7 2.2 %window_rows.1 = (f32[2,256,1]{2,1,0:T(8,128)S(1)}, f32[2,256,1]{2,1,0:T(8,128)S(1)}, f32[2,256,256]{2,1,0:T(8,128)S(1)}) custom-call(s32[2]{0:T(128)S(1)} %copy-done.3, s32[2,128]{1,0:T(2,128)S(1)} %get-tuple-element.31.limit_ref, bf16[2,512,256]{2,1,0:T(8,128)(2,1)S(1)} %get-tuple-element.30.turned_ref, ...), custom_call_target="tpu_custom_call" | custom-call | flops 1073741824 | bytes 65536 | tf_op jit(solution)/shard_map/window_rows/pallas_call | solution.py:562
  42.9 2.1 %all-to-all-done = bf16[8,32,256]{2,1,0:T(8,128)(2,1)S(1)} async-done(((bf16[8,32,256]{2,1,0:T(8,128)(2,1)}), bf16[8,32,256]{2,1,0:T(8,128)(2,1)S(1)}, u32[]{:S(2)}, u32[]{:S(2)}) %all-to-all-start) | async-done | bytes 131104 | tf_op jit(solution)/shard_map/all_to_all | solution.py:457
  45.1 2.2 %late_rows.1 = bf16[2,4,8192]{2,1,0:T(4,128)(2,1)} custom-call(s32[1,256]{1,0:T(1,128)S(1)} %get-tuple-element.29.column_slot_ref, bf16[2,512,256]{2,1,0:T(8,128)(2,1)S(1)} %get-tuple-element.30.turned_ref, f32[2,256,1]{2,1,0:T(8,128)S(1)} %get-tuple-element.39.peak_ref, f32[2,256,1]{2,1,0:T(8,128)S(1)} %get-tuple-element.40.total_ref, ...), custom_call_target="tpu_custom_call" | custom-call | tf_op jit(solution)/shard_map/late_rows/pallas_call | solution.py:571
  (29 shorter events, 1.2 us)
Async XLA Ops:
  0.0 25.5 %collective-permute-start.8 = (bf16[128,8192]{1,0:T(8,128)(2,1)}, bf16[128,8192]{1,0:T(8,128)(2,1)S(1)}, u32[]{:S(2)}, u32[]{:S(2)}) collective-permute-start(bf16[128,8192]{1,0:T(8,128)(2,1)} %refs_0_.7), channel_id=1, source_target_pairs={{0,1},{1,0},{2,3},{3,2},{4,5},{5,4},{6,7},{7,6},{8,9},{9,8},{10,11... | collective-permute-start | bytes 6291464 | tf_op jit(solution)/shard_map/ppermute | solution.py:331
  1.6 12.5 %collective-permute-start.3 = (bf16[16,8192]{1,0:T(8,128)(2,1)S(1)}, bf16[16,8192]{1,0:T(8,128)(2,1)S(1)}, u32[]{:S(2)}, u32[]{:S(2)}) collective-permute-start(bf16[16,8192]{1,0:T(8,128)(2,1)S(1)} %get-tuple-element.26.mine_ref.refs_2_), channel_id=1, source_target_pairs={{0,1},{1,0},{2,3},{3,2},{4,5},{5,4},{6,7},{7,6},{8,9},{9,8},{10,11... | collective-permute-start | bytes 786440 | tf_op jit(solution)/shard_map/ppermute | solution.py:331
  1.7 11.8 %collective-permute-start.1 = (bf16[272,256]{1,0:T(8,128)(2,1)S(1)}, bf16[272,256]{1,0:T(8,128)(2,1)S(1)}, u32[]{:S(2)}, u32[]{:S(2)}) collective-permute-start(bf16[272,256]{1,0:T(8,128)(2,1)S(1)} %get-tuple-element.24.refs_0_), channel_id=1, source_target_pairs={{0,4},{1,5},{2,6},{3,7},{4,0},{5,1},{6,2},{7,3},{8,12},{9,13},{10,... | collective-permute-start | bytes 417800 | tf_op jit(solution)/shard_map/ppermute | solution.py:331
  4.7 9.3 %collective-permute-start.2 = (bf16[272,256]{1,0:T(8,128)(2,1)S(1)}, bf16[272,256]{1,0:T(8,128)(2,1)S(1)}, u32[]{:S(2)}, u32[]{:S(2)}) collective-permute-start(bf16[272,256]{1,0:T(8,128)(2,1)S(1)} %get-tuple-element.24.refs_0_), channel_id=1, source_target_pairs={{0,8},{1,9},{2,10},{3,11},{4,12},{5,13},{6,14},{7,15},{8,0},{9,1},... | collective-permute-start | bytes 417800 | tf_op jit(solution)/shard_map/ppermute | solution.py:331
  7.3 10.3 %collective-permute-start = (bf16[528,256]{1,0:T(8,128)(2,1)S(1)}, bf16[528,256]{1,0:T(8,128)(2,1)S(1)}, u32[]{:S(2)}, u32[]{:S(2)}) collective-permute-start(bf16[528,256]{1,0:T(8,128)(2,1)S(1)} %get-tuple-element.25.refs_4_), channel_id=1, source_target_pairs={{0,2},{1,3},{2,0},{3,1},{4,6},{5,7},{6,4},{7,5},{8,10},{9,11},{10,... | collective-permute-start | bytes 811016 | tf_op jit(solution)/shard_map/ppermute | solution.py:331
  8.8 0.7 %copy-start.2 = (s32[2]{0:T(128)S(1)}, s32[2]{0:T(128)}, u32[]{:S(2)}) copy-start(s32[2]{0:T(128)} %context_ref.5) | copy-start | bytes 28
  13.5 13.1 %copy-start.4 = (f32[2,256,1]{2,1,0:T(8,128)}, f32[2,256,1]{2,1,0:T(8,128)S(1)}, u32[]{:S(2)}) copy-start(f32[2,256,1]{2,1,0:T(8,128)S(1)} %get-tuple-element.32.total_ref) | copy-start | bytes 6148
  13.5 12.8 %copy-start = (bf16[128,8192]{1,0:T(8,128)(2,1)S(1)}, bf16[128,8192]{1,0:T(8,128)(2,1)}, u32[]{:S(2)}) copy-start(bf16[128,8192]{1,0:T(8,128)(2,1)} %refs_0_.7) | copy-start | bytes 6291460
  14.1 8.0 %collective-permute-start.4 = (bf16[544,256]{1,0:T(8,128)(2,1)S(1)}, bf16[544,256]{1,0:T(8,128)(2,1)S(1)}, u32[]{:S(2)}, u32[]{:S(2)}) collective-permute-start(bf16[544,256]{1,0:T(8,128)(2,1)S(1)} %get-tuple-element.28.refs_2_.refs_4_), channel_id=1, source_target_pairs={{0,2},{1,3},{2,0},{3,1},{4,6},{5,7},{6,4},{7,5},{8,10},{9,11},{10,... | collective-permute-start | bytes 835592 | tf_op jit(solution)/shard_map/ppermute | solution.py:331
  15.7 6.5 %collective-permute-start.5 = (bf16[272,256]{1,0:T(8,128)(2,1)S(1)}, bf16[272,256]{1,0:T(8,128)(2,1)S(1)}, u32[]{:S(2)}, u32[]{:S(2)}) collective-permute-start(bf16[272,256]{1,0:T(8,128)(2,1)S(1)} %collective-permute-done.2.two_ref), channel_id=1, source_target_pairs={{0,4},{1,5},{2,6},{3,7},{4,0},{5,1},{6,2},{7,3},{8,12},{9,13},{10,... | collective-permute-start | bytes 417800 | tf_op jit(solution)/shard_map/ppermute | solution.py:331
  16.1 10.9 %collective-permute-start.9 = (bf16[512,256]{1,0:T(8,128)(2,1)S(1)}, bf16[512,256]{1,0:T(8,128)(2,1)S(1)}, u32[]{:S(2)}, u32[]{:S(2)}) collective-permute-start(bf16[512,256]{1,0:T(8,128)(2,1)S(1)} %get-tuple-element.35), channel_id=1, source_target_pairs={{0,16},{1,17},{2,18},{3,19},{4,20},{5,21},{6,22},{7,23},{8,24},{9,... | collective-permute-start | bytes 786440 | tf_op jit(solution)/shard_map/ppermute | solution.py:331
  17.6 7.4 %collective-permute-start.12 = (bf16[256,256]{1,0:T(8,128)(2,1)S(1)}, bf16[256,256]{1,0:T(8,128)(2,1)S(1)}, u32[]{:S(2)}, u32[]{:S(2)}) collective-permute-start(bf16[256,256]{1,0:T(8,128)(2,1)S(1)} %other_half.1), channel_id=1, source_target_pairs={{0,8},{1,9},{2,10},{3,11},{4,12},{5,13},{6,14},{7,15},{8,0},{9,1},... | collective-permute-start | bytes 393224 | tf_op jit(solution)/shard_map/ppermute | solution.py:331
  22.2 8.4 %collective-permute-start.6 = (bf16[272,256]{1,0:T(8,128)(2,1)S(1)}, bf16[272,256]{1,0:T(8,128)(2,1)S(1)}, u32[]{:S(2)}, u32[]{:S(2)}) collective-permute-start(bf16[272,256]{1,0:T(8,128)(2,1)S(1)} %copy_piece.3), channel_id=1, source_target_pairs={{0,2},{1,3},{2,0},{3,1},{4,6},{5,7},{6,4},{7,5},{8,10},{9,11},{10,... | collective-permute-start | bytes 417800 | tf_op jit(solution)/shard_map/ppermute | solution.py:331
  22.8 5.6 %collective-permute-start.10 = (bf16[256,256]{1,0:T(8,128)(2,1)S(1)}, bf16[256,256]{1,0:T(8,128)(2,1)S(1)}, u32[]{:S(2)}, u32[]{:S(2)}) collective-permute-start(bf16[256,256]{1,0:T(8,128)(2,1)S(1)} %copy_piece.4), channel_id=1, source_target_pairs={{0,16},{1,17},{2,18},{3,19},{4,20},{5,21},{6,22},{7,23},{8,24},{9,... | collective-permute-start | bytes 393224 | tf_op jit(solution)/shard_map/ppermute | solution.py:331
  25.1 5.0 %collective-permute-start.13 = (bf16[256,256]{1,0:T(8,128)(2,1)S(1)}, bf16[256,256]{1,0:T(8,128)(2,1)S(1)}, u32[]{:S(2)}, u32[]{:S(2)}) collective-permute-start(bf16[256,256]{1,0:T(8,128)(2,1)S(1)} %collective-permute-done.12.refs_9_), channel_id=1, source_target_pairs={{0,4},{1,5},{2,6},{3,7},{4,0},{5,1},{6,2},{7,3},{8,12},{9,13},{10,... | collective-permute-start | bytes 393224 | tf_op jit(solution)/shard_map/ppermute | solution.py:331
  25.5 5.0 %collective-permute-start.11 = (bf16[256,256]{1,0:T(8,128)(2,1)S(1)}, bf16[256,256]{1,0:T(8,128)(2,1)S(1)}, u32[]{:S(2)}, u32[]{:S(2)}) collective-permute-start(bf16[256,256]{1,0:T(8,128)(2,1)S(1)} %copy_piece.5), channel_id=1, source_target_pairs={{0,16},{1,17},{2,18},{3,19},{4,20},{5,21},{6,22},{7,23},{8,24},{9,... | collective-permute-start | bytes 393224 | tf_op jit(solution)/shard_map/ppermute | solution.py:331
  31.6 7.4 %copy-start.3 = (s32[2]{0:T(128)S(1)}, s32[2]{0:T(128)}, u32[]{:S(2)}) copy-start(s32[2]{0:T(128)} %context_ref.5) | copy-start | bytes 28
  31.6 1.6 %collective-permute-start.14 = (f32[264,256]{1,0:T(8,128)S(1)}, f32[264,256]{1,0:T(8,128)S(1)}, u32[]{:S(2)}, u32[]{:S(2)}) collective-permute-start(f32[264,256]{1,0:T(8,128)S(1)} %get-tuple-element.37), channel_id=1, source_target_pairs={{0,1},{1,0},{2,3},{3,2},{4,5},{5,4},{6,7},{7,6},{8,9},{9,8},{10,11... | collective-permute-start | bytes 811016 | tf_op jit(solution)/shard_map/ppermute | solution.py:331
  34.0 11.1 %all-to-all-start = ((bf16[8,32,256]{2,1,0:T(8,128)(2,1)}), bf16[8,32,256]{2,1,0:T(8,128)(2,1)S(1)}, u32[]{:S(2)}, u32[]{:S(2)}) async-start(bf16[8,32,256]{2,1,0:T(8,128)(2,1)} %bitcast.1), calls=%async_computation | async-start | bytes 262144 | tf_op jit(solution)/shard_map/all_to_all | solution.py:457
  37.7 7.3 %copy-start.1 = (bf16[256,1024]{1,0:T(8,128)(2,1)S(1)}, bf16[256,1024]{1,0:T(8,128)(2,1)}, u32[]{:S(2)}) copy-start(bf16[256,1024]{1,0:T(8,128)(2,1)} %value_up_ref.1) | copy-start | bytes 1572868
  37.7 1.3 %collective-permute-start.7 = (bf16[16,2048]{1,0:T(8,128)(2,1)S(1)}, bf16[16,2048]{1,0:T(8,128)(2,1)S(1)}, u32[]{:S(2)}, u32[]{:S(2)}) collective-permute-start(bf16[16,2048]{1,0:T(8,128)(2,1)S(1)} %pack_rows.1.mine_ref), channel_id=1, source_target_pairs={{0,1},{1,0},{2,3},{3,2},{4,5},{5,4},{6,7},{7,6},{8,9},{9,8},{10,11... | collective-permute-start | bytes 196616 | tf_op jit(solution)/shard_map/ppermute | solution.py:331
  39.7 1.0 %copy-start.5 = (f32[2,256,1]{2,1,0:T(8,128)S(1)}, f32[2,256,1]{2,1,0:T(8,128)}, u32[]{:S(2)}) copy-start(f32[2,256,1]{2,1,0:T(8,128)} %copy-done.4) | copy-start | bytes 6148

commit v13 on v12

--- a/solution.py
+++ b/solution.py
@@ -208,6 +208,12 @@
     bare_ref[rows - 16 :, :] = two_ref[: rows - 16, :]
 
 
+def append_kernel(one_ref, two_ref, out_ref):
+    rows = one_ref.shape[0]
+    out_ref[:rows, :] = one_ref[...]
+    out_ref[rows:, :] = two_ref[: out_ref.shape[0] - rows, :]
+
+
 def copy_kernel(spans, one_ref, *refs):
     done = 0
     for first, count in spans:
@@ -292,15 +298,17 @@
     block = incoming_refs[0].shape[0]
     for n, ref in enumerate(incoming_refs):
         rows_ref[n * block : (n + 1) * block, :] = ref[...]
+    ones = jnp.ones((rows_ref.shape[0], HEAD_SIZE), jnp.bfloat16)
     for b in range(slot_count):
         scores = join_rows(lax.dot_general(turned_ref[b], rows_ref[...], NT, preferred_element_type=jnp.float32))
         scores = jnp.where(column_slot_ref[...] == b, scores, FAR)
         peak = jnp.maximum(jnp.max(scores, 1, keepdims=True), peak_ref[b])
-        weights = jnp.exp2(scores - peak)
+        weights = split_rows(jnp.exp2(scores - peak))
         fade = jnp.exp2(peak_ref[b] - peak)
-        total = total_ref[b] * fade + jnp.sum(weights, 1, keepdims=True)
-        mixed = join_rows(jnp.dot(split_rows(weights), rows_ref[...], preferred_element_type=jnp.float32))
-        parted_ref[b] = split_rows((mixed_ref[b] * fade + mixed) / total)
+        added = join_rows(jnp.dot(weights, ones, preferred_element_type=jnp.float32))
+        total = total_ref[b] * fade + added[:, :1]
+        mixed = join_rows(jnp.dot(weights, rows_ref[...], preferred_element_type=jnp.float32))
+        parted_ref[b] = split_rows((mixed_ref[b] * fade + mixed) * (1.0 / total))
     for k in range(heads_kv):
         part = []
         for b in range(slot_count):
@@ -379,9 +387,11 @@
         specs=[WHOLE] * 2 + [UNREAD] * 2,
     )
     yab, xab = swap(zab, y=1), swap(bare, r=1)
-    zc, dc = swap(zb, z=1), swap(db, z=1)
+    quarter = half_rows // 2
+    zc = swap(call(append_kernel, array(ext + quarter), "append_piece", zb, rest), z=1)
+    dc = swap(db, z=1)
     xc = swap(copy(zc, [(0, half_rows)]), r=1)
-    xya = swap(copy(yab, [(0, half_rows)]), r=1)
+    xya = swap(copy(yab, [(quarter, quarter)]), r=1)
     yc = swap(copy(zc, [(0, ext)], yab), y=1)
 
     order = [
@@ -427,13 +437,14 @@
              (1, 0, half_rows, (0, 1, 1)), (1, ext, half_rows, (0, 2, 1))],
         ),
         (
-            [xab, zc],
-            [(0, 0, half_rows, (1, 1, 0)), (0, half_rows, half_rows, (1, 2, 0)), (1, 0, half_rows, (0, 3, 0))],
+            [xab, zc, xc],
+            [(0, 0, half_rows, (1, 1, 0)), (0, half_rows, half_rows, (1, 2, 0)), (1, 0, half_rows, (0, 3, 0)),
+             (1, ext, quarter, (1, 1, 1)), (2, 0, half_rows, (1, 3, 0))],
         ),
         (
-            [xc, yc, xya, db, dc],
-            [(0, 0, half_rows, (1, 3, 0)), (1, 0, half_rows, (0, 3, 1)), (2, 0, half_rows, (1, 1, 1)),
-             (3, 0, half_rows, (1, 2, 1)), (4, 0, half_rows, (1, 3, 1))],
+            [yc, xya, db, dc],
+            [(0, 0, half_rows, (0, 3, 1)), (1, 0, quarter, (1, 1, 1), quarter), (2, 0, half_rows, (1, 2, 1)),
+             (3, 0, half_rows, (1, 3, 1))],
         ),
     ]
     sums = []

time: 47.6 us -> 49 us (1.029)
  waiting for transfers between devices: 11.2 us -> 12.4 us
  starting transfers between devices: 21 us -> 21.5 us
    ppermute x15, waiting for transfers between devices: 9.08 us -> 10.3 us  [swap(): return lax.ppermute(x, ('rep', 'wide'), pairs)]
    all_to_all x1, starting transfers between devices: 3.76 us -> 4.47 us  [finish(): lax.all_to_all(outgoing.reshape(8, 2 * most_rows, width), 'wide', split_a...]
    pallas_call x14 -> x15, Pallas kernels: 4.76 us -> 4.71 us  [call(): pl.pallas_call(kernel, out_shape=out_shape, in_specs=specs or [WHOLE] * l...]
  transfers between devices with their start and end apart: 16 -> 16, of which waited for: 9 -> 7; matrix products, arithmetic and copies ran while one was open for 0% -> 0% of each run, Pallas kernels for 20% -> 19%
where the time goes in v13:
time: 49 us; the launch traced here: 48.7 us
  starting transfers between devices  21.5 us (44%)
  Pallas kernels  12.9 us (26%)
  waiting for transfers between devices  12.4 us (25%)
  local copies, waits for them, and re-layouts  1.62 us (3%)
    ppermute x15, starting transfers between devices, swap(): return lax.ppermute(x, ('rep', 'wide'), pairs)  17.1 us
    ppermute x15, waiting for transfers between devices, swap(): return lax.ppermute(x, ('rep', 'wide'), pairs)  10.3 us
    pallas_call x15, Pallas kernels, call(): pl.pallas_call(kernel, out_shape=out_shape, in_specs=specs or [WHOLE] * l...  4.71 us
    all_to_all x1, starting transfers between devices, finish(): lax.all_to_all(outgoing.reshape(8, 2 * most_rows, width), 'wide', split_a...  4.47 us
    pallas_call x1, Pallas kernels, local(): pl.pallas_call(functools.partial(held_kernel, arrived), out_shape=[jax.Sh...  4.01 us
    pallas_call x1, Pallas kernels, local(): pl.pallas_call(functools.partial(window_kernel, arrived, span_rows, draft...  2.25 us
    all_to_all x1, waiting for transfers between devices, finish(): lax.all_to_all(outgoing.reshape(8, 2 * most_rows, width), 'wide', split_a...  2.13 us
    pallas_call x1, Pallas kernels, local(): pl.pallas_call(late_kernel, out_shape=jax.ShapeDtypeStruct((slot_count, d...  1.94 us
  transfers between devices with their start and end apart: 16, of which 7 were waited for; matrix products, arithmetic and copies ran while one was open for 0% of the time, Pallas kernels for 19%

profile of v13, /device:TPU:0, one launch (start us, length us, event | category | flops | bytes accessed | tf_op | source)
XLA Modules:
  0.0 48.7 jit_solution(4119942528663342746)
XLA Ops:
  0.0 0.5 collective-permute-start.8
  0.5 1.1 %start_rows.1 = (bf16[272,256]{1,0:T(8,128)(2,1)S(1)}, bf16[528,256]{1,0:T(8,128)(2,1)S(1)}, bf16[16,8192]{1,0:T(8,128)(2,1)S(1)}) custom-call(s32[1,128]{1,0:T(1,128)} %bitcast.4, bf16[512,256]{1,0:T(8,128)(2,1)} %shard_hbm.1, bf16[2,4,8192]{2,1,0:T(4,128)(2,1)} %draft_hbm.1), custom_call_target="tpu_custom_call" | custom-call | flops 1048576 | bytes 65536 | tf_op jit(solution)/shard_map/start_rows/pallas_call | solution.py:345
  1.7 3.0 %collective-permute-start.1 = (bf16[272,256]{1,0:T(8,128)(2,1)S(1)}, bf16[272,256]{1,0:T(8,128)(2,1)S(1)}, u32[]{:S(2)}, u32[]{:S(2)}) collective-permute-start(bf16[272,256]{1,0:T(8,128)(2,1)S(1)} %get-tuple-element.24.refs_0_), channel_id=1, source_target_pairs={{0,4},{1,5},{2,6},{3,7},{4,0},{5,1},{6,2},{7,3},{8,12},{9,13},{10,... | collective-permute-start | bytes 417800 | tf_op jit(solution)/shard_map/ppermute | solution.py:339
  4.7 2.6 %collective-permute-start.2 = (bf16[272,256]{1,0:T(8,128)(2,1)S(1)}, bf16[272,256]{1,0:T(8,128)(2,1)S(1)}, u32[]{:S(2)}, u32[]{:S(2)}) collective-permute-start(bf16[272,256]{1,0:T(8,128)(2,1)S(1)} %get-tuple-element.24.refs_0_), channel_id=1, source_target_pairs={{0,8},{1,9},{2,10},{3,11},{4,12},{5,13},{6,14},{7,15},{8,0},{9,1},... | collective-permute-start | bytes 417800 | tf_op jit(solution)/shard_map/ppermute | solution.py:339
  7.3 1.5 %collective-permute-start = (bf16[528,256]{1,0:T(8,128)(2,1)S(1)}, bf16[528,256]{1,0:T(8,128)(2,1)S(1)}, u32[]{:S(2)}, u32[]{:S(2)}) collective-permute-start(bf16[528,256]{1,0:T(8,128)(2,1)S(1)} %get-tuple-element.25.refs_4_), channel_id=1, source_target_pairs={{0,2},{1,3},{2,0},{3,1},{4,6},{5,7},{6,4},{7,5},{8,10},{9,11},{10,... | collective-permute-start | bytes 811016 | tf_op jit(solution)/shard_map/ppermute | solution.py:339
  8.9 0.7 %copy-done.2 = s32[2]{0:T(128)S(1)} copy-done((s32[2]{0:T(128)S(1)}, s32[2]{0:T(128)}, u32[]{:S(2)}) %copy-start.2) | copy-done | bytes 32
  9.5 4.0 %held_rows.1 = (bf16[2,512,256]{2,1,0:T(8,128)(2,1)S(1)}, f32[2,256,1]{2,1,0:T(8,128)S(1)}, f32[2,256,1]{2,1,0:T(8,128)S(1)}, f32[2,256,256]{2,1,0:T(8,128)S(1)}, bf16[2,384,256]{2,1,0:T(8,128)(2,1)S(1)}) custom-call(s32[2]{0:T(128)S(1)} %copy-done.2, bf16[2,4,8192]{2,1,0:T(4,128)(2,1)} %query_hbm.1, bf16[256,1024]{1,0:T(8,128)(2,1)} %key_up_hbm.1, ...), custom_call_target="tpu_custom_call" | custom-call | flops 2147483648 | bytes 2097152 | tf_op jit(solution)/shard_map/held_rows/pallas_call | solution.py:547
  13.6 0.5 %collective-permute-done.2.two_ref.one_ref = bf16[272,256]{1,0:T(8,128)(2,1)S(1)} collective-permute-done((bf16[272,256]{1,0:T(8,128)(2,1)S(1)}, bf16[272,256]{1,0:T(8,128)(2,1)S(1)}, u32[]{:S(2)}, u32[]{:S(2)}) %collective-permute-start.2) | collective-permute-done | bytes 139296 | tf_op jit(solution)/shard_map/ppermute | solution.py:339
  14.1 1.6 %collective-permute-start.4 = (bf16[544,256]{1,0:T(8,128)(2,1)S(1)}, bf16[544,256]{1,0:T(8,128)(2,1)S(1)}, u32[]{:S(2)}, u32[]{:S(2)}) collective-permute-start(bf16[544,256]{1,0:T(8,128)(2,1)S(1)} %get-tuple-element.28.refs_2_.refs_4_), channel_id=1, source_target_pairs={{0,2},{1,3},{2,0},{3,1},{4,6},{5,7},{6,4},{7,5},{8,10},{9,11},{10,... | collective-permute-start | bytes 835592 | tf_op jit(solution)/shard_map/ppermute | solution.py:339
  15.7 0.5 %collective-permute-start.5 = (bf16[400,256]{1,0:T(8,128)(2,1)S(1)}, bf16[400,256]{1,0:T(8,128)(2,1)S(1)}, u32[]{:S(2)}, u32[]{:S(2)}) collective-permute-start(bf16[400,256]{1,0:T(8,128)(2,1)S(1)} %append_piece.1), channel_id=1, source_target_pairs={{0,4},{1,5},{2,6},{3,7},{4,0},{5,1},{6,2},{7,3},{8,12},{9,13},{10,... | collective-permute-start | bytes 614408 | tf_op jit(solution)/shard_map/ppermute | solution.py:339
  16.2 1.5 %collective-permute-start.9 = (bf16[512,256]{1,0:T(8,128)(2,1)S(1)}, bf16[512,256]{1,0:T(8,128)(2,1)S(1)}, u32[]{:S(2)}, u32[]{:S(2)}) collective-permute-start(bf16[512,256]{1,0:T(8,128)(2,1)S(1)} %get-tuple-element.35), channel_id=1, source_target_pairs={{0,16},{1,17},{2,18},{3,19},{4,20},{5,21},{6,22},{7,23},{8,24},{9,... | collective-permute-start | bytes 786440 | tf_op jit(solution)/shard_map/ppermute | solution.py:339
  17.7 2.6 %collective-permute-start.12 = (bf16[256,256]{1,0:T(8,128)(2,1)S(1)}, bf16[256,256]{1,0:T(8,128)(2,1)S(1)}, u32[]{:S(2)}, u32[]{:S(2)}) collective-permute-start(bf16[256,256]{1,0:T(8,128)(2,1)S(1)} %other_half.1.two_ref), channel_id=1, source_target_pairs={{0,8},{1,9},{2,10},{3,11},{4,12},{5,13},{6,14},{7,15},{8,0},{9,1},... | collective-permute-start | bytes 393224 | tf_op jit(solution)/shard_map/ppermute | solution.py:339
  20.3 3.8 %collective-permute-done.5.one_ref.refs_6_.refs_5_ = bf16[400,256]{1,0:T(8,128)(2,1)S(1)} collective-permute-done((bf16[400,256]{1,0:T(8,128)(2,1)S(1)}, bf16[400,256]{1,0:T(8,128)(2,1)S(1)}, u32[]{:S(2)}, u32[]{:S(2)}) %collective-permute-start.5) | collective-permute-done | bytes 204832 | tf_op jit(solution)/shard_map/ppermute | solution.py:339
  24.1 0.2 collective-permute-start.6
  24.3 2.4 %collective-permute-start.10 = (bf16[256,256]{1,0:T(8,128)(2,1)S(1)}, bf16[256,256]{1,0:T(8,128)(2,1)S(1)}, u32[]{:S(2)}, u32[]{:S(2)}) collective-permute-start(bf16[256,256]{1,0:T(8,128)(2,1)S(1)} %copy_piece.4), channel_id=1, source_target_pairs={{0,16},{1,17},{2,18},{3,19},{4,20},{5,21},{6,22},{7,23},{8,24},{9,... | collective-permute-start | bytes 393224 | tf_op jit(solution)/shard_map/ppermute | solution.py:339
  26.7 0.5 collective-permute-start.11
  27.2 0.2 place_rows.1.refs_4_
  27.3 0.3 down_rows.3.refs_6_
  27.7 0.4 down_rows.4.refs_7_
  28.1 1.6 %collective-permute-done.10.refs_6_ = bf16[256,256]{1,0:T(8,128)(2,1)S(1)} collective-permute-done((bf16[256,256]{1,0:T(8,128)(2,1)S(1)}, bf16[256,256]{1,0:T(8,128)(2,1)S(1)}, u32[]{:S(2)}, u32[]{:S(2)}) %collective-permute-start.10) | collective-permute-done | bytes 131104 | tf_op jit(solution)/shard_map/ppermute | solution.py:339
  29.6 0.4 down_rows.5.refs_5_
  30.0 1.6 %collective-permute-done.13.refs_9_ = bf16[256,256]{1,0:T(8,128)(2,1)S(1)} collective-permute-done((bf16[256,256]{1,0:T(8,128)(2,1)S(1)}, bf16[256,256]{1,0:T(8,128)(2,1)S(1)}, u32[]{:S(2)}, u32[]{:S(2)}) %collective-permute-start.13) | collective-permute-done | bytes 131104 | tf_op jit(solution)/shard_map/ppermute | solution.py:339
  31.7 0.9 %down_place_rows.1 = (f32[264,256]{1,0:T(8,128)S(1)}, f32[264,256]{1,0:T(8,128)S(1)}) custom-call(bf16[128,8192]{1,0:T(8,128)(2,1)S(1)} %copy-done, bf16[128,8192]{1,0:T(8,128)(2,1)S(1)} %collective-permute-done.8.refs_1_, bf16[16,8192]{1,0:T(8,128)(2,1)S(1)} %get-tuple-element.26.mine_ref.refs_2_, ...), custom_call_target="tpu_custom_call" | custom-call | flops 67108864 | bytes 65536 | tf_op jit(solution)/shard_map/down_place_rows/pallas_call | solution.py:345
  32.7 1.5 %collective-permute-done.14.came_ref = f32[264,256]{1,0:T(8,128)S(1)} collective-permute-done((f32[264,256]{1,0:T(8,128)S(1)}, f32[264,256]{1,0:T(8,128)S(1)}, u32[]{:S(2)}, u32[]{:S(2)}) %collective-permute-start.14) | collective-permute-done | bytes 270368 | tf_op jit(solution)/shard_map/ppermute | solution.py:339
  34.2 0.7 %route_rows.1 = (f32[8,256]{1,0:T(8,128)S(1)}, bf16[256,256]{1,0:T(8,128)(2,1)}) custom-call(f32[264,256]{1,0:T(8,128)S(1)} %get-tuple-element.36.keep_ref, f32[264,256]{1,0:T(8,128)S(1)} %collective-permute-done.14.came_ref), custom_call_target="tpu_custom_call" | custom-call | flops 1048576 | bytes 65536 | tf_op jit(solution)/shard_map/route_rows/pallas_call | solution.py:345
  34.9 4.5 %all-to-all-start = ((bf16[8,32,256]{2,1,0:T(8,128)(2,1)}), bf16[8,32,256]{2,1,0:T(8,128)(2,1)S(1)}, u32[]{:S(2)}, u32[]{:S(2)}) async-start(bf16[8,32,256]{2,1,0:T(8,128)(2,1)} %bitcast.1), calls=%async_computation | async-start | bytes 262144 | tf_op jit(solution)/shard_map/all_to_all | solution.py:468
  39.5 1.2 %collective-permute-done.7.other_ref = bf16[16,2048]{1,0:T(8,128)(2,1)S(1)} collective-permute-done((bf16[16,2048]{1,0:T(8,128)(2,1)S(1)}, bf16[16,2048]{1,0:T(8,128)(2,1)S(1)}, u32[]{:S(2)}, u32[]{:S(2)}) %collective-permute-start.7) | collective-permute-done | bytes 65568 | tf_op jit(solution)/shard_map/ppermute | solution.py:339
  40.7 0.7 %count_rows.1 = (s32[2,128]{1,0:T(2,128)S(1)}, s32[1,256]{1,0:T(1,128)S(1)}) custom-call(s32[2]{0:T(128)S(1)} %copy-done.3, bf16[16,2048]{1,0:T(8,128)(2,1)S(1)} %pack_rows.1.mine_ref, bf16[16,2048]{1,0:T(8,128)(2,1)S(1)} %collective-permute-done.7.other_ref), custom_call_target="tpu_custom_call" | custom-call | flops 1048576 | bytes 65536 | tf_op jit(solution)/shard_map/count_rows/pallas_call | solution.py:345
  41.4 0.9 %copy-done.5 = f32[2,256,1]{2,1,0:T(8,128)S(1)} copy-done((f32[2,256,1]{2,1,0:T(8,128)S(1)}, f32[2,256,1]{2,1,0:T(8,128)}, u32[]{:S(2)}) %copy-start.5) | copy-done | bytes 2072
  42.3 2.2 %window_rows.1 = (f32[2,256,1]{2,1,0:T(8,128)S(1)}, f32[2,256,1]{2,1,0:T(8,128)S(1)}, f32[2,256,256]{2,1,0:T(8,128)S(1)}) custom-call(s32[2]{0:T(128)S(1)} %copy-done.3, s32[2,128]{1,0:T(2,128)S(1)} %get-tuple-element.31.limit_ref, bf16[2,512,256]{2,1,0:T(8,128)(2,1)S(1)} %get-tuple-element.30.turned_ref, ...), custom_call_target="tpu_custom_call" | custom-call | flops 1073741824 | bytes 65536 | tf_op jit(solution)/shard_map/window_rows/pallas_call | solution.py:573
  44.6 2.1 %all-to-all-done = bf16[8,32,256]{2,1,0:T(8,128)(2,1)S(1)} async-done(((bf16[8,32,256]{2,1,0:T(8,128)(2,1)}), bf16[8,32,256]{2,1,0:T(8,128)(2,1)S(1)}, u32[]{:S(2)}, u32[]{:S(2)}) %all-to-all-start) | async-done | bytes 131104 | tf_op jit(solution)/shard_map/all_to_all | solution.py:468
  46.7 1.9 %late_rows.1 = bf16[2,4,8192]{2,1,0:T(4,128)(2,1)} custom-call(s32[1,256]{1,0:T(1,128)S(1)} %get-tuple-element.29.column_slot_ref, bf16[2,512,256]{2,1,0:T(8,128)(2,1)S(1)} %get-tuple-element.30.turned_ref, f32[2,256,1]{2,1,0:T(8,128)S(1)} %get-tuple-element.39.peak_ref, f32[2,256,1]{2,1,0:T(8,128)S(1)} %get-tuple-element.40.total_ref, ...), custom_call_target="tpu_custom_call" | custom-call | tf_op jit(solution)/shard_map/late_rows/pallas_call | solution.py:582
  (30 shorter events, 0.4 us)
Async XLA Ops:
  0.0 26.7 %collective-permute-start.8 = (bf16[128,8192]{1,0:T(8,128)(2,1)}, bf16[128,8192]{1,0:T(8,128)(2,1)S(1)}, u32[]{:S(2)}, u32[]{:S(2)}) collective-permute-start(bf16[128,8192]{1,0:T(8,128)(2,1)} %refs_0_.7), channel_id=1, source_target_pairs={{0,1},{1,0},{2,3},{3,2},{4,5},{5,4},{6,7},{7,6},{8,9},{9,8},{10,11... | collective-permute-start | bytes 6291464 | tf_op jit(solution)/shard_map/ppermute | solution.py:339
  1.6 12.5 %collective-permute-start.3 = (bf16[16,8192]{1,0:T(8,128)(2,1)S(1)}, bf16[16,8192]{1,0:T(8,128)(2,1)S(1)}, u32[]{:S(2)}, u32[]{:S(2)}) collective-permute-start(bf16[16,8192]{1,0:T(8,128)(2,1)S(1)} %get-tuple-element.26.mine_ref.refs_2_), channel_id=1, source_target_pairs={{0,1},{1,0},{2,3},{3,2},{4,5},{5,4},{6,7},{7,6},{8,9},{9,8},{10,11... | collective-permute-start | bytes 786440 | tf_op jit(solution)/shard_map/ppermute | solution.py:339
  1.7 11.8 %collective-permute-start.1 = (bf16[272,256]{1,0:T(8,128)(2,1)S(1)}, bf16[272,256]{1,0:T(8,128)(2,1)S(1)}, u32[]{:S(2)}, u32[]{:S(2)}) collective-permute-start(bf16[272,256]{1,0:T(8,128)(2,1)S(1)} %get-tuple-element.24.refs_0_), channel_id=1, source_target_pairs={{0,4},{1,5},{2,6},{3,7},{4,0},{5,1},{6,2},{7,3},{8,12},{9,13},{10,... | collective-permute-start | bytes 417800 | tf_op jit(solution)/shard_map/ppermute | solution.py:339
  4.7 9.3 %collective-permute-start.2 = (bf16[272,256]{1,0:T(8,128)(2,1)S(1)}, bf16[272,256]{1,0:T(8,128)(2,1)S(1)}, u32[]{:S(2)}, u32[]{:S(2)}) collective-permute-start(bf16[272,256]{1,0:T(8,128)(2,1)S(1)} %get-tuple-element.24.refs_0_), channel_id=1, source_target_pairs={{0,8},{1,9},{2,10},{3,11},{4,12},{5,13},{6,14},{7,15},{8,0},{9,1},... | collective-permute-start | bytes 417800 | tf_op jit(solution)/shard_map/ppermute | solution.py:339
  7.3 8.3 %collective-permute-start = (bf16[528,256]{1,0:T(8,128)(2,1)S(1)}, bf16[528,256]{1,0:T(8,128)(2,1)S(1)}, u32[]{:S(2)}, u32[]{:S(2)}) collective-permute-start(bf16[528,256]{1,0:T(8,128)(2,1)S(1)} %get-tuple-element.25.refs_4_), channel_id=1, source_target_pairs={{0,2},{1,3},{2,0},{3,1},{4,6},{5,7},{6,4},{7,5},{8,10},{9,11},{10,... | collective-permute-start | bytes 811016 | tf_op jit(solution)/shard_map/ppermute | solution.py:339
  8.8 0.7 %copy-start.2 = (s32[2]{0:T(128)S(1)}, s32[2]{0:T(128)}, u32[]{:S(2)}) copy-start(s32[2]{0:T(128)} %context_ref.5) | copy-start | bytes 28
  13.5 2.2 %copy-start.4 = (f32[2,256,1]{2,1,0:T(8,128)}, f32[2,256,1]{2,1,0:T(8,128)S(1)}, u32[]{:S(2)}) copy-start(f32[2,256,1]{2,1,0:T(8,128)S(1)} %get-tuple-element.32.total_ref) | copy-start | bytes 6148
  13.5 13.8 %copy-start = (bf16[128,8192]{1,0:T(8,128)(2,1)S(1)}, bf16[128,8192]{1,0:T(8,128)(2,1)}, u32[]{:S(2)}) copy-start(bf16[128,8192]{1,0:T(8,128)(2,1)} %refs_0_.7) | copy-start | bytes 6291460
  14.1 10.0 %collective-permute-start.4 = (bf16[544,256]{1,0:T(8,128)(2,1)S(1)}, bf16[544,256]{1,0:T(8,128)(2,1)S(1)}, u32[]{:S(2)}, u32[]{:S(2)}) collective-permute-start(bf16[544,256]{1,0:T(8,128)(2,1)S(1)} %get-tuple-element.28.refs_2_.refs_4_), channel_id=1, source_target_pairs={{0,2},{1,3},{2,0},{3,1},{4,6},{5,7},{6,4},{7,5},{8,10},{9,11},{10,... | collective-permute-start | bytes 835592 | tf_op jit(solution)/shard_map/ppermute | solution.py:339
  15.7 8.4 %collective-permute-start.5 = (bf16[400,256]{1,0:T(8,128)(2,1)S(1)}, bf16[400,256]{1,0:T(8,128)(2,1)S(1)}, u32[]{:S(2)}, u32[]{:S(2)}) collective-permute-start(bf16[400,256]{1,0:T(8,128)(2,1)S(1)} %append_piece.1), channel_id=1, source_target_pairs={{0,4},{1,5},{2,6},{3,7},{4,0},{5,1},{6,2},{7,3},{8,12},{9,13},{10,... | collective-permute-start | bytes 614408 | tf_op jit(solution)/shard_map/ppermute | solution.py:339
  16.2 11.8 %collective-permute-start.9 = (bf16[512,256]{1,0:T(8,128)(2,1)S(1)}, bf16[512,256]{1,0:T(8,128)(2,1)S(1)}, u32[]{:S(2)}, u32[]{:S(2)}) collective-permute-start(bf16[512,256]{1,0:T(8,128)(2,1)S(1)} %get-tuple-element.35), channel_id=1, source_target_pairs={{0,16},{1,17},{2,18},{3,19},{4,20},{5,21},{6,22},{7,23},{8,24},{9,... | collective-permute-start | bytes 786440 | tf_op jit(solution)/shard_map/ppermute | solution.py:339
  17.7 9.0 %collective-permute-start.12 = (bf16[256,256]{1,0:T(8,128)(2,1)S(1)}, bf16[256,256]{1,0:T(8,128)(2,1)S(1)}, u32[]{:S(2)}, u32[]{:S(2)}) collective-permute-start(bf16[256,256]{1,0:T(8,128)(2,1)S(1)} %other_half.1.two_ref), channel_id=1, source_target_pairs={{0,8},{1,9},{2,10},{3,11},{4,12},{5,13},{6,14},{7,15},{8,0},{9,1},... | collective-permute-start | bytes 393224 | tf_op jit(solution)/shard_map/ppermute | solution.py:339
  24.1 7.6 %collective-permute-start.6 = (bf16[272,256]{1,0:T(8,128)(2,1)S(1)}, bf16[272,256]{1,0:T(8,128)(2,1)S(1)}, u32[]{:S(2)}, u32[]{:S(2)}) collective-permute-start(bf16[272,256]{1,0:T(8,128)(2,1)S(1)} %copy_piece.3), channel_id=1, source_target_pairs={{0,2},{1,3},{2,0},{3,1},{4,6},{5,7},{6,4},{7,5},{8,10},{9,11},{10,... | collective-permute-start | bytes 417800 | tf_op jit(solution)/shard_map/ppermute | solution.py:339
  24.3 5.3 %collective-permute-start.10 = (bf16[256,256]{1,0:T(8,128)(2,1)S(1)}, bf16[256,256]{1,0:T(8,128)(2,1)S(1)}, u32[]{:S(2)}, u32[]{:S(2)}) collective-permute-start(bf16[256,256]{1,0:T(8,128)(2,1)S(1)} %copy_piece.4), channel_id=1, source_target_pairs={{0,16},{1,17},{2,18},{3,19},{4,20},{5,21},{6,22},{7,23},{8,24},{9,... | collective-permute-start | bytes 393224 | tf_op jit(solution)/shard_map/ppermute | solution.py:339
  26.7 5.0 %collective-permute-start.13 = (bf16[256,256]{1,0:T(8,128)(2,1)S(1)}, bf16[256,256]{1,0:T(8,128)(2,1)S(1)}, u32[]{:S(2)}, u32[]{:S(2)}) collective-permute-start(bf16[256,256]{1,0:T(8,128)(2,1)S(1)} %collective-permute-done.12.refs_8_), channel_id=1, source_target_pairs={{0,4},{1,5},{2,6},{3,7},{4,0},{5,1},{6,2},{7,3},{8,12},{9,13},{10,... | collective-permute-start | bytes 393224 | tf_op jit(solution)/shard_map/ppermute | solution.py:339
  26.7 4.9 %collective-permute-start.11 = (bf16[128,256]{1,0:T(8,128)(2,1)S(1)}, bf16[128,256]{1,0:T(8,128)(2,1)S(1)}, u32[]{:S(2)}, u32[]{:S(2)}) collective-permute-start(bf16[128,256]{1,0:T(8,128)(2,1)S(1)} %copy_piece.5), channel_id=1, source_target_pairs={{0,16},{1,17},{2,18},{3,19},{4,20},{5,21},{6,22},{7,23},{8,24},{9,... | collective-permute-start | bytes 196616 | tf_op jit(solution)/shard_map/ppermute | solution.py:339
  32.6 8.1 %copy-start.3 = (s32[2]{0:T(128)S(1)}, s32[2]{0:T(128)}, u32[]{:S(2)}) copy-start(s32[2]{0:T(128)} %context_ref.5) | copy-start | bytes 28
  32.6 1.6 %collective-permute-start.14 = (f32[264,256]{1,0:T(8,128)S(1)}, f32[264,256]{1,0:T(8,128)S(1)}, u32[]{:S(2)}, u32[]{:S(2)}) collective-permute-start(f32[264,256]{1,0:T(8,128)S(1)} %get-tuple-element.37), channel_id=1, source_target_pairs={{0,1},{1,0},{2,3},{3,2},{4,5},{5,4},{6,7},{7,6},{8,9},{9,8},{10,11... | collective-permute-start | bytes 811016 | tf_op jit(solution)/shard_map/ppermute | solution.py:339
  34.9 11.8 %all-to-all-start = ((bf16[8,32,256]{2,1,0:T(8,128)(2,1)}), bf16[8,32,256]{2,1,0:T(8,128)(2,1)S(1)}, u32[]{:S(2)}, u32[]{:S(2)}) async-start(bf16[8,32,256]{2,1,0:T(8,128)(2,1)} %bitcast.1), calls=%async_computation | async-start | bytes 262144 | tf_op jit(solution)/shard_map/all_to_all | solution.py:468
  39.4 7.3 %copy-start.1 = (bf16[256,1024]{1,0:T(8,128)(2,1)S(1)}, bf16[256,1024]{1,0:T(8,128)(2,1)}, u32[]{:S(2)}) copy-start(bf16[256,1024]{1,0:T(8,128)(2,1)} %value_up_ref.1) | copy-start | bytes 1572868
  39.4 1.3 %collective-permute-start.7 = (bf16[16,2048]{1,0:T(8,128)(2,1)S(1)}, bf16[16,2048]{1,0:T(8,128)(2,1)S(1)}, u32[]{:S(2)}, u32[]{:S(2)}) collective-permute-start(bf16[16,2048]{1,0:T(8,128)(2,1)S(1)} %pack_rows.1.mine_ref), channel_id=1, source_target_pairs={{0,1},{1,0},{2,3},{3,2},{4,5},{5,4},{6,7},{7,6},{8,9},{9,8},{10,11... | collective-permute-start | bytes 196616 | tf_op jit(solution)/shard_map/ppermute | solution.py:339
  41.4 1.0 %copy-start.5 = (f32[2,256,1]{2,1,0:T(8,128)S(1)}, f32[2,256,1]{2,1,0:T(8,128)}, u32[]{:S(2)}) copy-start(f32[2,256,1]{2,1,0:T(8,128)} %copy-done.4) | copy-start | bytes 6148

commit v14 on v12

--- a/solution.py
+++ b/solution.py
@@ -152,7 +152,7 @@
     count = place_ref.shape[1]
     parts = []
     left = total[:count]
-    for _ in range(3):
+    for _ in range(2):
         part = left.astype(jnp.bfloat16)
         parts.append(part)
         left = left - part.astype(jnp.float32)
@@ -162,7 +162,7 @@
     for ref, target, draft in ((keep_ref, core, count), (send_ref, 1 - core, count + 16)):
         chosen = jnp.where(spot + target * slots == place_ref[...], 1.0, 0.0).astype(jnp.bfloat16)
         moved = jnp.dot(chosen, parts, preferred_element_type=jnp.float32)
-        ref[:slots, :] = moved[:, :width] + moved[:, width : 2 * width] + moved[:, 2 * width :]
+        ref[:slots, :] = moved[:, :width] + moved[:, width:]
         ref[slots:, :] = total[draft : draft + 8]
 
 
@@ -283,7 +283,7 @@
 
 
 def late_kernel(column_slot_ref, turned_ref, peak_ref, total_ref, mixed_ref, value_up_ref, *refs):
-    incoming_refs, (out_ref, rows_ref, parted_ref) = refs[:-3], refs[-3:]
+    incoming_refs, (out_ref, rows_ref, mixed_latent_ref) = refs[:-3], refs[-3:]
     slot_count, draft_count, _ = out_ref.shape
     heads_kv = value_up_ref.shape[1] // HEAD_SIZE
     group_size = QUERY_HEADS // heads_kv
@@ -292,24 +292,23 @@
     block = incoming_refs[0].shape[0]
     for n, ref in enumerate(incoming_refs):
         rows_ref[n * block : (n + 1) * block, :] = ref[...]
+    ones = jnp.ones((rows_ref.shape[0], HEAD_SIZE), jnp.bfloat16)
     for b in range(slot_count):
         scores = join_rows(lax.dot_general(turned_ref[b], rows_ref[...], NT, preferred_element_type=jnp.float32))
         scores = jnp.where(column_slot_ref[...] == b, scores, FAR)
         peak = jnp.maximum(jnp.max(scores, 1, keepdims=True), peak_ref[b])
-        weights = jnp.exp2(scores - peak)
+        weights = jnp.exp2(scores - peak).astype(jnp.bfloat16)
         fade = jnp.exp2(peak_ref[b] - peak)
-        total = total_ref[b] * fade + jnp.sum(weights, 1, keepdims=True)
-        mixed = join_rows(jnp.dot(split_rows(weights), rows_ref[...], preferred_element_type=jnp.float32))
-        parted_ref[b] = split_rows((mixed_ref[b] * fade + mixed) / total)
+        added = jnp.dot(weights, ones, preferred_element_type=jnp.float32)
+        total = total_ref[b] * fade + added[:, :1]
+        mixed = jnp.dot(weights, rows_ref[...], preferred_element_type=jnp.float32)
+        mixed_latent_ref[b] = ((mixed_ref[b] * fade + mixed) * (1.0 / total)).astype(jnp.bfloat16)
     for k in range(heads_kv):
-        part = []
-        for b in range(slot_count):
-            part.append(parted_ref[b, k * head_rows : (k + 1) * head_rows, :])
-            part.append(parted_ref[b, rows + k * head_rows : rows + (k + 1) * head_rows, :])
+        part = [mixed_latent_ref[b, k * head_rows : (k + 1) * head_rows, :] for b in range(slot_count)]
         value_up = value_up_ref[:, k * HEAD_SIZE : (k + 1) * HEAD_SIZE]
         both = jnp.dot(jnp.concatenate(part, 0), value_up, preferred_element_type=jnp.float32)
         for b in range(slot_count):
-            result = join_rows(both[b * 2 * head_rows : (b + 1) * 2 * head_rows])
+            result = both[b * head_rows : (b + 1) * head_rows]
             wide = jnp.concatenate(
                 [result[g * draft_count : (g + 1) * draft_count] for g in range(group_size)], 1
             )
@@ -575,7 +574,7 @@
         out_specs=WHOLE,
         scratch_shapes=[
             pltpu.VMEM((arrived, latent_width), bf16),
-            pltpu.VMEM((slot_count, 2 * rows, latent_width), bf16),
+            pltpu.VMEM((slot_count, rows, latent_width), bf16),
         ],
         compiler_params=params(16),
         name="late_rows",

time: 47.6 us -> 47.3 us (level)
  no operation moved by 1% of the time
where the time goes in v14:
time: 47.3 us; the launch traced here: 47 us
  starting transfers between devices  21 us (44%)
  Pallas kernels  12.9 us (27%)
  waiting for transfers between devices  11.2 us (24%)
  local copies, waits for them, and re-layouts  1.62 us (3%)
    ppermute x15, starting transfers between devices, swap(): return lax.ppermute(x, ('rep', 'wide'), pairs)  17.3 us
    ppermute x15, waiting for transfers between devices, swap(): return lax.ppermute(x, ('rep', 'wide'), pairs)  9.08 us
    pallas_call x14, Pallas kernels, call(): pl.pallas_call(kernel, out_shape=out_shape, in_specs=specs or [WHOLE] * l...  4.61 us
    pallas_call x1, Pallas kernels, local(): pl.pallas_call(functools.partial(held_kernel, arrived), out_shape=[jax.Sh...  4.01 us
    all_to_all x1, starting transfers between devices, finish(): lax.all_to_all(outgoing.reshape(8, 2 * most_rows, width), 'wide', split_a...  3.76 us
    pallas_call x1, Pallas kernels, local(): pl.pallas_call(functools.partial(window_kernel, arrived, span_rows, draft...  2.24 us
    all_to_all x1, waiting for transfers between devices, finish(): lax.all_to_all(outgoing.reshape(8, 2 * most_rows, width), 'wide', split_a...  2.13 us
    pallas_call x1, Pallas kernels, local(): pl.pallas_call(late_kernel, out_shape=jax.ShapeDtypeStruct((slot_count, d...  2.06 us
  transfers between devices with their start and end apart: 16, of which 9 were waited for; matrix products, arithmetic and copies ran while one was open for 0% of the time, Pallas kernels for 20%

profile of v14, /device:TPU:0, one launch (start us, length us, event | category | flops | bytes accessed | tf_op | source)
XLA Modules:
  0.0 47.0 jit_solution(5013429686982485192)
XLA Ops:
  0.0 0.5 collective-permute-start.8
  0.5 1.1 %start_rows.1 = (bf16[272,256]{1,0:T(8,128)(2,1)S(1)}, bf16[528,256]{1,0:T(8,128)(2,1)S(1)}, bf16[16,8192]{1,0:T(8,128)(2,1)S(1)}) custom-call(s32[1,128]{1,0:T(1,128)} %bitcast.4, bf16[512,256]{1,0:T(8,128)(2,1)} %shard_hbm.1, bf16[2,4,8192]{2,1,0:T(4,128)(2,1)} %draft_hbm.1), custom_call_target="tpu_custom_call" | custom-call | flops 1048576 | bytes 65536 | tf_op jit(solution)/shard_map/start_rows/pallas_call | solution.py:336
  1.7 3.0 %collective-permute-start.1 = (bf16[272,256]{1,0:T(8,128)(2,1)S(1)}, bf16[272,256]{1,0:T(8,128)(2,1)S(1)}, u32[]{:S(2)}, u32[]{:S(2)}) collective-permute-start(bf16[272,256]{1,0:T(8,128)(2,1)S(1)} %get-tuple-element.24.refs_0_), channel_id=1, source_target_pairs={{0,4},{1,5},{2,6},{3,7},{4,0},{5,1},{6,2},{7,3},{8,12},{9,13},{10,... | collective-permute-start | bytes 417800 | tf_op jit(solution)/shard_map/ppermute | solution.py:330
  4.7 2.6 %collective-permute-start.2 = (bf16[272,256]{1,0:T(8,128)(2,1)S(1)}, bf16[272,256]{1,0:T(8,128)(2,1)S(1)}, u32[]{:S(2)}, u32[]{:S(2)}) collective-permute-start(bf16[272,256]{1,0:T(8,128)(2,1)S(1)} %get-tuple-element.24.refs_0_), channel_id=1, source_target_pairs={{0,8},{1,9},{2,10},{3,11},{4,12},{5,13},{6,14},{7,15},{8,0},{9,1},... | collective-permute-start | bytes 417800 | tf_op jit(solution)/shard_map/ppermute | solution.py:330
  7.3 1.5 %collective-permute-start = (bf16[528,256]{1,0:T(8,128)(2,1)S(1)}, bf16[528,256]{1,0:T(8,128)(2,1)S(1)}, u32[]{:S(2)}, u32[]{:S(2)}) collective-permute-start(bf16[528,256]{1,0:T(8,128)(2,1)S(1)} %get-tuple-element.25.refs_4_), channel_id=1, source_target_pairs={{0,2},{1,3},{2,0},{3,1},{4,6},{5,7},{6,4},{7,5},{8,10},{9,11},{10,... | collective-permute-start | bytes 811016 | tf_op jit(solution)/shard_map/ppermute | solution.py:330
  8.9 0.7 %copy-done.2 = s32[2]{0:T(128)S(1)} copy-done((s32[2]{0:T(128)S(1)}, s32[2]{0:T(128)}, u32[]{:S(2)}) %copy-start.2) | copy-done | bytes 32
  9.5 4.0 %held_rows.1 = (bf16[2,512,256]{2,1,0:T(8,128)(2,1)S(1)}, f32[2,256,1]{2,1,0:T(8,128)S(1)}, f32[2,256,1]{2,1,0:T(8,128)S(1)}, f32[2,256,256]{2,1,0:T(8,128)S(1)}, bf16[2,384,256]{2,1,0:T(8,128)(2,1)S(1)}) custom-call(s32[2]{0:T(128)S(1)} %copy-done.2, bf16[2,4,8192]{2,1,0:T(4,128)(2,1)} %query_hbm.1, bf16[256,1024]{1,0:T(8,128)(2,1)} %key_up_hbm.1, ...), custom_call_target="tpu_custom_call" | custom-call | flops 2147483648 | bytes 2097152 | tf_op jit(solution)/shard_map/held_rows/pallas_call | solution.py:535
  13.6 0.5 %collective-permute-done.2.two_ref = bf16[272,256]{1,0:T(8,128)(2,1)S(1)} collective-permute-done((bf16[272,256]{1,0:T(8,128)(2,1)S(1)}, bf16[272,256]{1,0:T(8,128)(2,1)S(1)}, u32[]{:S(2)}, u32[]{:S(2)}) %collective-permute-start.2) | collective-permute-done | bytes 139296 | tf_op jit(solution)/shard_map/ppermute | solution.py:330
  14.1 1.6 %collective-permute-start.4 = (bf16[544,256]{1,0:T(8,128)(2,1)S(1)}, bf16[544,256]{1,0:T(8,128)(2,1)S(1)}, u32[]{:S(2)}, u32[]{:S(2)}) collective-permute-start(bf16[544,256]{1,0:T(8,128)(2,1)S(1)} %get-tuple-element.28.refs_2_.refs_4_), channel_id=1, source_target_pairs={{0,2},{1,3},{2,0},{3,1},{4,6},{5,7},{6,4},{7,5},{8,10},{9,11},{10,... | collective-permute-start | bytes 835592 | tf_op jit(solution)/shard_map/ppermute | solution.py:330
  15.7 0.4 collective-permute-start.5
  16.1 1.5 %collective-permute-start.9 = (bf16[512,256]{1,0:T(8,128)(2,1)S(1)}, bf16[512,256]{1,0:T(8,128)(2,1)S(1)}, u32[]{:S(2)}, u32[]{:S(2)}) collective-permute-start(bf16[512,256]{1,0:T(8,128)(2,1)S(1)} %get-tuple-element.35), channel_id=1, source_target_pairs={{0,16},{1,17},{2,18},{3,19},{4,20},{5,21},{6,22},{7,23},{8,24},{9,... | collective-permute-start | bytes 786440 | tf_op jit(solution)/shard_map/ppermute | solution.py:330
  17.6 2.7 %collective-permute-start.12 = (bf16[256,256]{1,0:T(8,128)(2,1)S(1)}, bf16[256,256]{1,0:T(8,128)(2,1)S(1)}, u32[]{:S(2)}, u32[]{:S(2)}) collective-permute-start(bf16[256,256]{1,0:T(8,128)(2,1)S(1)} %other_half.1), channel_id=1, source_target_pairs={{0,8},{1,9},{2,10},{3,11},{4,12},{5,13},{6,14},{7,15},{8,0},{9,1},... | collective-permute-start | bytes 393224 | tf_op jit(solution)/shard_map/ppermute | solution.py:330
  20.3 1.9 %collective-permute-done.5.one_ref.refs_6_.refs_5_ = bf16[272,256]{1,0:T(8,128)(2,1)S(1)} collective-permute-done((bf16[272,256]{1,0:T(8,128)(2,1)S(1)}, bf16[272,256]{1,0:T(8,128)(2,1)S(1)}, u32[]{:S(2)}, u32[]{:S(2)}) %collective-permute-start.5) | collective-permute-done | bytes 139296 | tf_op jit(solution)/shard_map/ppermute | solution.py:330
  22.2 0.6 %collective-permute-start.6 = (bf16[272,256]{1,0:T(8,128)(2,1)S(1)}, bf16[272,256]{1,0:T(8,128)(2,1)S(1)}, u32[]{:S(2)}, u32[]{:S(2)}) collective-permute-start(bf16[272,256]{1,0:T(8,128)(2,1)S(1)} %copy_piece.3), channel_id=1, source_target_pairs={{0,2},{1,3},{2,0},{3,1},{4,6},{5,7},{6,4},{7,5},{8,10},{9,11},{10,... | collective-permute-start | bytes 417800 | tf_op jit(solution)/shard_map/ppermute | solution.py:330
  22.8 1.6 %collective-permute-start.10 = (bf16[256,256]{1,0:T(8,128)(2,1)S(1)}, bf16[256,256]{1,0:T(8,128)(2,1)S(1)}, u32[]{:S(2)}, u32[]{:S(2)}) collective-permute-start(bf16[256,256]{1,0:T(8,128)(2,1)S(1)} %copy_piece.4), channel_id=1, source_target_pairs={{0,16},{1,17},{2,18},{3,19},{4,20},{5,21},{6,22},{7,23},{8,24},{9,... | collective-permute-start | bytes 393224 | tf_op jit(solution)/shard_map/ppermute | solution.py:330
  24.4 0.7 %collective-permute-done.12.refs_9_ = bf16[256,256]{1,0:T(8,128)(2,1)S(1)} collective-permute-done((bf16[256,256]{1,0:T(8,128)(2,1)S(1)}, bf16[256,256]{1,0:T(8,128)(2,1)S(1)}, u32[]{:S(2)}, u32[]{:S(2)}) %collective-permute-start.12) | collective-permute-done | bytes 131104 | tf_op jit(solution)/shard_map/ppermute | solution.py:330
  25.1 0.4 collective-permute-start.13
  25.5 0.6 %collective-permute-start.11 = (bf16[256,256]{1,0:T(8,128)(2,1)S(1)}, bf16[256,256]{1,0:T(8,128)(2,1)S(1)}, u32[]{:S(2)}, u32[]{:S(2)}) collective-permute-start(bf16[256,256]{1,0:T(8,128)(2,1)S(1)} %copy_piece.5), channel_id=1, source_target_pairs={{0,16},{1,17},{2,18},{3,19},{4,20},{5,21},{6,22},{7,23},{8,24},{9,... | collective-permute-start | bytes 393224 | tf_op jit(solution)/shard_map/ppermute | solution.py:330
  26.7 0.4 down_rows.4.refs_6_
  27.3 1.1 %collective-permute-done.10.refs_6_ = bf16[256,256]{1,0:T(8,128)(2,1)S(1)} collective-permute-done((bf16[256,256]{1,0:T(8,128)(2,1)S(1)}, bf16[256,256]{1,0:T(8,128)(2,1)S(1)}, u32[]{:S(2)}, u32[]{:S(2)}) %collective-permute-start.10) | collective-permute-done | bytes 131104 | tf_op jit(solution)/shard_map/ppermute | solution.py:330
  28.4 1.6 %collective-permute-done.13.refs_10_ = bf16[256,256]{1,0:T(8,128)(2,1)S(1)} collective-permute-done((bf16[256,256]{1,0:T(8,128)(2,1)S(1)}, bf16[256,256]{1,0:T(8,128)(2,1)S(1)}, u32[]{:S(2)}, u32[]{:S(2)}) %collective-permute-start.13) | collective-permute-done | bytes 131104 | tf_op jit(solution)/shard_map/ppermute | solution.py:330
  30.0 0.5 %collective-permute-done.11.refs_8_ = bf16[256,256]{1,0:T(8,128)(2,1)S(1)} collective-permute-done((bf16[256,256]{1,0:T(8,128)(2,1)S(1)}, bf16[256,256]{1,0:T(8,128)(2,1)S(1)}, u32[]{:S(2)}, u32[]{:S(2)}) %collective-permute-start.11) | collective-permute-done | bytes 131104 | tf_op jit(solution)/shard_map/ppermute | solution.py:330
  30.6 0.9 %down_place_rows.1 = (f32[264,256]{1,0:T(8,128)S(1)}, f32[264,256]{1,0:T(8,128)S(1)}) custom-call(bf16[128,8192]{1,0:T(8,128)(2,1)S(1)} %copy-done, bf16[128,8192]{1,0:T(8,128)(2,1)S(1)} %collective-permute-done.8.refs_1_, bf16[16,8192]{1,0:T(8,128)(2,1)S(1)} %get-tuple-element.26.mine_ref.refs_2_, ...), custom_call_target="tpu_custom_call" | custom-call | flops 67108864 | bytes 65536 | tf_op jit(solution)/shard_map/down_place_rows/pallas_call | solution.py:336
  31.6 1.5 %collective-permute-done.14.came_ref = f32[264,256]{1,0:T(8,128)S(1)} collective-permute-done((f32[264,256]{1,0:T(8,128)S(1)}, f32[264,256]{1,0:T(8,128)S(1)}, u32[]{:S(2)}, u32[]{:S(2)}) %collective-permute-start.14) | collective-permute-done | bytes 270368 | tf_op jit(solution)/shard_map/ppermute | solution.py:330
  33.1 0.7 %route_rows.1 = (f32[8,256]{1,0:T(8,128)S(1)}, bf16[256,256]{1,0:T(8,128)(2,1)}) custom-call(f32[264,256]{1,0:T(8,128)S(1)} %get-tuple-element.36.keep_ref, f32[264,256]{1,0:T(8,128)S(1)} %collective-permute-done.14.came_ref), custom_call_target="tpu_custom_call" | custom-call | flops 1048576 | bytes 65536 | tf_op jit(solution)/shard_map/route_rows/pallas_call | solution.py:336
  33.8 3.8 %all-to-all-start = ((bf16[8,32,256]{2,1,0:T(8,128)(2,1)}), bf16[8,32,256]{2,1,0:T(8,128)(2,1)S(1)}, u32[]{:S(2)}, u32[]{:S(2)}) async-start(bf16[8,32,256]{2,1,0:T(8,128)(2,1)} %bitcast.1), calls=%async_computation | async-start | bytes 262144 | tf_op jit(solution)/shard_map/all_to_all | solution.py:456
  37.7 1.2 %collective-permute-done.7.other_ref = bf16[16,2048]{1,0:T(8,128)(2,1)S(1)} collective-permute-done((bf16[16,2048]{1,0:T(8,128)(2,1)S(1)}, bf16[16,2048]{1,0:T(8,128)(2,1)S(1)}, u32[]{:S(2)}, u32[]{:S(2)}) %collective-permute-start.7) | collective-permute-done | bytes 65568 | tf_op jit(solution)/shard_map/ppermute | solution.py:330
  38.9 0.7 %count_rows.1 = (s32[2,128]{1,0:T(2,128)S(1)}, s32[1,256]{1,0:T(1,128)S(1)}) custom-call(s32[2]{0:T(128)S(1)} %copy-done.3, bf16[16,2048]{1,0:T(8,128)(2,1)S(1)} %pack_rows.1.mine_ref, bf16[16,2048]{1,0:T(8,128)(2,1)S(1)} %collective-permute-done.7.other_ref), custom_call_target="tpu_custom_call" | custom-call | flops 1048576 | bytes 65536 | tf_op jit(solution)/shard_map/count_rows/pallas_call | solution.py:336
  39.6 0.9 %copy-done.5 = f32[2,256,1]{2,1,0:T(8,128)S(1)} copy-done((f32[2,256,1]{2,1,0:T(8,128)S(1)}, f32[2,256,1]{2,1,0:T(8,128)}, u32[]{:S(2)}) %copy-start.5) | copy-done | bytes 2072
  40.5 2.2 %window_rows.1 = (f32[2,256,1]{2,1,0:T(8,128)S(1)}, f32[2,256,1]{2,1,0:T(8,128)S(1)}, f32[2,256,256]{2,1,0:T(8,128)S(1)}) custom-call(s32[2]{0:T(128)S(1)} %copy-done.3, s32[2,128]{1,0:T(2,128)S(1)} %get-tuple-element.31.limit_ref, bf16[2,512,256]{2,1,0:T(8,128)(2,1)S(1)} %get-tuple-element.30.turned_ref, ...), custom_call_target="tpu_custom_call" | custom-call | flops 1073741824 | bytes 65536 | tf_op jit(solution)/shard_map/window_rows/pallas_call | solution.py:561
  42.8 2.1 %all-to-all-done = bf16[8,32,256]{2,1,0:T(8,128)(2,1)S(1)} async-done(((bf16[8,32,256]{2,1,0:T(8,128)(2,1)}), bf16[8,32,256]{2,1,0:T(8,128)(2,1)S(1)}, u32[]{:S(2)}, u32[]{:S(2)}) %all-to-all-start) | async-done | bytes 131104 | tf_op jit(solution)/shard_map/all_to_all | solution.py:456
  44.9 2.1 %late_rows.1 = bf16[2,4,8192]{2,1,0:T(4,128)(2,1)} custom-call(s32[1,256]{1,0:T(1,128)S(1)} %get-tuple-element.29.column_slot_ref, bf16[2,512,256]{2,1,0:T(8,128)(2,1)S(1)} %get-tuple-element.30.turned_ref, f32[2,256,1]{2,1,0:T(8,128)S(1)} %get-tuple-element.39.peak_ref, f32[2,256,1]{2,1,0:T(8,128)S(1)} %get-tuple-element.40.total_ref, ...), custom_call_target="tpu_custom_call" | custom-call | tf_op jit(solution)/shard_map/late_rows/pallas_call | solution.py:570
  (29 shorter events, 1.2 us)
Async XLA Ops:
  0.0 25.5 %collective-permute-start.8 = (bf16[128,8192]{1,0:T(8,128)(2,1)}, bf16[128,8192]{1,0:T(8,128)(2,1)S(1)}, u32[]{:S(2)}, u32[]{:S(2)}) collective-permute-start(bf16[128,8192]{1,0:T(8,128)(2,1)} %refs_0_.7), channel_id=1, source_target_pairs={{0,1},{1,0},{2,3},{3,2},{4,5},{5,4},{6,7},{7,6},{8,9},{9,8},{10,11... | collective-permute-start | bytes 6291464 | tf_op jit(solution)/shard_map/ppermute | solution.py:330
  1.6 12.5 %collective-permute-start.3 = (bf16[16,8192]{1,0:T(8,128)(2,1)S(1)}, bf16[16,8192]{1,0:T(8,128)(2,1)S(1)}, u32[]{:S(2)}, u32[]{:S(2)}) collective-permute-start(bf16[16,8192]{1,0:T(8,128)(2,1)S(1)} %get-tuple-element.26.mine_ref.refs_2_), channel_id=1, source_target_pairs={{0,1},{1,0},{2,3},{3,2},{4,5},{5,4},{6,7},{7,6},{8,9},{9,8},{10,11... | collective-permute-start | bytes 786440 | tf_op jit(solution)/shard_map/ppermute | solution.py:330
  1.7 11.8 %collective-permute-start.1 = (bf16[272,256]{1,0:T(8,128)(2,1)S(1)}, bf16[272,256]{1,0:T(8,128)(2,1)S(1)}, u32[]{:S(2)}, u32[]{:S(2)}) collective-permute-start(bf16[272,256]{1,0:T(8,128)(2,1)S(1)} %get-tuple-element.24.refs_0_), channel_id=1, source_target_pairs={{0,4},{1,5},{2,6},{3,7},{4,0},{5,1},{6,2},{7,3},{8,12},{9,13},{10,... | collective-permute-start | bytes 417800 | tf_op jit(solution)/shard_map/ppermute | solution.py:330
  4.7 9.3 %collective-permute-start.2 = (bf16[272,256]{1,0:T(8,128)(2,1)S(1)}, bf16[272,256]{1,0:T(8,128)(2,1)S(1)}, u32[]{:S(2)}, u32[]{:S(2)}) collective-permute-start(bf16[272,256]{1,0:T(8,128)(2,1)S(1)} %get-tuple-element.24.refs_0_), channel_id=1, source_target_pairs={{0,8},{1,9},{2,10},{3,11},{4,12},{5,13},{6,14},{7,15},{8,0},{9,1},... | collective-permute-start | bytes 417800 | tf_op jit(solution)/shard_map/ppermute | solution.py:330
  7.3 10.3 %collective-permute-start = (bf16[528,256]{1,0:T(8,128)(2,1)S(1)}, bf16[528,256]{1,0:T(8,128)(2,1)S(1)}, u32[]{:S(2)}, u32[]{:S(2)}) collective-permute-start(bf16[528,256]{1,0:T(8,128)(2,1)S(1)} %get-tuple-element.25.refs_4_), channel_id=1, source_target_pairs={{0,2},{1,3},{2,0},{3,1},{4,6},{5,7},{6,4},{7,5},{8,10},{9,11},{10,... | collective-permute-start | bytes 811016 | tf_op jit(solution)/shard_map/ppermute | solution.py:330
  8.8 0.7 %copy-start.2 = (s32[2]{0:T(128)S(1)}, s32[2]{0:T(128)}, u32[]{:S(2)}) copy-start(s32[2]{0:T(128)} %context_ref.5) | copy-start | bytes 28
  13.5 13.1 %copy-start.4 = (f32[2,256,1]{2,1,0:T(8,128)}, f32[2,256,1]{2,1,0:T(8,128)S(1)}, u32[]{:S(2)}) copy-start(f32[2,256,1]{2,1,0:T(8,128)S(1)} %get-tuple-element.32.total_ref) | copy-start | bytes 6148
  13.5 12.8 %copy-start = (bf16[128,8192]{1,0:T(8,128)(2,1)S(1)}, bf16[128,8192]{1,0:T(8,128)(2,1)}, u32[]{:S(2)}) copy-start(bf16[128,8192]{1,0:T(8,128)(2,1)} %refs_0_.7) | copy-start | bytes 6291460
  14.1 8.0 %collective-permute-start.4 = (bf16[544,256]{1,0:T(8,128)(2,1)S(1)}, bf16[544,256]{1,0:T(8,128)(2,1)S(1)}, u32[]{:S(2)}, u32[]{:S(2)}) collective-permute-start(bf16[544,256]{1,0:T(8,128)(2,1)S(1)} %get-tuple-element.28.refs_2_.refs_4_), channel_id=1, source_target_pairs={{0,2},{1,3},{2,0},{3,1},{4,6},{5,7},{6,4},{7,5},{8,10},{9,11},{10,... | collective-permute-start | bytes 835592 | tf_op jit(solution)/shard_map/ppermute | solution.py:330
  15.7 6.5 %collective-permute-start.5 = (bf16[272,256]{1,0:T(8,128)(2,1)S(1)}, bf16[272,256]{1,0:T(8,128)(2,1)S(1)}, u32[]{:S(2)}, u32[]{:S(2)}) collective-permute-start(bf16[272,256]{1,0:T(8,128)(2,1)S(1)} %collective-permute-done.2.two_ref), channel_id=1, source_target_pairs={{0,4},{1,5},{2,6},{3,7},{4,0},{5,1},{6,2},{7,3},{8,12},{9,13},{10,... | collective-permute-start | bytes 417800 | tf_op jit(solution)/shard_map/ppermute | solution.py:330
  16.1 10.9 %collective-permute-start.9 = (bf16[512,256]{1,0:T(8,128)(2,1)S(1)}, bf16[512,256]{1,0:T(8,128)(2,1)S(1)}, u32[]{:S(2)}, u32[]{:S(2)}) collective-permute-start(bf16[512,256]{1,0:T(8,128)(2,1)S(1)} %get-tuple-element.35), channel_id=1, source_target_pairs={{0,16},{1,17},{2,18},{3,19},{4,20},{5,21},{6,22},{7,23},{8,24},{9,... | collective-permute-start | bytes 786440 | tf_op jit(solution)/shard_map/ppermute | solution.py:330
  17.6 7.4 %collective-permute-start.12 = (bf16[256,256]{1,0:T(8,128)(2,1)S(1)}, bf16[256,256]{1,0:T(8,128)(2,1)S(1)}, u32[]{:S(2)}, u32[]{:S(2)}) collective-permute-start(bf16[256,256]{1,0:T(8,128)(2,1)S(1)} %other_half.1), channel_id=1, source_target_pairs={{0,8},{1,9},{2,10},{3,11},{4,12},{5,13},{6,14},{7,15},{8,0},{9,1},... | collective-permute-start | bytes 393224 | tf_op jit(solution)/shard_map/ppermute | solution.py:330
  22.2 8.4 %collective-permute-start.6 = (bf16[272,256]{1,0:T(8,128)(2,1)S(1)}, bf16[272,256]{1,0:T(8,128)(2,1)S(1)}, u32[]{:S(2)}, u32[]{:S(2)}) collective-permute-start(bf16[272,256]{1,0:T(8,128)(2,1)S(1)} %copy_piece.3), channel_id=1, source_target_pairs={{0,2},{1,3},{2,0},{3,1},{4,6},{5,7},{6,4},{7,5},{8,10},{9,11},{10,... | collective-permute-start | bytes 417800 | tf_op jit(solution)/shard_map/ppermute | solution.py:330
  22.8 5.6 %collective-permute-start.10 = (bf16[256,256]{1,0:T(8,128)(2,1)S(1)}, bf16[256,256]{1,0:T(8,128)(2,1)S(1)}, u32[]{:S(2)}, u32[]{:S(2)}) collective-permute-start(bf16[256,256]{1,0:T(8,128)(2,1)S(1)} %copy_piece.4), channel_id=1, source_target_pairs={{0,16},{1,17},{2,18},{3,19},{4,20},{5,21},{6,22},{7,23},{8,24},{9,... | collective-permute-start | bytes 393224 | tf_op jit(solution)/shard_map/ppermute | solution.py:330
  25.1 5.0 %collective-permute-start.13 = (bf16[256,256]{1,0:T(8,128)(2,1)S(1)}, bf16[256,256]{1,0:T(8,128)(2,1)S(1)}, u32[]{:S(2)}, u32[]{:S(2)}) collective-permute-start(bf16[256,256]{1,0:T(8,128)(2,1)S(1)} %collective-permute-done.12.refs_9_), channel_id=1, source_target_pairs={{0,4},{1,5},{2,6},{3,7},{4,0},{5,1},{6,2},{7,3},{8,12},{9,13},{10,... | collective-permute-start | bytes 393224 | tf_op jit(solution)/shard_map/ppermute | solution.py:330
  25.5 5.0 %collective-permute-start.11 = (bf16[256,256]{1,0:T(8,128)(2,1)S(1)}, bf16[256,256]{1,0:T(8,128)(2,1)S(1)}, u32[]{:S(2)}, u32[]{:S(2)}) collective-permute-start(bf16[256,256]{1,0:T(8,128)(2,1)S(1)} %copy_piece.5), channel_id=1, source_target_pairs={{0,16},{1,17},{2,18},{3,19},{4,20},{5,21},{6,22},{7,23},{8,24},{9,... | collective-permute-start | bytes 393224 | tf_op jit(solution)/shard_map/ppermute | solution.py:330
  31.5 7.4 %copy-start.3 = (s32[2]{0:T(128)S(1)}, s32[2]{0:T(128)}, u32[]{:S(2)}) copy-start(s32[2]{0:T(128)} %context_ref.5) | copy-start | bytes 28
  31.5 1.6 %collective-permute-start.14 = (f32[264,256]{1,0:T(8,128)S(1)}, f32[264,256]{1,0:T(8,128)S(1)}, u32[]{:S(2)}, u32[]{:S(2)}) collective-permute-start(f32[264,256]{1,0:T(8,128)S(1)} %get-tuple-element.37), channel_id=1, source_target_pairs={{0,1},{1,0},{2,3},{3,2},{4,5},{5,4},{6,7},{7,6},{8,9},{9,8},{10,11... | collective-permute-start | bytes 811016 | tf_op jit(solution)/shard_map/ppermute | solution.py:330
  33.8 11.1 %all-to-all-start = ((bf16[8,32,256]{2,1,0:T(8,128)(2,1)}), bf16[8,32,256]{2,1,0:T(8,128)(2,1)S(1)}, u32[]{:S(2)}, u32[]{:S(2)}) async-start(bf16[8,32,256]{2,1,0:T(8,128)(2,1)} %bitcast.1), calls=%async_computation | async-start | bytes 262144 | tf_op jit(solution)/shard_map/all_to_all | solution.py:456
  37.6 7.3 %copy-start.1 = (bf16[256,1024]{1,0:T(8,128)(2,1)S(1)}, bf16[256,1024]{1,0:T(8,128)(2,1)}, u32[]{:S(2)}) copy-start(bf16[256,1024]{1,0:T(8,128)(2,1)} %value_up_ref.1) | copy-start | bytes 1572868
  37.6 1.3 %collective-permute-start.7 = (bf16[16,2048]{1,0:T(8,128)(2,1)S(1)}, bf16[16,2048]{1,0:T(8,128)(2,1)S(1)}, u32[]{:S(2)}, u32[]{:S(2)}) collective-permute-start(bf16[16,2048]{1,0:T(8,128)(2,1)S(1)} %pack_rows.1.mine_ref), channel_id=1, source_target_pairs={{0,1},{1,0},{2,3},{3,2},{4,5},{5,4},{6,7},{7,6},{8,9},{9,8},{10,11... | collective-permute-start | bytes 196616 | tf_op jit(solution)/shard_map/ppermute | solution.py:330
  39.6 1.0 %copy-start.5 = (f32[2,256,1]{2,1,0:T(8,128)S(1)}, f32[2,256,1]{2,1,0:T(8,128)}, u32[]{:S(2)}) copy-start(f32[2,256,1]{2,1,0:T(8,128)} %copy-done.4) | copy-start | bytes 6148
